TPU v7x, 32 devices: a whole 2x2x4 slice. The times are simulated.
32 devices in a mesh: crop: 2 (over y), dap: 8 (over z, x), sub: 2 (over core).
Axes of the slice: x: 2, y: 2, z: 4, core: 2. Of those that a mesh axis runs over, the one named last changes fastest.
Arguments:
- pairwise_state: bfloat16 [64, 32, 128], P(('crop', 'dap', 'sub')), parts along dimension 0, may hold values from -27 to 27, as said below
- alignment_state: bfloat16 [64, 32, 256], P('crop', ('dap', 'sub')), parts along dimension 0, may hold values from -27 to 27, as said below
- alignment_mask: int32 [64, 32], P('crop', ('dap', 'sub')), parts along dimension 0, may hold values 0 or 1
- residue_crop_mask: int32 [64], P('crop'), parts along dimension 0, may hold values from 0 to 1, as said below
- outer_input_weight: bfloat16 [2, 256, 32], replicated, may hold values from -0.375 to 0.375
- outer_output_weight: bfloat16 [32, 32, 128], replicated, may hold values from -0.1875 to 0.1875
- triangle_input_weight: bfloat16 [4, 128, 128], replicated, may hold values from -0.5 to 0.5
- triangle_gate: bfloat16 [128, 128], replicated, may hold values from -0.5 to 0.5
- triangle_output_weight: bfloat16 [128, 128], replicated, may hold values from -0.5 to 0.5
- transition_up_weight: bfloat16 [128, 512], replicated, may hold values from -0.5 to 0.5
- transition_down_weight: bfloat16 [512, 128], replicated, may hold values from -0.25 to 0.25
Outputs:
- pair_out: bfloat16 [64, 32, 128], P(('crop', 'dap', 'sub')), parts along dimension 0
There are 2 independent parts, one for each index of `crop`. A program takes and returns all parts, laid end to end along the dimension named above; an argument that names none is the same for every part. Nothing has to cross between parts.
Inputs may be any that keep to these rules, and one draw needn't show every extreme that they name: `residue_crop_mask`: 0 on every residue after the crop's end, which lies at 16 or later and before 32; inside the crop a residue may also be 0. `pairwise_state`: finite real values. `alignment_state`: finite real values.
All inputs are finite; a program needn't handle non-finite values. No bound on the sum of `alignment_mask` on one device may be relied on, other than what follows from the above.
Results may differ from a plain program's by a relative error of at most 0.0075.
Values may be sent and summed in bfloat16 or wider, within the bound.
No kernel may reach another device: no remote copies, remote signals or barrier semaphores. Data moves between devices by JAX's collectives and lax.ppermute only.
A program may use at most 64 MiB of HBM per device.

v0:
```python
import jax
import jax.numpy as jnp
from jax import lax
from jax.sharding import PartitionSpec as P


def norm_layer(values, reduce_axis):
    average = jnp.mean(values, axis=reduce_axis, keepdims=True)
    centered = values - average
    variance = jnp.mean(centered * centered, axis=reduce_axis, keepdims=True)
    return centered * lax.rsqrt(variance + 1e-05)


def shards(
    pairwise_state,
    alignment_state,
    alignment_mask,
    residue_crop_mask,
    outer_input_weight,
    outer_output_weight,
    triangle_input_weight,
    triangle_gate,
    triangle_output_weight,
    transition_up_weight,
    transition_down_weight,
):
    row_count = pairwise_state.shape[0]
    start_row = lax.axis_index(("dap", "sub")) * row_count
    row_presence_mask = lax.dynamic_slice_in_dim(residue_crop_mask, start_row, row_count, 0).astype(
        jnp.float32
    )
    full_mask = residue_crop_mask.astype(jnp.float32)
    alignment_keep = alignment_mask.astype(jnp.float32) * row_presence_mask[None, :]
    alignment_normed = norm_layer(alignment_state.astype(jnp.float32), -1).astype(jnp.bfloat16)
    left_alignment = (
        jnp.einsum(
            "pxm,my->pxy",
            alignment_normed,
            outer_input_weight[0],
            preferred_element_type=jnp.float32,
        )
        * alignment_keep[:, :, None]
    ).astype(jnp.bfloat16)
    right_alignment = (
        jnp.einsum(
            "pxm,my->pxy",
            alignment_normed,
            outer_input_weight[1],
            preferred_element_type=jnp.float32,
        )
        * alignment_keep[:, :, None]
    ).astype(jnp.bfloat16)
    inner_alignment = jnp.einsum(
        "tqu,ulx->tqlx", left_alignment, outer_output_weight, preferred_element_type=jnp.float32
    ).astype(jnp.bfloat16)
    right_portion = lax.all_gather(right_alignment, ("dap", "sub"), axis=1, tiled=True)
    keep_portion = lax.all_gather(
        alignment_keep.astype(jnp.bfloat16), ("dap", "sub"), axis=1, tiled=True
    )
    numerator_sum = jnp.einsum(
        "zkwv,znw->knv", inner_alignment, right_portion, preferred_element_type=jnp.float32
    )
    pair_norm_count = jnp.einsum("cf,cg->fg", alignment_keep, keep_portion.astype(jnp.float32))
    block_part = numerator_sum / jnp.maximum(pair_norm_count, 1.0)[:, :, None]
    pair_one = (pairwise_state.astype(jnp.float32) + block_part).astype(jnp.bfloat16)
    ln_one = norm_layer(pair_one.astype(jnp.float32), -1).astype(jnp.bfloat16)
    pair_keep = row_presence_mask[:, None] * full_mask[None, :]

    def operand(gate_w, proj_w):
        gate_val = jnp.einsum("ijc,cd->dij", ln_one, gate_w, preferred_element_type=jnp.float32)
        proj_val = jnp.einsum("ijc,cd->dij", ln_one, proj_w, preferred_element_type=jnp.float32)
        return (jax.nn.sigmoid(gate_val) * proj_val * pair_keep[None]).astype(jnp.bfloat16)

    left_tri = operand(triangle_input_weight[0], triangle_input_weight[1])
    right_tri = operand(triangle_input_weight[2], triangle_input_weight[3])
    near_right = lax.all_gather(right_tri, "sub", axis=1, tiled=True)
    left_cols, right_all = (
        lax.all_to_all(left_tri, "dap", split_axis=0, concat_axis=1, tiled=True),
        lax.all_to_all(near_right, "dap", split_axis=0, concat_axis=1, tiled=True),
    )
    product = jnp.einsum(
        "cik,cjk->cij", left_cols, right_all, preferred_element_type=jnp.float32
    ).astype(jnp.bfloat16)
    returned = lax.all_to_all(product, "dap", split_axis=1, concat_axis=0, tiled=True)
    normed = norm_layer(returned.astype(jnp.float32), 0).astype(jnp.bfloat16)
    update = jnp.einsum(
        "cij,cd->ijd", normed, triangle_output_weight, preferred_element_type=jnp.float32
    )
    gate_out = jax.nn.sigmoid(
        jnp.einsum("ijc,cd->ijd", ln_one, triangle_gate, preferred_element_type=jnp.float32)
    )
    pair_two = (pair_one.astype(jnp.float32) + gate_out * update).astype(jnp.bfloat16)
    ln_two = norm_layer(pair_two.astype(jnp.float32), -1).astype(jnp.bfloat16)

    def transition(row_pair):
        row_ln, row_base = row_pair
        hidden = jax.nn.relu(
            jnp.dot(row_ln, transition_up_weight, preferred_element_type=jnp.float32)
        ).astype(jnp.bfloat16)
        return (
            row_base.astype(jnp.float32)
            + jnp.dot(hidden, transition_down_weight, preferred_element_type=jnp.float32)
        ).astype(jnp.bfloat16)

    return lax.map(transition, (ln_two, pair_two))


def solution(mesh):
    placed = (
        P(("crop", "dap", "sub"), None, None),
        P("crop", ("dap", "sub"), None),
        P("crop", ("dap", "sub")),
        P("crop"),
        P(),
        P(),
        P(),
        P(),
        P(),
        P(),
        P(),
    )
    return jax.shard_map(
        shards,
        mesh=mesh,
        in_specs=placed,
        out_specs=P(("crop", "dap", "sub"), None, None),
        check_vma=False,
    )
```

profile of v0, /device:TPU:0, one launch (start us, length us, event | category | flops | bytes accessed | tf_op | source)
XLA Modules:
  0.0 80.6 jit_solution(18318766200545910510)
XLA Ops:
  0.0 0.9 %convert_reduce_fusion = f32[32,2]{1,0:T(8,128)S(1)} fusion(bf16[32,2,256]{2,1,0:T(2,128)(2,1)} %param.14), kind=kLoop, calls=%fused_computation.60 | loop fusion | flops 32704 | bytes 33024 | tf_op jit(solution)/shard_map/reduce_sum | solution.py:8
  1.3 0.6 copy-done.11
  2.1 0.6 copy-done.5
  3.0 23.0 %all-gather = bf16[16,2,32]{2,1,0:T(2,128)(2,1)S(1)} all-gather(bf16[1,2,32]{2,1,0:T(2,128)(2,1)S(1)} %get-tuple-element.50), channel_id=1, replica_groups=mesh['crop'=2,'dap'=8,'sub'=2] {'dap','sub'}, dimensions={0}, use_global_device_ids=true | all-gather | bytes 2176 | tf_op jit(solution)/shard_map/all_gather | solution.py:57
  26.1 18.1 %all_gather.9 = bf16[32,32,32]{2,0,1:T(8,128)(2,1)S(1)} all-gather(bf16[32,2,32]{2,0,1:T(8,128)(2,1)S(1)} %fusion.30), channel_id=1, replica_groups=mesh['crop'=2,'dap'=8,'sub'=2] {'dap','sub'}, dimensions={1}, use_global_device_ids=true | all-gather | bytes 69632 | tf_op jit(solution)/shard_map/all_gather | solution.py:56
  44.2 0.4 copy.24
  44.6 0.5 copy-done.6
  45.1 0.6 fusion.73
  46.5 0.7 reshape.104
  47.2 3.3 %all-to-all-start = ((bf16[8,2,512]{2,1,0:T(2,128)(2,1)}), bf16[8,2,512]{2,1,0:T(2,128)(2,1)S(1)}, u32[]{:S(2)}, u32[]{:S(2)}) async-start(bf16[8,2,512]{2,1,0:T(2,128)(2,1)} %reshape.104), calls=%async_computation | async-start | bytes 32768 | tf_op jit(solution)/shard_map/all_to_all | solution.py:78
  50.8 1.9 %all_gather.11 = bf16[128,4,32]{0,2,1:T(8,128)(2,1)S(1)} all-gather(bf16[128,2,32]{0,2,1:T(8,128)(2,1)S(1)} %fusion.37), channel_id=1, replica_groups=mesh['crop'=2,'dap'=8,'sub'=2] {'sub'}, dimensions={1}, use_global_device_ids=true | all-gather | bytes 49152 | tf_op jit(solution)/shard_map/all_gather | solution.py:76
  52.8 0.8 reshape.106
  53.6 3.5 %all-to-all-done = bf16[8,2,512]{2,1,0:T(2,128)(2,1)S(1)} async-done(((bf16[8,2,512]{2,1,0:T(2,128)(2,1)}), bf16[8,2,512]{2,1,0:T(2,128)(2,1)S(1)}, u32[]{:S(2)}, u32[]{:S(2)}) %all-to-all-start) | async-done | bytes 16416 | tf_op jit(solution)/shard_map/all_to_all | solution.py:78
  57.1 3.3 %all-to-all-start.1 = ((bf16[8,2,1024]{2,1,0:T(2,128)(2,1)}), bf16[8,2,1024]{2,1,0:T(2,128)(2,1)S(1)}, u32[]{:S(2)}, u32[]{:S(2)}) async-start(bf16[8,2,1024]{2,1,0:T(2,128)(2,1)} %reshape.106), calls=%async_computation.1 | async-start | bytes 65536 | tf_op jit(solution)/shard_map/all_to_all | solution.py:79
  60.6 6.4 %all-to-all-done.1 = bf16[8,2,1024]{2,1,0:T(2,128)(2,1)S(1)} async-done(((bf16[8,2,1024]{2,1,0:T(2,128)(2,1)}), bf16[8,2,1024]{2,1,0:T(2,128)(2,1)S(1)}, u32[]{:S(2)}, u32[]{:S(2)}) %all-to-all-start.1) | async-done | bytes 32800 | tf_op jit(solution)/shard_map/all_to_all | solution.py:79
  67.5 0.7 reshape.108
  68.2 3.5 %all-to-all-start.2 = ((bf16[8,2,512]{2,1,0:T(2,128)(2,1)}), bf16[8,2,512]{2,1,0:T(2,128)(2,1)S(1)}, u32[]{:S(2)}, u32[]{:S(2)}) async-start(bf16[8,2,512]{2,1,0:T(2,128)(2,1)} %reshape.108), calls=%async_computation.2 | async-start | bytes 32768 | tf_op jit(solution)/shard_map/all_to_all | solution.py:84
  71.9 6.3 %all-to-all-done.2 = bf16[8,2,512]{2,1,0:T(2,128)(2,1)S(1)} async-done(((bf16[8,2,512]{2,1,0:T(2,128)(2,1)}), bf16[8,2,512]{2,1,0:T(2,128)(2,1)S(1)}, u32[]{:S(2)}, u32[]{:S(2)}) %all-to-all-start.2) | async-done | bytes 16416 | tf_op jit(solution)/shard_map/all_to_all | solution.py:84
  78.5 0.3 convert_reduce_fusion.1
  79.1 0.3 copy-done.2
  79.4 0.5 while.10
  79.4 0.3 fusion.96
  79.7 0.3 fusion.96
  80.0 0.6 copy-done.10
  (62 shorter events, 3.3 us)
Async XLA Ops:
  0.0 78.5 %copy-start = (bf16[128,128]{1,0:T(8,128)(2,1)S(1)}, bf16[128,128]{1,0:T(8,128)(2,1)}, u32[]{:S(2)}) copy-start(bf16[128,128]{1,0:T(8,128)(2,1)} %param.21) | copy-start | bytes 98308
  0.0 1.0 %copy-start.3 = (bf16[32,2,256]{2,1,0:T(2,128)(2,1)S(1)}, bf16[32,2,256]{2,1,0:T(2,128)(2,1)}, u32[]{:S(2)}) copy-start(bf16[32,2,256]{2,1,0:T(2,128)(2,1)} %param.14) | copy-start | bytes 98308
  1.2 1.6 %copy-start.7 = (bf16[2,256,32]{1,2,0:T(8,128)(2,1)S(1)}, bf16[2,256,32]{1,2,0:T(8,128)(2,1)}, u32[]{:S(2)}) copy-start(bf16[2,256,32]{1,2,0:T(8,128)(2,1)} %param.17) | copy-start | bytes 98308
  1.3 0.7 copy-start.11
  2.0 0.7 copy-start.5
  44.2 0.9 %copy-start.6 = (bf16[32,32,128]{2,1,0:T(8,128)(2,1)S(1)}, bf16[32,32,128]{2,1,0:T(8,128)(2,1)}, u32[]{:S(2)}) copy-start(bf16[32,32,128]{2,1,0:T(8,128)(2,1)} %param.18) | copy-start | bytes 786436
  44.2 1.0 %copy-start.9 = (bf16[2,32,128]{2,1,0:T(8,128)(2,1)S(1)}, bf16[2,32,128]{2,1,0:T(8,128)(2,1)}, u32[]{:S(2)}) copy-start(bf16[2,32,128]{2,1,0:T(8,128)(2,1)} %param.13) | copy-start | bytes 49156
  45.1 0.9 %copy-start.4 = (bf16[4,128,128]{2,1,0:T(8,128)(2,1)S(1)}, bf16[4,128,128]{2,1,0:T(8,128)(2,1)}, u32[]{:S(2)}) copy-start(bf16[4,128,128]{2,1,0:T(8,128)(2,1)} %param.19) | copy-start | bytes 393220
  47.2 9.9 %all-to-all-start = ((bf16[8,2,512]{2,1,0:T(2,128)(2,1)}), bf16[8,2,512]{2,1,0:T(2,128)(2,1)S(1)}, u32[]{:S(2)}, u32[]{:S(2)}) async-start(bf16[8,2,512]{2,1,0:T(2,128)(2,1)} %reshape.104), calls=%async_computation | async-start | bytes 32768 | tf_op jit(solution)/shard_map/all_to_all | solution.py:78
  57.1 10.0 %all-to-all-start.1 = ((bf16[8,2,1024]{2,1,0:T(2,128)(2,1)}), bf16[8,2,1024]{2,1,0:T(2,128)(2,1)S(1)}, u32[]{:S(2)}, u32[]{:S(2)}) async-start(bf16[8,2,1024]{2,1,0:T(2,128)(2,1)} %reshape.106), calls=%async_computation.1 | async-start | bytes 65536 | tf_op jit(solution)/shard_map/all_to_all | solution.py:79
  68.2 3.5 %copy-start.8 = (bf16[128,128]{1,0:T(8,128)(2,1)S(1)}, bf16[128,128]{1,0:T(8,128)(2,1)}, u32[]{:S(2)}) copy-start(bf16[128,128]{1,0:T(8,128)(2,1)} %param.20) | copy-start | bytes 98308
  68.2 10.0 %all-to-all-start.2 = ((bf16[8,2,512]{2,1,0:T(2,128)(2,1)}), bf16[8,2,512]{2,1,0:T(2,128)(2,1)S(1)}, u32[]{:S(2)}, u32[]{:S(2)}) async-start(bf16[8,2,512]{2,1,0:T(2,128)(2,1)} %reshape.108), calls=%async_computation.2 | async-start | bytes 32768 | tf_op jit(solution)/shard_map/all_to_all | solution.py:84
  78.5 0.9 %copy-start.2 = (bf16[512,128]{1,0:T(8,128)(2,1)S(1)}, bf16[512,128]{1,0:T(8,128)(2,1)}, u32[]{:S(2)}) copy-start(bf16[512,128]{1,0:T(8,128)(2,1)} %param.23) | copy-start | bytes 393220
  78.5 0.9 %copy-start.1 = (bf16[128,512]{1,0:T(8,128)(2,1)S(1)}, bf16[128,512]{1,0:T(8,128)(2,1)}, u32[]{:S(2)}) copy-start(bf16[128,512]{1,0:T(8,128)(2,1)} %param.22) | copy-start | bytes 393220
  80.0 0.6 copy-start.10
where the time goes:
time: 81.2 us; the launch traced here: 80.6 us
  blocking collectives  43 us (53%)
  waiting for transfers between devices  16.2 us (20%)
  starting transfers between devices  10.1 us (12%)
  local copies, waits for them, and re-layouts  6.32 us (8%)
  matrix products  2.43 us (3%)
  other arithmetic  2.14 us (3%)
    all_gather x1, blocking collectives, shards(): lax.all_gather(alignment_keep.astype(jnp.bfloat16), ('dap', 'sub'), axis=...  23 us
    all_gather x1, blocking collectives, shards(): lax.all_gather(right_alignment, ('dap', 'sub'), axis=1, tiled=True)  18.1 us
    all_to_all x1, waiting for transfers between devices, shards(): lax.all_to_all(near_right, 'dap', split_axis=0, concat_axis=1, tiled=True)  6.42 us
    all_to_all x1, waiting for transfers between devices, shards(): lax.all_to_all(product, 'dap', split_axis=1, concat_axis=0, tiled=True)  6.34 us
    unnamed x30, local copies, waits for them, and re-layouts  5.32 us
    all_to_all x1, waiting for transfers between devices, shards(): lax.all_to_all(left_tri, 'dap', split_axis=0, concat_axis=1, tiled=True)  3.48 us
    all_to_all x1, starting transfers between devices, shards(): lax.all_to_all(product, 'dap', split_axis=1, concat_axis=0, tiled=True)  3.47 us
    all_to_all x1, starting transfers between devices, shards(): lax.all_to_all(left_tri, 'dap', split_axis=0, concat_axis=1, tiled=True)  3.34 us
  transfers between devices with their start and end apart: 3, of which 3 were waited for; matrix products, arithmetic and copies ran while one was open for 2% of the time, Pallas kernels for 0%

commit v1 on v0

--- a/solution.py
+++ b/solution.py
@@ -2,6 +2,8 @@
 import jax.numpy as jnp
 from jax import lax
 from jax.sharding import PartitionSpec as P
+
+REPLICATED_PAIR_BYTES = 1 << 20
 
 
 def norm_layer(values, reduce_axis):
@@ -9,6 +11,111 @@
     centered = values - average
     variance = jnp.mean(centered * centered, axis=reduce_axis, keepdims=True)
     return centered * lax.rsqrt(variance + 1e-05)
+
+
+def transition(ln_two, pair_two, transition_up_weight, transition_down_weight):
+    hidden = jax.nn.relu(
+        jnp.dot(ln_two, transition_up_weight, preferred_element_type=jnp.float32)
+    ).astype(jnp.bfloat16)
+    return (
+        pair_two.astype(jnp.float32)
+        + jnp.dot(hidden, transition_down_weight, preferred_element_type=jnp.float32)
+    ).astype(jnp.bfloat16)
+
+
+def gather_rows(block, dap_count):
+    me = lax.axis_index("dap")
+    got = [block]
+    for offset in range(1, dap_count):
+        got.append(
+            lax.ppermute(block, "dap", [(src, src ^ offset) for src in range(dap_count)])
+        )
+    step = 1
+    while step < dap_count:
+        swap = (me & step) != 0
+        got = [
+            jnp.where(swap, got[place ^ step], got[place]) for place in range(dap_count)
+        ]
+        step *= 2
+    stacked = jnp.stack(got)
+    both = lax.all_gather(stacked, "sub", axis=1)
+    return both.reshape((-1,) + block.shape[1:])
+
+
+def shards_replicated(
+    dap_count,
+    pairwise_state,
+    alignment_state,
+    alignment_mask,
+    residue_crop_mask,
+    outer_input_weight,
+    outer_output_weight,
+    triangle_input_weight,
+    triangle_gate,
+    triangle_output_weight,
+    transition_up_weight,
+    transition_down_weight,
+):
+    row_count = pairwise_state.shape[0]
+    start_row = lax.axis_index(("dap", "sub")) * row_count
+    full_mask = residue_crop_mask.astype(jnp.float32)
+    row_mask = lax.dynamic_slice_in_dim(full_mask, start_row, row_count, 0)
+    pair_all = gather_rows(pairwise_state, dap_count)
+    alignment_keep = alignment_mask.astype(jnp.float32) * row_mask[None, :]
+    alignment_normed = norm_layer(alignment_state.astype(jnp.float32), -1).astype(jnp.bfloat16)
+    projected = jnp.einsum(
+        "pxm,qmy->xqyp", alignment_normed, outer_input_weight, preferred_element_type=jnp.float32
+    )
+    projected = (projected * alignment_keep.T[:, None, None, :]).astype(jnp.bfloat16)
+    channels = projected.shape[2]
+    sent = jnp.concatenate(
+        [
+            projected.reshape(row_count, 2 * channels, -1),
+            alignment_keep.T[:, None, :].astype(jnp.bfloat16),
+        ],
+        axis=1,
+    )
+    msa_all = gather_rows(sent, dap_count)
+    left = msa_all[:, :channels]
+    right = msa_all[:, channels : 2 * channels]
+    keep = msa_all[:, 2 * channels]
+    inner = jnp.einsum(
+        "iut,ulx->iltx", left, outer_output_weight, preferred_element_type=jnp.float32
+    ).astype(jnp.bfloat16)
+    numerator = jnp.einsum("iltx,jlt->ijx", inner, right, preferred_element_type=jnp.float32)
+    count = jnp.einsum("it,jt->ij", keep, keep, preferred_element_type=jnp.float32)
+    opm = numerator / jnp.maximum(count, 1.0)[:, :, None]
+    pair_one = (pair_all.astype(jnp.float32) + opm).astype(jnp.bfloat16)
+    ln_one = norm_layer(pair_one.astype(jnp.float32), -1).astype(jnp.bfloat16)
+    pair_keep = full_mask[:, None] * full_mask[None, :]
+
+    def operand(source, keep_rows, gate_w, proj_w):
+        gate_val = jnp.einsum("ijc,cd->ijd", source, gate_w, preferred_element_type=jnp.float32)
+        proj_val = jnp.einsum("ijc,cd->ijd", source, proj_w, preferred_element_type=jnp.float32)
+        return (jax.nn.sigmoid(gate_val) * proj_val * keep_rows[:, :, None]).astype(jnp.bfloat16)
+
+    own_ln = lax.dynamic_slice_in_dim(ln_one, start_row, row_count, 0)
+    own_pair = lax.dynamic_slice_in_dim(pair_one, start_row, row_count, 0)
+    left_tri = operand(
+        own_ln,
+        row_mask[:, None] * full_mask[None, :],
+        triangle_input_weight[0],
+        triangle_input_weight[1],
+    )
+    right_tri = operand(ln_one, pair_keep, triangle_input_weight[2], triangle_input_weight[3])
+    product = jnp.einsum(
+        "ikc,jkc->ijc", left_tri, right_tri, preferred_element_type=jnp.float32
+    ).astype(jnp.bfloat16)
+    normed = norm_layer(product.astype(jnp.float32), -1).astype(jnp.bfloat16)
+    update = jnp.einsum(
+        "ijc,cd->ijd", normed, triangle_output_weight, preferred_element_type=jnp.float32
+    )
+    gate_out = jax.nn.sigmoid(
+        jnp.einsum("ijc,cd->ijd", own_ln, triangle_gate, preferred_element_type=jnp.float32)
+    )
+    pair_two = (own_pair.astype(jnp.float32) + gate_out * update).astype(jnp.bfloat16)
+    ln_two = norm_layer(pair_two.astype(jnp.float32), -1).astype(jnp.bfloat16)
+    return transition(ln_two, pair_two, transition_up_weight, transition_down_weight)
 
 
 def shards(
@@ -92,17 +199,10 @@
     pair_two = (pair_one.astype(jnp.float32) + gate_out * update).astype(jnp.bfloat16)
     ln_two = norm_layer(pair_two.astype(jnp.float32), -1).astype(jnp.bfloat16)
 
-    def transition(row_pair):
-        row_ln, row_base = row_pair
-        hidden = jax.nn.relu(
-            jnp.dot(row_ln, transition_up_weight, preferred_element_type=jnp.float32)
-        ).astype(jnp.bfloat16)
-        return (
-            row_base.astype(jnp.float32)
-            + jnp.dot(hidden, transition_down_weight, preferred_element_type=jnp.float32)
-        ).astype(jnp.bfloat16)
-
-    return lax.map(transition, (ln_two, pair_two))
+    def step(row_pair):
+        return transition(*row_pair, transition_up_weight, transition_down_weight)
+
+    return lax.map(step, (ln_two, pair_two))
 
 
 def solution(mesh):
@@ -119,8 +219,16 @@
         P(),
         P(),
     )
+    dap_count = mesh.shape["dap"]
+
+    def body(pairwise_state, *rest):
+        residues, channels = pairwise_state.shape[1:]
+        if residues * residues * channels * 2 <= REPLICATED_PAIR_BYTES:
+            return shards_replicated(dap_count, pairwise_state, *rest)
+        return shards(pairwise_state, *rest)
+
     return jax.shard_map(
-        shards,
+        body,
         mesh=mesh,
         in_specs=placed,
         out_specs=P(("crop", "dap", "sub"), None, None),

time: 81.2 us -> 51.3 us (0.63)
  blocking collectives: 43 us -> 3.99 us
  starting transfers between devices: 10.1 us -> 23.2 us
  waiting for transfers between devices: 16.2 us -> 6.12 us
  matrix products: 2.43 us -> 7.56 us
  other arithmetic: 2.14 us -> 6.08 us
  local copies, waits for them, and re-layouts: 6.32 us -> 3.44 us
    all_gather x3 -> x2, blocking collectives: 43 us -> 3.99 us  [gather_rows(): both = lax.all_gather(stacked, 'sub', axis=1)]
    ppermute x0 -> x14, starting transfers between devices: none -> 23.2 us  [gather_rows(): lax.ppermute(block, 'dap', [(src, src ^ offset) for src in range(dap_coun...]
    all_to_all x3 -> x0, waiting for transfers between devices: 16.2 us -> none  [the longest x1 6.42 us: shards(): lax.all_to_all(near_right, 'dap', split_axis=0, concat_axis=1, tiled=True)]
    all_to_all x3 -> x0, starting transfers between devices: 10.1 us -> none  [the longest x1 3.47 us: shards(): lax.all_to_all(product, 'dap', split_axis=1, concat_axis=0, tiled=True)]
    ppermute x0 -> x14, waiting for transfers between devices: none -> 6.12 us  [gather_rows(): lax.ppermute(block, 'dap', [(src, src ^ offset) for src in range(dap_coun...]
    unnamed x30 -> x14, local copies, waits for them, and re-layouts: 5.32 us -> 0.5 us
    dot_general x11 -> x10, matrix products: 1.92 us -> 6.61 us  [the longest x1 3.82 us: shards_replicated(): jnp.einsum('iltx,jlt->ijx', inner, right, preferred_element_type=jnp.floa...]
    convert_element_type x7 -> x4, other arithmetic: 0.44 us -> 2.67 us  [the longest x1 0.89 us: shards_replicated(): norm_layer(alignment_state.astype(jnp.float32), -1).astype(jnp.bfloat16)]
  transfers between devices with their start and end apart: 3 -> 14, of which waited for: 3 -> 3; matrix products, arithmetic and copies ran while one was open for 2% -> 3% of each run, Pallas kernels for 0% -> 0%
where the time goes in v1:
time: 51.3 us; the launch traced here: 50.8 us
  starting transfers between devices  23.2 us (45%)
  matrix products  7.56 us (15%)
  waiting for transfers between devices  6.12 us (12%)
  other arithmetic  6.08 us (12%)
  blocking collectives  3.99 us (8%)
  local copies, waits for them, and re-layouts  3.44 us (7%)
    ppermute x14, starting transfers between devices, gather_rows(): lax.ppermute(block, 'dap', [(src, src ^ offset) for src in range(dap_coun...  23.2 us
    ppermute x14, waiting for transfers between devices, gather_rows(): lax.ppermute(block, 'dap', [(src, src ^ offset) for src in range(dap_coun...  6.12 us
    all_gather x2, blocking collectives, gather_rows(): both = lax.all_gather(stacked, 'sub', axis=1)  3.99 us
    dot_general x1, matrix products, shards_replicated(): jnp.einsum('iltx,jlt->ijx', inner, right, preferred_element_type=jnp.floa...  3.82 us
    reduce_sum x4, other arithmetic, norm_layer(): variance = jnp.mean(centered * centered, axis=reduce_axis, keepdims=True)  1.63 us
    convert_element_type x2, local copies, waits for them, and re-layouts, operand(): (jax.nn.sigmoid(gate_val) * proj_val * keep_rows[:, :, None]).astype(jnp....  1.63 us
  transfers between devices with their start and end apart: 14, of which 3 were waited for; matrix products, arithmetic and copies ran while one was open for 3% of the time, Pallas kernels for 0%

profile of v1, /device:TPU:0, one launch (start us, length us, event | category | flops | bytes accessed | tf_op | source)
XLA Modules:
  0.0 50.8 jit_solution(2607295178194569262)
XLA Ops:
  0.0 0.7 %convert_element_type.85 = f32[32]{0:T(128)S(1)} convert(s32[32]{0:T(128)} %param.14) | non-fusion elementwise | flops 32 | bytes 256 | tf_op jit(solution)/shard_map/convert_element_type | solution.py:61
  0.8 0.7 %convert_bitcast_fusion = (bf16[2,1,32]{2,0,1:T(2,128)(2,1)S(1)}, f32[2,32]{1,0:T(2,128)S(1)}) fusion(f32[2]{0:T(128)S(1)} %dynamic_slice.9, s32[32,2]{0,1:T(2,128)} %param.13), kind=kLoop, calls=%fused_computation.147 | loop fusion | flops 192 | bytes 648 | tf_op jit(solution)/shard_map/convert_element_type | solution.py:74
  1.6 0.9 %convert_reduce_fusion.1 = f32[32,2]{1,0:T(8,128)S(1)} fusion(bf16[32,2,256]{2,1,0:T(2,128)(2,1)} %param.12), kind=kLoop, calls=%fused_computation.53 | loop fusion | flops 32704 | bytes 33024 | tf_op jit(solution)/shard_map/reduce_sum | solution.py:10
  2.5 0.9 %fusion.53 = f32[32,2]{1,0:T(8,128)S(1)} fusion(bf16[32,2,256]{2,1,0:T(2,128)(2,1)} %param.12, f32[32,2]{1,0:T(8,128)S(1)} %broadcast_multiply_fusion.2), kind=kLoop, calls=%fused_computation.56 | loop fusion | flops 65472 | bytes 33280 | tf_op jit(solution)/shard_map/reduce_sum | solution.py:12
  3.5 0.9 %fusion.56 = bf16[32,2,256,1]{2,1,0,3:T(2,128)(2,1)S(1)} fusion(bf16[32,2,256]{2,1,0:T(2,128)(2,1)} %param.12, f32[32,2]{1,0:T(8,128)S(1)} %add_rsqrt_fusion.1, f32[32,2]{1,0:T(8,128)S(1)} %broadcast_multiply_fusion.2), kind=kLoop, calls=%fused_computation.75 | loop fusion | flops 65536 | bytes 66048 | tf_op jit(solution)/shard_map/convert_element_type | solution.py:65
  4.4 0.9 %fusion.25 = bf16[2,2,32,32]{2,3,1,0:T(8,128)(2,1)S(1)} fusion(bf16[2,256,32]{1,2,0:T(8,128)(2,1)} %param.15, bf16[32,2,256,1]{2,1,0,3:T(2,128)(2,1)S(1)} %fusion.56, f32[2,32]{1,0:T(2,128)S(1)} %get-tuple-element.16), kind=kOutput, calls=%fused_computation.20 | convolution fusion | flops 2105344 | bytes 73984 | tf_op jit(solution)/shard_map/pxm,qmy->xqyp/dot_general | solution.py:66
  5.5 2.9 %collective-permute-start.13 = (bf16[2,65,32]{1,2,0:T(8,128)(2,1)S(1)}, bf16[2,65,32]{1,2,0:T(8,128)(2,1)S(1)}, u32[]{:S(2)}, u32[]{:S(2)}) collective-permute-start(bf16[2,65,32]{1,2,0:T(8,128)(2,1)S(1)} %pad_maximum_fusion), channel_id=1, source_target_pairs={{0,2},{2,0},{4,6},{6,4},{8,10},{10,8},{12,14},{14,12},{1,3},{3,1},... | collective-permute-start | bytes 24968 | tf_op jit(solution)/shard_map/ppermute | solution.py:31
  8.5 1.6 %collective-permute-start.12 = (bf16[2,65,32]{1,2,0:T(8,128)(2,1)S(1)}, bf16[2,65,32]{1,2,0:T(8,128)(2,1)S(1)}, u32[]{:S(2)}, u32[]{:S(2)}) collective-permute-start(bf16[2,65,32]{1,2,0:T(8,128)(2,1)S(1)} %pad_maximum_fusion), channel_id=1, source_target_pairs={{0,4},{2,6},{4,0},{6,2},{8,12},{10,14},{12,8},{14,10},{1,5},{3,7},... | collective-permute-start | bytes 24968 | tf_op jit(solution)/shard_map/ppermute | solution.py:31
  10.0 3.0 %collective-permute-start.10 = (bf16[2,65,32]{1,2,0:T(8,128)(2,1)S(1)}, bf16[2,65,32]{1,2,0:T(8,128)(2,1)S(1)}, u32[]{:S(2)}, u32[]{:S(2)}) collective-permute-start(bf16[2,65,32]{1,2,0:T(8,128)(2,1)S(1)} %pad_maximum_fusion), channel_id=1, source_target_pairs={{0,8},{2,10},{4,12},{6,14},{8,0},{10,2},{12,4},{14,6},{1,9},{3,11}... | collective-permute-start | bytes 24968 | tf_op jit(solution)/shard_map/ppermute | solution.py:31
  13.1 1.3 %collective-permute-start.9 = (bf16[2,65,32]{1,2,0:T(8,128)(2,1)S(1)}, bf16[2,65,32]{1,2,0:T(8,128)(2,1)S(1)}, u32[]{:S(2)}, u32[]{:S(2)}) collective-permute-start(bf16[2,65,32]{1,2,0:T(8,128)(2,1)S(1)} %pad_maximum_fusion), channel_id=1, source_target_pairs={{0,10},{2,8},{4,14},{6,12},{8,2},{10,0},{12,6},{14,4},{1,11},{3,9}... | collective-permute-start | bytes 24968 | tf_op jit(solution)/shard_map/ppermute | solution.py:31
  14.4 3.6 %collective-permute-start.8 = (bf16[2,65,32]{1,2,0:T(8,128)(2,1)S(1)}, bf16[2,65,32]{1,2,0:T(8,128)(2,1)S(1)}, u32[]{:S(2)}, u32[]{:S(2)}) collective-permute-start(bf16[2,65,32]{1,2,0:T(8,128)(2,1)S(1)} %pad_maximum_fusion), channel_id=1, source_target_pairs={{0,12},{2,14},{4,8},{6,10},{8,4},{10,6},{12,0},{14,2},{1,13},{3,15... | collective-permute-start | bytes 24968 | tf_op jit(solution)/shard_map/ppermute | solution.py:31
  18.1 1.6 %collective-permute-start.6 = (bf16[2,32,128]{2,1,0:T(8,128)(2,1)}, bf16[2,32,128]{2,1,0:T(8,128)(2,1)S(1)}, u32[]{:S(2)}, u32[]{:S(2)}) collective-permute-start(bf16[2,32,128]{2,1,0:T(8,128)(2,1)} %param.11), channel_id=1, source_target_pairs={{0,2},{2,0},{4,6},{6,4},{8,10},{10,8},{12,14},{14,12},{1,3},{3,1},... | collective-permute-start | bytes 49160 | tf_op jit(solution)/shard_map/ppermute | solution.py:31
  19.8 1.9 %collective-permute-start.4 = (bf16[2,32,128]{2,1,0:T(8,128)(2,1)}, bf16[2,32,128]{2,1,0:T(8,128)(2,1)S(1)}, u32[]{:S(2)}, u32[]{:S(2)}) collective-permute-start(bf16[2,32,128]{2,1,0:T(8,128)(2,1)} %param.11), channel_id=1, source_target_pairs={{0,6},{2,4},{4,2},{6,0},{8,14},{10,12},{12,10},{14,8},{1,7},{3,5},... | collective-permute-start | bytes 49160 | tf_op jit(solution)/shard_map/ppermute | solution.py:31
  21.6 2.4 %collective-permute-start.3 = (bf16[2,32,128]{2,1,0:T(8,128)(2,1)}, bf16[2,32,128]{2,1,0:T(8,128)(2,1)S(1)}, u32[]{:S(2)}, u32[]{:S(2)}) collective-permute-start(bf16[2,32,128]{2,1,0:T(8,128)(2,1)} %param.11), channel_id=1, source_target_pairs={{0,8},{2,10},{4,12},{6,14},{8,0},{10,2},{12,4},{14,6},{1,9},{3,11}... | collective-permute-start | bytes 49160 | tf_op jit(solution)/shard_map/ppermute | solution.py:31
  24.5 1.1 %collective-permute-start.2 = (bf16[2,32,128]{2,1,0:T(8,128)(2,1)}, bf16[2,32,128]{2,1,0:T(8,128)(2,1)S(1)}, u32[]{:S(2)}, u32[]{:S(2)}) collective-permute-start(bf16[2,32,128]{2,1,0:T(8,128)(2,1)} %param.11), channel_id=1, source_target_pairs={{0,10},{2,8},{4,14},{6,12},{8,2},{10,0},{12,6},{14,4},{1,11},{3,9}... | collective-permute-start | bytes 49160 | tf_op jit(solution)/shard_map/ppermute | solution.py:31
  26.0 2.0 %all-gather.1 = bf16[8,4,65,32]{2,3,1,0:T(8,128)(2,1)S(1)} all-gather(bf16[8,2,65,32]{2,3,1,0:T(8,128)(2,1)S(1)} %constant_dynamic-update-slice_fusion.8), channel_id=3, replica_groups=mesh['crop'=2,'dap'=8,'sub'=2] {'sub'}, dimensions={1}, use_global_device_ids=true | all-gather | bytes 199680 | tf_op jit(solution)/shard_map/all_gather | solution.py:41
  28.3 3.7 %collective-permute-start.1 = (bf16[2,32,128]{2,1,0:T(8,128)(2,1)S(1)}, bf16[2,32,128]{2,1,0:T(8,128)(2,1)S(1)}, u32[]{:S(2)}, u32[]{:S(2)}) collective-permute-start(bf16[2,32,128]{2,1,0:T(8,128)(2,1)S(1)} %copy-done.1), channel_id=1, source_target_pairs={{0,12},{2,14},{4,8},{6,10},{8,4},{10,6},{12,0},{14,2},{1,13},{3,15... | collective-permute-start | bytes 49160 | tf_op jit(solution)/shard_map/ppermute | solution.py:31
  32.8 1.1 %collective-permute-done.1 = bf16[2,32,128]{2,1,0:T(8,128)(2,1)S(1)} collective-permute-done((bf16[2,32,128]{2,1,0:T(8,128)(2,1)S(1)}, bf16[2,32,128]{2,1,0:T(8,128)(2,1)S(1)}, u32[]{:S(2)}, u32[]{:S(2)}) %collective-permute-start.1) | collective-permute-done | bytes 16416 | tf_op jit(solution)/shard_map/ppermute | solution.py:31
  33.9 4.5 %collective-permute-done = bf16[2,32,128]{2,1,0:T(8,128)(2,1)S(1)} collective-permute-done((bf16[2,32,128]{2,1,0:T(8,128)(2,1)S(1)}, bf16[2,32,128]{2,1,0:T(8,128)(2,1)S(1)}, u32[]{:S(2)}, u32[]{:S(2)}) %collective-permute-start) | collective-permute-done | bytes 16416 | tf_op jit(solution)/shard_map/ppermute | solution.py:31
  38.7 2.0 %all-gather = bf16[8,4,32,128]{3,2,1,0:T(8,128)(2,1)S(1)} all-gather(bf16[8,2,32,128]{3,2,1,0:T(8,128)(2,1)S(1)} %constant_dynamic-update-slice_fusion), channel_id=2, replica_groups=mesh['crop'=2,'dap'=8,'sub'=2] {'sub'}, dimensions={1}, use_global_device_ids=true | all-gather | bytes 393216 | tf_op jit(solution)/shard_map/all_gather | solution.py:41
  40.7 3.8 %convert_reduce_fusion = (f32[32,32]{1,0:T(8,128)S(1)}, bf16[32,32,128]{2,1,0:T(8,128)(2,1)S(1)}) fusion(f32[32,32]{1,0:T(8,128)S(1)} %convolution_maximum_fusion.1, bf16[32,65,32]{1,2,0:T(8,128)(2,1)S(1)} %bitcast.149, bf16[32,32,128]{2,1,0:T(8,128)(2,1)S(1)} %copy-done.4, bf16[32,32,32]{2,0,1:T(8,128)(2,1)S(1)} %copy.40, ...), kind=kOutput, calls=%fused_computation.40 | convolution fusion | flops 541850624 | bytes 993280 | tf_op jit(solution)/shard_map/iltx,jlt->ijx/dot_general | solution.py:85
  46.8 1.4 %copy.41 = bf16[32,32,128]{1,0,2:T(8,128)(2,1)S(1)} copy(bf16[32,32,128]{2,1,0:T(8,128)(2,1)S(1)} %fusion.21) | data formatting | bytes 524288 | tf_op jit(solution)/shard_map/convert_element_type | solution.py:95
  48.3 0.6 %fusion.91 = bf16[128,32,2]{1,2,0:T(2,128)(2,1)S(1)} fusion(bf16[32,32,128]{1,0,2:T(8,128)(2,1)S(1)} %copy.41, bf16[2,32,128]{1,0,2:T(2,128)(2,1)S(1)} %copy.42), kind=kOutput, calls=%fused_computation.154 | convolution fusion | flops 524288 | bytes 294912 | tf_op jit(solution)/shard_map/ikc,jkc->ijc/dot_general | solution.py:106
  49.8 0.9 %fusion.38 = bf16[2,32,128]{2,1,0:T(8,128)(2,1)} fusion(f32[2,32,128]{2,1,0:T(8,128)S(1)} %get-tuple-element.30, bf16[512,128]{1,0:T(8,128)(2,1)S(1)} %copy-done, bf16[128,512]{1,0:T(8,128)(2,1)S(1)} %copy-done.5, f32[2,32]{1,0:T(2,128)S(1)} %add_rsqrt_fusion.2, f32[2,32]{1,0:T(2,128)S(1)} %broadcast_multiply_fusion.3), kind=kOutput, calls=%fused_computation.37 | convolution fusion | flops 16883712 | bytes 311808 | tf_op jit(solution)/shard_map/dot_general | solution.py:22
  (78 shorter events, 5.8 us)
Async XLA Ops:
  0.0 49.8 %copy-start = (bf16[512,128]{1,0:T(8,128)(2,1)S(1)}, bf16[512,128]{1,0:T(8,128)(2,1)}, u32[]{:S(2)}) copy-start(bf16[512,128]{1,0:T(8,128)(2,1)} %param.21) | copy-start | bytes 393220
  3.5 24.9 %copy-start.1 = (bf16[2,32,128]{2,1,0:T(8,128)(2,1)S(1)}, bf16[2,32,128]{2,1,0:T(8,128)(2,1)}, u32[]{:S(2)}) copy-start(bf16[2,32,128]{2,1,0:T(8,128)(2,1)} %param.11) | copy-start | bytes 49156
  5.5 8.9 %collective-permute-start.13 = (bf16[2,65,32]{1,2,0:T(8,128)(2,1)S(1)}, bf16[2,65,32]{1,2,0:T(8,128)(2,1)S(1)}, u32[]{:S(2)}, u32[]{:S(2)}) collective-permute-start(bf16[2,65,32]{1,2,0:T(8,128)(2,1)S(1)} %pad_maximum_fusion), channel_id=1, source_target_pairs={{0,2},{2,0},{4,6},{6,4},{8,10},{10,8},{12,14},{14,12},{1,3},{3,1},... | collective-permute-start | bytes 24968 | tf_op jit(solution)/shard_map/ppermute | solution.py:31
  8.5 9.5 %collective-permute-start.12 = (bf16[2,65,32]{1,2,0:T(8,128)(2,1)S(1)}, bf16[2,65,32]{1,2,0:T(8,128)(2,1)S(1)}, u32[]{:S(2)}, u32[]{:S(2)}) collective-permute-start(bf16[2,65,32]{1,2,0:T(8,128)(2,1)S(1)} %pad_maximum_fusion), channel_id=1, source_target_pairs={{0,4},{2,6},{4,0},{6,2},{8,12},{10,14},{12,8},{14,10},{1,5},{3,7},... | collective-permute-start | bytes 24968 | tf_op jit(solution)/shard_map/ppermute | solution.py:31
  10.0 8.1 %collective-permute-start.11 = (bf16[2,65,32]{1,2,0:T(8,128)(2,1)S(1)}, bf16[2,65,32]{1,2,0:T(8,128)(2,1)S(1)}, u32[]{:S(2)}, u32[]{:S(2)}) collective-permute-start(bf16[2,65,32]{1,2,0:T(8,128)(2,1)S(1)} %pad_maximum_fusion), channel_id=1, source_target_pairs={{0,6},{2,4},{4,2},{6,0},{8,14},{10,12},{12,10},{14,8},{1,7},{3,5},... | collective-permute-start | bytes 24968 | tf_op jit(solution)/shard_map/ppermute | solution.py:31
  10.0 9.7 %collective-permute-start.10 = (bf16[2,65,32]{1,2,0:T(8,128)(2,1)S(1)}, bf16[2,65,32]{1,2,0:T(8,128)(2,1)S(1)}, u32[]{:S(2)}, u32[]{:S(2)}) collective-permute-start(bf16[2,65,32]{1,2,0:T(8,128)(2,1)S(1)} %pad_maximum_fusion), channel_id=1, source_target_pairs={{0,8},{2,10},{4,12},{6,14},{8,0},{10,2},{12,4},{14,6},{1,9},{3,11}... | collective-permute-start | bytes 24968 | tf_op jit(solution)/shard_map/ppermute | solution.py:31
  13.1 6.7 %collective-permute-start.9 = (bf16[2,65,32]{1,2,0:T(8,128)(2,1)S(1)}, bf16[2,65,32]{1,2,0:T(8,128)(2,1)S(1)}, u32[]{:S(2)}, u32[]{:S(2)}) collective-permute-start(bf16[2,65,32]{1,2,0:T(8,128)(2,1)S(1)} %pad_maximum_fusion), channel_id=1, source_target_pairs={{0,10},{2,8},{4,14},{6,12},{8,2},{10,0},{12,6},{14,4},{1,11},{3,9}... | collective-permute-start | bytes 24968 | tf_op jit(solution)/shard_map/ppermute | solution.py:31
  14.4 7.2 %collective-permute-start.8 = (bf16[2,65,32]{1,2,0:T(8,128)(2,1)S(1)}, bf16[2,65,32]{1,2,0:T(8,128)(2,1)S(1)}, u32[]{:S(2)}, u32[]{:S(2)}) collective-permute-start(bf16[2,65,32]{1,2,0:T(8,128)(2,1)S(1)} %pad_maximum_fusion), channel_id=1, source_target_pairs={{0,12},{2,14},{4,8},{6,10},{8,4},{10,6},{12,0},{14,2},{1,13},{3,15... | collective-permute-start | bytes 24968 | tf_op jit(solution)/shard_map/ppermute | solution.py:31
  18.0 6.5 %collective-permute-start.7 = (bf16[2,65,32]{1,2,0:T(8,128)(2,1)S(1)}, bf16[2,65,32]{1,2,0:T(8,128)(2,1)S(1)}, u32[]{:S(2)}, u32[]{:S(2)}) collective-permute-start(bf16[2,65,32]{1,2,0:T(8,128)(2,1)S(1)} %pad_maximum_fusion), channel_id=1, source_target_pairs={{0,14},{2,12},{4,10},{6,8},{8,6},{10,4},{12,2},{14,0},{1,15},{3,13... | collective-permute-start | bytes 24968 | tf_op jit(solution)/shard_map/ppermute | solution.py:31
  18.1 10.2 %collective-permute-start.6 = (bf16[2,32,128]{2,1,0:T(8,128)(2,1)}, bf16[2,32,128]{2,1,0:T(8,128)(2,1)S(1)}, u32[]{:S(2)}, u32[]{:S(2)}) collective-permute-start(bf16[2,32,128]{2,1,0:T(8,128)(2,1)} %param.11), channel_id=1, source_target_pairs={{0,2},{2,0},{4,6},{6,4},{8,10},{10,8},{12,14},{14,12},{1,3},{3,1},... | collective-permute-start | bytes 49160 | tf_op jit(solution)/shard_map/ppermute | solution.py:31
  19.8 12.2 %collective-permute-start.5 = (bf16[2,32,128]{2,1,0:T(8,128)(2,1)}, bf16[2,32,128]{2,1,0:T(8,128)(2,1)S(1)}, u32[]{:S(2)}, u32[]{:S(2)}) collective-permute-start(bf16[2,32,128]{2,1,0:T(8,128)(2,1)} %param.11), channel_id=1, source_target_pairs={{0,4},{2,6},{4,0},{6,2},{8,12},{10,14},{12,8},{14,10},{1,5},{3,7},... | collective-permute-start | bytes 49160 | tf_op jit(solution)/shard_map/ppermute | solution.py:31
  19.8 13.0 %collective-permute-start.4 = (bf16[2,32,128]{2,1,0:T(8,128)(2,1)}, bf16[2,32,128]{2,1,0:T(8,128)(2,1)S(1)}, u32[]{:S(2)}, u32[]{:S(2)}) collective-permute-start(bf16[2,32,128]{2,1,0:T(8,128)(2,1)} %param.11), channel_id=1, source_target_pairs={{0,6},{2,4},{4,2},{6,0},{8,14},{10,12},{12,10},{14,8},{1,7},{3,5},... | collective-permute-start | bytes 49160 | tf_op jit(solution)/shard_map/ppermute | solution.py:31
  21.6 11.2 %collective-permute-start.3 = (bf16[2,32,128]{2,1,0:T(8,128)(2,1)}, bf16[2,32,128]{2,1,0:T(8,128)(2,1)S(1)}, u32[]{:S(2)}, u32[]{:S(2)}) collective-permute-start(bf16[2,32,128]{2,1,0:T(8,128)(2,1)} %param.11), channel_id=1, source_target_pairs={{0,8},{2,10},{4,12},{6,14},{8,0},{10,2},{12,4},{14,6},{1,9},{3,11}... | collective-permute-start | bytes 49160 | tf_op jit(solution)/shard_map/ppermute | solution.py:31
  24.5 8.3 %collective-permute-start.2 = (bf16[2,32,128]{2,1,0:T(8,128)(2,1)}, bf16[2,32,128]{2,1,0:T(8,128)(2,1)S(1)}, u32[]{:S(2)}, u32[]{:S(2)}) collective-permute-start(bf16[2,32,128]{2,1,0:T(8,128)(2,1)} %param.11), channel_id=1, source_target_pairs={{0,10},{2,8},{4,14},{6,12},{8,2},{10,0},{12,6},{14,4},{1,11},{3,9}... | collective-permute-start | bytes 49160 | tf_op jit(solution)/shard_map/ppermute | solution.py:31
  28.3 5.6 %collective-permute-start.1 = (bf16[2,32,128]{2,1,0:T(8,128)(2,1)S(1)}, bf16[2,32,128]{2,1,0:T(8,128)(2,1)S(1)}, u32[]{:S(2)}, u32[]{:S(2)}) collective-permute-start(bf16[2,32,128]{2,1,0:T(8,128)(2,1)S(1)} %copy-done.1), channel_id=1, source_target_pairs={{0,12},{2,14},{4,8},{6,10},{8,4},{10,6},{12,0},{14,2},{1,13},{3,15... | collective-permute-start | bytes 49160 | tf_op jit(solution)/shard_map/ppermute | solution.py:31
  32.0 6.4 %collective-permute-start = (bf16[2,32,128]{2,1,0:T(8,128)(2,1)S(1)}, bf16[2,32,128]{2,1,0:T(8,128)(2,1)S(1)}, u32[]{:S(2)}, u32[]{:S(2)}) collective-permute-start(bf16[2,32,128]{2,1,0:T(8,128)(2,1)S(1)} %copy-done.1), channel_id=1, source_target_pairs={{0,14},{2,12},{4,10},{6,8},{8,6},{10,4},{12,2},{14,0},{1,15},{3,13... | collective-permute-start | bytes 49160 | tf_op jit(solution)/shard_map/ppermute | solution.py:31
  32.3 8.3 %copy-start.4 = (bf16[32,32,128]{2,1,0:T(8,128)(2,1)S(1)}, bf16[32,32,128]{2,1,0:T(8,128)(2,1)}, u32[]{:S(2)}) copy-start(bf16[32,32,128]{2,1,0:T(8,128)(2,1)} %param.16) | copy-start | bytes 786436
  40.7 4.6 %copy-start.2 = (bf16[4,128,128]{2,1,0:T(8,128)(2,1)S(1)}, bf16[4,128,128]{2,1,0:T(8,128)(2,1)}, u32[]{:S(2)}) copy-start(bf16[4,128,128]{2,1,0:T(8,128)(2,1)} %param.17) | copy-start | bytes 393220
  45.4 0.8 %copy-start.6 = (bf16[128,128]{1,0:T(8,128)(2,1)S(1)}, bf16[128,128]{1,0:T(8,128)(2,1)}, u32[]{:S(2)}) copy-start(bf16[128,128]{1,0:T(8,128)(2,1)} %param.18) | copy-start | bytes 98308
  46.8 2.5 %copy-start.3 = (bf16[128,128]{1,0:T(8,128)(2,1)S(1)}, bf16[128,128]{1,0:T(8,128)(2,1)}, u32[]{:S(2)}) copy-start(bf16[128,128]{1,0:T(8,128)(2,1)} %param.19) | copy-start | bytes 98308
  48.3 1.5 %copy-start.5 = (bf16[128,512]{1,0:T(8,128)(2,1)S(1)}, bf16[128,512]{1,0:T(8,128)(2,1)}, u32[]{:S(2)}) copy-start(bf16[128,512]{1,0:T(8,128)(2,1)} %param.20) | copy-start | bytes 393220

commit v2 on v1

--- a/solution.py
+++ b/solution.py
@@ -1,7 +1,7 @@
 import jax
 import jax.numpy as jnp
 from jax import lax
-from jax.sharding import PartitionSpec as P
+from jax.sharding import Mesh, PartitionSpec as P
 
 REPLICATED_PAIR_BYTES = 1 << 20
 
@@ -23,27 +23,15 @@
     ).astype(jnp.bfloat16)
 
 
-def gather_rows(block, dap_count):
-    me = lax.axis_index("dap")
-    got = [block]
-    for offset in range(1, dap_count):
-        got.append(
-            lax.ppermute(block, "dap", [(src, src ^ offset) for src in range(dap_count)])
-        )
-    step = 1
-    while step < dap_count:
-        swap = (me & step) != 0
-        got = [
-            jnp.where(swap, got[place ^ step], got[place]) for place in range(dap_count)
-        ]
-        step *= 2
-    stacked = jnp.stack(got)
-    both = lax.all_gather(stacked, "sub", axis=1)
-    return both.reshape((-1,) + block.shape[1:])
+def gather_all(block):
+    held = block[None]
+    for axis in ("x", "z_low", "z_high"):
+        held = lax.all_gather(held, axis, axis=0, tiled=True)
+    both = lax.all_gather(held, "sub", axis=0).swapaxes(0, 1)
+    return both.reshape((-1,) + block.shape)
 
 
 def shards_replicated(
-    dap_count,
     pairwise_state,
     alignment_state,
     alignment_mask,
@@ -57,28 +45,35 @@
     transition_down_weight,
 ):
     row_count = pairwise_state.shape[0]
-    start_row = lax.axis_index(("dap", "sub")) * row_count
+    start_row = lax.axis_index(("z_high", "z_low", "x", "sub")) * row_count
     full_mask = residue_crop_mask.astype(jnp.float32)
     row_mask = lax.dynamic_slice_in_dim(full_mask, start_row, row_count, 0)
-    pair_all = gather_rows(pairwise_state, dap_count)
     alignment_keep = alignment_mask.astype(jnp.float32) * row_mask[None, :]
     alignment_normed = norm_layer(alignment_state.astype(jnp.float32), -1).astype(jnp.bfloat16)
     projected = jnp.einsum(
-        "pxm,qmy->xqyp", alignment_normed, outer_input_weight, preferred_element_type=jnp.float32
-    )
-    projected = (projected * alignment_keep.T[:, None, None, :]).astype(jnp.bfloat16)
-    channels = projected.shape[2]
+        "pxm,qmy->pxqy", alignment_normed, outer_input_weight, preferred_element_type=jnp.float32
+    )
+    projected = (projected * alignment_keep[:, :, None, None]).astype(jnp.bfloat16)
+    sequences, _, _, channels = projected.shape
+    wide = pairwise_state.shape[-1]
+    pair_rows = row_count * pairwise_state.shape[1]
     sent = jnp.concatenate(
         [
-            projected.reshape(row_count, 2 * channels, -1),
-            alignment_keep.T[:, None, :].astype(jnp.bfloat16),
+            pairwise_state.reshape(pair_rows, wide),
+            projected.reshape(-1, wide),
+            jnp.pad(alignment_keep.T.astype(jnp.bfloat16), ((0, 0), (0, wide - sequences))),
         ],
-        axis=1,
-    )
-    msa_all = gather_rows(sent, dap_count)
-    left = msa_all[:, :channels]
-    right = msa_all[:, channels : 2 * channels]
-    keep = msa_all[:, 2 * channels]
+        axis=0,
+    )
+    held = gather_all(sent)
+    pair_all = held[:, :pair_rows].reshape((-1,) + pairwise_state.shape[1:])
+    msa_all = held[:, pair_rows:-row_count].reshape(-1, sequences, row_count, 2, channels)
+    left, right = (
+        msa_all[:, :, :, q].transpose(0, 2, 1, 3).reshape(-1, sequences, channels) for q in (0, 1)
+    )
+    left = left.transpose(0, 2, 1)
+    right = right.transpose(0, 2, 1)
+    keep = held[:, -row_count:, :sequences].reshape(-1, sequences)
     inner = jnp.einsum(
         "iut,ulx->iltx", left, outer_output_weight, preferred_element_type=jnp.float32
     ).astype(jnp.bfloat16)
@@ -219,18 +214,36 @@
         P(),
         P(),
     )
-    dap_count = mesh.shape["dap"]
-
-    def body(pairwise_state, *rest):
+
+    def distributed(*arrays):
+        return jax.shard_map(
+            shards,
+            mesh=mesh,
+            in_specs=placed,
+            out_specs=P(("crop", "dap", "sub"), None, None),
+            check_vma=False,
+        )(*arrays)
+
+    def replicated(*arrays):
+        dap = ("z_high", "z_low", "x")
+        fine = Mesh(
+            mesh.devices.reshape(mesh.shape["crop"], 2, 2, -1, mesh.shape["sub"]),
+            ("crop",) + dap + ("sub",),
+        )
+        rows = ("crop",) + dap + ("sub",)
+        return jax.shard_map(
+            shards_replicated,
+            mesh=fine,
+            in_specs=(P(rows, None, None), P("crop", rows[1:], None), P("crop", rows[1:]))
+            + placed[3:],
+            out_specs=P(rows, None, None),
+            check_vma=False,
+        )(*arrays)
+
+    def whole(pairwise_state, *rest):
         residues, channels = pairwise_state.shape[1:]
         if residues * residues * channels * 2 <= REPLICATED_PAIR_BYTES:
-            return shards_replicated(dap_count, pairwise_state, *rest)
-        return shards(pairwise_state, *rest)
-
-    return jax.shard_map(
-        body,
-        mesh=mesh,
-        in_specs=placed,
-        out_specs=P(("crop", "dap", "sub"), None, None),
-        check_vma=False,
-    )
+            return replicated(pairwise_state, *rest)
+        return distributed(pairwise_state, *rest)
+
+    return whole

time: 51.3 us -> 38.1 us (0.74)
  the two profiles are of different devices: /device:TPU:0 before, /device:TPU:5 now
where the time goes in v2:
time: 38.1 us; the launch traced here: 37.6 us
  blocking collectives  19.1 us (50%)
  matrix products  7.61 us (20%)
  other arithmetic  6.2 us (16%)
  local copies, waits for them, and re-layouts  4.33 us (11%)
    all_gather x3, blocking collectives, gather_all(): held = lax.all_gather(held, axis, axis=0, tiled=True)  13.3 us
    all_gather x1, blocking collectives, gather_all(): both = lax.all_gather(held, 'sub', axis=0).swapaxes(0, 1)  5.85 us
    dot_general x1, matrix products, shards_replicated(): jnp.einsum('iltx,jlt->ijx', inner, right, preferred_element_type=jnp.floa...  3.81 us
    reduce_sum x4, other arithmetic, norm_layer(): variance = jnp.mean(centered * centered, axis=reduce_axis, keepdims=True)  1.63 us
    convert_element_type x2, local copies, waits for them, and re-layouts, operand(): (jax.nn.sigmoid(gate_val) * proj_val * keep_rows[:, :, None]).astype(jnp....  1.57 us
    slice x3, local copies, waits for them, and re-layouts, shards_replicated(): msa_all[:, :, :, q].transpose(0, 2, 1, 3).reshape(-1, sequences, channels)  1.21 us
    reduce_sum x2, other arithmetic, norm_layer(): average = jnp.mean(values, axis=reduce_axis, keepdims=True)  0.96 us
    dot_general x1, matrix products, transition(): jnp.dot(hidden, transition_down_weight, preferred_element_type=jnp.float32)  0.95 us

profile of v2, /device:TPU:5, one launch (start us, length us, event | category | flops | bytes accessed | tf_op | source)
XLA Modules:
  0.0 37.6 jit_solution(5874958244411064816)
XLA Ops:
  0.0 0.7 %convert_element_type.85 = f32[32]{0:T(128)S(1)} convert(s32[32]{0:T(128)} %param.14) | non-fusion elementwise | flops 32 | bytes 256 | tf_op jit(solution)/shard_map/convert_element_type | solution.py:49
  0.8 0.7 %convert_bitcast_fusion = (bf16[2,32]{1,0:T(2,128)(2,1)S(1)}, f32[32,2]{0,1:T(2,128)S(1)}) fusion(f32[2]{0:T(128)S(1)} %dynamic_slice.9, s32[32,2]{0,1:T(2,128)} %param.13), kind=kLoop, calls=%fused_computation.99 | loop fusion | flops 192 | bytes 648 | tf_op jit(solution)/shard_map/convert_element_type | solution.py:64
  1.7 0.9 %convert_reduce_fusion.1 = f32[32,2]{1,0:T(8,128)S(1)} fusion(bf16[32,2,256]{2,1,0:T(2,128)(2,1)} %param.12), kind=kLoop, calls=%fused_computation.50 | loop fusion | flops 32704 | bytes 33024 | tf_op jit(solution)/shard_map/reduce_sum | solution.py:10
  2.6 0.9 %fusion.51 = f32[32,2]{1,0:T(8,128)S(1)} fusion(bf16[32,2,256]{2,1,0:T(2,128)(2,1)} %param.12, f32[32,2]{1,0:T(8,128)S(1)} %broadcast_multiply_fusion.2), kind=kLoop, calls=%fused_computation.53 | loop fusion | flops 65472 | bytes 33280 | tf_op jit(solution)/shard_map/reduce_sum | solution.py:12
  3.5 0.9 %fusion.55 = bf16[32,2,256,1]{2,1,0,3:T(2,128)(2,1)S(1)} fusion(bf16[32,2,256]{2,1,0:T(2,128)(2,1)} %param.12, f32[32,2]{1,0:T(8,128)S(1)} %add_rsqrt_fusion.1, f32[32,2]{1,0:T(8,128)S(1)} %broadcast_multiply_fusion.2), kind=kLoop, calls=%fused_computation.58 | loop fusion | flops 65536 | bytes 66048 | tf_op jit(solution)/shard_map/convert_element_type | solution.py:52
  4.4 0.9 %fusion.24 = bf16[32,2,2,32]{3,0,2,1:T(8,128)(2,1)S(1)} fusion(bf16[2,256,32]{1,2,0:T(8,128)(2,1)} %param.15, bf16[32,2,256,1]{2,1,0,3:T(2,128)(2,1)S(1)} %fusion.55, f32[32,2]{0,1:T(2,128)S(1)} %get-tuple-element.6), kind=kOutput, calls=%fused_computation.19 | convolution fusion | flops 2105344 | bytes 73984 | tf_op jit(solution)/shard_map/pxm,qmy->pxqy/dot_general | solution.py:53
  5.5 0.7 %fusion.73 = bf16[1,98,128]{2,1,0:T(8,128)(2,1)S(1)} fusion(bf16[2,32]{1,0:T(2,128)(2,1)S(1)} %get-tuple-element.5, bf16[32,128]{1,0:T(8,128)(2,1)S(1)} %reshape.128, bf16[64,128]{1,0:T(8,128)(2,1)} %bitcast.130), kind=kLoop, calls=%fused_computation.80 | loop fusion | flops 100352 | bytes 49792
  6.2 3.4 %all-gather.2 = bf16[2,98,128]{2,1,0:T(8,128)(2,1)S(1)} all-gather(bf16[1,98,128]{2,1,0:T(8,128)(2,1)S(1)} %fusion.73), channel_id=2, replica_groups=mesh['crop'=2,'z_high'=2,'z_low'=2,'x'=2,'sub'=2] {'x'}, dimensions={0}, use_global_device_ids=true | all-gather | bytes 75264 | tf_op jit(solution)/shard_map/all_gather | solution.py:29
  9.6 3.6 %all_gather.16 = bf16[4,98,128]{2,1,0:T(8,128)(2,1)S(1)} all-gather(bf16[2,98,128]{2,1,0:T(8,128)(2,1)S(1)} %all-gather.2), channel_id=1, replica_groups=mesh['crop'=2,'z_high'=2,'z_low'=2,'x'=2,'sub'=2] {'z_low'}, dimensions={0}, use_global_device_ids=true | all-gather | bytes 150528 | tf_op jit(solution)/shard_map/all_gather | solution.py:29
  13.2 6.3 %all_gather.17 = bf16[8,98,128]{2,1,0:T(8,128)(2,1)S(1)} all-gather(bf16[4,98,128]{2,1,0:T(8,128)(2,1)S(1)} %all_gather.16), channel_id=1, replica_groups=mesh['crop'=2,'z_high'=2,'z_low'=2,'x'=2,'sub'=2] {'z_high'}, dimensions={0}, use_global_device_ids=true | all-gather | bytes 301056 | tf_op jit(solution)/shard_map/all_gather | solution.py:29
  19.5 5.8 %all-gather.1 = bf16[16,98,128]{2,0,1:T(8,128)(2,1)S(1)} all-gather(bf16[8,98,128]{2,0,1:T(8,128)(2,1)S(1)} %copy.45), channel_id=3, replica_groups=mesh['crop'=2,'z_high'=2,'z_low'=2,'x'=2,'sub'=2] {'sub'}, dimensions={0}, use_global_device_ids=true | all-gather | bytes 602112 | tf_op jit(solution)/shard_map/all_gather | solution.py:30
  25.6 0.2 reshape.130
  25.9 1.1 %fusion.89 = (bf16[16,32,2,1,32]{4,3,2,1,0:T(2,128)(2,1)S(1)}, bf16[16,32,2,1,32]{4,3,2,1,0:T(2,128)(2,1)S(1)}) fusion(bf16[16,32,2,2,32]{4,3,2,1,0:T(2,128)(2,1)S(1)} %reshape.130), kind=kLoop, calls=%fused_computation.105 | loop fusion | bytes 262144 | tf_op jit(solution)/shard_map/slice | solution.py:72
  27.1 0.4 %copy.48 = bf16[16,2,32,32]{2,1,0,3:T(2,128)(2,1)S(1)} copy(bf16[16,2,32,32]{3,2,1,0:T(8,128)(2,1)S(1)} %bitcast.125) | data formatting | bytes 131072 | tf_op jit(solution)/shard_map/transpose | solution.py:72
  27.5 0.4 %copy-done.3 = bf16[32,32,128]{2,1,0:T(8,128)(2,1)S(1)} copy-done((bf16[32,32,128]{2,1,0:T(8,128)(2,1)S(1)}, bf16[32,32,128]{2,1,0:T(8,128)(2,1)}, u32[]{:S(2)}) %copy-start.3) | copy-done | bytes 262168
  28.0 3.8 %convert_reduce_fusion = (f32[32,32]{1,0:T(8,128)S(1)}, bf16[32,32,128]{2,1,0:T(8,128)(2,1)S(1)}) fusion(f32[32,32]{1,0:T(8,128)S(1)} %convolution_maximum_fusion.1, bf16[32,32,32,1]{2,0,1,3:T(8,128)(2,1)S(1)} %bitcast.128, bf16[32,32,32,1]{1,2,3,0:T(8,128)(2,1)S(1)} %bitcast.126, bf16[32,32,128]{2,1,0:T(8,128)(2,1)S(1)} %copy-done.3, ...), kind=kOutput, calls=%fused_computation.39 | convolution fusion | flops 541850624 | bytes 925696 | tf_op jit(solution)/shard_map/iltx,jlt->ijx/dot_general | solution.py:80
  31.8 0.4 %fusion.40 = f32[32,32]{1,0:T(8,128)S(1)} fusion(bf16[32,32,128]{2,1,0:T(8,128)(2,1)S(1)} %get-tuple-element.10, f32[32,32]{1,0:T(8,128)S(1)} %broadcast_multiply_fusion.1), kind=kLoop, calls=%fused_computation.42 | loop fusion | flops 523264 | bytes 270336 | tf_op jit(solution)/shard_map/reduce_sum | solution.py:12
  32.2 0.3 fusion.41
  33.1 0.3 fusion.10
  33.4 0.2 fusion.21
  33.7 1.4 %copy.51 = bf16[32,32,128]{1,0,2:T(8,128)(2,1)S(1)} copy(bf16[32,32,128]{2,1,0:T(8,128)(2,1)S(1)} %fusion.21) | data formatting | bytes 524288 | tf_op jit(solution)/shard_map/convert_element_type | solution.py:90
  35.1 0.6 %fusion.93 = bf16[128,32,2]{1,2,0:T(2,128)(2,1)S(1)} fusion(bf16[32,32,128]{1,0,2:T(8,128)(2,1)S(1)} %copy.51, bf16[2,32,128]{1,0,2:T(2,128)(2,1)S(1)} %copy.52), kind=kOutput, calls=%fused_computation.107 | convolution fusion | flops 524288 | bytes 294912 | tf_op jit(solution)/shard_map/ikc,jkc->ijc/dot_general | solution.py:101
  36.2 0.3 fusion.92
  36.7 0.9 %fusion.37 = bf16[2,32,128]{2,1,0:T(8,128)(2,1)} fusion(f32[2,32,128]{2,1,0:T(8,128)S(1)} %get-tuple-element.12, bf16[512,128]{1,0:T(8,128)(2,1)S(1)} %copy-done, bf16[128,512]{1,0:T(8,128)(2,1)S(1)} %copy-done.4, f32[2,32]{1,0:T(2,128)S(1)} %add_rsqrt_fusion.2, f32[2,32]{1,0:T(2,128)S(1)} %broadcast_multiply_fusion.3), kind=kOutput, calls=%fused_computation.36 | convolution fusion | flops 16883712 | bytes 311808 | tf_op jit(solution)/shard_map/dot_general | solution.py:22
  (40 shorter events, 1.9 us)
Async XLA Ops:
  0.0 36.6 %copy-start = (bf16[512,128]{1,0:T(8,128)(2,1)S(1)}, bf16[512,128]{1,0:T(8,128)(2,1)}, u32[]{:S(2)}) copy-start(bf16[512,128]{1,0:T(8,128)(2,1)} %param.21) | copy-start | bytes 393220
  27.0 1.0 %copy-start.3 = (bf16[32,32,128]{2,1,0:T(8,128)(2,1)S(1)}, bf16[32,32,128]{2,1,0:T(8,128)(2,1)}, u32[]{:S(2)}) copy-start(bf16[32,32,128]{2,1,0:T(8,128)(2,1)} %param.16) | copy-start | bytes 786436
  28.0 4.6 %copy-start.1 = (bf16[4,128,128]{2,1,0:T(8,128)(2,1)S(1)}, bf16[4,128,128]{2,1,0:T(8,128)(2,1)}, u32[]{:S(2)}) copy-start(bf16[4,128,128]{2,1,0:T(8,128)(2,1)} %param.17) | copy-start | bytes 393220
  31.8 1.0 %copy-start.5 = (bf16[128,128]{1,0:T(8,128)(2,1)S(1)}, bf16[128,128]{1,0:T(8,128)(2,1)}, u32[]{:S(2)}) copy-start(bf16[128,128]{1,0:T(8,128)(2,1)} %param.18) | copy-start | bytes 98308
  33.7 2.5 %copy-start.2 = (bf16[128,128]{1,0:T(8,128)(2,1)S(1)}, bf16[128,128]{1,0:T(8,128)(2,1)}, u32[]{:S(2)}) copy-start(bf16[128,128]{1,0:T(8,128)(2,1)} %param.19) | copy-start | bytes 98308
  35.1 1.5 %copy-start.4 = (bf16[128,512]{1,0:T(8,128)(2,1)S(1)}, bf16[128,512]{1,0:T(8,128)(2,1)}, u32[]{:S(2)}) copy-start(bf16[128,512]{1,0:T(8,128)(2,1)} %param.20) | copy-start | bytes 393220

commit v3 on v2

--- a/solution.py
+++ b/solution.py
@@ -1,7 +1,7 @@
 import jax
 import jax.numpy as jnp
 from jax import lax
-from jax.sharding import Mesh, PartitionSpec as P
+from jax.sharding import PartitionSpec as P
 
 REPLICATED_PAIR_BYTES = 1 << 20
 
@@ -24,9 +24,9 @@
 
 
 def gather_all(block):
-    held = block[None]
-    for axis in ("x", "z_low", "z_high"):
-        held = lax.all_gather(held, axis, axis=0, tiled=True)
+    dap_count = lax.axis_size("dap")
+    copies = jnp.broadcast_to(block, (dap_count,) + block.shape)
+    held = lax.all_to_all(copies, "dap", split_axis=0, concat_axis=0)
     both = lax.all_gather(held, "sub", axis=0).swapaxes(0, 1)
     return both.reshape((-1,) + block.shape)
 
@@ -45,7 +45,7 @@
     transition_down_weight,
 ):
     row_count = pairwise_state.shape[0]
-    start_row = lax.axis_index(("z_high", "z_low", "x", "sub")) * row_count
+    start_row = lax.axis_index(("dap", "sub")) * row_count
     full_mask = residue_crop_mask.astype(jnp.float32)
     row_mask = lax.dynamic_slice_in_dim(full_mask, start_row, row_count, 0)
     alignment_keep = alignment_mask.astype(jnp.float32) * row_mask[None, :]
@@ -215,35 +215,16 @@
         P(),
     )
 
-    def distributed(*arrays):
-        return jax.shard_map(
-            shards,
-            mesh=mesh,
-            in_specs=placed,
-            out_specs=P(("crop", "dap", "sub"), None, None),
-            check_vma=False,
-        )(*arrays)
-
-    def replicated(*arrays):
-        dap = ("z_high", "z_low", "x")
-        fine = Mesh(
-            mesh.devices.reshape(mesh.shape["crop"], 2, 2, -1, mesh.shape["sub"]),
-            ("crop",) + dap + ("sub",),
-        )
-        rows = ("crop",) + dap + ("sub",)
-        return jax.shard_map(
-            shards_replicated,
-            mesh=fine,
-            in_specs=(P(rows, None, None), P("crop", rows[1:], None), P("crop", rows[1:]))
-            + placed[3:],
-            out_specs=P(rows, None, None),
-            check_vma=False,
-        )(*arrays)
-
-    def whole(pairwise_state, *rest):
+    def body(pairwise_state, *rest):
         residues, channels = pairwise_state.shape[1:]
         if residues * residues * channels * 2 <= REPLICATED_PAIR_BYTES:
-            return replicated(pairwise_state, *rest)
-        return distributed(pairwise_state, *rest)
-
-    return whole
+            return shards_replicated(pairwise_state, *rest)
+        return shards(pairwise_state, *rest)
+
+    return jax.shard_map(
+        body,
+        mesh=mesh,
+        in_specs=placed,
+        out_specs=P(("crop", "dap", "sub"), None, None),
+        check_vma=False,
+    )

time: 38.1 us -> 37.5 us (0.984)
  the two profiles are of different devices: /device:TPU:5 before, /device:TPU:0 now
where the time goes in v3:
time: 37.5 us; the launch traced here: 36.9 us
  waiting for transfers between devices  8.05 us (21%)
  matrix products  7.56 us (20%)
  starting transfers between devices  7.25 us (19%)
  other arithmetic  6.23 us (17%)
  local copies, waits for them, and re-layouts  5.32 us (14%)
  blocking collectives  2.09 us (6%)
    all_to_all x1, waiting for transfers between devices, gather_all(): held = lax.all_to_all(copies, 'dap', split_axis=0, concat_axis=0)  8.05 us
    all_to_all x1, starting transfers between devices, gather_all(): held = lax.all_to_all(copies, 'dap', split_axis=0, concat_axis=0)  7.25 us
    dot_general x1, matrix products, shards_replicated(): jnp.einsum('iltx,jlt->ijx', inner, right, preferred_element_type=jnp.floa...  3.8 us
    all_gather x1, blocking collectives, gather_all(): both = lax.all_gather(held, 'sub', axis=0).swapaxes(0, 1)  2.09 us
    reduce_sum x4, other arithmetic, norm_layer(): variance = jnp.mean(centered * centered, axis=reduce_axis, keepdims=True)  1.63 us
    convert_element_type x2, local copies, waits for them, and re-layouts, operand(): (jax.nn.sigmoid(gate_val) * proj_val * keep_rows[:, :, None]).astype(jnp....  1.63 us
    reduce_sum x2, other arithmetic, norm_layer(): average = jnp.mean(values, axis=reduce_axis, keepdims=True)  0.96 us
    dot_general x1, matrix products, transition(): jnp.dot(hidden, transition_down_weight, preferred_element_type=jnp.float32)  0.95 us
  transfers between devices with their start and end apart: 1, of which 1 were waited for; matrix products, arithmetic and copies ran while one was open for 0% of the time, Pallas kernels for 0%

profile of v3, /device:TPU:0, one launch (start us, length us, event | category | flops | bytes accessed | tf_op | source)
XLA Modules:
  0.0 36.9 jit_solution(1582252740613942055)
XLA Ops:
  0.0 0.7 %convert_element_type.85 = f32[32]{0:T(128)S(1)} convert(s32[32]{0:T(128)} %param.14) | non-fusion elementwise | flops 32 | bytes 256 | tf_op jit(solution)/shard_map/convert_element_type | solution.py:49
  0.7 0.9 %convert_reduce_fusion.1 = f32[32,2]{1,0:T(8,128)S(1)} fusion(bf16[32,2,256]{2,1,0:T(2,128)(2,1)} %param.12), kind=kLoop, calls=%fused_computation.51 | loop fusion | flops 32704 | bytes 33024 | tf_op jit(solution)/shard_map/reduce_sum | solution.py:10
  1.6 0.9 %fusion.51 = f32[32,2]{1,0:T(8,128)S(1)} fusion(bf16[32,2,256]{2,1,0:T(2,128)(2,1)} %param.12, f32[32,2]{1,0:T(8,128)S(1)} %broadcast_multiply_fusion.2), kind=kLoop, calls=%fused_computation.54 | loop fusion | flops 65472 | bytes 33280 | tf_op jit(solution)/shard_map/reduce_sum | solution.py:12
  2.5 0.9 %fusion.55 = bf16[32,2,256,1]{2,1,0,3:T(2,128)(2,1)S(1)} fusion(bf16[32,2,256]{2,1,0:T(2,128)(2,1)} %param.12, f32[32,2]{1,0:T(8,128)S(1)} %add_rsqrt_fusion.1, f32[32,2]{1,0:T(8,128)S(1)} %broadcast_multiply_fusion.2), kind=kLoop, calls=%fused_computation.59 | loop fusion | flops 65536 | bytes 66048 | tf_op jit(solution)/shard_map/convert_element_type | solution.py:52
  3.5 0.7 %convert_bitcast_fusion = (bf16[2,32]{1,0:T(2,128)(2,1)S(1)}, f32[32,2]{0,1:T(2,128)S(1)}) fusion(f32[2]{0:T(128)S(1)} %dynamic_slice.9, s32[32,2]{0,1:T(2,128)} %param.13), kind=kLoop, calls=%fused_computation.99 | loop fusion | flops 192 | bytes 648 | tf_op jit(solution)/shard_map/convert_element_type | solution.py:64
  4.3 0.9 %fusion.24 = bf16[32,2,2,32]{3,0,2,1:T(8,128)(2,1)S(1)} fusion(bf16[2,256,32]{1,2,0:T(8,128)(2,1)} %param.15, bf16[32,2,256,1]{2,1,0,3:T(2,128)(2,1)S(1)} %fusion.55, f32[32,2]{0,1:T(2,128)S(1)} %get-tuple-element.6), kind=kOutput, calls=%fused_computation.19 | convolution fusion | flops 2105344 | bytes 73984 | tf_op jit(solution)/shard_map/pxm,qmy->pxqy/dot_general | solution.py:53
  5.3 0.7 %fusion.72 = bf16[98,128]{1,0:T(8,128)(2,1)S(1)} fusion(bf16[2,32]{1,0:T(2,128)(2,1)S(1)} %get-tuple-element.5, bf16[32,128]{1,0:T(8,128)(2,1)S(1)} %reshape.128, bf16[64,128]{1,0:T(8,128)(2,1)} %bitcast.127), kind=kLoop, calls=%fused_computation.80 | loop fusion | flops 100352 | bytes 49792 | tf_op jit(solution)/shard_map/concatenate | solution.py:60
  6.0 0.7 %broadcast_in_dim.2 = bf16[8,98,128]{2,1,0:T(8,128)(2,1)} broadcast(bf16[98,128]{1,0:T(8,128)(2,1)S(1)} %fusion.72), dimensions={1,2} | broadcast | bytes 225792 | tf_op jit(solution)/shard_map/broadcast_in_dim | solution.py:28
  6.7 7.3 %all-to-all-start = ((bf16[8,98,128]{2,1,0:T(8,128)(2,1)}), bf16[8,98,128]{2,1,0:T(8,128)(2,1)S(1)}, u32[]{:S(2)}, u32[]{:S(2)}) async-start(bf16[8,98,128]{2,1,0:T(8,128)(2,1)} %broadcast_in_dim.2), calls=%async_computation | async-start | bytes 425984 | tf_op jit(solution)/shard_map/all_to_all | solution.py:29
  14.1 8.1 %all-to-all-done = bf16[8,98,128]{2,1,0:T(8,128)(2,1)S(1)} async-done(((bf16[8,98,128]{2,1,0:T(8,128)(2,1)}), bf16[8,98,128]{2,1,0:T(8,128)(2,1)S(1)}, u32[]{:S(2)}, u32[]{:S(2)}) %all-to-all-start) | async-done | bytes 200736 | tf_op jit(solution)/shard_map/all_to_all | solution.py:29
  22.2 2.1 %all-gather = bf16[16,98,128]{2,0,1:T(8,128)(2,1)S(1)} all-gather(bf16[8,98,128]{2,0,1:T(8,128)(2,1)S(1)} %copy.61), channel_id=2, replica_groups=mesh['crop'=2,'dap'=8,'sub'=2] {'sub'}, dimensions={0}, use_global_device_ids=true | all-gather | bytes 602112 | tf_op jit(solution)/shard_map/all_gather | solution.py:30
  24.3 0.3 copy.62
  24.8 0.2 reshape.130
  25.0 0.8 %fusion.88 = (bf16[16,32,2,1,32]{4,3,2,1,0:T(2,128)(2,1)S(1)}, bf16[16,32,2,1,32]{4,3,2,1,0:T(2,128)(2,1)S(1)}) fusion(bf16[16,32,2,2,32]{4,3,2,1,0:T(2,128)(2,1)S(1)} %reshape.130), kind=kLoop, calls=%fused_computation.105 | loop fusion | bytes 262144 | tf_op jit(solution)/shard_map/slice | solution.py:72
  25.9 0.4 %copy.66 = bf16[16,2,32,32]{2,1,0,3:T(2,128)(2,1)S(1)} copy(bf16[16,2,32,32]{3,2,1,0:T(8,128)(2,1)S(1)} %bitcast.122) | data formatting | bytes 131072 | tf_op jit(solution)/shard_map/transpose | solution.py:72
  26.7 0.6 %copy-done.3 = bf16[32,32,128]{2,1,0:T(8,128)(2,1)S(1)} copy-done((bf16[32,32,128]{2,1,0:T(8,128)(2,1)S(1)}, bf16[32,32,128]{2,1,0:T(8,128)(2,1)}, u32[]{:S(2)}) %copy-start.3) | copy-done | bytes 262168
  27.2 3.8 %convert_reduce_fusion = (f32[32,32]{1,0:T(8,128)S(1)}, bf16[32,32,128]{2,1,0:T(8,128)(2,1)S(1)}) fusion(f32[32,32,128]{2,1,0:T(8,128)S(1)} %bitcast.123, f32[32,32]{1,0:T(8,128)S(1)} %convolution_maximum_fusion.1, bf16[32,32,32,1]{2,0,1,3:T(8,128)(2,1)S(1)} %bitcast.125, bf16[32,32,32,1]{1,2,3,0:T(8,128)(2,1)S(1)} %bitcast.124, ...), kind=kOutput, calls=%fused_computation.39 | convolution fusion | flops 541719552 | bytes 1187840 | tf_op jit(solution)/shard_map/iltx,jlt->ijx/dot_general | solution.py:80
  31.0 0.4 %fusion.40 = f32[32,32]{1,0:T(8,128)S(1)} fusion(bf16[32,32,128]{2,1,0:T(8,128)(2,1)S(1)} %get-tuple-element.10, f32[32,32]{1,0:T(8,128)S(1)} %broadcast_multiply_fusion.1), kind=kLoop, calls=%fused_computation.42 | loop fusion | flops 523264 | bytes 270336 | tf_op jit(solution)/shard_map/reduce_sum | solution.py:12
  31.4 0.3 fusion.41
  32.0 0.3 fusion.10
  32.8 1.4 %copy.70 = bf16[32,32,128]{1,0,2:T(8,128)(2,1)S(1)} copy(bf16[32,32,128]{2,1,0:T(8,128)(2,1)S(1)} %fusion.21) | data formatting | bytes 524288 | tf_op jit(solution)/shard_map/convert_element_type | solution.py:90
  34.2 0.6 %fusion.92 = bf16[128,32,2]{1,2,0:T(2,128)(2,1)S(1)} fusion(bf16[32,32,128]{1,0,2:T(8,128)(2,1)S(1)} %copy.70, bf16[2,32,128]{1,0,2:T(2,128)(2,1)S(1)} %copy.71), kind=kOutput, calls=%fused_computation.107 | convolution fusion | flops 524288 | bytes 294912 | tf_op jit(solution)/shard_map/ikc,jkc->ijc/dot_general | solution.py:101
  35.4 0.3 fusion.91
  35.9 0.9 %fusion.37 = bf16[2,32,128]{2,1,0:T(8,128)(2,1)} fusion(f32[2,32,128]{2,1,0:T(8,128)S(1)} %get-tuple-element.12, bf16[512,128]{1,0:T(8,128)(2,1)S(1)} %copy-done, bf16[128,512]{1,0:T(8,128)(2,1)S(1)} %copy-done.4, f32[2,32]{1,0:T(2,128)S(1)} %add_rsqrt_fusion.2, f32[2,32]{1,0:T(2,128)S(1)} %broadcast_multiply_fusion.3), kind=kOutput, calls=%fused_computation.36 | convolution fusion | flops 16883712 | bytes 311808 | tf_op jit(solution)/shard_map/dot_general | solution.py:22
  (43 shorter events, 2.2 us)
Async XLA Ops:
  0.0 35.9 %copy-start = (bf16[512,128]{1,0:T(8,128)(2,1)S(1)}, bf16[512,128]{1,0:T(8,128)(2,1)}, u32[]{:S(2)}) copy-start(bf16[512,128]{1,0:T(8,128)(2,1)} %param.21) | copy-start | bytes 393220
  6.7 15.4 %all-to-all-start = ((bf16[8,98,128]{2,1,0:T(8,128)(2,1)}), bf16[8,98,128]{2,1,0:T(8,128)(2,1)S(1)}, u32[]{:S(2)}, u32[]{:S(2)}) async-start(bf16[8,98,128]{2,1,0:T(8,128)(2,1)} %broadcast_in_dim.2), calls=%async_computation | async-start | bytes 425984 | tf_op jit(solution)/shard_map/all_to_all | solution.py:29
  26.3 1.0 %copy-start.3 = (bf16[32,32,128]{2,1,0:T(8,128)(2,1)S(1)}, bf16[32,32,128]{2,1,0:T(8,128)(2,1)}, u32[]{:S(2)}) copy-start(bf16[32,32,128]{2,1,0:T(8,128)(2,1)} %param.16) | copy-start | bytes 786436
  27.2 4.6 %copy-start.1 = (bf16[4,128,128]{2,1,0:T(8,128)(2,1)S(1)}, bf16[4,128,128]{2,1,0:T(8,128)(2,1)}, u32[]{:S(2)}) copy-start(bf16[4,128,128]{2,1,0:T(8,128)(2,1)} %param.17) | copy-start | bytes 393220
  32.8 2.5 %copy-start.5 = (bf16[128,128]{1,0:T(8,128)(2,1)S(1)}, bf16[128,128]{1,0:T(8,128)(2,1)}, u32[]{:S(2)}) copy-start(bf16[128,128]{1,0:T(8,128)(2,1)} %param.18) | copy-start | bytes 98308
  34.2 1.2 %copy-start.2 = (bf16[128,128]{1,0:T(8,128)(2,1)S(1)}, bf16[128,128]{1,0:T(8,128)(2,1)}, u32[]{:S(2)}) copy-start(bf16[128,128]{1,0:T(8,128)(2,1)} %param.19) | copy-start | bytes 98308
  34.2 1.7 %copy-start.4 = (bf16[128,512]{1,0:T(8,128)(2,1)S(1)}, bf16[128,512]{1,0:T(8,128)(2,1)}, u32[]{:S(2)}) copy-start(bf16[128,512]{1,0:T(8,128)(2,1)} %param.20) | copy-start | bytes 393220

commit v4 on v0

--- a/solution.py
+++ b/solution.py
@@ -1,7 +1,11 @@
 import jax
 import jax.numpy as jnp
 from jax import lax
+from jax.experimental import pallas as pl
+from jax.experimental.pallas import tpu as pltpu
 from jax.sharding import PartitionSpec as P
+
+REPLICATED_PAIR_BYTES = 1 << 20
 
 
 def norm_layer(values, reduce_axis):
@@ -9,6 +13,260 @@
     centered = values - average
     variance = jnp.mean(centered * centered, axis=reduce_axis, keepdims=True)
     return centered * lax.rsqrt(variance + 1e-05)
+
+
+def transition(ln_two, pair_two, transition_up_weight, transition_down_weight):
+    hidden = jax.nn.relu(
+        jnp.dot(ln_two, transition_up_weight, preferred_element_type=jnp.float32)
+    ).astype(jnp.bfloat16)
+    return (
+        pair_two.astype(jnp.float32)
+        + jnp.dot(hidden, transition_down_weight, preferred_element_type=jnp.float32)
+    ).astype(jnp.bfloat16)
+
+
+def layer_norm(values):
+    count = values.shape[-1]
+    centered = values - jnp.sum(values, axis=-1, keepdims=True) * (1.0 / count)
+    variance = jnp.sum(centered * centered, axis=-1, keepdims=True) * (1.0 / count)
+    return centered * lax.rsqrt(variance + 1e-05)
+
+
+def pack_kernel(place_ref, mask_ref, keep_ref, state_ref, weight_ref, pair_ref, out_ref, normed_ref):
+    rows, residues, wide = pair_ref.shape
+    sequences = state_ref.shape[0]
+    channels = weight_ref.shape[1]
+    base = rows * residues
+    start = place_ref[0]
+    second_core = place_ref[1] == 1
+    for row in range(rows):
+        out_ref[row * residues : (row + 1) * residues] = pair_ref[row]
+    normed_ref[...] = layer_norm(state_ref[...].astype(jnp.float32))
+    eye = lax.broadcasted_iota(jnp.int32, (sequences, sequences), 0) == lax.broadcasted_iota(
+        jnp.int32, (sequences, sequences), 1
+    )
+    lefts, rights, keeps = [], [], []
+    for row in range(rows):
+        present = mask_ref[start + row].astype(jnp.float32)
+        keep_row = keep_ref[row : row + 1].astype(jnp.float32) * present
+        keep_column = jnp.sum(
+            jnp.where(eye, jnp.broadcast_to(keep_row, eye.shape), 0.0), axis=1, keepdims=True
+        )
+        normed = normed_ref[:, row].astype(jnp.bfloat16)
+        last = (((1,), (1,)), ((), ()))
+        left = lax.dot_general(weight_ref[0], normed, last, preferred_element_type=jnp.float32)
+        right = lax.dot_general(normed, weight_ref[1], last, preferred_element_type=jnp.float32)
+        lefts.append(left * keep_row)
+        rights.append(right * keep_column)
+        keeps.append(keep_row)
+    left = jnp.concatenate(lefts, axis=1)
+    right = jnp.concatenate(rights, axis=1)
+    first = jnp.concatenate([right, left], axis=1)
+    other = jnp.concatenate([left, right], axis=1)
+    out_ref[base : base + sequences] = jnp.where(second_core, other, first).astype(jnp.bfloat16)
+    keep = jnp.concatenate(
+        keeps + [jnp.zeros((16 - rows, sequences), jnp.float32)], axis=0
+    )
+    out_ref[base + sequences :] = jnp.concatenate(
+        [keep, jnp.zeros((16, wide - sequences), jnp.float32)], axis=1
+    ).astype(jnp.bfloat16)
+
+
+def update_kernel(
+    place_ref,
+    mask_ref,
+    held_ref,
+    outer_ref,
+    triangle_ref,
+    gate_ref,
+    output_ref,
+    up_ref,
+    down_ref,
+    out_ref,
+    block_ref,
+    left_ref,
+    right_ref,
+    keep_ref,
+    outer_product_ref,
+    pair_ref,
+    pair_one_ref,
+    ln_one_ref,
+):
+    rows, residues, wide = out_ref.shape
+    cores, chips = held_ref.shape[:2]
+    channels = outer_ref.shape[0]
+    sequences = channels
+    base = rows * residues
+    group = cores * rows
+    start = place_ref[0]
+    bf16 = jnp.bfloat16
+    f32 = jnp.float32
+
+    block_ref[...] = jnp.zeros_like(block_ref)
+    for d in range(channels):
+        weight = outer_ref[d]
+        for part in range(group):
+            block_ref[
+                (d * group + part) * channels : (d * group + part + 1) * channels,
+                part * wide : (part + 1) * wide,
+            ] = weight
+
+    lane = lax.broadcasted_iota(jnp.int32, (channels, wide), 1)
+    lane_block = lane // channels
+    for chip in range(chips):
+        packed = [held_ref[core, chip, base : base + sequences].astype(f32) for core in range(cores)]
+        right = jnp.where(lane < wide // 2, packed[0], packed[1]).astype(bf16)
+        for copy in range(group):
+            right_ref[copy * sequences : (copy + 1) * sequences, chip * wide : (chip + 1) * wide] = right
+        for core in range(cores):
+            for row in range(rows):
+                residue = (chip * cores + core) * rows + row
+                at = (rows if core == 0 else 0) + row
+                left_ref[residue] = jnp.where(lane_block == at, packed[core], 0.0)
+            presence = held_ref[core, chip, base + sequences :].astype(f32)
+            keep_ref[(chip * cores + core) * rows : (chip * cores + core + 1) * rows] = presence[:rows]
+            pair_ref[(chip * cores + core) * rows : (chip * cores + core + 1) * rows] = (
+                held_ref[core, chip, :base].astype(f32).reshape(rows, residues, wide)
+            )
+
+    last = (((1,), (1,)), ((), ()))
+    keep = keep_ref[...].astype(bf16)
+    count = lax.dot_general(keep, keep, last, preferred_element_type=f32)
+    inverse = 1.0 / jnp.maximum(count, 1.0)
+
+    step = 8
+    for first in range(0, channels, step):
+        left = jnp.concatenate(
+            [left_ref[:, d] for d in range(first, first + step)], axis=0
+        ).astype(bf16)
+        outer = jnp.dot(left, right_ref[...], preferred_element_type=f32).astype(bf16)
+        for d in range(first, first + step):
+            for chip in range(chips):
+                outer_product_ref[
+                    chip * residues : (chip + 1) * residues, d * wide : (d + 1) * wide
+                ] = outer[
+                    (d - first) * residues : (d - first + 1) * residues,
+                    chip * wide : (chip + 1) * wide,
+                ]
+    numerator = jnp.dot(outer_product_ref[...], block_ref[...], preferred_element_type=f32)
+
+    for k in range(residues):
+        chip, part = k // group, k % group
+        opm = numerator[
+            chip * residues : (chip + 1) * residues, part * wide : (part + 1) * wide
+        ] * jnp.broadcast_to(inverse[:, k : k + 1], (residues, wide))
+        pair_one = (pair_ref[:, k] + opm).astype(bf16).astype(f32)
+        pair_one_ref[k] = pair_one
+        ln_one_ref[k] = layer_norm(pair_one)
+
+    ln_all = ln_one_ref[...].reshape(residues * residues, wide).astype(bf16)
+    gate_value = jnp.dot(ln_all, triangle_ref[2], preferred_element_type=f32)
+    value = jnp.dot(ln_all, triangle_ref[3], preferred_element_type=f32)
+    right_tri = (jax.nn.sigmoid(gate_value) * value).astype(bf16).astype(f32)
+
+    mask_column = jnp.zeros((residues, 1), f32)
+    place = lax.broadcasted_iota(jnp.int32, (residues, 1), 0)
+    for k in range(residues):
+        mask_column = jnp.where(place == k, mask_ref[k].astype(f32), mask_column)
+
+    own_pair = jnp.concatenate([pair_one_ref[:, start + row] for row in range(rows)], axis=0)
+    own_ln = jnp.concatenate([ln_one_ref[:, start + row] for row in range(rows)], axis=0).astype(bf16)
+    gate_value = jnp.dot(own_ln, triangle_ref[0], preferred_element_type=f32)
+    value = jnp.dot(own_ln, triangle_ref[1], preferred_element_type=f32)
+    left_tri = jax.nn.sigmoid(gate_value) * value * jnp.concatenate([mask_column] * rows, axis=0)
+    left_tri = left_tri.astype(bf16).astype(f32)
+    products = []
+    for row in range(rows):
+        total = jnp.zeros((residues, wide), f32)
+        for k in range(residues):
+            at = row * residues + k
+            total += left_tri[at : at + 1] * right_tri[k * residues : (k + 1) * residues]
+        products.append(total * (mask_column * mask_ref[start + row].astype(f32)))
+    product = jnp.concatenate(products, axis=0).astype(bf16).astype(f32)
+    normed = layer_norm(product).astype(bf16)
+    update = jnp.dot(normed, output_ref[...], preferred_element_type=f32)
+    gate_out = jax.nn.sigmoid(jnp.dot(own_ln, gate_ref[...], preferred_element_type=f32))
+    pair_two = (own_pair + gate_out * update).astype(bf16).astype(f32)
+    ln_two = layer_norm(pair_two).astype(bf16)
+    hidden = jnp.maximum(jnp.dot(ln_two, up_ref[...], preferred_element_type=f32), 0.0).astype(bf16)
+    result = pair_two + jnp.dot(hidden, down_ref[...], preferred_element_type=f32)
+    out_ref[...] = result.astype(bf16).reshape(rows, residues, wide)
+
+
+def gather_all(block):
+    dap_count = lax.axis_size("dap")
+    copies = jnp.broadcast_to(block, (dap_count,) + block.shape)
+    held = lax.all_to_all(copies, "dap", split_axis=0, concat_axis=0)
+    return lax.all_gather(held, "sub", axis=0)
+
+
+def shards_replicated(
+    pairwise_state,
+    alignment_state,
+    alignment_mask,
+    residue_crop_mask,
+    outer_input_weight,
+    outer_output_weight,
+    triangle_input_weight,
+    triangle_gate,
+    triangle_output_weight,
+    transition_up_weight,
+    transition_down_weight,
+):
+    rows, residues, wide = pairwise_state.shape
+    sequences = alignment_state.shape[0]
+    channels = outer_input_weight.shape[2]
+    sub = lax.axis_index("sub")
+    start = (lax.axis_index("dap") * lax.axis_size("sub") + sub) * rows
+    place = jnp.stack([start, sub]).astype(jnp.int32)
+    scalar = pl.BlockSpec(memory_space=pltpu.SMEM)
+    vector = pl.BlockSpec(memory_space=pltpu.VMEM)
+    params = pltpu.CompilerParams(vmem_limit_bytes=40 << 20)
+    packed = pl.pallas_call(
+        pack_kernel,
+        out_shape=jax.ShapeDtypeStruct((rows * residues + sequences + 16, wide), jnp.bfloat16),
+        in_specs=[scalar] * 2 + [vector] * 4,
+        out_specs=vector,
+        scratch_shapes=[pltpu.VMEM(alignment_state.shape, jnp.float32)],
+        compiler_params=params,
+    )(
+        place,
+        residue_crop_mask,
+        alignment_mask.T,
+        alignment_state,
+        outer_input_weight.transpose(0, 2, 1),
+        pairwise_state,
+    )
+    held = gather_all(packed)
+    cores, chips = held.shape[:2]
+    group = cores * rows
+    return pl.pallas_call(
+        update_kernel,
+        out_shape=jax.ShapeDtypeStruct(pairwise_state.shape, jnp.bfloat16),
+        in_specs=[scalar] * 2 + [vector] * 7,
+        out_specs=vector,
+        scratch_shapes=[
+            pltpu.VMEM((channels * group * channels, group * wide), jnp.bfloat16),
+            pltpu.VMEM((residues, channels, wide), jnp.float32),
+            pltpu.VMEM((group * sequences, chips * wide), jnp.bfloat16),
+            pltpu.VMEM((residues, wide), jnp.float32),
+            pltpu.VMEM((chips * residues, channels * wide), jnp.bfloat16),
+            pltpu.VMEM((residues, residues, wide), jnp.float32),
+            pltpu.VMEM((residues, residues, wide), jnp.float32),
+            pltpu.VMEM((residues, residues, wide), jnp.float32),
+        ],
+        compiler_params=params,
+    )(
+        place,
+        residue_crop_mask,
+        held,
+        outer_output_weight,
+        triangle_input_weight,
+        triangle_gate,
+        triangle_output_weight,
+        transition_up_weight,
+        transition_down_weight,
+    )
 
 
 def shards(
@@ -92,17 +350,10 @@
     pair_two = (pair_one.astype(jnp.float32) + gate_out * update).astype(jnp.bfloat16)
     ln_two = norm_layer(pair_two.astype(jnp.float32), -1).astype(jnp.bfloat16)
 
-    def transition(row_pair):
-        row_ln, row_base = row_pair
-        hidden = jax.nn.relu(
-            jnp.dot(row_ln, transition_up_weight, preferred_element_type=jnp.float32)
-        ).astype(jnp.bfloat16)
-        return (
-            row_base.astype(jnp.float32)
-            + jnp.dot(hidden, transition_down_weight, preferred_element_type=jnp.float32)
-        ).astype(jnp.bfloat16)
-
-    return lax.map(transition, (ln_two, pair_two))
+    def step(row_pair):
+        return transition(*row_pair, transition_up_weight, transition_down_weight)
+
+    return lax.map(step, (ln_two, pair_two))
 
 
 def solution(mesh):
@@ -119,8 +370,15 @@
         P(),
         P(),
     )
+
+    def body(pairwise_state, *rest):
+        residues, channels = pairwise_state.shape[1:]
+        if residues * residues * channels * 2 <= REPLICATED_PAIR_BYTES:
+            return shards_replicated(pairwise_state, *rest)
+        return shards(pairwise_state, *rest)
+
     return jax.shard_map(
-        shards,
+        body,
         mesh=mesh,
         in_specs=placed,
         out_specs=P(("crop", "dap", "sub"), None, None),

time: 81.2 us -> 26.5 us (0.33)
  blocking collectives: 43 us -> 17.8 us
  waiting for transfers between devices: 16.2 us -> 0 us
  starting transfers between devices: 10.1 us -> 0 us
  Pallas kernels: 0 us -> 5.94 us
  local copies, waits for them, and re-layouts: 6.32 us -> 2.28 us
  matrix products: 2.43 us -> 0 us
  other arithmetic: 2.14 us -> 0.07 us
    all_gather x3 -> x1, blocking collectives: 43 us -> 2.27 us  [gather_all(): return lax.all_gather(held, 'sub', axis=0)]
    all_to_all x3 -> x0, waiting for transfers between devices: 16.2 us -> none  [the longest x1 6.42 us: shards(): lax.all_to_all(near_right, 'dap', split_axis=0, concat_axis=1, tiled=True)]
    all_to_all x0 -> x1, blocking collectives: none -> 15.5 us  [gather_all(): held = lax.all_to_all(copies, 'dap', split_axis=0, concat_axis=0)]
    all_to_all x3 -> x0, starting transfers between devices: 10.1 us -> none  [the longest x1 3.47 us: shards(): lax.all_to_all(product, 'dap', split_axis=1, concat_axis=0, tiled=True)]
    pallas_call x0 -> x2, Pallas kernels: none -> 5.94 us  [the longest x1 4.86 us: shards_replicated(): pl.pallas_call(update_kernel, out_shape=jax.ShapeDtypeStruct(pairwise_sta...]
    unnamed x30 -> x22, local copies, waits for them, and re-layouts: 5.32 us -> 2.24 us
    dot_general x13 -> x0, matrix products: 2.43 us -> none  [the longest x1 0.58 us: shards(): jnp.einsum('zkwv,znw->knv', inner_alignment, right_portion, preferred_ele...]
    reduce_sum x6 -> x0, other arithmetic: 1.5 us -> none  [the longest x2 0.97 us: norm_layer(): average = jnp.mean(values, axis=reduce_axis, keepdims=True)]
  transfers between devices with their start and end apart: 3 -> 0, of which waited for: 3 -> 0; matrix products, arithmetic and copies ran while one was open for 2% -> 0% of each run, Pallas kernels for 0% -> 0%
where the time goes in v4:
time: 26.5 us; the launch traced here: 26.1 us
  blocking collectives  17.8 us (67%)
  Pallas kernels  5.94 us (22%)
  local copies, waits for them, and re-layouts  2.28 us (9%)
    all_to_all x1, blocking collectives, gather_all(): held = lax.all_to_all(copies, 'dap', split_axis=0, concat_axis=0)  15.5 us
    pallas_call x1, Pallas kernels, shards_replicated(): pl.pallas_call(update_kernel, out_shape=jax.ShapeDtypeStruct(pairwise_sta...  4.86 us
    all_gather x1, blocking collectives, gather_all(): return lax.all_gather(held, 'sub', axis=0)  2.27 us
    unnamed x22, local copies, waits for them, and re-layouts  2.24 us
    pallas_call x1, Pallas kernels, shards_replicated(): pl.pallas_call(pack_kernel, out_shape=jax.ShapeDtypeStruct((rows * residu...  1.07 us

profile of v4, /device:TPU:0, one launch (start us, length us, event | category | flops | bytes accessed | tf_op | source)
XLA Modules:
  0.0 26.1 jit_solution(13414327610934175467)
XLA Ops:
  0.0 0.0 copy-start.8
  0.0 0.1 pad_add_fusion.place_ref
  0.1 0.0 copy-start.9
  0.1 0.0 copy-start.10
  0.1 0.6 %copy-done.8 = bf16[2,32,128]{2,1,0:T(8,128)(2,1)S(1)} copy-done((bf16[2,32,128]{2,1,0:T(8,128)(2,1)S(1)}, bf16[2,32,128]{2,1,0:T(8,128)(2,1)}, u32[]{:S(2)}) %copy-start.8) | copy-done | bytes 16408
  0.7 0.0 copy-done.9
  0.7 0.0 copy-done.10
  0.8 0.0 copy-start.4
  0.8 0.8 %copy-done.4 = bf16[32,2,256]{2,1,0:T(2,128)(2,1)S(1)} copy-done((bf16[32,2,256]{2,1,0:T(2,128)(2,1)S(1)}, bf16[32,2,256]{2,1,0:T(2,128)(2,1)}, u32[]{:S(2)}) %copy-start.4) | copy-done | bytes 32792
  1.5 0.0 copy-start.5
  1.5 0.8 %copy-done.5 = bf16[2,256,32]{1,2,0:T(8,128)(2,1)S(1)} copy-done((bf16[2,256,32]{1,2,0:T(8,128)(2,1)S(1)}, bf16[2,256,32]{1,2,0:T(8,128)(2,1)}, u32[]{:S(2)}) %copy-start.5) | copy-done | bytes 32792
  2.3 1.1 %shard_map.109 = bf16[112,128]{1,0:T(8,128)(2,1)S(1)} custom-call(s32[2]{0:T(128)S(1)} %pad_add_fusion.place_ref, s32[32]{0:T(128)S(1)} %copy-done.9, s32[2,32]{1,0:T(2,128)S(1)} %bitcast.7, bf16[32,2,256]{2,1,0:T(2,128)(2,1)S(1)} %copy-done.4, bf16[2,32,256]{2,1,0:T(8,128)(2,1)S(1)} %bitcast.6, bf16[2,32,128]{2,1,0:T(8,128)(2,1)S(1)} %copy-done.8), custom_call_target="tpu_custom_call" | custom-call | tf_op jit(solution)/shard_map/pallas_call | solution.py:225
  3.4 0.0 copy-start.7
  3.4 15.5 %all_to_all.5 = bf16[8,112,128]{2,1,0:T(8,128)(2,1)S(1)} all-to-all(bf16[8,112,128]{2,1,0:T(8,128)(2,1)S(1)} %broadcast_in_dim.3), channel_id=1, replica_groups=mesh['crop'=2,'dap'=8,'sub'=2] {'dap'}, dimensions={0} | all-to-all | bytes 458752 | tf_op jit(solution)/shard_map/all_to_all | solution.py:199
  18.9 0.0 copy-start
  18.9 0.0 copy-start.6
  18.9 2.3 %all-gather = bf16[16,112,128]{2,1,0:T(8,128)(2,1)S(1)} all-gather(bf16[8,112,128]{2,1,0:T(8,128)(2,1)S(1)} %all_to_all.5), channel_id=2, replica_groups=mesh['crop'=2,'dap'=8,'sub'=2] {'sub'}, dimensions={0}, use_global_device_ids=true | all-gather | bytes 688128 | tf_op jit(solution)/shard_map/all_gather | solution.py:200
  21.2 0.0 copy-done.7
  21.2 0.0 copy-done
  21.2 0.0 copy-done.1
  21.2 0.0 copy-done.2
  21.2 0.0 copy-done.3
  21.2 0.0 copy-done.6
  21.2 4.9 %shard_map.110 = bf16[2,32,128]{2,1,0:T(8,128)(2,1)} custom-call(s32[2]{0:T(128)S(1)} %pad_add_fusion.place_ref, s32[32]{0:T(128)S(1)} %copy-done.9, bf16[2,8,112,128]{3,2,1,0:T(8,128)(2,1)S(1)} %bitcast.5, bf16[32,32,128]{2,1,0:T(8,128)(2,1)S(1)} %copy-done, bf16[4,128,128]{2,1,0:T(8,128)(2,1)S(1)} %copy-done.1, bf16[128,128]{1,0:T(8,128)(2,1)S(1)} %copy-done.6, ...), custom_call_target="tpu_custom_call" | custom-call | tf_op jit(solution)/shard_map/pallas_call | solution.py:243
  (4 shorter events, 0.0 us)
Async XLA Ops:
  0.0 0.7 %copy-start.8 = (bf16[2,32,128]{2,1,0:T(8,128)(2,1)S(1)}, bf16[2,32,128]{2,1,0:T(8,128)(2,1)}, u32[]{:S(2)}) copy-start(bf16[2,32,128]{2,1,0:T(8,128)(2,1)} %pair_ref.1) | copy-start | bytes 49156
  0.1 0.7 %copy-start.9 = (s32[32]{0:T(128)S(1)}, s32[32]{0:T(128)}, u32[]{:S(2)}) copy-start(s32[32]{0:T(128)} %mask_ref.3) | copy-start | bytes 388
  0.1 0.7 %copy-start.10 = (s32[32,2]{0,1:T(2,128)S(1)}, s32[32,2]{0,1:T(2,128)}, u32[]{:S(2)}) copy-start(s32[32,2]{0,1:T(2,128)} %param.13) | copy-start | bytes 772
  0.8 0.8 %copy-start.4 = (bf16[32,2,256]{2,1,0:T(2,128)(2,1)S(1)}, bf16[32,2,256]{2,1,0:T(2,128)(2,1)}, u32[]{:S(2)}) copy-start(bf16[32,2,256]{2,1,0:T(2,128)(2,1)} %state_ref.1) | copy-start | bytes 98308
  1.5 0.8 %copy-start.5 = (bf16[2,256,32]{1,2,0:T(8,128)(2,1)S(1)}, bf16[2,256,32]{1,2,0:T(8,128)(2,1)}, u32[]{:S(2)}) copy-start(bf16[2,256,32]{1,2,0:T(8,128)(2,1)} %param.15) | copy-start | bytes 98308
  3.4 17.8 %copy-start.7 = (bf16[128,128]{1,0:T(8,128)(2,1)S(1)}, bf16[128,128]{1,0:T(8,128)(2,1)}, u32[]{:S(2)}) copy-start(bf16[128,128]{1,0:T(8,128)(2,1)} %output_ref.1) | copy-start | bytes 98308
  18.9 2.3 %copy-start = (bf16[32,32,128]{2,1,0:T(8,128)(2,1)S(1)}, bf16[32,32,128]{2,1,0:T(8,128)(2,1)}, u32[]{:S(2)}) copy-start(bf16[32,32,128]{2,1,0:T(8,128)(2,1)} %outer_ref.1) | copy-start | bytes 786436
  18.9 2.3 %copy-start.1 = (bf16[4,128,128]{2,1,0:T(8,128)(2,1)S(1)}, bf16[4,128,128]{2,1,0:T(8,128)(2,1)}, u32[]{:S(2)}) copy-start(bf16[4,128,128]{2,1,0:T(8,128)(2,1)} %triangle_ref.1) | copy-start | bytes 393220
  18.9 2.3 %copy-start.2 = (bf16[128,512]{1,0:T(8,128)(2,1)S(1)}, bf16[128,512]{1,0:T(8,128)(2,1)}, u32[]{:S(2)}) copy-start(bf16[128,512]{1,0:T(8,128)(2,1)} %up_ref.1) | copy-start | bytes 393220
  18.9 2.3 %copy-start.3 = (bf16[512,128]{1,0:T(8,128)(2,1)S(1)}, bf16[512,128]{1,0:T(8,128)(2,1)}, u32[]{:S(2)}) copy-start(bf16[512,128]{1,0:T(8,128)(2,1)} %down_ref.1) | copy-start | bytes 393220
  18.9 2.3 %copy-start.6 = (bf16[128,128]{1,0:T(8,128)(2,1)S(1)}, bf16[128,128]{1,0:T(8,128)(2,1)}, u32[]{:S(2)}) copy-start(bf16[128,128]{1,0:T(8,128)(2,1)} %gate_ref.1) | copy-start | bytes 98308

commit v5 on v4

--- a/solution.py
+++ b/solution.py
@@ -32,20 +32,48 @@
     return centered * lax.rsqrt(variance + 1e-05)
 
 
-def pack_kernel(place_ref, mask_ref, keep_ref, state_ref, weight_ref, pair_ref, out_ref, normed_ref):
-    rows, residues, wide = pair_ref.shape
+def first_row(rows):
+    return (lax.axis_index("dap") * lax.axis_size("sub") + lax.axis_index("sub")) * rows
+
+
+def pack_kernel(
+    mask_ref,
+    keep_hbm,
+    state_hbm,
+    weight_hbm,
+    pair_hbm,
+    out_ref,
+    keep_ref,
+    state_ref,
+    weight_ref,
+    normed_ref,
+    sems,
+):
+    rows, residues, wide = pair_hbm.shape
     sequences = state_ref.shape[0]
-    channels = weight_ref.shape[1]
     base = rows * residues
-    start = place_ref[0]
-    second_core = place_ref[1] == 1
-    for row in range(rows):
-        out_ref[row * residues : (row + 1) * residues] = pair_ref[row]
+    start = first_row(rows)
+    second_core = lax.axis_index("sub") == 1
+    loads = [
+        pltpu.make_async_copy(state_hbm, state_ref, sems.at[0]),
+        pltpu.make_async_copy(weight_hbm, weight_ref, sems.at[1]),
+        pltpu.make_async_copy(keep_hbm, keep_ref, sems.at[2]),
+    ] + [
+        pltpu.make_async_copy(
+            pair_hbm.at[row], out_ref.at[pl.ds(row * residues, residues)], sems.at[3 + row]
+        )
+        for row in range(rows)
+    ]
+    for load in loads:
+        load.start()
+    loads[0].wait()
     normed_ref[...] = layer_norm(state_ref[...].astype(jnp.float32))
     eye = lax.broadcasted_iota(jnp.int32, (sequences, sequences), 0) == lax.broadcasted_iota(
         jnp.int32, (sequences, sequences), 1
     )
     lefts, rights, keeps = [], [], []
+    for load in loads[1:]:
+        load.wait()
     for row in range(rows):
         present = mask_ref[start + row].astype(jnp.float32)
         keep_row = keep_ref[row : row + 1].astype(jnp.float32) * present
@@ -73,7 +101,6 @@
 
 
 def update_kernel(
-    place_ref,
     mask_ref,
     held_ref,
     outer_ref,
@@ -98,7 +125,7 @@
     sequences = channels
     base = rows * residues
     group = cores * rows
-    start = place_ref[0]
+    start = first_row(rows)
     bf16 = jnp.bfloat16
     f32 = jnp.float32
 
@@ -194,10 +221,7 @@
 
 
 def gather_all(block):
-    dap_count = lax.axis_size("dap")
-    copies = jnp.broadcast_to(block, (dap_count,) + block.shape)
-    held = lax.all_to_all(copies, "dap", split_axis=0, concat_axis=0)
-    return lax.all_gather(held, "sub", axis=0)
+    return lax.all_gather(lax.all_gather(block, "dap", axis=0), "sub", axis=0)
 
 
 def shards_replicated(
@@ -216,21 +240,24 @@
     rows, residues, wide = pairwise_state.shape
     sequences = alignment_state.shape[0]
     channels = outer_input_weight.shape[2]
-    sub = lax.axis_index("sub")
-    start = (lax.axis_index("dap") * lax.axis_size("sub") + sub) * rows
-    place = jnp.stack([start, sub]).astype(jnp.int32)
     scalar = pl.BlockSpec(memory_space=pltpu.SMEM)
     vector = pl.BlockSpec(memory_space=pltpu.VMEM)
     params = pltpu.CompilerParams(vmem_limit_bytes=40 << 20)
+    hbm = pl.BlockSpec(memory_space=pltpu.HBM)
     packed = pl.pallas_call(
         pack_kernel,
         out_shape=jax.ShapeDtypeStruct((rows * residues + sequences + 16, wide), jnp.bfloat16),
-        in_specs=[scalar] * 2 + [vector] * 4,
+        in_specs=[scalar] + [hbm] * 4,
         out_specs=vector,
-        scratch_shapes=[pltpu.VMEM(alignment_state.shape, jnp.float32)],
-        compiler_params=params,
+        scratch_shapes=[
+            pltpu.VMEM((rows, sequences), jnp.int32),
+            pltpu.VMEM(alignment_state.shape, jnp.bfloat16),
+            pltpu.VMEM((2, channels, alignment_state.shape[2]), jnp.bfloat16),
+            pltpu.VMEM(alignment_state.shape, jnp.float32),
+            pltpu.SemaphoreType.DMA((3 + rows,)),
+        ],
+        compiler_params=pltpu.CompilerParams(vmem_limit_bytes=63 << 20),
     )(
-        place,
         residue_crop_mask,
         alignment_mask.T,
         alignment_state,
@@ -243,7 +270,7 @@
     return pl.pallas_call(
         update_kernel,
         out_shape=jax.ShapeDtypeStruct(pairwise_state.shape, jnp.bfloat16),
-        in_specs=[scalar] * 2 + [vector] * 7,
+        in_specs=[scalar] + [vector] * 7,
         out_specs=vector,
         scratch_shapes=[
             pltpu.VMEM((channels * group * channels, group * wide), jnp.bfloat16),
@@ -257,7 +284,6 @@
         ],
         compiler_params=params,
     )(
-        place,
         residue_crop_mask,
         held,
         outer_output_weight,

time: 26.5 us -> 43.4 us (1.64)
  blocking collectives: 17.8 us -> 34.9 us
  local copies, waits for them, and re-layouts: 2.28 us -> 0.64 us
  Pallas kernels: 5.94 us -> 7.46 us
    all_gather x1 -> x2, blocking collectives: 2.27 us -> 34.9 us  [gather_all(): return lax.all_gather(lax.all_gather(block, 'dap', axis=0), 'sub', axis=0)]
    all_to_all x1 -> x0, blocking collectives: 15.5 us -> none  [gather_all(): held = lax.all_to_all(copies, 'dap', split_axis=0, concat_axis=0)]
    unnamed x22 -> x14, local copies, waits for them, and re-layouts: 2.24 us -> 0.64 us
    pallas_call x1, Pallas kernels: 1.07 us -> 2.63 us  [shards_replicated(): pl.pallas_call(pack_kernel, out_shape=jax.ShapeDtypeStruct((rows * residu...]
where the time goes in v5:
time: 43.4 us; the launch traced here: 43.1 us
  blocking collectives  34.9 us (80%)
  Pallas kernels  7.46 us (17%)
  local copies, waits for them, and re-layouts  0.64 us (1%)
    all_gather x2, blocking collectives, gather_all(): return lax.all_gather(lax.all_gather(block, 'dap', axis=0), 'sub', axis=0)  34.9 us
    pallas_call x1, Pallas kernels, shards_replicated(): pl.pallas_call(update_kernel, out_shape=jax.ShapeDtypeStruct(pairwise_sta...  4.84 us
    pallas_call x1, Pallas kernels, shards_replicated(): pl.pallas_call(pack_kernel, out_shape=jax.ShapeDtypeStruct((rows * residu...  2.63 us

profile of v5, /device:TPU:0, one launch (start us, length us, event | category | flops | bytes accessed | tf_op | source)
XLA Modules:
  0.0 43.1 jit_solution(14006538050295419359)
XLA Ops:
  0.0 2.6 %shard_map.109 = bf16[112,128]{1,0:T(8,128)(2,1)} custom-call(s32[32]{0:T(128)} %mask_ref.3, s32[2,32]{1,0:T(2,128)} %bitcast.7, bf16[32,2,256]{2,1,0:T(2,128)(2,1)} %state_hbm.1, bf16[2,32,256]{2,1,0:T(8,128)(2,1)} %bitcast.6, bf16[2,32,128]{2,1,0:T(8,128)(2,1)} %pair_hbm.1), custom_call_target="tpu_custom_call" | custom-call | tf_op jit(solution)/shard_map/pallas_call | solution.py:247
  2.6 0.0 copy-start.5
  2.6 32.7 %all-gather = bf16[896,128]{1,0:T(8,128)(2,1)S(1)} all-gather(bf16[112,128]{1,0:T(8,128)(2,1)} %shard_map.109), channel_id=2, replica_groups=mesh['crop'=2,'dap'=8,'sub'=2] {'dap'}, dimensions={0}, use_global_device_ids=true | all-gather | bytes 258048 | tf_op jit(solution)/shard_map/all_gather | solution.py:224
  35.3 0.0 copy-start
  35.3 0.0 copy-start.1
  35.3 0.0 copy-start.2
  35.3 0.0 copy-start.3
  35.4 0.0 copy-start.4
  35.4 2.3 %all-gather.1 = bf16[16,112,128]{2,1,0:T(8,128)(2,1)S(1)} all-gather(bf16[8,112,128]{2,1,0:T(8,128)(2,1)S(1)} %bitcast.5), channel_id=3, replica_groups=mesh['crop'=2,'dap'=8,'sub'=2] {'sub'}, dimensions={0}, use_global_device_ids=true | all-gather | bytes 688128 | tf_op jit(solution)/shard_map/all_gather | solution.py:224
  37.6 0.0 copy-start.6
  37.6 0.0 copy-done.5
  37.6 0.0 copy-done
  37.6 0.0 copy-done.1
  37.6 0.0 copy-done.2
  37.7 0.0 copy-done.3
  37.7 0.0 copy-done.4
  37.7 0.6 %copy-done.6 = s32[32]{0:T(128)S(1)} copy-done((s32[32]{0:T(128)S(1)}, s32[32]{0:T(128)}, u32[]{:S(2)}) %copy-start.6) | copy-done | bytes 152
  38.3 4.8 %shard_map.110 = bf16[2,32,128]{2,1,0:T(8,128)(2,1)} custom-call(s32[32]{0:T(128)S(1)} %copy-done.6, bf16[2,8,112,128]{3,2,1,0:T(8,128)(2,1)S(1)} %bitcast.4, bf16[32,32,128]{2,1,0:T(8,128)(2,1)S(1)} %copy-done, bf16[4,128,128]{2,1,0:T(8,128)(2,1)S(1)} %copy-done.1, bf16[128,128]{1,0:T(8,128)(2,1)S(1)} %copy-done.4, bf16[128,128]{1,0:T(8,128)(2,1)S(1)} %copy-done.5, ...), custom_call_target="tpu_custom_call" | custom-call | tf_op jit(solution)/shard_map/pallas_call | solution.py:270
Async XLA Ops:
  2.6 35.0 %copy-start.5 = (bf16[128,128]{1,0:T(8,128)(2,1)S(1)}, bf16[128,128]{1,0:T(8,128)(2,1)}, u32[]{:S(2)}) copy-start(bf16[128,128]{1,0:T(8,128)(2,1)} %output_ref.1) | copy-start | bytes 98308
  35.3 2.3 %copy-start = (bf16[32,32,128]{2,1,0:T(8,128)(2,1)S(1)}, bf16[32,32,128]{2,1,0:T(8,128)(2,1)}, u32[]{:S(2)}) copy-start(bf16[32,32,128]{2,1,0:T(8,128)(2,1)} %outer_ref.1) | copy-start | bytes 786436
  35.3 2.3 %copy-start.1 = (bf16[4,128,128]{2,1,0:T(8,128)(2,1)S(1)}, bf16[4,128,128]{2,1,0:T(8,128)(2,1)}, u32[]{:S(2)}) copy-start(bf16[4,128,128]{2,1,0:T(8,128)(2,1)} %triangle_ref.1) | copy-start | bytes 393220
  35.3 2.3 %copy-start.2 = (bf16[128,512]{1,0:T(8,128)(2,1)S(1)}, bf16[128,512]{1,0:T(8,128)(2,1)}, u32[]{:S(2)}) copy-start(bf16[128,512]{1,0:T(8,128)(2,1)} %up_ref.1) | copy-start | bytes 393220
  35.3 2.3 %copy-start.3 = (bf16[512,128]{1,0:T(8,128)(2,1)S(1)}, bf16[512,128]{1,0:T(8,128)(2,1)}, u32[]{:S(2)}) copy-start(bf16[512,128]{1,0:T(8,128)(2,1)} %down_ref.1) | copy-start | bytes 393220
  35.4 2.3 %copy-start.4 = (bf16[128,128]{1,0:T(8,128)(2,1)S(1)}, bf16[128,128]{1,0:T(8,128)(2,1)}, u32[]{:S(2)}) copy-start(bf16[128,128]{1,0:T(8,128)(2,1)} %gate_ref.1) | copy-start | bytes 98308
  37.6 0.7 %copy-start.6 = (s32[32]{0:T(128)S(1)}, s32[32]{0:T(128)}, u32[]{:S(2)}) copy-start(s32[32]{0:T(128)} %mask_ref.3) | copy-start | bytes 388

commit v6 on v5

--- a/solution.py
+++ b/solution.py
@@ -37,16 +37,17 @@
 
 
 def pack_kernel(
-    mask_ref,
+    mask_hbm,
     keep_hbm,
     state_hbm,
     weight_hbm,
     pair_hbm,
     out_ref,
+    mask_ref,
     keep_ref,
     state_ref,
     weight_ref,
-    normed_ref,
+    wide_ref,
     sems,
 ):
     rows, residues, wide = pair_hbm.shape
@@ -58,16 +59,18 @@
         pltpu.make_async_copy(state_hbm, state_ref, sems.at[0]),
         pltpu.make_async_copy(weight_hbm, weight_ref, sems.at[1]),
         pltpu.make_async_copy(keep_hbm, keep_ref, sems.at[2]),
+        pltpu.make_async_copy(mask_hbm, mask_ref, sems.at[3]),
     ] + [
         pltpu.make_async_copy(
-            pair_hbm.at[row], out_ref.at[pl.ds(row * residues, residues)], sems.at[3 + row]
+            pair_hbm.at[row], out_ref.at[pl.ds(row * residues, residues)], sems.at[4 + row]
         )
         for row in range(rows)
     ]
     for load in loads:
         load.start()
     loads[0].wait()
-    normed_ref[...] = layer_norm(state_ref[...].astype(jnp.float32))
+    wide_ref[...] = state_ref[...].astype(jnp.float32)
+    normed_rows = [layer_norm(wide_ref[:, row]).astype(jnp.bfloat16) for row in range(rows)]
     eye = lax.broadcasted_iota(jnp.int32, (sequences, sequences), 0) == lax.broadcasted_iota(
         jnp.int32, (sequences, sequences), 1
     )
@@ -80,7 +83,7 @@
         keep_column = jnp.sum(
             jnp.where(eye, jnp.broadcast_to(keep_row, eye.shape), 0.0), axis=1, keepdims=True
         )
-        normed = normed_ref[:, row].astype(jnp.bfloat16)
+        normed = normed_rows[row]
         last = (((1,), (1,)), ((), ()))
         left = lax.dot_general(weight_ref[0], normed, last, preferred_element_type=jnp.float32)
         right = lax.dot_general(normed, weight_ref[1], last, preferred_element_type=jnp.float32)
@@ -103,6 +106,7 @@
 def update_kernel(
     mask_ref,
     held_ref,
+    other_ref,
     outer_ref,
     triangle_ref,
     gate_ref,
@@ -120,12 +124,13 @@
     ln_one_ref,
 ):
     rows, residues, wide = out_ref.shape
-    cores, chips = held_ref.shape[:2]
+    cores, chips = 2, held_ref.shape[0]
     channels = outer_ref.shape[0]
     sequences = channels
     base = rows * residues
     group = cores * rows
     start = first_row(rows)
+    second_core = lax.axis_index("sub") == 1
     bf16 = jnp.bfloat16
     f32 = jnp.float32
 
@@ -141,7 +146,10 @@
     lane = lax.broadcasted_iota(jnp.int32, (channels, wide), 1)
     lane_block = lane // channels
     for chip in range(chips):
-        packed = [held_ref[core, chip, base : base + sequences].astype(f32) for core in range(cores)]
+        place = xor_place(chip, chips)
+        mine, other = held_ref[place], other_ref[place]
+        blocks = [jnp.where(second_core, other, mine), jnp.where(second_core, mine, other)]
+        packed = [block[base : base + sequences].astype(f32) for block in blocks]
         right = jnp.where(lane < wide // 2, packed[0], packed[1]).astype(bf16)
         for copy in range(group):
             right_ref[copy * sequences : (copy + 1) * sequences, chip * wide : (chip + 1) * wide] = right
@@ -150,10 +158,10 @@
                 residue = (chip * cores + core) * rows + row
                 at = (rows if core == 0 else 0) + row
                 left_ref[residue] = jnp.where(lane_block == at, packed[core], 0.0)
-            presence = held_ref[core, chip, base + sequences :].astype(f32)
+            presence = blocks[core][base + sequences :].astype(f32)
             keep_ref[(chip * cores + core) * rows : (chip * cores + core + 1) * rows] = presence[:rows]
             pair_ref[(chip * cores + core) * rows : (chip * cores + core + 1) * rows] = (
-                held_ref[core, chip, :base].astype(f32).reshape(rows, residues, wide)
+                blocks[core][:base].astype(f32).reshape(rows, residues, wide)
             )
 
     last = (((1,), (1,)), ((), ()))
@@ -221,7 +229,25 @@
 
 
 def gather_all(block):
-    return lax.all_gather(lax.all_gather(block, "dap", axis=0), "sub", axis=0)
+    dap_count = lax.axis_size("dap")
+    held = block[None]
+    step = dap_count // 2
+    while step:
+        got = lax.ppermute(held, "dap", [(src, src ^ step) for src in range(dap_count)])
+        held = jnp.concatenate([held, got], axis=0)
+        step //= 2
+    return held, lax.ppermute(held, "sub", [(0, 1), (1, 0)])
+
+
+def xor_place(chip, chips):
+    difference = lax.bitwise_xor(lax.axis_index("dap"), chip)
+    place = 0
+    step, bit = chips // 2, 1
+    while step:
+        place = place + jnp.where(lax.bitwise_and(difference, step) != 0, bit, 0)
+        step //= 2
+        bit *= 2
+    return place
 
 
 def shards_replicated(
@@ -247,14 +273,15 @@
     packed = pl.pallas_call(
         pack_kernel,
         out_shape=jax.ShapeDtypeStruct((rows * residues + sequences + 16, wide), jnp.bfloat16),
-        in_specs=[scalar] + [hbm] * 4,
+        in_specs=[hbm] * 5,
         out_specs=vector,
         scratch_shapes=[
+            pltpu.SMEM((residues,), jnp.int32),
             pltpu.VMEM((rows, sequences), jnp.int32),
             pltpu.VMEM(alignment_state.shape, jnp.bfloat16),
             pltpu.VMEM((2, channels, alignment_state.shape[2]), jnp.bfloat16),
             pltpu.VMEM(alignment_state.shape, jnp.float32),
-            pltpu.SemaphoreType.DMA((3 + rows,)),
+            pltpu.SemaphoreType.DMA((4 + rows,)),
         ],
         compiler_params=pltpu.CompilerParams(vmem_limit_bytes=63 << 20),
     )(
@@ -264,13 +291,13 @@
         outer_input_weight.transpose(0, 2, 1),
         pairwise_state,
     )
-    held = gather_all(packed)
-    cores, chips = held.shape[:2]
+    held, other = gather_all(packed)
+    cores, chips = 2, held.shape[0]
     group = cores * rows
     return pl.pallas_call(
         update_kernel,
         out_shape=jax.ShapeDtypeStruct(pairwise_state.shape, jnp.bfloat16),
-        in_specs=[scalar] + [vector] * 7,
+        in_specs=[scalar] + [vector] * 8,
         out_specs=vector,
         scratch_shapes=[
             pltpu.VMEM((channels * group * channels, group * wide), jnp.bfloat16),
@@ -286,6 +313,7 @@
     )(
         residue_crop_mask,
         held,
+        other,
         outer_output_weight,
         triangle_input_weight,
         triangle_gate,

time: 43.4 us -> 24.7 us (0.57)
  blocking collectives: 34.9 us -> 0 us
  waiting for transfers between devices: 0 us -> 8.62 us
  starting transfers between devices: 0 us -> 8.13 us
  other arithmetic: 0 us -> 0.8 us
  Pallas kernels: 7.46 us -> 6.78 us
  local copies, waits for them, and re-layouts: 0.64 us -> 0.04 us
    all_gather x2 -> x0, blocking collectives: 34.9 us -> none  [gather_all(): return lax.all_gather(lax.all_gather(block, 'dap', axis=0), 'sub', axis=0)]
    ppermute x0 -> x4, waiting for transfers between devices: none -> 8.62 us  [the longest x3 7.15 us: gather_all(): lax.ppermute(held, 'dap', [(src, src ^ step) for src in range(dap_count)])]
    ppermute x0 -> x4, starting transfers between devices: none -> 8.13 us  [the longest x3 8.06 us: gather_all(): lax.ppermute(held, 'dap', [(src, src ^ step) for src in range(dap_count)])]
    concatenate x0 -> x3, other arithmetic: none -> 0.8 us  [gather_all(): held = jnp.concatenate([held, got], axis=0)]
    pallas_call x1, Pallas kernels: 2.63 us -> 1.92 us  [shards_replicated(): pl.pallas_call(pack_kernel, out_shape=jax.ShapeDtypeStruct((rows * residu...]
    unnamed x14 -> x16, local copies, waits for them, and re-layouts: 0.64 us -> 0.04 us
  transfers between devices with their start and end apart: 0 -> 4, of which waited for: 0 -> 4; matrix products, arithmetic and copies ran while one was open for 0% -> 0% of each run, Pallas kernels for 0% -> 0%
where the time goes in v6:
time: 24.7 us; the launch traced here: 24.5 us
  waiting for transfers between devices  8.62 us (35%)
  starting transfers between devices  8.13 us (33%)
  Pallas kernels  6.78 us (27%)
  other arithmetic  0.8 us (3%)
    ppermute x3, starting transfers between devices, gather_all(): lax.ppermute(held, 'dap', [(src, src ^ step) for src in range(dap_count)])  8.06 us
    ppermute x3, waiting for transfers between devices, gather_all(): lax.ppermute(held, 'dap', [(src, src ^ step) for src in range(dap_count)])  7.15 us
    pallas_call x1, Pallas kernels, shards_replicated(): pl.pallas_call(update_kernel, out_shape=jax.ShapeDtypeStruct(pairwise_sta...  4.87 us
    pallas_call x1, Pallas kernels, shards_replicated(): pl.pallas_call(pack_kernel, out_shape=jax.ShapeDtypeStruct((rows * residu...  1.92 us
    ppermute x1, waiting for transfers between devices, gather_all(): return (held, lax.ppermute(held, 'sub', [(0, 1), (1, 0)]))  1.48 us
    concatenate x3, other arithmetic, gather_all(): held = jnp.concatenate([held, got], axis=0)  0.8 us
  transfers between devices with their start and end apart: 4, of which 4 were waited for; matrix products, arithmetic and copies ran while one was open for 0% of the time, Pallas kernels for 0%

profile of v6, /device:TPU:0, one launch (start us, length us, event | category | flops | bytes accessed | tf_op | source)
XLA Modules:
  0.0 24.5 jit_solution(8846433443696284166)
XLA Ops:
  0.0 1.9 %shard_map.109 = bf16[112,128]{1,0:T(8,128)(2,1)} custom-call(s32[32]{0:T(128)} %mask_ref.1, s32[2,32]{1,0:T(2,128)} %bitcast.8, bf16[32,2,256]{2,1,0:T(2,128)(2,1)} %state_hbm.1, bf16[2,32,256]{2,1,0:T(8,128)(2,1)} %bitcast.7, bf16[2,32,128]{2,1,0:T(8,128)(2,1)} %pair_hbm.1), custom_call_target="tpu_custom_call" | custom-call | tf_op jit(solution)/shard_map/pallas_call | solution.py:273
  1.9 0.0 copy-start.7
  1.9 4.1 %collective-permute-start = (bf16[1,112,128]{2,1,0:T(8,128)(2,1)}, bf16[1,112,128]{2,1,0:T(8,128)(2,1)S(1)}, u32[]{:S(2)}, u32[]{:S(2)}) collective-permute-start(bf16[1,112,128]{2,1,0:T(8,128)(2,1)} %bitcast.3), channel_id=1, source_target_pairs={{0,8},{2,10},{4,12},{6,14},{8,0},{10,2},{12,4},{14,6},{1,9},{3,11}... | collective-permute-start | bytes 86024 | tf_op jit(solution)/shard_map/ppermute | solution.py:236
  6.0 2.1 %collective-permute-done = bf16[1,112,128]{2,1,0:T(8,128)(2,1)S(1)} collective-permute-done((bf16[1,112,128]{2,1,0:T(8,128)(2,1)}, bf16[1,112,128]{2,1,0:T(8,128)(2,1)S(1)}, u32[]{:S(2)}, u32[]{:S(2)}) %collective-permute-start) | collective-permute-done | bytes 28704 | tf_op jit(solution)/shard_map/ppermute | solution.py:236
  8.1 0.0 copy-start.5
  8.1 0.8 %pad_maximum_fusion.2 = bf16[2,112,128]{2,1,0:T(8,128)(2,1)S(1)} fusion(bf16[1,112,128]{2,1,0:T(8,128)(2,1)S(1)} %collective-permute-done, bf16[1,112,128]{2,1,0:T(8,128)(2,1)} %bitcast.4), kind=kLoop, calls=%fused_computation.2 | loop fusion | flops 28672 | bytes 114688 | tf_op jit(solution)/shard_map/concatenate | solution.py:237
  8.9 1.9 %collective-permute-start.1 = (bf16[2,112,128]{2,1,0:T(8,128)(2,1)S(1)}, bf16[2,112,128]{2,1,0:T(8,128)(2,1)S(1)}, u32[]{:S(2)}, u32[]{:S(2)}) collective-permute-start(bf16[2,112,128]{2,1,0:T(8,128)(2,1)S(1)} %pad_maximum_fusion.2), channel_id=1, source_target_pairs={{0,4},{2,6},{4,0},{6,2},{8,12},{10,14},{12,8},{14,10},{1,5},{3,7},... | collective-permute-start | bytes 172040 | tf_op jit(solution)/shard_map/ppermute | solution.py:236
  10.8 2.3 %collective-permute-done.1 = bf16[2,112,128]{2,1,0:T(8,128)(2,1)S(1)} collective-permute-done((bf16[2,112,128]{2,1,0:T(8,128)(2,1)S(1)}, bf16[2,112,128]{2,1,0:T(8,128)(2,1)S(1)}, u32[]{:S(2)}, u32[]{:S(2)}) %collective-permute-start.1) | collective-permute-done | bytes 57376 | tf_op jit(solution)/shard_map/ppermute | solution.py:236
  13.1 0.0 copy-done.7
  13.1 0.0 copy-start
  13.1 0.0 copy-start.1
  13.1 0.0 copy-start.4
  13.1 2.1 %collective-permute-start.2 = (bf16[4,112,128]{2,1,0:T(8,128)(2,1)S(1)}, bf16[4,112,128]{2,1,0:T(8,128)(2,1)S(1)}, u32[]{:S(2)}, u32[]{:S(2)}) collective-permute-start(bf16[4,112,128]{2,1,0:T(8,128)(2,1)S(1)} %pad_maximum_fusion.1), channel_id=1, source_target_pairs={{0,2},{2,0},{4,6},{6,4},{8,10},{10,8},{12,14},{14,12},{1,3},{3,1},... | collective-permute-start | bytes 344072 | tf_op jit(solution)/shard_map/ppermute | solution.py:236
  15.2 2.8 %collective-permute-done.2 = bf16[4,112,128]{2,1,0:T(8,128)(2,1)S(1)} collective-permute-done((bf16[4,112,128]{2,1,0:T(8,128)(2,1)S(1)}, bf16[4,112,128]{2,1,0:T(8,128)(2,1)S(1)}, u32[]{:S(2)}, u32[]{:S(2)}) %collective-permute-start.2) | collective-permute-done | bytes 114720 | tf_op jit(solution)/shard_map/ppermute | solution.py:236
  18.0 0.1 collective-permute-start.3
  18.1 1.5 %collective-permute-done.3.other_ref = bf16[8,112,128]{2,1,0:T(8,128)(2,1)S(1)} collective-permute-done((bf16[8,112,128]{2,1,0:T(8,128)(2,1)S(1)}, bf16[8,112,128]{2,1,0:T(8,128)(2,1)S(1)}, u32[]{:S(2)}, u32[]{:S(2)}) %collective-permute-start.3) | collective-permute-done | bytes 229408 | tf_op jit(solution)/shard_map/ppermute | solution.py:239
  19.6 0.0 copy-done.5
  19.6 0.0 copy-done.6
  19.6 0.0 copy-done.2
  19.6 0.0 copy-done.3
  19.6 0.0 copy-done
  19.6 0.0 copy-done.1
  19.6 0.0 copy-done.4
  19.6 4.9 %shard_map.110 = bf16[2,32,128]{2,1,0:T(8,128)(2,1)} custom-call(s32[32]{0:T(128)S(1)} %copy-done.6, bf16[8,112,128]{2,1,0:T(8,128)(2,1)S(1)} %pad_maximum_fusion.held_ref, bf16[8,112,128]{2,1,0:T(8,128)(2,1)S(1)} %collective-permute-done.3.other_ref, bf16[32,32,128]{2,1,0:T(8,128)(2,1)S(1)} %copy-done, bf16[4,128,128]{2,1,0:T(8,128)(2,1)S(1)} %copy-done.1, ...), custom_call_target="tpu_custom_call" | custom-call | tf_op jit(solution)/shard_map/pallas_call | solution.py:297
  (5 shorter events, 0.0 us)
Async XLA Ops:
  1.9 11.1 %copy-start.7 = (bf16[112,128]{1,0:T(8,128)(2,1)S(1)}, bf16[112,128]{1,0:T(8,128)(2,1)}, u32[]{:S(2)}) copy-start(bf16[112,128]{1,0:T(8,128)(2,1)} %shard_map.109) | copy-start | bytes 86020
  1.9 6.2 %collective-permute-start = (bf16[1,112,128]{2,1,0:T(8,128)(2,1)}, bf16[1,112,128]{2,1,0:T(8,128)(2,1)S(1)}, u32[]{:S(2)}, u32[]{:S(2)}) collective-permute-start(bf16[1,112,128]{2,1,0:T(8,128)(2,1)} %bitcast.3), channel_id=1, source_target_pairs={{0,8},{2,10},{4,12},{6,14},{8,0},{10,2},{12,4},{14,6},{1,9},{3,11}... | collective-permute-start | bytes 86024 | tf_op jit(solution)/shard_map/ppermute | solution.py:236
  8.1 11.4 %copy-start.5 = (bf16[128,128]{1,0:T(8,128)(2,1)S(1)}, bf16[128,128]{1,0:T(8,128)(2,1)}, u32[]{:S(2)}) copy-start(bf16[128,128]{1,0:T(8,128)(2,1)} %output_ref.1) | copy-start | bytes 98308
  8.1 11.4 %copy-start.6 = (s32[32]{0:T(128)S(1)}, s32[32]{0:T(128)}, u32[]{:S(2)}) copy-start(s32[32]{0:T(128)} %mask_ref.1) | copy-start | bytes 388
  8.9 4.2 %collective-permute-start.1 = (bf16[2,112,128]{2,1,0:T(8,128)(2,1)S(1)}, bf16[2,112,128]{2,1,0:T(8,128)(2,1)S(1)}, u32[]{:S(2)}, u32[]{:S(2)}) collective-permute-start(bf16[2,112,128]{2,1,0:T(8,128)(2,1)S(1)} %pad_maximum_fusion.2), channel_id=1, source_target_pairs={{0,4},{2,6},{4,0},{6,2},{8,12},{10,14},{12,8},{14,10},{1,5},{3,7},... | collective-permute-start | bytes 172040 | tf_op jit(solution)/shard_map/ppermute | solution.py:236
  13.1 6.5 %copy-start.2 = (bf16[128,512]{1,0:T(8,128)(2,1)S(1)}, bf16[128,512]{1,0:T(8,128)(2,1)}, u32[]{:S(2)}) copy-start(bf16[128,512]{1,0:T(8,128)(2,1)} %up_ref.1) | copy-start | bytes 393220
  13.1 6.5 %copy-start.3 = (bf16[512,128]{1,0:T(8,128)(2,1)S(1)}, bf16[512,128]{1,0:T(8,128)(2,1)}, u32[]{:S(2)}) copy-start(bf16[512,128]{1,0:T(8,128)(2,1)} %down_ref.1) | copy-start | bytes 393220
  13.1 6.5 %copy-start = (bf16[32,32,128]{2,1,0:T(8,128)(2,1)S(1)}, bf16[32,32,128]{2,1,0:T(8,128)(2,1)}, u32[]{:S(2)}) copy-start(bf16[32,32,128]{2,1,0:T(8,128)(2,1)} %outer_ref.1) | copy-start | bytes 786436
  13.1 6.5 %copy-start.1 = (bf16[4,128,128]{2,1,0:T(8,128)(2,1)S(1)}, bf16[4,128,128]{2,1,0:T(8,128)(2,1)}, u32[]{:S(2)}) copy-start(bf16[4,128,128]{2,1,0:T(8,128)(2,1)} %triangle_ref.1) | copy-start | bytes 393220
  13.1 6.5 %copy-start.4 = (bf16[128,128]{1,0:T(8,128)(2,1)S(1)}, bf16[128,128]{1,0:T(8,128)(2,1)}, u32[]{:S(2)}) copy-start(bf16[128,128]{1,0:T(8,128)(2,1)} %gate_ref.1) | copy-start | bytes 98308
  13.1 4.9 %collective-permute-start.2 = (bf16[4,112,128]{2,1,0:T(8,128)(2,1)S(1)}, bf16[4,112,128]{2,1,0:T(8,128)(2,1)S(1)}, u32[]{:S(2)}, u32[]{:S(2)}) collective-permute-start(bf16[4,112,128]{2,1,0:T(8,128)(2,1)S(1)} %pad_maximum_fusion.1), channel_id=1, source_target_pairs={{0,2},{2,0},{4,6},{6,4},{8,10},{10,8},{12,14},{14,12},{1,3},{3,1},... | collective-permute-start | bytes 344072 | tf_op jit(solution)/shard_map/ppermute | solution.py:236
  18.0 1.6 %collective-permute-start.3 = (bf16[8,112,128]{2,1,0:T(8,128)(2,1)S(1)}, bf16[8,112,128]{2,1,0:T(8,128)(2,1)S(1)}, u32[]{:S(2)}, u32[]{:S(2)}) collective-permute-start(bf16[8,112,128]{2,1,0:T(8,128)(2,1)S(1)} %pad_maximum_fusion.held_ref), channel_id=1, source_target_pairs={{0,1},{1,0},{2,3},{3,2},{4,5},{5,4},{6,7},{7,6},{8,9},{9,8},{10,11... | collective-permute-start | bytes 688136 | tf_op jit(solution)/shard_map/ppermute | solution.py:239

commit v7 on v6

--- a/solution.py
+++ b/solution.py
@@ -103,18 +103,31 @@
     ).astype(jnp.bfloat16)
 
 
+def weight_kernel(outer_ref, packed_ref, block_ref, held_ref):
+    channels, _, wide = outer_ref.shape
+    group = block_ref.shape[1] // wide
+    held_ref[0] = packed_ref[...]
+    block_ref[...] = jnp.zeros_like(block_ref)
+    for d in range(channels):
+        weight = outer_ref[d]
+        for part in range(group):
+            block_ref[
+                (d * group + part) * channels : (d * group + part + 1) * channels,
+                part * wide : (part + 1) * wide,
+            ] = weight
+
+
 def update_kernel(
     mask_ref,
     held_ref,
     other_ref,
-    outer_ref,
+    block_ref,
     triangle_ref,
     gate_ref,
     output_ref,
     up_ref,
     down_ref,
     out_ref,
-    block_ref,
     left_ref,
     right_ref,
     keep_ref,
@@ -125,8 +138,7 @@
 ):
     rows, residues, wide = out_ref.shape
     cores, chips = 2, held_ref.shape[0]
-    channels = outer_ref.shape[0]
-    sequences = channels
+    sequences, channels = left_ref.shape[2] // (cores * rows), left_ref.shape[1]
     base = rows * residues
     group = cores * rows
     start = first_row(rows)
@@ -134,21 +146,14 @@
     bf16 = jnp.bfloat16
     f32 = jnp.float32
 
-    block_ref[...] = jnp.zeros_like(block_ref)
-    for d in range(channels):
-        weight = outer_ref[d]
-        for part in range(group):
-            block_ref[
-                (d * group + part) * channels : (d * group + part + 1) * channels,
-                part * wide : (part + 1) * wide,
-            ] = weight
-
     lane = lax.broadcasted_iota(jnp.int32, (channels, wide), 1)
     lane_block = lane // channels
     for chip in range(chips):
-        place = xor_place(chip, chips)
-        mine, other = held_ref[place], other_ref[place]
-        blocks = [jnp.where(second_core, other, mine), jnp.where(second_core, mine, other)]
+        places = [block_place(chip, core, chips) for core in range(cores)]
+        blocks = [
+            jnp.where(second_core, other_ref[places[0]], held_ref[places[0]]),
+            jnp.where(second_core, held_ref[places[1]], other_ref[places[1]]),
+        ]
         packed = [block[base : base + sequences].astype(f32) for block in blocks]
         right = jnp.where(lane < wide // 2, packed[0], packed[1]).astype(bf16)
         for copy in range(group):
@@ -228,25 +233,25 @@
     out_ref[...] = result.astype(bf16).reshape(rows, residues, wide)
 
 
-def gather_all(block):
-    dap_count = lax.axis_size("dap")
-    held = block[None]
-    step = dap_count // 2
-    while step:
-        got = lax.ppermute(held, "dap", [(src, src ^ step) for src in range(dap_count)])
-        held = jnp.concatenate([held, got], axis=0)
-        step //= 2
-    return held, lax.ppermute(held, "sub", [(0, 1), (1, 0)])
-
-
-def xor_place(chip, chips):
+def stage_steps(dap_count, core):
+    low = [1 << bit for bit in range(dap_count.bit_length() - 2)]
+    steps = [dap_count // 2] + low
+    return steps if core == 0 else steps[-1:] + steps[:-1]
+
+
+def double(held, dap_count, stage):
+    pairs = []
+    for core in range(2):
+        step = stage_steps(dap_count, core)[stage]
+        pairs += [(2 * chip + core, 2 * (chip ^ step) + core) for chip in range(dap_count)]
+    return lax.ppermute(held, ("dap", "sub"), pairs)
+
+
+def block_place(chip, core, chips):
     difference = lax.bitwise_xor(lax.axis_index("dap"), chip)
     place = 0
-    step, bit = chips // 2, 1
-    while step:
-        place = place + jnp.where(lax.bitwise_and(difference, step) != 0, bit, 0)
-        step //= 2
-        bit *= 2
+    for stage, step in enumerate(stage_steps(chips, core)):
+        place = place + jnp.where(lax.bitwise_and(difference, step) != 0, 1 << stage, 0)
     return place
 
 
@@ -268,7 +273,7 @@
     channels = outer_input_weight.shape[2]
     scalar = pl.BlockSpec(memory_space=pltpu.SMEM)
     vector = pl.BlockSpec(memory_space=pltpu.VMEM)
-    params = pltpu.CompilerParams(vmem_limit_bytes=40 << 20)
+    params = pltpu.CompilerParams(vmem_limit_bytes=32 << 20)
     hbm = pl.BlockSpec(memory_space=pltpu.HBM)
     packed = pl.pallas_call(
         pack_kernel,
@@ -291,16 +296,32 @@
         outer_input_weight.transpose(0, 2, 1),
         pairwise_state,
     )
-    held, other = gather_all(packed)
-    cores, chips = 2, held.shape[0]
+    dap_count, cores = lax.axis_size("dap"), lax.axis_size("sub")
     group = cores * rows
+    got = double(packed[None], dap_count, 0)
+    block_weight, held = pl.pallas_call(
+        weight_kernel,
+        out_shape=(
+            jax.ShapeDtypeStruct((channels * group * channels, group * wide), jnp.bfloat16),
+            jax.ShapeDtypeStruct((1,) + packed.shape, jnp.bfloat16),
+        ),
+        in_specs=[vector] * 2,
+        out_specs=(vector, vector),
+        compiler_params=pltpu.CompilerParams(vmem_limit_bytes=16 << 20),
+        cost_estimate=pl.CostEstimate(flops=0, bytes_accessed=6 << 20, transcendentals=0),
+    )(outer_output_weight, packed)
+    for stage in range(1, dap_count.bit_length()):
+        held = jnp.concatenate([held, got], axis=0)
+        if stage < dap_count.bit_length() - 1:
+            got = double(held, dap_count, stage)
+    other = lax.ppermute(held, "sub", [(0, 1), (1, 0)])
+    chips = held.shape[0]
     return pl.pallas_call(
         update_kernel,
         out_shape=jax.ShapeDtypeStruct(pairwise_state.shape, jnp.bfloat16),
         in_specs=[scalar] + [vector] * 8,
         out_specs=vector,
         scratch_shapes=[
-            pltpu.VMEM((channels * group * channels, group * wide), jnp.bfloat16),
             pltpu.VMEM((residues, channels, wide), jnp.float32),
             pltpu.VMEM((group * sequences, chips * wide), jnp.bfloat16),
             pltpu.VMEM((residues, wide), jnp.float32),
@@ -314,7 +335,7 @@
         residue_crop_mask,
         held,
         other,
-        outer_output_weight,
+        block_weight,
         triangle_input_weight,
         triangle_gate,
         triangle_output_weight,
@@ -425,9 +446,11 @@
         P(),
     )
 
+    small = mesh.shape["sub"] == 2 and mesh.shape["dap"] == 8
+
     def body(pairwise_state, *rest):
         residues, channels = pairwise_state.shape[1:]
-        if residues * residues * channels * 2 <= REPLICATED_PAIR_BYTES:
+        if small and residues * residues * channels * 2 <= REPLICATED_PAIR_BYTES:
             return shards_replicated(pairwise_state, *rest)
         return shards(pairwise_state, *rest)
 

time: 24.7 us -> 29 us (1.17)
  local copies, waits for them, and re-layouts: 0.04 us -> 6.62 us
  waiting for transfers between devices: 8.62 us -> 6.84 us
  other arithmetic: 0.8 us -> 0.02 us
  Pallas kernels: 6.78 us -> 7.11 us
    unnamed x16 -> x19, local copies, waits for them, and re-layouts: 0.04 us -> 6.6 us
    ppermute x4, waiting for transfers between devices: 8.62 us -> 6.84 us  [the longest x3 5.37 us: double(): return lax.ppermute(held, ('dap', 'sub'), pairs)]
    concatenate x3 -> x2, other arithmetic: 0.8 us -> 0.02 us  [shards_replicated(): held = jnp.concatenate([held, got], axis=0)]
    pallas_call x0 -> x1, Pallas kernels: none -> 0.41 us  [shards_replicated(): pl.pallas_call(weight_kernel, out_shape=(jax.ShapeDtypeStruct((channels *...]
  transfers between devices with their start and end apart: 4 -> 4, of which waited for: 4 -> 3; matrix products, arithmetic and copies ran while one was open for 0% -> 0% of each run, Pallas kernels for 0% -> 1%
where the time goes in v7:
time: 29 us; the launch traced here: 28.5 us
  starting transfers between devices  7.88 us (27%)
  Pallas kernels  7.11 us (25%)
  waiting for transfers between devices  6.84 us (24%)
  local copies, waits for them, and re-layouts  6.62 us (23%)
    ppermute x3, starting transfers between devices, double(): return lax.ppermute(held, ('dap', 'sub'), pairs)  7.81 us
    unnamed x19, local copies, waits for them, and re-layouts  6.6 us
    ppermute x3, waiting for transfers between devices, double(): return lax.ppermute(held, ('dap', 'sub'), pairs)  5.37 us
    pallas_call x1, Pallas kernels, shards_replicated(): pl.pallas_call(update_kernel, out_shape=jax.ShapeDtypeStruct(pairwise_sta...  4.77 us
    pallas_call x1, Pallas kernels, shards_replicated(): pl.pallas_call(pack_kernel, out_shape=jax.ShapeDtypeStruct((rows * residu...  1.93 us
    ppermute x1, waiting for transfers between devices, shards_replicated(): other = lax.ppermute(held, 'sub', [(0, 1), (1, 0)])  1.48 us
  transfers between devices with their start and end apart: 4, of which 3 were waited for; matrix products, arithmetic and copies ran while one was open for 0% of the time, Pallas kernels for 1%

profile of v7, /device:TPU:0, one launch (start us, length us, event | category | flops | bytes accessed | tf_op | source)
XLA Modules:
  0.0 28.5 jit_solution(18216434546427002588)
XLA Ops:
  0.0 1.9 %shard_map.109.packed_ref = bf16[112,128]{1,0:T(8,128)(2,1)} custom-call(s32[32]{0:T(128)} %mask_ref.1, s32[2,32]{1,0:T(2,128)} %bitcast.5, bf16[32,2,256]{2,1,0:T(2,128)(2,1)} %state_hbm.1, bf16[2,32,256]{2,1,0:T(8,128)(2,1)} %bitcast.4, bf16[2,32,128]{2,1,0:T(8,128)(2,1)} %pair_hbm.1), custom_call_target="tpu_custom_call" | custom-call | tf_op jit(solution)/shard_map/pallas_call | solution.py:278
  1.9 4.1 %collective-permute-start = (bf16[1,112,128]{2,1,0:T(8,128)(2,1)}, bf16[1,112,128]{2,1,0:T(8,128)(2,1)S(1)}, u32[]{:S(2)}, u32[]{:S(2)}) collective-permute-start(bf16[1,112,128]{2,1,0:T(8,128)(2,1)} %bitcast.3), channel_id=1, source_target_pairs={{0,8},{2,10},{4,12},{6,14},{8,0},{10,2},{12,4},{14,6},{1,5},{3,7},... | collective-permute-start | bytes 86024 | tf_op jit(solution)/shard_map/ppermute | solution.py:247
  6.0 0.0 copy-start
  6.0 0.9 %copy-done = bf16[32,32,128]{2,1,0:T(8,128)(2,1)S(1)} copy-done((bf16[32,32,128]{2,1,0:T(8,128)(2,1)S(1)}, bf16[32,32,128]{2,1,0:T(8,128)(2,1)}, u32[]{:S(2)}) %copy-start) | copy-done | bytes 262168
  7.0 0.0 copy-start.4
  7.0 0.7 %copy-done.4 = bf16[112,128]{1,0:T(8,128)(2,1)S(1)} copy-done((bf16[112,128]{1,0:T(8,128)(2,1)S(1)}, bf16[112,128]{1,0:T(8,128)(2,1)}, u32[]{:S(2)}) %copy-start.4) | copy-done | bytes 28696
  7.7 0.4 %shard_map.110 = (bf16[4096,512]{1,0:T(8,128)(2,1)S(1)}, bf16[1,112,128]{2,1,0:T(8,128)(2,1)S(1)}) custom-call(bf16[32,32,128]{2,1,0:T(8,128)(2,1)S(1)} %copy-done, bf16[112,128]{1,0:T(8,128)(2,1)S(1)} %copy-done.4), custom_call_target="tpu_custom_call" | custom-call | bytes 6291456 | tf_op jit(solution)/shard_map/pallas_call | solution.py:302
  8.2 0.0 collective-permute-done
  8.2 1.8 %collective-permute-start.1 = (bf16[2,112,128]{2,1,0:T(8,128)(2,1)S(1)}, bf16[2,112,128]{2,1,0:T(8,128)(2,1)S(1)}, u32[]{:S(2)}, u32[]{:S(2)}) collective-permute-start(bf16[2,112,128]{2,1,0:T(8,128)(2,1)S(1)} %pad_maximum_fusion.1), channel_id=1, source_target_pairs={{0,2},{2,0},{4,6},{6,4},{8,10},{10,8},{12,14},{14,12},{1,9},{3,11}... | collective-permute-start | bytes 172040 | tf_op jit(solution)/shard_map/ppermute | solution.py:247
  10.0 2.4 %collective-permute-done.1 = bf16[2,112,128]{2,1,0:T(8,128)(2,1)S(1)} collective-permute-done((bf16[2,112,128]{2,1,0:T(8,128)(2,1)S(1)}, bf16[2,112,128]{2,1,0:T(8,128)(2,1)S(1)}, u32[]{:S(2)}, u32[]{:S(2)}) %collective-permute-start.1) | collective-permute-done | bytes 57376 | tf_op jit(solution)/shard_map/ppermute | solution.py:247
  12.4 1.9 %collective-permute-start.2 = (bf16[4,112,128]{2,1,0:T(8,128)(2,1)S(1)}, bf16[4,112,128]{2,1,0:T(8,128)(2,1)S(1)}, u32[]{:S(2)}, u32[]{:S(2)}) collective-permute-start(bf16[4,112,128]{2,1,0:T(8,128)(2,1)S(1)} %pad_maximum_fusion), channel_id=1, source_target_pairs={{0,4},{2,6},{4,0},{6,2},{8,12},{10,14},{12,8},{14,10},{1,3},{3,1},... | collective-permute-start | bytes 344072 | tf_op jit(solution)/shard_map/ppermute | solution.py:247
  14.4 2.9 %collective-permute-done.2 = bf16[4,112,128]{2,1,0:T(8,128)(2,1)S(1)} collective-permute-done((bf16[4,112,128]{2,1,0:T(8,128)(2,1)S(1)}, bf16[4,112,128]{2,1,0:T(8,128)(2,1)S(1)}, u32[]{:S(2)}, u32[]{:S(2)}) %collective-permute-start.2) | collective-permute-done | bytes 114720 | tf_op jit(solution)/shard_map/ppermute | solution.py:247
  17.3 0.1 collective-permute-start.3
  17.4 1.5 %collective-permute-done.3.other_ref = bf16[8,112,128]{2,1,0:T(8,128)(2,1)S(1)} collective-permute-done((bf16[8,112,128]{2,1,0:T(8,128)(2,1)S(1)}, bf16[8,112,128]{2,1,0:T(8,128)(2,1)S(1)}, u32[]{:S(2)}, u32[]{:S(2)}) %collective-permute-start.3) | collective-permute-done | bytes 229408 | tf_op jit(solution)/shard_map/ppermute | solution.py:317
  18.9 0.0 copy-start.1
  18.9 0.9 %copy-done.1 = bf16[4,128,128]{2,1,0:T(8,128)(2,1)S(1)} copy-done((bf16[4,128,128]{2,1,0:T(8,128)(2,1)S(1)}, bf16[4,128,128]{2,1,0:T(8,128)(2,1)}, u32[]{:S(2)}) %copy-start.1) | copy-done | bytes 131096
  19.8 0.0 copy-start.2
  19.8 0.9 %copy-done.2 = bf16[128,512]{1,0:T(8,128)(2,1)S(1)} copy-done((bf16[128,512]{1,0:T(8,128)(2,1)S(1)}, bf16[128,512]{1,0:T(8,128)(2,1)}, u32[]{:S(2)}) %copy-start.2) | copy-done | bytes 131096
  20.7 0.0 copy-start.3
  20.7 0.9 %copy-done.3 = bf16[512,128]{1,0:T(8,128)(2,1)S(1)} copy-done((bf16[512,128]{1,0:T(8,128)(2,1)S(1)}, bf16[512,128]{1,0:T(8,128)(2,1)}, u32[]{:S(2)}) %copy-start.3) | copy-done | bytes 131096
  21.6 0.8 %copy-done.5 = bf16[128,128]{1,0:T(8,128)(2,1)S(1)} copy-done((bf16[128,128]{1,0:T(8,128)(2,1)S(1)}, bf16[128,128]{1,0:T(8,128)(2,1)}, u32[]{:S(2)}) %copy-start.5) | copy-done | bytes 32792
  22.3 0.8 %copy-done.6 = bf16[128,128]{1,0:T(8,128)(2,1)S(1)} copy-done((bf16[128,128]{1,0:T(8,128)(2,1)S(1)}, bf16[128,128]{1,0:T(8,128)(2,1)}, u32[]{:S(2)}) %copy-start.6) | copy-done | bytes 32792
  23.1 0.7 %copy-done.7 = s32[32]{0:T(128)S(1)} copy-done((s32[32]{0:T(128)S(1)}, s32[32]{0:T(128)}, u32[]{:S(2)}) %copy-start.7) | copy-done | bytes 152
  23.8 4.8 %shard_map.111 = bf16[2,32,128]{2,1,0:T(8,128)(2,1)} custom-call(s32[32]{0:T(128)S(1)} %copy-done.7, bf16[8,112,128]{2,1,0:T(8,128)(2,1)S(1)} %constant_dynamic-update-slice_fusion.held_ref, bf16[8,112,128]{2,1,0:T(8,128)(2,1)S(1)} %collective-permute-done.3.other_ref, bf16[4096,512]{1,0:T(8,128)(2,1)S(1)} %get-tuple-element.8.block_ref, ...), custom_call_target="tpu_custom_call" | custom-call | tf_op jit(solution)/shard_map/pallas_call | solution.py:319
  (9 shorter events, 0.1 us)
Async XLA Ops:
  1.9 6.2 %collective-permute-start = (bf16[1,112,128]{2,1,0:T(8,128)(2,1)}, bf16[1,112,128]{2,1,0:T(8,128)(2,1)S(1)}, u32[]{:S(2)}, u32[]{:S(2)}) collective-permute-start(bf16[1,112,128]{2,1,0:T(8,128)(2,1)} %bitcast.3), channel_id=1, source_target_pairs={{0,8},{2,10},{4,12},{6,14},{8,0},{10,2},{12,4},{14,6},{1,5},{3,7},... | collective-permute-start | bytes 86024 | tf_op jit(solution)/shard_map/ppermute | solution.py:247
  6.0 0.9 %copy-start = (bf16[32,32,128]{2,1,0:T(8,128)(2,1)S(1)}, bf16[32,32,128]{2,1,0:T(8,128)(2,1)}, u32[]{:S(2)}) copy-start(bf16[32,32,128]{2,1,0:T(8,128)(2,1)} %outer_ref.1) | copy-start | bytes 786436
  7.0 0.7 %copy-start.4 = (bf16[112,128]{1,0:T(8,128)(2,1)S(1)}, bf16[112,128]{1,0:T(8,128)(2,1)}, u32[]{:S(2)}) copy-start(bf16[112,128]{1,0:T(8,128)(2,1)} %shard_map.109.packed_ref) | copy-start | bytes 86020
  8.2 4.2 %collective-permute-start.1 = (bf16[2,112,128]{2,1,0:T(8,128)(2,1)S(1)}, bf16[2,112,128]{2,1,0:T(8,128)(2,1)S(1)}, u32[]{:S(2)}, u32[]{:S(2)}) collective-permute-start(bf16[2,112,128]{2,1,0:T(8,128)(2,1)S(1)} %pad_maximum_fusion.1), channel_id=1, source_target_pairs={{0,2},{2,0},{4,6},{6,4},{8,10},{10,8},{12,14},{14,12},{1,9},{3,11}... | collective-permute-start | bytes 172040 | tf_op jit(solution)/shard_map/ppermute | solution.py:247
  12.4 4.9 %collective-permute-start.2 = (bf16[4,112,128]{2,1,0:T(8,128)(2,1)S(1)}, bf16[4,112,128]{2,1,0:T(8,128)(2,1)S(1)}, u32[]{:S(2)}, u32[]{:S(2)}) collective-permute-start(bf16[4,112,128]{2,1,0:T(8,128)(2,1)S(1)} %pad_maximum_fusion), channel_id=1, source_target_pairs={{0,4},{2,6},{4,0},{6,2},{8,12},{10,14},{12,8},{14,10},{1,3},{3,1},... | collective-permute-start | bytes 344072 | tf_op jit(solution)/shard_map/ppermute | solution.py:247
  17.3 1.6 %collective-permute-start.3 = (bf16[8,112,128]{2,1,0:T(8,128)(2,1)S(1)}, bf16[8,112,128]{2,1,0:T(8,128)(2,1)S(1)}, u32[]{:S(2)}, u32[]{:S(2)}) collective-permute-start(bf16[8,112,128]{2,1,0:T(8,128)(2,1)S(1)} %constant_dynamic-update-slice_fusion.held_ref), channel_id=1, source_target_pairs={{0,1},{1,0},{2,3},{3,2},{4,5},{5,4},{6,7},{7,6},{8,9},{9,8},{10,11... | collective-permute-start | bytes 688136 | tf_op jit(solution)/shard_map/ppermute | solution.py:317
  18.9 0.9 %copy-start.1 = (bf16[4,128,128]{2,1,0:T(8,128)(2,1)S(1)}, bf16[4,128,128]{2,1,0:T(8,128)(2,1)}, u32[]{:S(2)}) copy-start(bf16[4,128,128]{2,1,0:T(8,128)(2,1)} %triangle_ref.1) | copy-start | bytes 393220
  19.8 0.9 %copy-start.2 = (bf16[128,512]{1,0:T(8,128)(2,1)S(1)}, bf16[128,512]{1,0:T(8,128)(2,1)}, u32[]{:S(2)}) copy-start(bf16[128,512]{1,0:T(8,128)(2,1)} %up_ref.1) | copy-start | bytes 393220
  20.7 0.9 %copy-start.3 = (bf16[512,128]{1,0:T(8,128)(2,1)S(1)}, bf16[512,128]{1,0:T(8,128)(2,1)}, u32[]{:S(2)}) copy-start(bf16[512,128]{1,0:T(8,128)(2,1)} %down_ref.1) | copy-start | bytes 393220
  21.6 0.8 %copy-start.5 = (bf16[128,128]{1,0:T(8,128)(2,1)S(1)}, bf16[128,128]{1,0:T(8,128)(2,1)}, u32[]{:S(2)}) copy-start(bf16[128,128]{1,0:T(8,128)(2,1)} %gate_ref.1) | copy-start | bytes 98308
  22.3 0.8 %copy-start.6 = (bf16[128,128]{1,0:T(8,128)(2,1)S(1)}, bf16[128,128]{1,0:T(8,128)(2,1)}, u32[]{:S(2)}) copy-start(bf16[128,128]{1,0:T(8,128)(2,1)} %output_ref.1) | copy-start | bytes 98308
  23.1 0.7 %copy-start.7 = (s32[32]{0:T(128)S(1)}, s32[32]{0:T(128)}, u32[]{:S(2)}) copy-start(s32[32]{0:T(128)} %mask_ref.1) | copy-start | bytes 388

commit v8 on v6

--- a/solution.py
+++ b/solution.py
@@ -105,7 +105,8 @@
 
 def update_kernel(
     mask_ref,
-    held_ref,
+    both_ref,
+    mine_ref,
     other_ref,
     outer_ref,
     triangle_ref,
@@ -124,13 +125,12 @@
     ln_one_ref,
 ):
     rows, residues, wide = out_ref.shape
-    cores, chips = 2, held_ref.shape[0]
+    cores, chips = both_ref.shape[0], lax.axis_size("dap")
     channels = outer_ref.shape[0]
     sequences = channels
     base = rows * residues
     group = cores * rows
     start = first_row(rows)
-    second_core = lax.axis_index("sub") == 1
     bf16 = jnp.bfloat16
     f32 = jnp.float32
 
@@ -146,9 +146,9 @@
     lane = lax.broadcasted_iota(jnp.int32, (channels, wide), 1)
     lane_block = lane // channels
     for chip in range(chips):
-        place = xor_place(chip, chips)
-        mine, other = held_ref[place], other_ref[place]
-        blocks = [jnp.where(second_core, other, mine), jnp.where(second_core, mine, other)]
+        blocks = [
+            chip_block(both_ref, mine_ref, other_ref, chip, core) for core in range(cores)
+        ]
         packed = [block[base : base + sequences].astype(f32) for block in blocks]
         right = jnp.where(lane < wide // 2, packed[0], packed[1]).astype(bf16)
         for copy in range(group):
@@ -228,26 +228,51 @@
     out_ref[...] = result.astype(bf16).reshape(rows, residues, wide)
 
 
-def gather_all(block):
+def copy_kernel(packed_ref, out_ref):
+    out_ref[0] = packed_ref[...]
+
+
+def chip_offsets(dap_count, core):
+    near = dap_count // 2 - 1
+    return list(range(1, near + 1)) if core == 0 else list(range(near + 1, dap_count))
+
+
+def gather_all(packed):
     dap_count = lax.axis_size("dap")
-    held = block[None]
-    step = dap_count // 2
-    while step:
-        got = lax.ppermute(held, "dap", [(src, src ^ step) for src in range(dap_count)])
-        held = jnp.concatenate([held, got], axis=0)
-        step //= 2
-    return held, lax.ppermute(held, "sub", [(0, 1), (1, 0)])
-
-
-def xor_place(chip, chips):
-    difference = lax.bitwise_xor(lax.axis_index("dap"), chip)
-    place = 0
-    step, bit = chips // 2, 1
-    while step:
-        place = place + jnp.where(lax.bitwise_and(difference, step) != 0, bit, 0)
-        step //= 2
-        bit *= 2
-    return place
+    sibling = [(0, 1), (1, 0)]
+    near = lax.ppermute(packed[None], "sub", sibling)
+    own = pl.pallas_call(
+        copy_kernel,
+        out_shape=jax.ShapeDtypeStruct((1,) + packed.shape, packed.dtype),
+        in_specs=[pl.BlockSpec(memory_space=pltpu.VMEM)],
+        out_specs=pl.BlockSpec(memory_space=pltpu.VMEM),
+        compiler_params=pltpu.CompilerParams(vmem_limit_bytes=4 << 20),
+    )(packed)
+    both = jnp.concatenate([own, near], axis=0)
+    offsets = [chip_offsets(dap_count, core) for core in range(2)]
+    got = []
+    for turn in range(max(map(len, offsets))):
+        pairs = [
+            (2 * chip + core, 2 * (chip ^ offsets[core][turn]) + core)
+            for core in range(2)
+            for chip in range(dap_count)
+            if turn < len(offsets[core])
+        ]
+        got.append(lax.ppermute(both, ("dap", "sub"), pairs))
+    mine = jnp.concatenate(got, axis=0)
+    return both, mine, lax.ppermute(mine, "sub", sibling)
+
+
+def chip_block(both_ref, mine_ref, other_ref, chip, core):
+    chips = lax.axis_size("dap")
+    sub = lax.axis_index("sub")
+    offset = lax.bitwise_xor(lax.axis_index("dap"), chip)
+    near = len(chip_offsets(chips, 0))
+    carrier = jnp.where(offset > near, 1, 0)
+    turn = jnp.where(offset > near, offset - near, jnp.maximum(offset, 1)) - 1
+    place = 2 * turn + jnp.where(carrier == core, 0, 1)
+    away = jnp.where(carrier == sub, mine_ref[place], other_ref[place])
+    return jnp.where(offset == 0, both_ref[jnp.where(sub == core, 0, 1)], away)
 
 
 def shards_replicated(
@@ -291,13 +316,13 @@
         outer_input_weight.transpose(0, 2, 1),
         pairwise_state,
     )
-    held, other = gather_all(packed)
-    cores, chips = 2, held.shape[0]
+    both, mine, other = gather_all(packed)
+    cores, chips = lax.axis_size("sub"), lax.axis_size("dap")
     group = cores * rows
     return pl.pallas_call(
         update_kernel,
         out_shape=jax.ShapeDtypeStruct(pairwise_state.shape, jnp.bfloat16),
-        in_specs=[scalar] + [vector] * 8,
+        in_specs=[scalar] + [vector] * 9,
         out_specs=vector,
         scratch_shapes=[
             pltpu.VMEM((channels * group * channels, group * wide), jnp.bfloat16),
@@ -312,7 +337,8 @@
         compiler_params=params,
     )(
         residue_crop_mask,
-        held,
+        both,
+        mine,
         other,
         outer_output_weight,
         triangle_input_weight,
@@ -425,9 +451,11 @@
         P(),
     )
 
+    small = mesh.shape["sub"] == 2 and mesh.shape["dap"] == 8
+
     def body(pairwise_state, *rest):
         residues, channels = pairwise_state.shape[1:]
-        if residues * residues * channels * 2 <= REPLICATED_PAIR_BYTES:
+        if small and residues * residues * channels * 2 <= REPLICATED_PAIR_BYTES:
             return shards_replicated(pairwise_state, *rest)
         return shards(pairwise_state, *rest)
 

time: 24.7 us -> 25.8 us (1.045)
  starting transfers between devices: 8.13 us -> 11.8 us
  waiting for transfers between devices: 8.62 us -> 5.79 us
  other arithmetic: 0.8 us -> 0.01 us
  local copies, waits for them, and re-layouts: 0.04 us -> 0.82 us
    ppermute x4 -> x6, starting transfers between devices: 8.13 us -> 11.8 us  [the longest x1 6.19 us: gather_all(): return (both, mine, lax.ppermute(mine, 'sub', sibling))]
    ppermute x4 -> x6, waiting for transfers between devices: 8.62 us -> 5.79 us  [the longest x4 4.37 us: gather_all(): got.append(lax.ppermute(both, ('dap', 'sub'), pairs))]
    concatenate x3 -> x1, other arithmetic: 0.8 us -> 0.01 us  [gather_all(): both = jnp.concatenate([own, near], axis=0)]
    unnamed x16 -> x19, local copies, waits for them, and re-layouts: 0.04 us -> 0.81 us
  transfers between devices with their start and end apart: 4 -> 6, of which waited for: 4 -> 4; matrix products, arithmetic and copies ran while one was open for 0% -> 0% of each run, Pallas kernels for 0% -> 0%
where the time goes in v8:
time: 25.8 us; the launch traced here: 25.6 us
  starting transfers between devices  11.8 us (46%)
  Pallas kernels  6.99 us (27%)
  waiting for transfers between devices  5.79 us (22%)
  local copies, waits for them, and re-layouts  0.82 us (3%)
    ppermute x1, starting transfers between devices, gather_all(): return (both, mine, lax.ppermute(mine, 'sub', sibling))  6.19 us
    ppermute x4, starting transfers between devices, gather_all(): got.append(lax.ppermute(both, ('dap', 'sub'), pairs))  5.12 us
    pallas_call x1, Pallas kernels, shards_replicated(): pl.pallas_call(update_kernel, out_shape=jax.ShapeDtypeStruct(pairwise_sta...  5.04 us
    ppermute x4, waiting for transfers between devices, gather_all(): got.append(lax.ppermute(both, ('dap', 'sub'), pairs))  4.37 us
    pallas_call x1, Pallas kernels, shards_replicated(): pl.pallas_call(pack_kernel, out_shape=jax.ShapeDtypeStruct((rows * residu...  1.95 us
    ppermute x1, waiting for transfers between devices, gather_all(): return (both, mine, lax.ppermute(mine, 'sub', sibling))  1.12 us
    unnamed x19, local copies, waits for them, and re-layouts  0.81 us
    ppermute x1, starting transfers between devices, gather_all(): near = lax.ppermute(packed[None], 'sub', sibling)  0.52 us
  transfers between devices with their start and end apart: 6, of which 4 were waited for; matrix products, arithmetic and copies ran while one was open for 0% of the time, Pallas kernels for 0%

profile of v8, /device:TPU:0, one launch (start us, length us, event | category | flops | bytes accessed | tf_op | source)
XLA Modules:
  0.0 25.6 jit_solution(13828067821914932653)
XLA Ops:
  0.0 2.0 %shard_map.109.packed_ref = bf16[112,128]{1,0:T(8,128)(2,1)} custom-call(s32[32]{0:T(128)} %mask_ref.1, s32[2,32]{1,0:T(2,128)} %bitcast.5, bf16[32,2,256]{2,1,0:T(2,128)(2,1)} %state_hbm.1, bf16[2,32,256]{2,1,0:T(8,128)(2,1)} %bitcast.4, bf16[2,32,128]{2,1,0:T(8,128)(2,1)} %pair_hbm.1), custom_call_target="tpu_custom_call" | custom-call | tf_op jit(solution)/shard_map/pallas_call | solution.py:298
  2.0 0.5 %collective-permute-start = (bf16[1,112,128]{2,1,0:T(8,128)(2,1)}, bf16[1,112,128]{2,1,0:T(8,128)(2,1)S(1)}, u32[]{:S(2)}, u32[]{:S(2)}) collective-permute-start(bf16[1,112,128]{2,1,0:T(8,128)(2,1)} %bitcast.3), channel_id=1, source_target_pairs={{0,1},{1,0},{2,3},{3,2},{4,5},{5,4},{6,7},{7,6},{8,9},{9,8},{10,11... | collective-permute-start | bytes 86024 | tf_op jit(solution)/shard_map/ppermute | solution.py:243
  2.5 0.7 %copy-done.4 = bf16[112,128]{1,0:T(8,128)(2,1)S(1)} copy-done((bf16[112,128]{1,0:T(8,128)(2,1)S(1)}, bf16[112,128]{1,0:T(8,128)(2,1)}, u32[]{:S(2)}) %copy-start.4) | copy-done | bytes 28696
  3.2 0.3 %collective-permute-done = bf16[1,112,128]{2,1,0:T(8,128)(2,1)S(1)} collective-permute-done((bf16[1,112,128]{2,1,0:T(8,128)(2,1)}, bf16[1,112,128]{2,1,0:T(8,128)(2,1)S(1)}, u32[]{:S(2)}, u32[]{:S(2)}) %collective-permute-start) | collective-permute-done | bytes 28704 | tf_op jit(solution)/shard_map/ppermute | solution.py:243
  3.6 2.9 %collective-permute-start.1 = (bf16[2,112,128]{2,1,0:T(8,128)(2,1)S(1)}, bf16[2,112,128]{2,1,0:T(8,128)(2,1)S(1)}, u32[]{:S(2)}, u32[]{:S(2)}) collective-permute-start(bf16[2,112,128]{2,1,0:T(8,128)(2,1)S(1)} %pad_maximum_fusion.both_ref), channel_id=1, source_target_pairs={{0,2},{2,0},{4,6},{6,4},{8,10},{10,8},{12,14},{14,12},{1,9},{3,11}... | collective-permute-start | bytes 172040 | tf_op jit(solution)/shard_map/ppermute | solution.py:261
  6.5 1.6 %collective-permute-start.2 = (bf16[2,112,128]{2,1,0:T(8,128)(2,1)S(1)}, bf16[2,112,128]{2,1,0:T(8,128)(2,1)S(1)}, u32[]{:S(2)}, u32[]{:S(2)}) collective-permute-start(bf16[2,112,128]{2,1,0:T(8,128)(2,1)S(1)} %pad_maximum_fusion.both_ref), channel_id=1, source_target_pairs={{0,4},{2,6},{4,0},{6,2},{8,12},{10,14},{12,8},{14,10},{1,11},{3,9}... | collective-permute-start | bytes 172040 | tf_op jit(solution)/shard_map/ppermute | solution.py:261
  8.0 0.0 collective-permute-start.3
  8.0 0.7 %collective-permute-start.4 = (bf16[2,112,128]{2,1,0:T(8,128)(2,1)S(1)}, bf16[2,112,128]{2,1,0:T(8,128)(2,1)S(1)}, u32[]{:S(2)}, u32[]{:S(2)}) collective-permute-start(bf16[2,112,128]{2,1,0:T(8,128)(2,1)S(1)} %pad_maximum_fusion.both_ref), channel_id=1, source_target_pairs={{1,15},{3,13},{5,11},{7,9},{9,7},{11,5},{13,3},{15,1},{17,31},{19,... | collective-permute-start | bytes 172040 | tf_op jit(solution)/shard_map/ppermute | solution.py:261
  8.7 0.0 collective-permute-done.1
  8.7 1.9 %collective-permute-done.2 = bf16[2,112,128]{2,1,0:T(8,128)(2,1)S(1)} collective-permute-done((bf16[2,112,128]{2,1,0:T(8,128)(2,1)S(1)}, bf16[2,112,128]{2,1,0:T(8,128)(2,1)S(1)}, u32[]{:S(2)}, u32[]{:S(2)}) %collective-permute-start.2) | collective-permute-done | bytes 57376 | tf_op jit(solution)/shard_map/ppermute | solution.py:261
  10.6 0.0 copy-start.1
  10.7 2.4 %collective-permute-done.3 = bf16[2,112,128]{2,1,0:T(8,128)(2,1)S(1)} collective-permute-done((bf16[2,112,128]{2,1,0:T(8,128)(2,1)S(1)}, bf16[2,112,128]{2,1,0:T(8,128)(2,1)S(1)}, u32[]{:S(2)}, u32[]{:S(2)}) %collective-permute-start.3) | collective-permute-done | bytes 57376 | tf_op jit(solution)/shard_map/ppermute | solution.py:261
  13.1 0.0 copy-start.5
  13.1 0.0 copy-start.7
  13.1 0.0 collective-permute-done.4
  13.2 6.2 %collective-permute-start.5 = (bf16[8,112,128]{2,1,0:T(8,128)(2,1)S(1)}, bf16[8,112,128]{2,1,0:T(8,128)(2,1)S(1)}, u32[]{:S(2)}, u32[]{:S(2)}) collective-permute-start(bf16[8,112,128]{2,1,0:T(8,128)(2,1)S(1)} %constant_dynamic-update-slice_fusion.mine_ref), channel_id=1, source_target_pairs={{0,1},{1,0},{2,3},{3,2},{4,5},{5,4},{6,7},{7,6},{8,9},{9,8},{10,11... | collective-permute-start | bytes 688136 | tf_op jit(solution)/shard_map/ppermute | solution.py:263
  19.4 1.1 %collective-permute-done.5.other_ref = bf16[8,112,128]{2,1,0:T(8,128)(2,1)S(1)} collective-permute-done((bf16[8,112,128]{2,1,0:T(8,128)(2,1)S(1)}, bf16[8,112,128]{2,1,0:T(8,128)(2,1)S(1)}, u32[]{:S(2)}, u32[]{:S(2)}) %collective-permute-start.5) | collective-permute-done | bytes 229408 | tf_op jit(solution)/shard_map/ppermute | solution.py:263
  20.5 0.0 copy-done.3
  20.5 0.0 copy-done.6
  20.5 0.0 copy-done
  20.5 0.0 copy-done.2
  20.5 0.0 copy-done.1
  20.5 0.0 copy-done.5
  20.5 5.0 %shard_map.111 = bf16[2,32,128]{2,1,0:T(8,128)(2,1)} custom-call(s32[32]{0:T(128)S(1)} %copy-done.7, bf16[2,112,128]{2,1,0:T(8,128)(2,1)S(1)} %pad_maximum_fusion.both_ref, bf16[8,112,128]{2,1,0:T(8,128)(2,1)S(1)} %constant_dynamic-update-slice_fusion.mine_ref, bf16[8,112,128]{2,1,0:T(8,128)(2,1)S(1)} %collective-permute-done.5.other_ref, ...), custom_call_target="tpu_custom_call" | custom-call | tf_op jit(solution)/shard_map/pallas_call | solution.py:322
  (12 shorter events, 0.1 us)
Async XLA Ops:
  0.0 20.5 %copy-start.3 = (bf16[512,128]{1,0:T(8,128)(2,1)S(1)}, bf16[512,128]{1,0:T(8,128)(2,1)}, u32[]{:S(2)}) copy-start(bf16[512,128]{1,0:T(8,128)(2,1)} %down_ref.1) | copy-start | bytes 393220
  2.0 1.6 %collective-permute-start = (bf16[1,112,128]{2,1,0:T(8,128)(2,1)}, bf16[1,112,128]{2,1,0:T(8,128)(2,1)S(1)}, u32[]{:S(2)}, u32[]{:S(2)}) collective-permute-start(bf16[1,112,128]{2,1,0:T(8,128)(2,1)} %bitcast.3), channel_id=1, source_target_pairs={{0,1},{1,0},{2,3},{3,2},{4,5},{5,4},{6,7},{7,6},{8,9},{9,8},{10,11... | collective-permute-start | bytes 86024 | tf_op jit(solution)/shard_map/ppermute | solution.py:243
  2.5 0.7 %copy-start.4 = (bf16[112,128]{1,0:T(8,128)(2,1)S(1)}, bf16[112,128]{1,0:T(8,128)(2,1)}, u32[]{:S(2)}) copy-start(bf16[112,128]{1,0:T(8,128)(2,1)} %shard_map.109.packed_ref) | copy-start | bytes 86020
  3.2 17.2 %copy-start.6 = (bf16[128,128]{1,0:T(8,128)(2,1)S(1)}, bf16[128,128]{1,0:T(8,128)(2,1)}, u32[]{:S(2)}) copy-start(bf16[128,128]{1,0:T(8,128)(2,1)} %output_ref.1) | copy-start | bytes 98308
  3.2 17.2 %copy-start = (bf16[32,32,128]{2,1,0:T(8,128)(2,1)S(1)}, bf16[32,32,128]{2,1,0:T(8,128)(2,1)}, u32[]{:S(2)}) copy-start(bf16[32,32,128]{2,1,0:T(8,128)(2,1)} %outer_ref.1) | copy-start | bytes 786436
  3.6 5.1 %collective-permute-start.1 = (bf16[2,112,128]{2,1,0:T(8,128)(2,1)S(1)}, bf16[2,112,128]{2,1,0:T(8,128)(2,1)S(1)}, u32[]{:S(2)}, u32[]{:S(2)}) collective-permute-start(bf16[2,112,128]{2,1,0:T(8,128)(2,1)S(1)} %pad_maximum_fusion.both_ref), channel_id=1, source_target_pairs={{0,2},{2,0},{4,6},{6,4},{8,10},{10,8},{12,14},{14,12},{1,9},{3,11}... | collective-permute-start | bytes 172040 | tf_op jit(solution)/shard_map/ppermute | solution.py:261
  6.5 4.2 %collective-permute-start.2 = (bf16[2,112,128]{2,1,0:T(8,128)(2,1)S(1)}, bf16[2,112,128]{2,1,0:T(8,128)(2,1)S(1)}, u32[]{:S(2)}, u32[]{:S(2)}) collective-permute-start(bf16[2,112,128]{2,1,0:T(8,128)(2,1)S(1)} %pad_maximum_fusion.both_ref), channel_id=1, source_target_pairs={{0,4},{2,6},{4,0},{6,2},{8,12},{10,14},{12,8},{14,10},{1,11},{3,9}... | collective-permute-start | bytes 172040 | tf_op jit(solution)/shard_map/ppermute | solution.py:261
  8.0 5.1 %collective-permute-start.3 = (bf16[2,112,128]{2,1,0:T(8,128)(2,1)S(1)}, bf16[2,112,128]{2,1,0:T(8,128)(2,1)S(1)}, u32[]{:S(2)}, u32[]{:S(2)}) collective-permute-start(bf16[2,112,128]{2,1,0:T(8,128)(2,1)S(1)} %pad_maximum_fusion.both_ref), channel_id=1, source_target_pairs={{0,6},{2,4},{4,2},{6,0},{8,14},{10,12},{12,10},{14,8},{1,13},{3,15... | collective-permute-start | bytes 172040 | tf_op jit(solution)/shard_map/ppermute | solution.py:261
  8.0 5.1 %collective-permute-start.4 = (bf16[2,112,128]{2,1,0:T(8,128)(2,1)S(1)}, bf16[2,112,128]{2,1,0:T(8,128)(2,1)S(1)}, u32[]{:S(2)}, u32[]{:S(2)}) collective-permute-start(bf16[2,112,128]{2,1,0:T(8,128)(2,1)S(1)} %pad_maximum_fusion.both_ref), channel_id=1, source_target_pairs={{1,15},{3,13},{5,11},{7,9},{9,7},{11,5},{13,3},{15,1},{17,31},{19,... | collective-permute-start | bytes 172040 | tf_op jit(solution)/shard_map/ppermute | solution.py:261
  10.6 9.9 %copy-start.2 = (bf16[128,512]{1,0:T(8,128)(2,1)S(1)}, bf16[128,512]{1,0:T(8,128)(2,1)}, u32[]{:S(2)}) copy-start(bf16[128,512]{1,0:T(8,128)(2,1)} %up_ref.1) | copy-start | bytes 393220
  10.6 9.8 %copy-start.1 = (bf16[4,128,128]{2,1,0:T(8,128)(2,1)S(1)}, bf16[4,128,128]{2,1,0:T(8,128)(2,1)}, u32[]{:S(2)}) copy-start(bf16[4,128,128]{2,1,0:T(8,128)(2,1)} %triangle_ref.1) | copy-start | bytes 393220
  13.1 7.4 %copy-start.5 = (bf16[128,128]{1,0:T(8,128)(2,1)S(1)}, bf16[128,128]{1,0:T(8,128)(2,1)}, u32[]{:S(2)}) copy-start(bf16[128,128]{1,0:T(8,128)(2,1)} %gate_ref.1) | copy-start | bytes 98308
  13.1 7.4 %copy-start.7 = (s32[32]{0:T(128)S(1)}, s32[32]{0:T(128)}, u32[]{:S(2)}) copy-start(s32[32]{0:T(128)} %mask_ref.1) | copy-start | bytes 388
  13.2 7.3 %collective-permute-start.5 = (bf16[8,112,128]{2,1,0:T(8,128)(2,1)S(1)}, bf16[8,112,128]{2,1,0:T(8,128)(2,1)S(1)}, u32[]{:S(2)}, u32[]{:S(2)}) collective-permute-start(bf16[8,112,128]{2,1,0:T(8,128)(2,1)S(1)} %constant_dynamic-update-slice_fusion.mine_ref), channel_id=1, source_target_pairs={{0,1},{1,0},{2,3},{3,2},{4,5},{5,4},{6,7},{7,6},{8,9},{9,8},{10,11... | collective-permute-start | bytes 688136 | tf_op jit(solution)/shard_map/ppermute | solution.py:263

commit v9 on v6

--- a/solution.py
+++ b/solution.py
@@ -124,7 +124,7 @@
     ln_one_ref,
 ):
     rows, residues, wide = out_ref.shape
-    cores, chips = 2, held_ref.shape[0]
+    cores, chips = 2, lax.axis_size("dap")
     channels = outer_ref.shape[0]
     sequences = channels
     base = rows * residues
@@ -146,7 +146,7 @@
     lane = lax.broadcasted_iota(jnp.int32, (channels, wide), 1)
     lane_block = lane // channels
     for chip in range(chips):
-        place = xor_place(chip, chips)
+        place = block_place(chip, chips)
         mine, other = held_ref[place], other_ref[place]
         blocks = [jnp.where(second_core, other, mine), jnp.where(second_core, mine, other)]
         packed = [block[base : base + sequences].astype(f32) for block in blocks]
@@ -228,26 +228,34 @@
     out_ref[...] = result.astype(bf16).reshape(rows, residues, wide)
 
 
-def gather_all(block):
+def copy_kernel(packed_ref, out_ref):
+    out_ref[0] = packed_ref[...]
+
+
+def gather_all(packed):
     dap_count = lax.axis_size("dap")
-    held = block[None]
-    step = dap_count // 2
-    while step:
-        got = lax.ppermute(held, "dap", [(src, src ^ step) for src in range(dap_count)])
-        held = jnp.concatenate([held, got], axis=0)
-        step //= 2
+    half = dap_count // 2
+    far = lax.ppermute(packed[None], "dap", [(src, src ^ half) for src in range(dap_count)])
+    own = pl.pallas_call(
+        copy_kernel,
+        out_shape=jax.ShapeDtypeStruct((1,) + packed.shape, packed.dtype),
+        in_specs=[pl.BlockSpec(memory_space=pltpu.VMEM)],
+        out_specs=pl.BlockSpec(memory_space=pltpu.VMEM),
+        compiler_params=pltpu.CompilerParams(vmem_limit_bytes=4 << 20),
+    )(packed)
+    both = jnp.concatenate([own, far], axis=0)
+    held = [both] + [
+        lax.ppermute(both, "dap", [(src, src ^ offset) for src in range(dap_count)])
+        for offset in range(1, half)
+    ]
+    held = jnp.concatenate(held, axis=0)
     return held, lax.ppermute(held, "sub", [(0, 1), (1, 0)])
 
 
-def xor_place(chip, chips):
-    difference = lax.bitwise_xor(lax.axis_index("dap"), chip)
-    place = 0
-    step, bit = chips // 2, 1
-    while step:
-        place = place + jnp.where(lax.bitwise_and(difference, step) != 0, bit, 0)
-        step //= 2
-        bit *= 2
-    return place
+def block_place(chip, chips):
+    offset = lax.bitwise_xor(lax.axis_index("dap"), chip)
+    half = chips // 2
+    return jnp.where(offset >= half, 2 * (offset - half) + 1, 2 * offset)
 
 
 def shards_replicated(
@@ -292,7 +300,7 @@
         pairwise_state,
     )
     held, other = gather_all(packed)
-    cores, chips = 2, held.shape[0]
+    cores, chips = lax.axis_size("sub"), lax.axis_size("dap")
     group = cores * rows
     return pl.pallas_call(
         update_kernel,
@@ -425,9 +433,11 @@
         P(),
     )
 
+    small = mesh.shape["sub"] == 2 and mesh.shape["dap"] == 8
+
     def body(pairwise_state, *rest):
         residues, channels = pairwise_state.shape[1:]
-        if residues * residues * channels * 2 <= REPLICATED_PAIR_BYTES:
+        if small and residues * residues * channels * 2 <= REPLICATED_PAIR_BYTES:
             return shards_replicated(pairwise_state, *rest)
         return shards(pairwise_state, *rest)
 

time: 24.7 us -> 23.4 us (0.947)
  waiting for transfers between devices: 8.62 us -> 7.59 us
  local copies, waits for them, and re-layouts: 0.04 us -> 0.86 us
  other arithmetic: 0.8 us -> 0.01 us
  starting transfers between devices: 8.13 us -> 7.77 us
    ppermute x3 -> x4, waiting for transfers between devices: 7.15 us -> 6.12 us  [the longest x3 4.85 us: gather_all(): lax.ppermute(both, 'dap', [(src, src ^ offset) for src in range(dap_count)])]
    unnamed x16 -> x20, local copies, waits for them, and re-layouts: 0.04 us -> 0.85 us
    concatenate x3 -> x1, other arithmetic: 0.8 us -> 0.01 us  [gather_all(): both = jnp.concatenate([own, far], axis=0)]
    ppermute x3 -> x4, starting transfers between devices: 8.06 us -> 7.7 us  [the longest x1 4.1 us: gather_all(): lax.ppermute(packed[None], 'dap', [(src, src ^ half) for src in range(dap...]
  transfers between devices with their start and end apart: 4 -> 5, of which waited for: 4 -> 5; matrix products, arithmetic and copies ran while one was open for 0% -> 0% of each run, Pallas kernels for 0% -> 0%
where the time goes in v9:
time: 23.4 us; the launch traced here: 23.2 us
  starting transfers between devices  7.77 us (33%)
  waiting for transfers between devices  7.59 us (32%)
  Pallas kernels  6.86 us (29%)
  local copies, waits for them, and re-layouts  0.86 us (4%)
    pallas_call x1, Pallas kernels, shards_replicated(): pl.pallas_call(update_kernel, out_shape=jax.ShapeDtypeStruct(pairwise_sta...  4.9 us
    ppermute x3, waiting for transfers between devices, gather_all(): lax.ppermute(both, 'dap', [(src, src ^ offset) for src in range(dap_count)])  4.85 us
    ppermute x1, starting transfers between devices, gather_all(): lax.ppermute(packed[None], 'dap', [(src, src ^ half) for src in range(dap...  4.1 us
    ppermute x3, starting transfers between devices, gather_all(): lax.ppermute(both, 'dap', [(src, src ^ offset) for src in range(dap_count)])  3.59 us
    pallas_call x1, Pallas kernels, shards_replicated(): pl.pallas_call(pack_kernel, out_shape=jax.ShapeDtypeStruct((rows * residu...  1.96 us
    ppermute x1, waiting for transfers between devices, gather_all(): return (held, lax.ppermute(held, 'sub', [(0, 1), (1, 0)]))  1.48 us
    ppermute x1, waiting for transfers between devices, gather_all(): lax.ppermute(packed[None], 'dap', [(src, src ^ half) for src in range(dap...  1.26 us
    unnamed x20, local copies, waits for them, and re-layouts  0.85 us
  transfers between devices with their start and end apart: 5, of which 5 were waited for; matrix products, arithmetic and copies ran while one was open for 0% of the time, Pallas kernels for 0%

profile of v9, /device:TPU:0, one launch (start us, length us, event | category | flops | bytes accessed | tf_op | source)
XLA Modules:
  0.0 23.2 jit_solution(6159539279385607012)
XLA Ops:
  0.0 2.0 %shard_map.109.packed_ref = bf16[112,128]{1,0:T(8,128)(2,1)} custom-call(s32[32]{0:T(128)} %mask_ref.1, s32[2,32]{1,0:T(2,128)} %bitcast.5, bf16[32,2,256]{2,1,0:T(2,128)(2,1)} %state_hbm.1, bf16[2,32,256]{2,1,0:T(8,128)(2,1)} %bitcast.4, bf16[2,32,128]{2,1,0:T(8,128)(2,1)} %pair_hbm.1), custom_call_target="tpu_custom_call" | custom-call | tf_op jit(solution)/shard_map/pallas_call | solution.py:281
  2.0 4.1 %collective-permute-start = (bf16[1,112,128]{2,1,0:T(8,128)(2,1)}, bf16[1,112,128]{2,1,0:T(8,128)(2,1)S(1)}, u32[]{:S(2)}, u32[]{:S(2)}) collective-permute-start(bf16[1,112,128]{2,1,0:T(8,128)(2,1)} %bitcast.3), channel_id=1, source_target_pairs={{0,8},{2,10},{4,12},{6,14},{8,0},{10,2},{12,4},{14,6},{1,9},{3,11}... | collective-permute-start | bytes 86024 | tf_op jit(solution)/shard_map/ppermute | solution.py:238
  6.1 0.8 %copy-done.4 = bf16[112,128]{1,0:T(8,128)(2,1)S(1)} copy-done((bf16[112,128]{1,0:T(8,128)(2,1)S(1)}, bf16[112,128]{1,0:T(8,128)(2,1)}, u32[]{:S(2)}) %copy-start.4) | copy-done | bytes 28696
  6.9 0.0 copy-start
  6.9 1.3 %collective-permute-done = bf16[1,112,128]{2,1,0:T(8,128)(2,1)S(1)} collective-permute-done((bf16[1,112,128]{2,1,0:T(8,128)(2,1)}, bf16[1,112,128]{2,1,0:T(8,128)(2,1)S(1)}, u32[]{:S(2)}, u32[]{:S(2)}) %collective-permute-start) | collective-permute-done | bytes 28704 | tf_op jit(solution)/shard_map/ppermute | solution.py:238
  8.2 2.1 %collective-permute-start.1 = (bf16[2,112,128]{2,1,0:T(8,128)(2,1)S(1)}, bf16[2,112,128]{2,1,0:T(8,128)(2,1)S(1)}, u32[]{:S(2)}, u32[]{:S(2)}) collective-permute-start(bf16[2,112,128]{2,1,0:T(8,128)(2,1)S(1)} %pad_maximum_fusion), channel_id=1, source_target_pairs={{0,2},{2,0},{4,6},{6,4},{8,10},{10,8},{12,14},{14,12},{1,3},{3,1},... | collective-permute-start | bytes 172040 | tf_op jit(solution)/shard_map/ppermute | solution.py:248
  10.2 1.4 %collective-permute-start.2 = (bf16[2,112,128]{2,1,0:T(8,128)(2,1)S(1)}, bf16[2,112,128]{2,1,0:T(8,128)(2,1)S(1)}, u32[]{:S(2)}, u32[]{:S(2)}) collective-permute-start(bf16[2,112,128]{2,1,0:T(8,128)(2,1)S(1)} %pad_maximum_fusion), channel_id=1, source_target_pairs={{0,4},{2,6},{4,0},{6,2},{8,12},{10,14},{12,8},{14,10},{1,5},{3,7},... | collective-permute-start | bytes 172040 | tf_op jit(solution)/shard_map/ppermute | solution.py:248
  11.6 0.2 collective-permute-start.3
  11.8 0.8 %collective-permute-done.1 = bf16[2,112,128]{2,1,0:T(8,128)(2,1)S(1)} collective-permute-done((bf16[2,112,128]{2,1,0:T(8,128)(2,1)S(1)}, bf16[2,112,128]{2,1,0:T(8,128)(2,1)S(1)}, u32[]{:S(2)}, u32[]{:S(2)}) %collective-permute-start.1) | collective-permute-done | bytes 57376 | tf_op jit(solution)/shard_map/ppermute | solution.py:248
  12.6 0.0 copy-start.1
  12.6 1.8 %collective-permute-done.2 = bf16[2,112,128]{2,1,0:T(8,128)(2,1)S(1)} collective-permute-done((bf16[2,112,128]{2,1,0:T(8,128)(2,1)S(1)}, bf16[2,112,128]{2,1,0:T(8,128)(2,1)S(1)}, u32[]{:S(2)}, u32[]{:S(2)}) %collective-permute-start.2) | collective-permute-done | bytes 57376 | tf_op jit(solution)/shard_map/ppermute | solution.py:248
  14.4 0.0 copy-start.5
  14.4 0.0 copy-start.7
  14.4 2.3 %collective-permute-done.3 = bf16[2,112,128]{2,1,0:T(8,128)(2,1)S(1)} collective-permute-done((bf16[2,112,128]{2,1,0:T(8,128)(2,1)S(1)}, bf16[2,112,128]{2,1,0:T(8,128)(2,1)S(1)}, u32[]{:S(2)}, u32[]{:S(2)}) %collective-permute-start.3) | collective-permute-done | bytes 57376 | tf_op jit(solution)/shard_map/ppermute | solution.py:248
  16.7 0.1 collective-permute-start.4
  16.8 1.5 %collective-permute-done.4.other_ref = bf16[8,112,128]{2,1,0:T(8,128)(2,1)S(1)} collective-permute-done((bf16[8,112,128]{2,1,0:T(8,128)(2,1)S(1)}, bf16[8,112,128]{2,1,0:T(8,128)(2,1)S(1)}, u32[]{:S(2)}, u32[]{:S(2)}) %collective-permute-start.4) | collective-permute-done | bytes 229408 | tf_op jit(solution)/shard_map/ppermute | solution.py:252
  18.2 0.0 copy-done.3
  18.2 0.0 copy-done.6
  18.3 0.0 copy-done.2
  18.3 0.0 copy-done
  18.3 0.0 copy-done.1
  18.3 0.0 copy-done.5
  18.3 0.0 copy-done.7
  18.3 4.9 %shard_map.111 = bf16[2,32,128]{2,1,0:T(8,128)(2,1)} custom-call(s32[32]{0:T(128)S(1)} %copy-done.7, bf16[8,112,128]{2,1,0:T(8,128)(2,1)S(1)} %constant_dynamic-update-slice_fusion.held_ref, bf16[8,112,128]{2,1,0:T(8,128)(2,1)S(1)} %collective-permute-done.4.other_ref, bf16[32,32,128]{2,1,0:T(8,128)(2,1)S(1)} %copy-done, bf16[4,128,128]{2,1,0:T(8,128)(2,1)S(1)} %copy-done.1, ...), custom_call_target="tpu_custom_call" | custom-call | tf_op jit(solution)/shard_map/pallas_call | solution.py:305
  (11 shorter events, 0.1 us)
Async XLA Ops:
  0.0 18.2 %copy-start.3 = (bf16[512,128]{1,0:T(8,128)(2,1)S(1)}, bf16[512,128]{1,0:T(8,128)(2,1)}, u32[]{:S(2)}) copy-start(bf16[512,128]{1,0:T(8,128)(2,1)} %down_ref.1) | copy-start | bytes 393220
  2.0 6.2 %collective-permute-start = (bf16[1,112,128]{2,1,0:T(8,128)(2,1)}, bf16[1,112,128]{2,1,0:T(8,128)(2,1)S(1)}, u32[]{:S(2)}, u32[]{:S(2)}) collective-permute-start(bf16[1,112,128]{2,1,0:T(8,128)(2,1)} %bitcast.3), channel_id=1, source_target_pairs={{0,8},{2,10},{4,12},{6,14},{8,0},{10,2},{12,4},{14,6},{1,9},{3,11}... | collective-permute-start | bytes 86024 | tf_op jit(solution)/shard_map/ppermute | solution.py:238
  6.1 0.8 %copy-start.4 = (bf16[112,128]{1,0:T(8,128)(2,1)S(1)}, bf16[112,128]{1,0:T(8,128)(2,1)}, u32[]{:S(2)}) copy-start(bf16[112,128]{1,0:T(8,128)(2,1)} %shard_map.109.packed_ref) | copy-start | bytes 86020
  6.9 11.4 %copy-start.6 = (bf16[128,128]{1,0:T(8,128)(2,1)S(1)}, bf16[128,128]{1,0:T(8,128)(2,1)}, u32[]{:S(2)}) copy-start(bf16[128,128]{1,0:T(8,128)(2,1)} %output_ref.1) | copy-start | bytes 98308
  6.9 11.4 %copy-start.2 = (bf16[128,512]{1,0:T(8,128)(2,1)S(1)}, bf16[128,512]{1,0:T(8,128)(2,1)}, u32[]{:S(2)}) copy-start(bf16[128,512]{1,0:T(8,128)(2,1)} %up_ref.1) | copy-start | bytes 393220
  6.9 11.4 %copy-start = (bf16[32,32,128]{2,1,0:T(8,128)(2,1)S(1)}, bf16[32,32,128]{2,1,0:T(8,128)(2,1)}, u32[]{:S(2)}) copy-start(bf16[32,32,128]{2,1,0:T(8,128)(2,1)} %outer_ref.1) | copy-start | bytes 786436
  8.2 4.4 %collective-permute-start.1 = (bf16[2,112,128]{2,1,0:T(8,128)(2,1)S(1)}, bf16[2,112,128]{2,1,0:T(8,128)(2,1)S(1)}, u32[]{:S(2)}, u32[]{:S(2)}) collective-permute-start(bf16[2,112,128]{2,1,0:T(8,128)(2,1)S(1)} %pad_maximum_fusion), channel_id=1, source_target_pairs={{0,2},{2,0},{4,6},{6,4},{8,10},{10,8},{12,14},{14,12},{1,3},{3,1},... | collective-permute-start | bytes 172040 | tf_op jit(solution)/shard_map/ppermute | solution.py:248
  10.2 4.2 %collective-permute-start.2 = (bf16[2,112,128]{2,1,0:T(8,128)(2,1)S(1)}, bf16[2,112,128]{2,1,0:T(8,128)(2,1)S(1)}, u32[]{:S(2)}, u32[]{:S(2)}) collective-permute-start(bf16[2,112,128]{2,1,0:T(8,128)(2,1)S(1)} %pad_maximum_fusion), channel_id=1, source_target_pairs={{0,4},{2,6},{4,0},{6,2},{8,12},{10,14},{12,8},{14,10},{1,5},{3,7},... | collective-permute-start | bytes 172040 | tf_op jit(solution)/shard_map/ppermute | solution.py:248
  11.6 5.1 %collective-permute-start.3 = (bf16[2,112,128]{2,1,0:T(8,128)(2,1)S(1)}, bf16[2,112,128]{2,1,0:T(8,128)(2,1)S(1)}, u32[]{:S(2)}, u32[]{:S(2)}) collective-permute-start(bf16[2,112,128]{2,1,0:T(8,128)(2,1)S(1)} %pad_maximum_fusion), channel_id=1, source_target_pairs={{0,6},{2,4},{4,2},{6,0},{8,14},{10,12},{12,10},{14,8},{1,7},{3,5},... | collective-permute-start | bytes 172040 | tf_op jit(solution)/shard_map/ppermute | solution.py:248
  12.6 5.7 %copy-start.1 = (bf16[4,128,128]{2,1,0:T(8,128)(2,1)S(1)}, bf16[4,128,128]{2,1,0:T(8,128)(2,1)}, u32[]{:S(2)}) copy-start(bf16[4,128,128]{2,1,0:T(8,128)(2,1)} %triangle_ref.1) | copy-start | bytes 393220
  14.4 3.9 %copy-start.5 = (bf16[128,128]{1,0:T(8,128)(2,1)S(1)}, bf16[128,128]{1,0:T(8,128)(2,1)}, u32[]{:S(2)}) copy-start(bf16[128,128]{1,0:T(8,128)(2,1)} %gate_ref.1) | copy-start | bytes 98308
  14.4 3.9 %copy-start.7 = (s32[32]{0:T(128)S(1)}, s32[32]{0:T(128)}, u32[]{:S(2)}) copy-start(s32[32]{0:T(128)} %mask_ref.1) | copy-start | bytes 388
  16.7 1.6 %collective-permute-start.4 = (bf16[8,112,128]{2,1,0:T(8,128)(2,1)S(1)}, bf16[8,112,128]{2,1,0:T(8,128)(2,1)S(1)}, u32[]{:S(2)}, u32[]{:S(2)}) collective-permute-start(bf16[8,112,128]{2,1,0:T(8,128)(2,1)S(1)} %constant_dynamic-update-slice_fusion.held_ref), channel_id=1, source_target_pairs={{0,1},{1,0},{2,3},{3,2},{4,5},{5,4},{6,7},{7,6},{8,9},{9,8},{10,11... | collective-permute-start | bytes 688136 | tf_op jit(solution)/shard_map/ppermute | solution.py:252

commit v10 on v9

--- a/solution.py
+++ b/solution.py
@@ -43,6 +43,7 @@
     weight_hbm,
     pair_hbm,
     out_ref,
+    column_ref,
     mask_ref,
     keep_ref,
     state_ref,
@@ -98,9 +99,18 @@
     keep = jnp.concatenate(
         keeps + [jnp.zeros((16 - rows, sequences), jnp.float32)], axis=0
     )
+    place = lax.broadcasted_iota(jnp.int32, (residues, 1), 0)
+    column = jnp.zeros((residues, 1), jnp.float32)
+    for k in range(residues):
+        column = jnp.where(place == k, mask_ref[k].astype(jnp.float32), column)
+    column_ref[...] = jnp.broadcast_to(column, (residues, wide))
     out_ref[base + sequences :] = jnp.concatenate(
         [keep, jnp.zeros((16, wide - sequences), jnp.float32)], axis=1
     ).astype(jnp.bfloat16)
+
+
+def sigmoid(values):
+    return 0.5 * jnp.tanh(0.5 * values) + 0.5
 
 
 def update_kernel(
@@ -118,7 +128,8 @@
     left_ref,
     right_ref,
     keep_ref,
-    outer_product_ref,
+    first_ref,
+    second_ref,
     pair_ref,
     pair_one_ref,
     ln_one_ref,
@@ -128,39 +139,48 @@
     channels = outer_ref.shape[0]
     sequences = channels
     base = rows * residues
+    half = wide // 2
     group = cores * rows
     start = first_row(rows)
     second_core = lax.axis_index("sub") == 1
     bf16 = jnp.bfloat16
     f32 = jnp.float32
 
-    block_ref[...] = jnp.zeros_like(block_ref)
-    for d in range(channels):
-        weight = outer_ref[d]
-        for part in range(group):
-            block_ref[
-                (d * group + part) * channels : (d * group + part + 1) * channels,
-                part * wide : (part + 1) * wide,
-            ] = weight
+    parts = block_ref.shape[0]
+    span = channels // parts
+    nothing = jnp.zeros((channels, wide), bf16)
+    for part in range(parts):
+        for step in range(span + 1):
+            weight = outer_ref[part * span + step % span]
+            at = step * 2 * channels
+            block_ref[part, at : at + channels, :wide] = weight
+            block_ref[part, at : at + channels, wide:] = nothing
+            block_ref[part, at + channels : at + 2 * channels, :wide] = nothing
+            block_ref[part, at + channels : at + 2 * channels, wide:] = weight
 
     lane = lax.broadcasted_iota(jnp.int32, (channels, wide), 1)
     lane_block = lane // channels
+    low = lane < half
     for chip in range(chips):
         place = block_place(chip, chips)
         mine, other = held_ref[place], other_ref[place]
         blocks = [jnp.where(second_core, other, mine), jnp.where(second_core, mine, other)]
         packed = [block[base : base + sequences].astype(f32) for block in blocks]
-        right = jnp.where(lane < wide // 2, packed[0], packed[1]).astype(bf16)
-        for copy in range(group):
-            right_ref[copy * sequences : (copy + 1) * sequences, chip * wide : (chip + 1) * wide] = right
+        right = jnp.where(low, packed[0], packed[1])
+        for turn, value in enumerate((right, pltpu.roll(right, half, 1))):
+            for copy in range(group):
+                right_ref[
+                    turn,
+                    copy * sequences : (copy + 1) * sequences,
+                    chip * wide : (chip + 1) * wide,
+                ] = value.astype(bf16)
         for core in range(cores):
+            residue = (chip * cores + core) * rows
             for row in range(rows):
-                residue = (chip * cores + core) * rows + row
                 at = (rows if core == 0 else 0) + row
-                left_ref[residue] = jnp.where(lane_block == at, packed[core], 0.0)
-            presence = blocks[core][base + sequences :].astype(f32)
-            keep_ref[(chip * cores + core) * rows : (chip * cores + core + 1) * rows] = presence[:rows]
-            pair_ref[(chip * cores + core) * rows : (chip * cores + core + 1) * rows] = (
+                left_ref[residue + row] = jnp.where(lane_block == at, packed[core], 0.0)
+            keep_ref[residue : residue + rows] = blocks[core][base + sequences :].astype(f32)[:rows]
+            pair_ref[residue : residue + rows] = (
                 blocks[core][:base].astype(f32).reshape(rows, residues, wide)
             )
 
@@ -169,58 +189,79 @@
     count = lax.dot_general(keep, keep, last, preferred_element_type=f32)
     inverse = 1.0 / jnp.maximum(count, 1.0)
 
-    step = 8
-    for first in range(0, channels, step):
-        left = jnp.concatenate(
-            [left_ref[:, d] for d in range(first, first + step)], axis=0
-        ).astype(bf16)
-        outer = jnp.dot(left, right_ref[...], preferred_element_type=f32).astype(bf16)
-        for d in range(first, first + step):
+    low = lax.broadcasted_iota(jnp.int32, (residues, wide), 1) < half
+    totals = [0.0, 0.0]
+    for part in range(parts):
+        outer = []
+        for turn in range(2):
+            left = jnp.concatenate(
+                [left_ref[:, d] for d in range(part * span + turn, (part + 1) * span, 2)], axis=0
+            ).astype(bf16)
+            outer.append(jnp.dot(left, right_ref[turn], preferred_element_type=f32))
+
+        def piece(turn, at, chip):
+            return outer[turn][
+                at * residues : (at + 1) * residues, chip * wide : (chip + 1) * wide
+            ]
+
+        for at in range(span // 2):
+            follow = (at + 1) % (span // 2)
             for chip in range(chips):
-                outer_product_ref[
-                    chip * residues : (chip + 1) * residues, d * wide : (d + 1) * wide
-                ] = outer[
-                    (d - first) * residues : (d - first + 1) * residues,
-                    chip * wide : (chip + 1) * wide,
-                ]
-    numerator = jnp.dot(outer_product_ref[...], block_ref[...], preferred_element_type=f32)
-
-    for k in range(residues):
-        chip, part = k // group, k % group
-        opm = numerator[
-            chip * residues : (chip + 1) * residues, part * wide : (part + 1) * wide
-        ] * jnp.broadcast_to(inverse[:, k : k + 1], (residues, wide))
-        pair_one = (pair_ref[:, k] + opm).astype(bf16).astype(f32)
-        pair_one_ref[k] = pair_one
-        ln_one_ref[k] = layer_norm(pair_one)
-
-    ln_all = ln_one_ref[...].reshape(residues * residues, wide).astype(bf16)
-    gate_value = jnp.dot(ln_all, triangle_ref[2], preferred_element_type=f32)
-    value = jnp.dot(ln_all, triangle_ref[3], preferred_element_type=f32)
-    right_tri = (jax.nn.sigmoid(gate_value) * value).astype(bf16).astype(f32)
-
-    mask_column = jnp.zeros((residues, 1), f32)
-    place = lax.broadcasted_iota(jnp.int32, (residues, 1), 0)
-    for k in range(residues):
-        mask_column = jnp.where(place == k, mask_ref[k].astype(f32), mask_column)
-
+                place = (
+                    part,
+                    slice(chip * residues, (chip + 1) * residues),
+                    slice(at * wide, (at + 1) * wide),
+                )
+                first_ref[place] = jnp.where(low, piece(0, at, chip), piece(1, at, chip)).astype(bf16)
+                second_ref[place] = jnp.where(
+                    low, piece(1, at, chip), piece(0, follow, chip)
+                ).astype(bf16)
+        depth = span * 2 * channels
+        totals[0] += jnp.dot(first_ref[part], block_ref[part, :depth], preferred_element_type=f32)
+        totals[1] += jnp.dot(
+            second_ref[part], block_ref[part, 2 * channels :], preferred_element_type=f32
+        )
+
+    right_weight = jnp.concatenate([triangle_ref[2], triangle_ref[3]], axis=1)
+    right_tri = []
+    stride = 8
+    for first in range(0, residues, stride):
+        normed = []
+        for k in range(first, first + stride):
+            chip, pick = k // group, k % group
+            at = (pick % 2) * wide
+            numerator = totals[pick // 2][chip * residues : (chip + 1) * residues, at : at + wide]
+            opm = numerator * jnp.broadcast_to(inverse[:, k : k + 1], (residues, wide))
+            pair_one = (pair_ref[:, k] + opm).astype(bf16).astype(f32)
+            pair_one_ref[k] = pair_one
+            ln_one = layer_norm(pair_one)
+            ln_one_ref[k] = ln_one
+            normed.append(ln_one.astype(bf16))
+        both = jnp.dot(
+            jnp.concatenate(normed, axis=0), right_weight, preferred_element_type=f32
+        )
+        right_tri.append((sigmoid(both[:, :wide]) * both[:, wide:]).astype(bf16).astype(f32))
+
+    mask = mask_ref[...]
     own_pair = jnp.concatenate([pair_one_ref[:, start + row] for row in range(rows)], axis=0)
     own_ln = jnp.concatenate([ln_one_ref[:, start + row] for row in range(rows)], axis=0).astype(bf16)
-    gate_value = jnp.dot(own_ln, triangle_ref[0], preferred_element_type=f32)
-    value = jnp.dot(own_ln, triangle_ref[1], preferred_element_type=f32)
-    left_tri = jax.nn.sigmoid(gate_value) * value * jnp.concatenate([mask_column] * rows, axis=0)
+    left_weight = jnp.concatenate([triangle_ref[0], triangle_ref[1]], axis=1)
+    both = jnp.dot(own_ln, left_weight, preferred_element_type=f32)
+    left_tri = sigmoid(both[:, :wide]) * both[:, wide:] * jnp.concatenate([mask] * rows, axis=0)
     left_tri = left_tri.astype(bf16).astype(f32)
     products = []
     for row in range(rows):
-        total = jnp.zeros((residues, wide), f32)
+        sums = [jnp.zeros((residues, wide), f32) for _ in range(4)]
         for k in range(residues):
             at = row * residues + k
-            total += left_tri[at : at + 1] * right_tri[k * residues : (k + 1) * residues]
-        products.append(total * (mask_column * mask_ref[start + row].astype(f32)))
+            place = (k % stride) * residues
+            sums[k % 4] += left_tri[at : at + 1] * right_tri[k // stride][place : place + residues]
+        total = (sums[0] + sums[1]) + (sums[2] + sums[3])
+        products.append(total * (mask * mask_ref[pl.ds(start + row, 1), :]))
     product = jnp.concatenate(products, axis=0).astype(bf16).astype(f32)
     normed = layer_norm(product).astype(bf16)
     update = jnp.dot(normed, output_ref[...], preferred_element_type=f32)
-    gate_out = jax.nn.sigmoid(jnp.dot(own_ln, gate_ref[...], preferred_element_type=f32))
+    gate_out = sigmoid(jnp.dot(own_ln, gate_ref[...], preferred_element_type=f32))
     pair_two = (own_pair + gate_out * update).astype(bf16).astype(f32)
     ln_two = layer_norm(pair_two).astype(bf16)
     hidden = jnp.maximum(jnp.dot(ln_two, up_ref[...], preferred_element_type=f32), 0.0).astype(bf16)
@@ -274,15 +315,17 @@
     rows, residues, wide = pairwise_state.shape
     sequences = alignment_state.shape[0]
     channels = outer_input_weight.shape[2]
-    scalar = pl.BlockSpec(memory_space=pltpu.SMEM)
     vector = pl.BlockSpec(memory_space=pltpu.VMEM)
     params = pltpu.CompilerParams(vmem_limit_bytes=40 << 20)
     hbm = pl.BlockSpec(memory_space=pltpu.HBM)
-    packed = pl.pallas_call(
+    packed, mask = pl.pallas_call(
         pack_kernel,
-        out_shape=jax.ShapeDtypeStruct((rows * residues + sequences + 16, wide), jnp.bfloat16),
+        out_shape=(
+            jax.ShapeDtypeStruct((rows * residues + sequences + 16, wide), jnp.bfloat16),
+            jax.ShapeDtypeStruct((residues, wide), jnp.float32),
+        ),
         in_specs=[hbm] * 5,
-        out_specs=vector,
+        out_specs=(vector, vector),
         scratch_shapes=[
             pltpu.SMEM((residues,), jnp.int32),
             pltpu.VMEM((rows, sequences), jnp.int32),
@@ -302,24 +345,26 @@
     held, other = gather_all(packed)
     cores, chips = lax.axis_size("sub"), lax.axis_size("dap")
     group = cores * rows
+    parts = 2
     return pl.pallas_call(
         update_kernel,
         out_shape=jax.ShapeDtypeStruct(pairwise_state.shape, jnp.bfloat16),
-        in_specs=[scalar] + [vector] * 8,
+        in_specs=[vector] * 9,
         out_specs=vector,
         scratch_shapes=[
-            pltpu.VMEM((channels * group * channels, group * wide), jnp.bfloat16),
+            pltpu.VMEM((parts, (channels // parts + 1) * 2 * channels, 2 * wide), jnp.bfloat16),
             pltpu.VMEM((residues, channels, wide), jnp.float32),
-            pltpu.VMEM((group * sequences, chips * wide), jnp.bfloat16),
+            pltpu.VMEM((2, group * sequences, chips * wide), jnp.bfloat16),
             pltpu.VMEM((residues, wide), jnp.float32),
-            pltpu.VMEM((chips * residues, channels * wide), jnp.bfloat16),
+            pltpu.VMEM((parts, chips * residues, channels // parts * wide // 2), jnp.bfloat16),
+            pltpu.VMEM((parts, chips * residues, channels // parts * wide // 2), jnp.bfloat16),
             pltpu.VMEM((residues, residues, wide), jnp.float32),
             pltpu.VMEM((residues, residues, wide), jnp.float32),
             pltpu.VMEM((residues, residues, wide), jnp.float32),
         ],
         compiler_params=params,
     )(
-        residue_crop_mask,
+        mask,
         held,
         other,
         outer_output_weight,

time: 23.4 us -> 23.2 us (level)
  Pallas kernels: 6.86 us -> 5.86 us
  local copies, waits for them, and re-layouts: 0.86 us -> 1.61 us
    pallas_call x1, Pallas kernels: 4.9 us -> 3.9 us  [shards_replicated(): pl.pallas_call(update_kernel, out_shape=jax.ShapeDtypeStruct(pairwise_sta...]
    unnamed x20, local copies, waits for them, and re-layouts: 0.85 us -> 1.6 us
where the time goes in v10:
time: 23.2 us; the launch traced here: 22.9 us
  starting transfers between devices  7.77 us (33%)
  waiting for transfers between devices  7.59 us (33%)
  Pallas kernels  5.86 us (25%)
  local copies, waits for them, and re-layouts  1.61 us (7%)
    ppermute x3, waiting for transfers between devices, gather_all(): lax.ppermute(both, 'dap', [(src, src ^ offset) for src in range(dap_count)])  4.85 us
    ppermute x1, starting transfers between devices, gather_all(): lax.ppermute(packed[None], 'dap', [(src, src ^ half) for src in range(dap...  4.1 us
    pallas_call x1, Pallas kernels, shards_replicated(): pl.pallas_call(update_kernel, out_shape=jax.ShapeDtypeStruct(pairwise_sta...  3.9 us
    ppermute x3, starting transfers between devices, gather_all(): lax.ppermute(both, 'dap', [(src, src ^ offset) for src in range(dap_count)])  3.59 us
    pallas_call x1, Pallas kernels, shards_replicated(): pl.pallas_call(pack_kernel, out_shape=(jax.ShapeDtypeStruct((rows * resid...  1.96 us
    unnamed x20, local copies, waits for them, and re-layouts  1.6 us
    ppermute x1, waiting for transfers between devices, gather_all(): return (held, lax.ppermute(held, 'sub', [(0, 1), (1, 0)]))  1.48 us
    ppermute x1, waiting for transfers between devices, gather_all(): lax.ppermute(packed[None], 'dap', [(src, src ^ half) for src in range(dap...  1.26 us
  transfers between devices with their start and end apart: 5, of which 5 were waited for; matrix products, arithmetic and copies ran while one was open for 0% of the time, Pallas kernels for 0%

profile of v10, /device:TPU:0, one launch (start us, length us, event | category | flops | bytes accessed | tf_op | source)
XLA Modules:
  0.0 22.9 jit_solution(10899373619045135274)
XLA Ops:
  0.0 2.0 %shard_map.109 = (bf16[112,128]{1,0:T(8,128)(2,1)}, f32[32,128]{1,0:T(8,128)}) custom-call(s32[32]{0:T(128)} %mask_hbm.1, s32[2,32]{1,0:T(2,128)} %bitcast.5, bf16[32,2,256]{2,1,0:T(2,128)(2,1)} %state_hbm.1, bf16[2,32,256]{2,1,0:T(8,128)(2,1)} %bitcast.4, bf16[2,32,128]{2,1,0:T(8,128)(2,1)} %pair_hbm.1), custom_call_target="tpu_custom_call" | custom-call | tf_op jit(solution)/shard_map/pallas_call | solution.py:321
  2.0 4.1 %collective-permute-start = (bf16[1,112,128]{2,1,0:T(8,128)(2,1)}, bf16[1,112,128]{2,1,0:T(8,128)(2,1)S(1)}, u32[]{:S(2)}, u32[]{:S(2)}) collective-permute-start(bf16[1,112,128]{2,1,0:T(8,128)(2,1)} %bitcast.3), channel_id=1, source_target_pairs={{0,8},{2,10},{4,12},{6,14},{8,0},{10,2},{12,4},{14,6},{1,9},{3,11}... | collective-permute-start | bytes 86024 | tf_op jit(solution)/shard_map/ppermute | solution.py:279
  6.1 0.8 %copy-done.6 = bf16[112,128]{1,0:T(8,128)(2,1)S(1)} copy-done((bf16[112,128]{1,0:T(8,128)(2,1)S(1)}, bf16[112,128]{1,0:T(8,128)(2,1)}, u32[]{:S(2)}) %copy-start.6) | copy-done | bytes 28696
  6.9 0.0 copy-start
  6.9 1.3 %collective-permute-done = bf16[1,112,128]{2,1,0:T(8,128)(2,1)S(1)} collective-permute-done((bf16[1,112,128]{2,1,0:T(8,128)(2,1)}, bf16[1,112,128]{2,1,0:T(8,128)(2,1)S(1)}, u32[]{:S(2)}, u32[]{:S(2)}) %collective-permute-start) | collective-permute-done | bytes 28704 | tf_op jit(solution)/shard_map/ppermute | solution.py:279
  8.2 2.1 %collective-permute-start.1 = (bf16[2,112,128]{2,1,0:T(8,128)(2,1)S(1)}, bf16[2,112,128]{2,1,0:T(8,128)(2,1)S(1)}, u32[]{:S(2)}, u32[]{:S(2)}) collective-permute-start(bf16[2,112,128]{2,1,0:T(8,128)(2,1)S(1)} %pad_maximum_fusion), channel_id=1, source_target_pairs={{0,2},{2,0},{4,6},{6,4},{8,10},{10,8},{12,14},{14,12},{1,3},{3,1},... | collective-permute-start | bytes 172040 | tf_op jit(solution)/shard_map/ppermute | solution.py:289
  10.2 1.4 %collective-permute-start.2 = (bf16[2,112,128]{2,1,0:T(8,128)(2,1)S(1)}, bf16[2,112,128]{2,1,0:T(8,128)(2,1)S(1)}, u32[]{:S(2)}, u32[]{:S(2)}) collective-permute-start(bf16[2,112,128]{2,1,0:T(8,128)(2,1)S(1)} %pad_maximum_fusion), channel_id=1, source_target_pairs={{0,4},{2,6},{4,0},{6,2},{8,12},{10,14},{12,8},{14,10},{1,5},{3,7},... | collective-permute-start | bytes 172040 | tf_op jit(solution)/shard_map/ppermute | solution.py:289
  11.6 0.2 collective-permute-start.3
  11.8 0.8 %collective-permute-done.1 = bf16[2,112,128]{2,1,0:T(8,128)(2,1)S(1)} collective-permute-done((bf16[2,112,128]{2,1,0:T(8,128)(2,1)S(1)}, bf16[2,112,128]{2,1,0:T(8,128)(2,1)S(1)}, u32[]{:S(2)}, u32[]{:S(2)}) %collective-permute-start.1) | collective-permute-done | bytes 57376 | tf_op jit(solution)/shard_map/ppermute | solution.py:289
  12.6 0.0 copy-start.1
  12.6 1.8 %collective-permute-done.2 = bf16[2,112,128]{2,1,0:T(8,128)(2,1)S(1)} collective-permute-done((bf16[2,112,128]{2,1,0:T(8,128)(2,1)S(1)}, bf16[2,112,128]{2,1,0:T(8,128)(2,1)S(1)}, u32[]{:S(2)}, u32[]{:S(2)}) %collective-permute-start.2) | collective-permute-done | bytes 57376 | tf_op jit(solution)/shard_map/ppermute | solution.py:289
  14.4 0.0 copy-start.4
  14.4 0.0 copy-start.7
  14.4 2.3 %collective-permute-done.3 = bf16[2,112,128]{2,1,0:T(8,128)(2,1)S(1)} collective-permute-done((bf16[2,112,128]{2,1,0:T(8,128)(2,1)S(1)}, bf16[2,112,128]{2,1,0:T(8,128)(2,1)S(1)}, u32[]{:S(2)}, u32[]{:S(2)}) %collective-permute-start.3) | collective-permute-done | bytes 57376 | tf_op jit(solution)/shard_map/ppermute | solution.py:289
  16.7 0.1 collective-permute-start.4
  16.8 1.5 %collective-permute-done.4.other_ref = bf16[8,112,128]{2,1,0:T(8,128)(2,1)S(1)} collective-permute-done((bf16[8,112,128]{2,1,0:T(8,128)(2,1)S(1)}, bf16[8,112,128]{2,1,0:T(8,128)(2,1)S(1)}, u32[]{:S(2)}, u32[]{:S(2)}) %collective-permute-start.4) | collective-permute-done | bytes 229408 | tf_op jit(solution)/shard_map/ppermute | solution.py:293
  18.2 0.0 copy-done.3
  18.2 0.0 copy-done.2
  18.2 0.0 copy-done
  18.3 0.0 copy-done.1
  18.3 0.0 copy-done.4
  18.3 0.0 copy-start.5
  18.3 0.7 %copy-done.5 = bf16[128,128]{1,0:T(8,128)(2,1)S(1)} copy-done((bf16[128,128]{1,0:T(8,128)(2,1)S(1)}, bf16[128,128]{1,0:T(8,128)(2,1)}, u32[]{:S(2)}) %copy-start.5) | copy-done | bytes 32792
  19.0 3.9 %shard_map.111 = bf16[2,32,128]{2,1,0:T(8,128)(2,1)} custom-call(f32[32,128]{1,0:T(8,128)S(1)} %copy-done.7, bf16[8,112,128]{2,1,0:T(8,128)(2,1)S(1)} %constant_dynamic-update-slice_fusion.held_ref, bf16[8,112,128]{2,1,0:T(8,128)(2,1)S(1)} %collective-permute-done.4.other_ref, bf16[32,32,128]{2,1,0:T(8,128)(2,1)S(1)} %copy-done, ...), custom_call_target="tpu_custom_call" | custom-call | tf_op jit(solution)/shard_map/pallas_call | solution.py:349
  (11 shorter events, 0.1 us)
Async XLA Ops:
  0.0 18.2 %copy-start.3 = (bf16[512,128]{1,0:T(8,128)(2,1)S(1)}, bf16[512,128]{1,0:T(8,128)(2,1)}, u32[]{:S(2)}) copy-start(bf16[512,128]{1,0:T(8,128)(2,1)} %down_ref.1) | copy-start | bytes 393220
  2.0 6.2 %collective-permute-start = (bf16[1,112,128]{2,1,0:T(8,128)(2,1)}, bf16[1,112,128]{2,1,0:T(8,128)(2,1)S(1)}, u32[]{:S(2)}, u32[]{:S(2)}) collective-permute-start(bf16[1,112,128]{2,1,0:T(8,128)(2,1)} %bitcast.3), channel_id=1, source_target_pairs={{0,8},{2,10},{4,12},{6,14},{8,0},{10,2},{12,4},{14,6},{1,9},{3,11}... | collective-permute-start | bytes 86024 | tf_op jit(solution)/shard_map/ppermute | solution.py:279
  6.1 0.8 %copy-start.6 = (bf16[112,128]{1,0:T(8,128)(2,1)S(1)}, bf16[112,128]{1,0:T(8,128)(2,1)}, u32[]{:S(2)}) copy-start(bf16[112,128]{1,0:T(8,128)(2,1)} %get-tuple-element.8.packed_ref) | copy-start | bytes 86020
  6.9 11.4 %copy-start.2 = (bf16[128,512]{1,0:T(8,128)(2,1)S(1)}, bf16[128,512]{1,0:T(8,128)(2,1)}, u32[]{:S(2)}) copy-start(bf16[128,512]{1,0:T(8,128)(2,1)} %up_ref.1) | copy-start | bytes 393220
  6.9 11.4 %copy-start = (bf16[32,32,128]{2,1,0:T(8,128)(2,1)S(1)}, bf16[32,32,128]{2,1,0:T(8,128)(2,1)}, u32[]{:S(2)}) copy-start(bf16[32,32,128]{2,1,0:T(8,128)(2,1)} %outer_ref.1) | copy-start | bytes 786436
  8.2 4.4 %collective-permute-start.1 = (bf16[2,112,128]{2,1,0:T(8,128)(2,1)S(1)}, bf16[2,112,128]{2,1,0:T(8,128)(2,1)S(1)}, u32[]{:S(2)}, u32[]{:S(2)}) collective-permute-start(bf16[2,112,128]{2,1,0:T(8,128)(2,1)S(1)} %pad_maximum_fusion), channel_id=1, source_target_pairs={{0,2},{2,0},{4,6},{6,4},{8,10},{10,8},{12,14},{14,12},{1,3},{3,1},... | collective-permute-start | bytes 172040 | tf_op jit(solution)/shard_map/ppermute | solution.py:289
  10.2 4.2 %collective-permute-start.2 = (bf16[2,112,128]{2,1,0:T(8,128)(2,1)S(1)}, bf16[2,112,128]{2,1,0:T(8,128)(2,1)S(1)}, u32[]{:S(2)}, u32[]{:S(2)}) collective-permute-start(bf16[2,112,128]{2,1,0:T(8,128)(2,1)S(1)} %pad_maximum_fusion), channel_id=1, source_target_pairs={{0,4},{2,6},{4,0},{6,2},{8,12},{10,14},{12,8},{14,10},{1,5},{3,7},... | collective-permute-start | bytes 172040 | tf_op jit(solution)/shard_map/ppermute | solution.py:289
  11.6 5.1 %collective-permute-start.3 = (bf16[2,112,128]{2,1,0:T(8,128)(2,1)S(1)}, bf16[2,112,128]{2,1,0:T(8,128)(2,1)S(1)}, u32[]{:S(2)}, u32[]{:S(2)}) collective-permute-start(bf16[2,112,128]{2,1,0:T(8,128)(2,1)S(1)} %pad_maximum_fusion), channel_id=1, source_target_pairs={{0,6},{2,4},{4,2},{6,0},{8,14},{10,12},{12,10},{14,8},{1,7},{3,5},... | collective-permute-start | bytes 172040 | tf_op jit(solution)/shard_map/ppermute | solution.py:289
  12.6 5.7 %copy-start.1 = (bf16[4,128,128]{2,1,0:T(8,128)(2,1)S(1)}, bf16[4,128,128]{2,1,0:T(8,128)(2,1)}, u32[]{:S(2)}) copy-start(bf16[4,128,128]{2,1,0:T(8,128)(2,1)} %triangle_ref.1) | copy-start | bytes 393220
  14.4 3.9 %copy-start.4 = (bf16[128,128]{1,0:T(8,128)(2,1)S(1)}, bf16[128,128]{1,0:T(8,128)(2,1)}, u32[]{:S(2)}) copy-start(bf16[128,128]{1,0:T(8,128)(2,1)} %gate_ref.1) | copy-start | bytes 98308
  14.4 3.9 %copy-start.7 = (f32[32,128]{1,0:T(8,128)S(1)}, f32[32,128]{1,0:T(8,128)}, u32[]{:S(2)}) copy-start(f32[32,128]{1,0:T(8,128)} %get-tuple-element.7.mask_ref) | copy-start | bytes 49156
  16.7 1.6 %collective-permute-start.4 = (bf16[8,112,128]{2,1,0:T(8,128)(2,1)S(1)}, bf16[8,112,128]{2,1,0:T(8,128)(2,1)S(1)}, u32[]{:S(2)}, u32[]{:S(2)}) collective-permute-start(bf16[8,112,128]{2,1,0:T(8,128)(2,1)S(1)} %constant_dynamic-update-slice_fusion.held_ref), channel_id=1, source_target_pairs={{0,1},{1,0},{2,3},{3,2},{4,5},{5,4},{6,7},{7,6},{8,9},{9,8},{10,11... | collective-permute-start | bytes 688136 | tf_op jit(solution)/shard_map/ppermute | solution.py:293
  18.3 0.8 %copy-start.5 = (bf16[128,128]{1,0:T(8,128)(2,1)S(1)}, bf16[128,128]{1,0:T(8,128)(2,1)}, u32[]{:S(2)}) copy-start(bf16[128,128]{1,0:T(8,128)(2,1)} %output_ref.1) | copy-start | bytes 98308

commit v11 on v10

--- a/solution.py
+++ b/solution.py
@@ -42,13 +42,13 @@
     state_hbm,
     weight_hbm,
     pair_hbm,
-    out_ref,
-    column_ref,
+    out_hbm,
     mask_ref,
     keep_ref,
     state_ref,
     weight_ref,
     wide_ref,
+    out_ref,
     sems,
 ):
     rows, residues, wide = pair_hbm.shape
@@ -63,7 +63,7 @@
         pltpu.make_async_copy(mask_hbm, mask_ref, sems.at[3]),
     ] + [
         pltpu.make_async_copy(
-            pair_hbm.at[row], out_ref.at[pl.ds(row * residues, residues)], sems.at[4 + row]
+            pair_hbm.at[row], out_hbm.at[pl.ds(row * residues, residues)], sems.at[5 + row]
         )
         for row in range(rows)
     ]
@@ -76,7 +76,7 @@
         jnp.int32, (sequences, sequences), 1
     )
     lefts, rights, keeps = [], [], []
-    for load in loads[1:]:
+    for load in loads[1:4]:
         load.wait()
     for row in range(rows):
         present = mask_ref[start + row].astype(jnp.float32)
@@ -90,23 +90,26 @@
         right = lax.dot_general(normed, weight_ref[1], last, preferred_element_type=jnp.float32)
         lefts.append(left * keep_row)
         rights.append(right * keep_column)
-        keeps.append(keep_row)
+        keeps.append(
+            jnp.concatenate(
+                [keep_row, jnp.full((1, wide - sequences), present, jnp.float32)], axis=1
+            )
+        )
     left = jnp.concatenate(lefts, axis=1)
     right = jnp.concatenate(rights, axis=1)
     first = jnp.concatenate([right, left], axis=1)
     other = jnp.concatenate([left, right], axis=1)
-    out_ref[base : base + sequences] = jnp.where(second_core, other, first).astype(jnp.bfloat16)
-    keep = jnp.concatenate(
-        keeps + [jnp.zeros((16 - rows, sequences), jnp.float32)], axis=0
-    )
-    place = lax.broadcasted_iota(jnp.int32, (residues, 1), 0)
-    column = jnp.zeros((residues, 1), jnp.float32)
-    for k in range(residues):
-        column = jnp.where(place == k, mask_ref[k].astype(jnp.float32), column)
-    column_ref[...] = jnp.broadcast_to(column, (residues, wide))
-    out_ref[base + sequences :] = jnp.concatenate(
-        [keep, jnp.zeros((16, wide - sequences), jnp.float32)], axis=1
-    ).astype(jnp.bfloat16)
+    out_ref[:sequences] = jnp.where(second_core, other, first).astype(jnp.bfloat16)
+    out_ref[sequences:] = jnp.concatenate(
+        keeps + [jnp.zeros((16 - rows, wide), jnp.float32)], axis=0
+    ).astype(jnp.bfloat16)
+    store = pltpu.make_async_copy(
+        out_ref, out_hbm.at[pl.ds(base, sequences + 16)], sems.at[4]
+    )
+    store.start()
+    store.wait()
+    for load in loads[4:]:
+        load.wait()
 
 
 def sigmoid(values):
@@ -114,7 +117,6 @@
 
 
 def update_kernel(
-    mask_ref,
     held_ref,
     other_ref,
     outer_ref,
@@ -185,8 +187,15 @@
             )
 
     last = (((1,), (1,)), ((), ()))
-    keep = keep_ref[...].astype(bf16)
-    count = lax.dot_general(keep, keep, last, preferred_element_type=f32)
+    keep = keep_ref[...]
+    mask = jnp.broadcast_to(keep[:, sequences : sequences + 1], (residues, wide))
+    counted = lax.broadcasted_iota(jnp.int32, (residues, wide), 1) < sequences
+    count = lax.dot_general(
+        jnp.where(counted, keep, 0.0).astype(bf16),
+        keep.astype(bf16),
+        last,
+        preferred_element_type=f32,
+    )
     inverse = 1.0 / jnp.maximum(count, 1.0)
 
     low = lax.broadcasted_iota(jnp.int32, (residues, wide), 1) < half
@@ -242,7 +251,6 @@
         )
         right_tri.append((sigmoid(both[:, :wide]) * both[:, wide:]).astype(bf16).astype(f32))
 
-    mask = mask_ref[...]
     own_pair = jnp.concatenate([pair_one_ref[:, start + row] for row in range(rows)], axis=0)
     own_ln = jnp.concatenate([ln_one_ref[:, start + row] for row in range(rows)], axis=0).astype(bf16)
     left_weight = jnp.concatenate([triangle_ref[0], triangle_ref[1]], axis=1)
@@ -257,7 +265,8 @@
             place = (k % stride) * residues
             sums[k % 4] += left_tri[at : at + 1] * right_tri[k // stride][place : place + residues]
         total = (sums[0] + sums[1]) + (sums[2] + sums[3])
-        products.append(total * (mask * mask_ref[pl.ds(start + row, 1), :]))
+        own_mask = keep_ref[pl.ds(start + row, 1), :][:, sequences : sequences + 1]
+        products.append(total * (mask * own_mask))
     product = jnp.concatenate(products, axis=0).astype(bf16).astype(f32)
     normed = layer_norm(product).astype(bf16)
     update = jnp.dot(normed, output_ref[...], preferred_element_type=f32)
@@ -318,21 +327,19 @@
     vector = pl.BlockSpec(memory_space=pltpu.VMEM)
     params = pltpu.CompilerParams(vmem_limit_bytes=40 << 20)
     hbm = pl.BlockSpec(memory_space=pltpu.HBM)
-    packed, mask = pl.pallas_call(
+    packed = pl.pallas_call(
         pack_kernel,
-        out_shape=(
-            jax.ShapeDtypeStruct((rows * residues + sequences + 16, wide), jnp.bfloat16),
-            jax.ShapeDtypeStruct((residues, wide), jnp.float32),
-        ),
+        out_shape=jax.ShapeDtypeStruct((rows * residues + sequences + 16, wide), jnp.bfloat16),
         in_specs=[hbm] * 5,
-        out_specs=(vector, vector),
+        out_specs=hbm,
         scratch_shapes=[
             pltpu.SMEM((residues,), jnp.int32),
             pltpu.VMEM((rows, sequences), jnp.int32),
             pltpu.VMEM(alignment_state.shape, jnp.bfloat16),
             pltpu.VMEM((2, channels, alignment_state.shape[2]), jnp.bfloat16),
             pltpu.VMEM(alignment_state.shape, jnp.float32),
-            pltpu.SemaphoreType.DMA((4 + rows,)),
+            pltpu.VMEM((sequences + 16, wide), jnp.bfloat16),
+            pltpu.SemaphoreType.DMA((5 + rows,)),
         ],
         compiler_params=pltpu.CompilerParams(vmem_limit_bytes=63 << 20),
     )(
@@ -349,7 +356,7 @@
     return pl.pallas_call(
         update_kernel,
         out_shape=jax.ShapeDtypeStruct(pairwise_state.shape, jnp.bfloat16),
-        in_specs=[vector] * 9,
+        in_specs=[vector] * 8,
         out_specs=vector,
         scratch_shapes=[
             pltpu.VMEM((parts, (channels // parts + 1) * 2 * channels, 2 * wide), jnp.bfloat16),
@@ -364,7 +371,6 @@
         ],
         compiler_params=params,
     )(
-        mask,
         held,
         other,
         outer_output_weight,

time: 23.2 us -> 22.4 us (0.966)
  local copies, waits for them, and re-layouts: 1.61 us -> 0.86 us
    unnamed x20 -> x18, local copies, waits for them, and re-layouts: 1.6 us -> 0.84 us
where the time goes in v11:
time: 22.4 us; the launch traced here: 22.2 us
  starting transfers between devices  7.77 us (35%)
  waiting for transfers between devices  7.6 us (34%)
  Pallas kernels  5.87 us (26%)
  local copies, waits for them, and re-layouts  0.86 us (4%)
    ppermute x3, waiting for transfers between devices, gather_all(): lax.ppermute(both, 'dap', [(src, src ^ offset) for src in range(dap_count)])  4.87 us
    ppermute x1, starting transfers between devices, gather_all(): lax.ppermute(packed[None], 'dap', [(src, src ^ half) for src in range(dap...  4.1 us
    pallas_call x1, Pallas kernels, shards_replicated(): pl.pallas_call(update_kernel, out_shape=jax.ShapeDtypeStruct(pairwise_sta...  3.91 us
    ppermute x3, starting transfers between devices, gather_all(): lax.ppermute(both, 'dap', [(src, src ^ offset) for src in range(dap_count)])  3.6 us
    pallas_call x1, Pallas kernels, shards_replicated(): pl.pallas_call(pack_kernel, out_shape=jax.ShapeDtypeStruct((rows * residu...  1.95 us
    ppermute x1, waiting for transfers between devices, gather_all(): return (held, lax.ppermute(held, 'sub', [(0, 1), (1, 0)]))  1.48 us
    ppermute x1, waiting for transfers between devices, gather_all(): lax.ppermute(packed[None], 'dap', [(src, src ^ half) for src in range(dap...  1.26 us
    unnamed x18, local copies, waits for them, and re-layouts  0.84 us
  transfers between devices with their start and end apart: 5, of which 5 were waited for; matrix products, arithmetic and copies ran while one was open for 0% of the time, Pallas kernels for 0%

profile of v11, /device:TPU:0, one launch (start us, length us, event | category | flops | bytes accessed | tf_op | source)
XLA Modules:
  0.0 22.2 jit_solution(10761476363930189284)
XLA Ops:
  0.0 0.0 copy-start.3
  0.0 2.0 %shard_map.109.packed_ref = bf16[112,128]{1,0:T(8,128)(2,1)} custom-call(s32[32]{0:T(128)} %mask_hbm.1, s32[2,32]{1,0:T(2,128)} %bitcast.5, bf16[32,2,256]{2,1,0:T(2,128)(2,1)} %state_hbm.1, bf16[2,32,256]{2,1,0:T(8,128)(2,1)} %bitcast.4, bf16[2,32,128]{2,1,0:T(8,128)(2,1)} %pair_hbm.1), custom_call_target="tpu_custom_call" | custom-call | tf_op jit(solution)/shard_map/pallas_call | solution.py:330
  2.0 4.1 %collective-permute-start = (bf16[1,112,128]{2,1,0:T(8,128)(2,1)}, bf16[1,112,128]{2,1,0:T(8,128)(2,1)S(1)}, u32[]{:S(2)}, u32[]{:S(2)}) collective-permute-start(bf16[1,112,128]{2,1,0:T(8,128)(2,1)} %bitcast.3), channel_id=1, source_target_pairs={{0,8},{2,10},{4,12},{6,14},{8,0},{10,2},{12,4},{14,6},{1,9},{3,11}... | collective-permute-start | bytes 86024 | tf_op jit(solution)/shard_map/ppermute | solution.py:288
  6.1 0.0 copy-start.4
  6.1 0.8 %copy-done.4 = bf16[112,128]{1,0:T(8,128)(2,1)S(1)} copy-done((bf16[112,128]{1,0:T(8,128)(2,1)S(1)}, bf16[112,128]{1,0:T(8,128)(2,1)}, u32[]{:S(2)}) %copy-start.4) | copy-done | bytes 28696
  6.9 0.0 copy-start
  6.9 1.3 %collective-permute-done = bf16[1,112,128]{2,1,0:T(8,128)(2,1)S(1)} collective-permute-done((bf16[1,112,128]{2,1,0:T(8,128)(2,1)}, bf16[1,112,128]{2,1,0:T(8,128)(2,1)S(1)}, u32[]{:S(2)}, u32[]{:S(2)}) %collective-permute-start) | collective-permute-done | bytes 28704 | tf_op jit(solution)/shard_map/ppermute | solution.py:288
  8.1 2.1 %collective-permute-start.1 = (bf16[2,112,128]{2,1,0:T(8,128)(2,1)S(1)}, bf16[2,112,128]{2,1,0:T(8,128)(2,1)S(1)}, u32[]{:S(2)}, u32[]{:S(2)}) collective-permute-start(bf16[2,112,128]{2,1,0:T(8,128)(2,1)S(1)} %pad_maximum_fusion), channel_id=1, source_target_pairs={{0,2},{2,0},{4,6},{6,4},{8,10},{10,8},{12,14},{14,12},{1,3},{3,1},... | collective-permute-start | bytes 172040 | tf_op jit(solution)/shard_map/ppermute | solution.py:298
  10.2 1.4 %collective-permute-start.2 = (bf16[2,112,128]{2,1,0:T(8,128)(2,1)S(1)}, bf16[2,112,128]{2,1,0:T(8,128)(2,1)S(1)}, u32[]{:S(2)}, u32[]{:S(2)}) collective-permute-start(bf16[2,112,128]{2,1,0:T(8,128)(2,1)S(1)} %pad_maximum_fusion), channel_id=1, source_target_pairs={{0,4},{2,6},{4,0},{6,2},{8,12},{10,14},{12,8},{14,10},{1,5},{3,7},... | collective-permute-start | bytes 172040 | tf_op jit(solution)/shard_map/ppermute | solution.py:298
  11.6 0.1 collective-permute-start.3
  11.8 0.8 %collective-permute-done.1 = bf16[2,112,128]{2,1,0:T(8,128)(2,1)S(1)} collective-permute-done((bf16[2,112,128]{2,1,0:T(8,128)(2,1)S(1)}, bf16[2,112,128]{2,1,0:T(8,128)(2,1)S(1)}, u32[]{:S(2)}, u32[]{:S(2)}) %collective-permute-start.1) | collective-permute-done | bytes 57376 | tf_op jit(solution)/shard_map/ppermute | solution.py:298
  12.6 0.0 copy-start.1
  12.6 1.8 %collective-permute-done.2 = bf16[2,112,128]{2,1,0:T(8,128)(2,1)S(1)} collective-permute-done((bf16[2,112,128]{2,1,0:T(8,128)(2,1)S(1)}, bf16[2,112,128]{2,1,0:T(8,128)(2,1)S(1)}, u32[]{:S(2)}, u32[]{:S(2)}) %collective-permute-start.2) | collective-permute-done | bytes 57376 | tf_op jit(solution)/shard_map/ppermute | solution.py:298
  14.4 0.0 copy-start.5
  14.4 2.3 %collective-permute-done.3 = bf16[2,112,128]{2,1,0:T(8,128)(2,1)S(1)} collective-permute-done((bf16[2,112,128]{2,1,0:T(8,128)(2,1)S(1)}, bf16[2,112,128]{2,1,0:T(8,128)(2,1)S(1)}, u32[]{:S(2)}, u32[]{:S(2)}) %collective-permute-start.3) | collective-permute-done | bytes 57376 | tf_op jit(solution)/shard_map/ppermute | solution.py:298
  16.7 0.1 collective-permute-start.4
  16.8 1.5 %collective-permute-done.4.other_ref = bf16[8,112,128]{2,1,0:T(8,128)(2,1)S(1)} collective-permute-done((bf16[8,112,128]{2,1,0:T(8,128)(2,1)S(1)}, bf16[8,112,128]{2,1,0:T(8,128)(2,1)S(1)}, u32[]{:S(2)}, u32[]{:S(2)}) %collective-permute-start.4) | collective-permute-done | bytes 229408 | tf_op jit(solution)/shard_map/ppermute | solution.py:302
  18.2 0.0 copy-done.3
  18.2 0.0 copy-done.6
  18.2 0.0 copy-done.2
  18.2 0.0 copy-done
  18.3 0.0 copy-done.1
  18.3 0.0 copy-done.5
  18.3 3.9 %shard_map.111 = bf16[2,32,128]{2,1,0:T(8,128)(2,1)} custom-call(bf16[8,112,128]{2,1,0:T(8,128)(2,1)S(1)} %constant_dynamic-update-slice_fusion.held_ref, bf16[8,112,128]{2,1,0:T(8,128)(2,1)S(1)} %collective-permute-done.4.other_ref, bf16[32,32,128]{2,1,0:T(8,128)(2,1)S(1)} %copy-done, bf16[4,128,128]{2,1,0:T(8,128)(2,1)S(1)} %copy-done.1, ...), custom_call_target="tpu_custom_call" | custom-call | tf_op jit(solution)/shard_map/pallas_call | solution.py:356
  (9 shorter events, 0.1 us)
Async XLA Ops:
  0.0 18.2 %copy-start.3 = (bf16[512,128]{1,0:T(8,128)(2,1)S(1)}, bf16[512,128]{1,0:T(8,128)(2,1)}, u32[]{:S(2)}) copy-start(bf16[512,128]{1,0:T(8,128)(2,1)} %down_ref.1) | copy-start | bytes 393220
  2.0 6.2 %collective-permute-start = (bf16[1,112,128]{2,1,0:T(8,128)(2,1)}, bf16[1,112,128]{2,1,0:T(8,128)(2,1)S(1)}, u32[]{:S(2)}, u32[]{:S(2)}) collective-permute-start(bf16[1,112,128]{2,1,0:T(8,128)(2,1)} %bitcast.3), channel_id=1, source_target_pairs={{0,8},{2,10},{4,12},{6,14},{8,0},{10,2},{12,4},{14,6},{1,9},{3,11}... | collective-permute-start | bytes 86024 | tf_op jit(solution)/shard_map/ppermute | solution.py:288
  6.1 0.8 %copy-start.4 = (bf16[112,128]{1,0:T(8,128)(2,1)S(1)}, bf16[112,128]{1,0:T(8,128)(2,1)}, u32[]{:S(2)}) copy-start(bf16[112,128]{1,0:T(8,128)(2,1)} %shard_map.109.packed_ref) | copy-start | bytes 86020
  6.8 11.4 %copy-start.6 = (bf16[128,128]{1,0:T(8,128)(2,1)S(1)}, bf16[128,128]{1,0:T(8,128)(2,1)}, u32[]{:S(2)}) copy-start(bf16[128,128]{1,0:T(8,128)(2,1)} %output_ref.1) | copy-start | bytes 98308
  6.9 11.4 %copy-start.2 = (bf16[128,512]{1,0:T(8,128)(2,1)S(1)}, bf16[128,512]{1,0:T(8,128)(2,1)}, u32[]{:S(2)}) copy-start(bf16[128,512]{1,0:T(8,128)(2,1)} %up_ref.1) | copy-start | bytes 393220
  6.9 11.4 %copy-start = (bf16[32,32,128]{2,1,0:T(8,128)(2,1)S(1)}, bf16[32,32,128]{2,1,0:T(8,128)(2,1)}, u32[]{:S(2)}) copy-start(bf16[32,32,128]{2,1,0:T(8,128)(2,1)} %outer_ref.1) | copy-start | bytes 786436
  8.1 4.4 %collective-permute-start.1 = (bf16[2,112,128]{2,1,0:T(8,128)(2,1)S(1)}, bf16[2,112,128]{2,1,0:T(8,128)(2,1)S(1)}, u32[]{:S(2)}, u32[]{:S(2)}) collective-permute-start(bf16[2,112,128]{2,1,0:T(8,128)(2,1)S(1)} %pad_maximum_fusion), channel_id=1, source_target_pairs={{0,2},{2,0},{4,6},{6,4},{8,10},{10,8},{12,14},{14,12},{1,3},{3,1},... | collective-permute-start | bytes 172040 | tf_op jit(solution)/shard_map/ppermute | solution.py:298
  10.2 4.2 %collective-permute-start.2 = (bf16[2,112,128]{2,1,0:T(8,128)(2,1)S(1)}, bf16[2,112,128]{2,1,0:T(8,128)(2,1)S(1)}, u32[]{:S(2)}, u32[]{:S(2)}) collective-permute-start(bf16[2,112,128]{2,1,0:T(8,128)(2,1)S(1)} %pad_maximum_fusion), channel_id=1, source_target_pairs={{0,4},{2,6},{4,0},{6,2},{8,12},{10,14},{12,8},{14,10},{1,5},{3,7},... | collective-permute-start | bytes 172040 | tf_op jit(solution)/shard_map/ppermute | solution.py:298
  11.6 5.1 %collective-permute-start.3 = (bf16[2,112,128]{2,1,0:T(8,128)(2,1)S(1)}, bf16[2,112,128]{2,1,0:T(8,128)(2,1)S(1)}, u32[]{:S(2)}, u32[]{:S(2)}) collective-permute-start(bf16[2,112,128]{2,1,0:T(8,128)(2,1)S(1)} %pad_maximum_fusion), channel_id=1, source_target_pairs={{0,6},{2,4},{4,2},{6,0},{8,14},{10,12},{12,10},{14,8},{1,7},{3,5},... | collective-permute-start | bytes 172040 | tf_op jit(solution)/shard_map/ppermute | solution.py:298
  12.6 5.7 %copy-start.1 = (bf16[4,128,128]{2,1,0:T(8,128)(2,1)S(1)}, bf16[4,128,128]{2,1,0:T(8,128)(2,1)}, u32[]{:S(2)}) copy-start(bf16[4,128,128]{2,1,0:T(8,128)(2,1)} %triangle_ref.1) | copy-start | bytes 393220
  14.4 3.9 %copy-start.5 = (bf16[128,128]{1,0:T(8,128)(2,1)S(1)}, bf16[128,128]{1,0:T(8,128)(2,1)}, u32[]{:S(2)}) copy-start(bf16[128,128]{1,0:T(8,128)(2,1)} %gate_ref.1) | copy-start | bytes 98308
  16.7 1.6 %collective-permute-start.4 = (bf16[8,112,128]{2,1,0:T(8,128)(2,1)S(1)}, bf16[8,112,128]{2,1,0:T(8,128)(2,1)S(1)}, u32[]{:S(2)}, u32[]{:S(2)}) collective-permute-start(bf16[8,112,128]{2,1,0:T(8,128)(2,1)S(1)} %constant_dynamic-update-slice_fusion.held_ref), channel_id=1, source_target_pairs={{0,1},{1,0},{2,3},{3,2},{4,5},{5,4},{6,7},{7,6},{8,9},{9,8},{10,11... | collective-permute-start | bytes 688136 | tf_op jit(solution)/shard_map/ppermute | solution.py:302

commit v12 on v11

--- a/solution.py
+++ b/solution.py
@@ -294,10 +294,11 @@
         compiler_params=pltpu.CompilerParams(vmem_limit_bytes=4 << 20),
     )(packed)
     both = jnp.concatenate([own, far], axis=0)
-    held = [both] + [
-        lax.ppermute(both, "dap", [(src, src ^ offset) for src in range(dap_count)])
-        for offset in range(1, half)
-    ]
+    swaps = {
+        offset: lax.ppermute(both, "dap", [(src, src ^ offset) for src in range(dap_count)])
+        for offset in range(half - 1, 0, -1)
+    }
+    held = [both] + [swaps[offset] for offset in range(1, half)]
     held = jnp.concatenate(held, axis=0)
     return held, lax.ppermute(held, "sub", [(0, 1), (1, 0)])
 

time: 22.4 us -> 22.4 us (level)
  no operation moved by 1% of the time
where the time goes in v12:
time: 22.4 us; the launch traced here: 22.2 us
  starting transfers between devices  7.77 us (35%)
  waiting for transfers between devices  7.6 us (34%)
  Pallas kernels  5.87 us (26%)
  local copies, waits for them, and re-layouts  0.86 us (4%)
    ppermute x3, waiting for transfers between devices, gather_all(): lax.ppermute(both, 'dap', [(src, src ^ offset) for src in range(dap_count)])  4.87 us
    ppermute x1, starting transfers between devices, gather_all(): lax.ppermute(packed[None], 'dap', [(src, src ^ half) for src in range(dap...  4.1 us
    pallas_call x1, Pallas kernels, shards_replicated(): pl.pallas_call(update_kernel, out_shape=jax.ShapeDtypeStruct(pairwise_sta...  3.91 us
    ppermute x3, starting transfers between devices, gather_all(): lax.ppermute(both, 'dap', [(src, src ^ offset) for src in range(dap_count)])  3.6 us
    pallas_call x1, Pallas kernels, shards_replicated(): pl.pallas_call(pack_kernel, out_shape=jax.ShapeDtypeStruct((rows * residu...  1.95 us
    ppermute x1, waiting for transfers between devices, gather_all(): return (held, lax.ppermute(held, 'sub', [(0, 1), (1, 0)]))  1.48 us
    ppermute x1, waiting for transfers between devices, gather_all(): lax.ppermute(packed[None], 'dap', [(src, src ^ half) for src in range(dap...  1.26 us
    unnamed x18, local copies, waits for them, and re-layouts  0.84 us
  transfers between devices with their start and end apart: 5, of which 5 were waited for; matrix products, arithmetic and copies ran while one was open for 0% of the time, Pallas kernels for 0%

profile of v12, /device:TPU:0, one launch (start us, length us, event | category | flops | bytes accessed | tf_op | source)
XLA Modules:
  0.0 22.2 jit_solution(10761476363930189284)
XLA Ops:
  0.0 0.0 copy-start.3
  0.0 2.0 %shard_map.109.packed_ref = bf16[112,128]{1,0:T(8,128)(2,1)} custom-call(s32[32]{0:T(128)} %mask_hbm.1, s32[2,32]{1,0:T(2,128)} %bitcast.5, bf16[32,2,256]{2,1,0:T(2,128)(2,1)} %state_hbm.1, bf16[2,32,256]{2,1,0:T(8,128)(2,1)} %bitcast.4, bf16[2,32,128]{2,1,0:T(8,128)(2,1)} %pair_hbm.1), custom_call_target="tpu_custom_call" | custom-call | tf_op jit(solution)/shard_map/pallas_call | solution.py:331
  2.0 4.1 %collective-permute-start = (bf16[1,112,128]{2,1,0:T(8,128)(2,1)}, bf16[1,112,128]{2,1,0:T(8,128)(2,1)S(1)}, u32[]{:S(2)}, u32[]{:S(2)}) collective-permute-start(bf16[1,112,128]{2,1,0:T(8,128)(2,1)} %bitcast.3), channel_id=1, source_target_pairs={{0,8},{2,10},{4,12},{6,14},{8,0},{10,2},{12,4},{14,6},{1,9},{3,11}... | collective-permute-start | bytes 86024 | tf_op jit(solution)/shard_map/ppermute | solution.py:288
  6.1 0.0 copy-start.4
  6.1 0.8 %copy-done.4 = bf16[112,128]{1,0:T(8,128)(2,1)S(1)} copy-done((bf16[112,128]{1,0:T(8,128)(2,1)S(1)}, bf16[112,128]{1,0:T(8,128)(2,1)}, u32[]{:S(2)}) %copy-start.4) | copy-done | bytes 28696
  6.9 0.0 copy-start
  6.9 1.3 %collective-permute-done = bf16[1,112,128]{2,1,0:T(8,128)(2,1)S(1)} collective-permute-done((bf16[1,112,128]{2,1,0:T(8,128)(2,1)}, bf16[1,112,128]{2,1,0:T(8,128)(2,1)S(1)}, u32[]{:S(2)}, u32[]{:S(2)}) %collective-permute-start) | collective-permute-done | bytes 28704 | tf_op jit(solution)/shard_map/ppermute | solution.py:288
  8.1 2.1 %collective-permute-start.1 = (bf16[2,112,128]{2,1,0:T(8,128)(2,1)S(1)}, bf16[2,112,128]{2,1,0:T(8,128)(2,1)S(1)}, u32[]{:S(2)}, u32[]{:S(2)}) collective-permute-start(bf16[2,112,128]{2,1,0:T(8,128)(2,1)S(1)} %pad_maximum_fusion), channel_id=1, source_target_pairs={{0,2},{2,0},{4,6},{6,4},{8,10},{10,8},{12,14},{14,12},{1,3},{3,1},... | collective-permute-start | bytes 172040 | tf_op jit(solution)/shard_map/ppermute | solution.py:298
  10.2 1.4 %collective-permute-start.2 = (bf16[2,112,128]{2,1,0:T(8,128)(2,1)S(1)}, bf16[2,112,128]{2,1,0:T(8,128)(2,1)S(1)}, u32[]{:S(2)}, u32[]{:S(2)}) collective-permute-start(bf16[2,112,128]{2,1,0:T(8,128)(2,1)S(1)} %pad_maximum_fusion), channel_id=1, source_target_pairs={{0,4},{2,6},{4,0},{6,2},{8,12},{10,14},{12,8},{14,10},{1,5},{3,7},... | collective-permute-start | bytes 172040 | tf_op jit(solution)/shard_map/ppermute | solution.py:298
  11.6 0.1 collective-permute-start.3
  11.8 0.8 %collective-permute-done.1 = bf16[2,112,128]{2,1,0:T(8,128)(2,1)S(1)} collective-permute-done((bf16[2,112,128]{2,1,0:T(8,128)(2,1)S(1)}, bf16[2,112,128]{2,1,0:T(8,128)(2,1)S(1)}, u32[]{:S(2)}, u32[]{:S(2)}) %collective-permute-start.1) | collective-permute-done | bytes 57376 | tf_op jit(solution)/shard_map/ppermute | solution.py:298
  12.6 0.0 copy-start.1
  12.6 1.8 %collective-permute-done.2 = bf16[2,112,128]{2,1,0:T(8,128)(2,1)S(1)} collective-permute-done((bf16[2,112,128]{2,1,0:T(8,128)(2,1)S(1)}, bf16[2,112,128]{2,1,0:T(8,128)(2,1)S(1)}, u32[]{:S(2)}, u32[]{:S(2)}) %collective-permute-start.2) | collective-permute-done | bytes 57376 | tf_op jit(solution)/shard_map/ppermute | solution.py:298
  14.4 0.0 copy-start.5
  14.4 2.3 %collective-permute-done.3 = bf16[2,112,128]{2,1,0:T(8,128)(2,1)S(1)} collective-permute-done((bf16[2,112,128]{2,1,0:T(8,128)(2,1)S(1)}, bf16[2,112,128]{2,1,0:T(8,128)(2,1)S(1)}, u32[]{:S(2)}, u32[]{:S(2)}) %collective-permute-start.3) | collective-permute-done | bytes 57376 | tf_op jit(solution)/shard_map/ppermute | solution.py:298
  16.7 0.1 collective-permute-start.4
  16.8 1.5 %collective-permute-done.4.other_ref = bf16[8,112,128]{2,1,0:T(8,128)(2,1)S(1)} collective-permute-done((bf16[8,112,128]{2,1,0:T(8,128)(2,1)S(1)}, bf16[8,112,128]{2,1,0:T(8,128)(2,1)S(1)}, u32[]{:S(2)}, u32[]{:S(2)}) %collective-permute-start.4) | collective-permute-done | bytes 229408 | tf_op jit(solution)/shard_map/ppermute | solution.py:303
  18.2 0.0 copy-done.3
  18.2 0.0 copy-done.6
  18.2 0.0 copy-done.2
  18.2 0.0 copy-done
  18.3 0.0 copy-done.1
  18.3 0.0 copy-done.5
  18.3 3.9 %shard_map.111 = bf16[2,32,128]{2,1,0:T(8,128)(2,1)} custom-call(bf16[8,112,128]{2,1,0:T(8,128)(2,1)S(1)} %constant_dynamic-update-slice_fusion.held_ref, bf16[8,112,128]{2,1,0:T(8,128)(2,1)S(1)} %collective-permute-done.4.other_ref, bf16[32,32,128]{2,1,0:T(8,128)(2,1)S(1)} %copy-done, bf16[4,128,128]{2,1,0:T(8,128)(2,1)S(1)} %copy-done.1, ...), custom_call_target="tpu_custom_call" | custom-call | tf_op jit(solution)/shard_map/pallas_call | solution.py:357
  (9 shorter events, 0.1 us)
Async XLA Ops:
  0.0 18.2 %copy-start.3 = (bf16[512,128]{1,0:T(8,128)(2,1)S(1)}, bf16[512,128]{1,0:T(8,128)(2,1)}, u32[]{:S(2)}) copy-start(bf16[512,128]{1,0:T(8,128)(2,1)} %down_ref.1) | copy-start | bytes 393220
  2.0 6.2 %collective-permute-start = (bf16[1,112,128]{2,1,0:T(8,128)(2,1)}, bf16[1,112,128]{2,1,0:T(8,128)(2,1)S(1)}, u32[]{:S(2)}, u32[]{:S(2)}) collective-permute-start(bf16[1,112,128]{2,1,0:T(8,128)(2,1)} %bitcast.3), channel_id=1, source_target_pairs={{0,8},{2,10},{4,12},{6,14},{8,0},{10,2},{12,4},{14,6},{1,9},{3,11}... | collective-permute-start | bytes 86024 | tf_op jit(solution)/shard_map/ppermute | solution.py:288
  6.1 0.8 %copy-start.4 = (bf16[112,128]{1,0:T(8,128)(2,1)S(1)}, bf16[112,128]{1,0:T(8,128)(2,1)}, u32[]{:S(2)}) copy-start(bf16[112,128]{1,0:T(8,128)(2,1)} %shard_map.109.packed_ref) | copy-start | bytes 86020
  6.8 11.4 %copy-start.6 = (bf16[128,128]{1,0:T(8,128)(2,1)S(1)}, bf16[128,128]{1,0:T(8,128)(2,1)}, u32[]{:S(2)}) copy-start(bf16[128,128]{1,0:T(8,128)(2,1)} %output_ref.1) | copy-start | bytes 98308
  6.9 11.4 %copy-start.2 = (bf16[128,512]{1,0:T(8,128)(2,1)S(1)}, bf16[128,512]{1,0:T(8,128)(2,1)}, u32[]{:S(2)}) copy-start(bf16[128,512]{1,0:T(8,128)(2,1)} %up_ref.1) | copy-start | bytes 393220
  6.9 11.4 %copy-start = (bf16[32,32,128]{2,1,0:T(8,128)(2,1)S(1)}, bf16[32,32,128]{2,1,0:T(8,128)(2,1)}, u32[]{:S(2)}) copy-start(bf16[32,32,128]{2,1,0:T(8,128)(2,1)} %outer_ref.1) | copy-start | bytes 786436
  8.1 4.4 %collective-permute-start.1 = (bf16[2,112,128]{2,1,0:T(8,128)(2,1)S(1)}, bf16[2,112,128]{2,1,0:T(8,128)(2,1)S(1)}, u32[]{:S(2)}, u32[]{:S(2)}) collective-permute-start(bf16[2,112,128]{2,1,0:T(8,128)(2,1)S(1)} %pad_maximum_fusion), channel_id=1, source_target_pairs={{0,2},{2,0},{4,6},{6,4},{8,10},{10,8},{12,14},{14,12},{1,3},{3,1},... | collective-permute-start | bytes 172040 | tf_op jit(solution)/shard_map/ppermute | solution.py:298
  10.2 4.2 %collective-permute-start.2 = (bf16[2,112,128]{2,1,0:T(8,128)(2,1)S(1)}, bf16[2,112,128]{2,1,0:T(8,128)(2,1)S(1)}, u32[]{:S(2)}, u32[]{:S(2)}) collective-permute-start(bf16[2,112,128]{2,1,0:T(8,128)(2,1)S(1)} %pad_maximum_fusion), channel_id=1, source_target_pairs={{0,4},{2,6},{4,0},{6,2},{8,12},{10,14},{12,8},{14,10},{1,5},{3,7},... | collective-permute-start | bytes 172040 | tf_op jit(solution)/shard_map/ppermute | solution.py:298
  11.6 5.1 %collective-permute-start.3 = (bf16[2,112,128]{2,1,0:T(8,128)(2,1)S(1)}, bf16[2,112,128]{2,1,0:T(8,128)(2,1)S(1)}, u32[]{:S(2)}, u32[]{:S(2)}) collective-permute-start(bf16[2,112,128]{2,1,0:T(8,128)(2,1)S(1)} %pad_maximum_fusion), channel_id=1, source_target_pairs={{0,6},{2,4},{4,2},{6,0},{8,14},{10,12},{12,10},{14,8},{1,7},{3,5},... | collective-permute-start | bytes 172040 | tf_op jit(solution)/shard_map/ppermute | solution.py:298
  12.6 5.7 %copy-start.1 = (bf16[4,128,128]{2,1,0:T(8,128)(2,1)S(1)}, bf16[4,128,128]{2,1,0:T(8,128)(2,1)}, u32[]{:S(2)}) copy-start(bf16[4,128,128]{2,1,0:T(8,128)(2,1)} %triangle_ref.1) | copy-start | bytes 393220
  14.4 3.9 %copy-start.5 = (bf16[128,128]{1,0:T(8,128)(2,1)S(1)}, bf16[128,128]{1,0:T(8,128)(2,1)}, u32[]{:S(2)}) copy-start(bf16[128,128]{1,0:T(8,128)(2,1)} %gate_ref.1) | copy-start | bytes 98308
  16.7 1.6 %collective-permute-start.4 = (bf16[8,112,128]{2,1,0:T(8,128)(2,1)S(1)}, bf16[8,112,128]{2,1,0:T(8,128)(2,1)S(1)}, u32[]{:S(2)}, u32[]{:S(2)}) collective-permute-start(bf16[8,112,128]{2,1,0:T(8,128)(2,1)S(1)} %constant_dynamic-update-slice_fusion.held_ref), channel_id=1, source_target_pairs={{0,1},{1,0},{2,3},{3,2},{4,5},{5,4},{6,7},{7,6},{8,9},{9,8},{10,11... | collective-permute-start | bytes 688136 | tf_op jit(solution)/shard_map/ppermute | solution.py:303

commit v13 on v11

--- a/solution.py
+++ b/solution.py
@@ -296,16 +296,22 @@
     both = jnp.concatenate([own, far], axis=0)
     held = [both] + [
         lax.ppermute(both, "dap", [(src, src ^ offset) for src in range(dap_count)])
-        for offset in range(1, half)
+        for offset in swap_order(dap_count)
     ]
     held = jnp.concatenate(held, axis=0)
     return held, lax.ppermute(held, "sub", [(0, 1), (1, 0)])
 
 
+def swap_order(dap_count):
+    return list(range(dap_count // 2 - 1, 0, -1))
+
+
 def block_place(chip, chips):
     offset = lax.bitwise_xor(lax.axis_index("dap"), chip)
     half = chips // 2
-    return jnp.where(offset >= half, 2 * (offset - half) + 1, 2 * offset)
+    near = jnp.where(offset >= half, offset - half, offset)
+    turn = jnp.where(near == 0, 0, half - near)
+    return 2 * turn + jnp.where(offset >= half, 1, 0)
 
 
 def shards_replicated(

time: 22.4 us -> 21.5 us (0.960)
  waiting for transfers between devices: 7.6 us -> 6.82 us
    ppermute x3, waiting for transfers between devices: 4.87 us -> 4.09 us  [gather_all(): lax.ppermute(both, 'dap', [(src, src ^ offset) for src in range(dap_count)])]
where the time goes in v13:
time: 21.5 us; the launch traced here: 21.4 us
  starting transfers between devices  7.72 us (36%)
  waiting for transfers between devices  6.82 us (32%)
  Pallas kernels  5.86 us (27%)
  local copies, waits for them, and re-layouts  0.86 us (4%)
    ppermute x1, starting transfers between devices, gather_all(): lax.ppermute(packed[None], 'dap', [(src, src ^ half) for src in range(dap...  4.1 us
    ppermute x3, waiting for transfers between devices, gather_all(): lax.ppermute(both, 'dap', [(src, src ^ offset) for src in range(dap_count)])  4.09 us
    pallas_call x1, Pallas kernels, shards_replicated(): pl.pallas_call(update_kernel, out_shape=jax.ShapeDtypeStruct(pairwise_sta...  3.9 us
    ppermute x3, starting transfers between devices, gather_all(): lax.ppermute(both, 'dap', [(src, src ^ offset) for src in range(dap_count)])  3.55 us
    pallas_call x1, Pallas kernels, shards_replicated(): pl.pallas_call(pack_kernel, out_shape=jax.ShapeDtypeStruct((rows * residu...  1.95 us
    ppermute x1, waiting for transfers between devices, gather_all(): return (held, lax.ppermute(held, 'sub', [(0, 1), (1, 0)]))  1.48 us
    ppermute x1, waiting for transfers between devices, gather_all(): lax.ppermute(packed[None], 'dap', [(src, src ^ half) for src in range(dap...  1.26 us
    unnamed x18, local copies, waits for them, and re-layouts  0.84 us
  transfers between devices with their start and end apart: 5, of which 5 were waited for; matrix products, arithmetic and copies ran while one was open for 0% of the time, Pallas kernels for 0%

profile of v13, /device:TPU:0, one launch (start us, length us, event | category | flops | bytes accessed | tf_op | source)
XLA Modules:
  0.0 21.4 jit_solution(10520695658988736552)
XLA Ops:
  0.0 0.0 copy-start.3
  0.0 2.0 %shard_map.109.packed_ref = bf16[112,128]{1,0:T(8,128)(2,1)} custom-call(s32[32]{0:T(128)} %mask_hbm.1, s32[2,32]{1,0:T(2,128)} %bitcast.5, bf16[32,2,256]{2,1,0:T(2,128)(2,1)} %state_hbm.1, bf16[2,32,256]{2,1,0:T(8,128)(2,1)} %bitcast.4, bf16[2,32,128]{2,1,0:T(8,128)(2,1)} %pair_hbm.1), custom_call_target="tpu_custom_call" | custom-call | tf_op jit(solution)/shard_map/pallas_call | solution.py:336
  2.0 4.1 %collective-permute-start = (bf16[1,112,128]{2,1,0:T(8,128)(2,1)}, bf16[1,112,128]{2,1,0:T(8,128)(2,1)S(1)}, u32[]{:S(2)}, u32[]{:S(2)}) collective-permute-start(bf16[1,112,128]{2,1,0:T(8,128)(2,1)} %bitcast.3), channel_id=1, source_target_pairs={{0,8},{2,10},{4,12},{6,14},{8,0},{10,2},{12,4},{14,6},{1,9},{3,11}... | collective-permute-start | bytes 86024 | tf_op jit(solution)/shard_map/ppermute | solution.py:288
  6.1 0.0 copy-start.4
  6.1 0.8 %copy-done.4 = bf16[112,128]{1,0:T(8,128)(2,1)S(1)} copy-done((bf16[112,128]{1,0:T(8,128)(2,1)S(1)}, bf16[112,128]{1,0:T(8,128)(2,1)}, u32[]{:S(2)}) %copy-start.4) | copy-done | bytes 28696
  6.9 0.0 copy-start
  6.9 1.3 %collective-permute-done = bf16[1,112,128]{2,1,0:T(8,128)(2,1)S(1)} collective-permute-done((bf16[1,112,128]{2,1,0:T(8,128)(2,1)}, bf16[1,112,128]{2,1,0:T(8,128)(2,1)S(1)}, u32[]{:S(2)}, u32[]{:S(2)}) %collective-permute-start) | collective-permute-done | bytes 28704 | tf_op jit(solution)/shard_map/ppermute | solution.py:288
  8.1 2.9 %collective-permute-start.1 = (bf16[2,112,128]{2,1,0:T(8,128)(2,1)S(1)}, bf16[2,112,128]{2,1,0:T(8,128)(2,1)S(1)}, u32[]{:S(2)}, u32[]{:S(2)}) collective-permute-start(bf16[2,112,128]{2,1,0:T(8,128)(2,1)S(1)} %pad_maximum_fusion), channel_id=1, source_target_pairs={{0,6},{2,4},{4,2},{6,0},{8,14},{10,12},{12,10},{14,8},{1,7},{3,5},... | collective-permute-start | bytes 172040 | tf_op jit(solution)/shard_map/ppermute | solution.py:298
  11.0 0.6 %collective-permute-start.2 = (bf16[2,112,128]{2,1,0:T(8,128)(2,1)S(1)}, bf16[2,112,128]{2,1,0:T(8,128)(2,1)S(1)}, u32[]{:S(2)}, u32[]{:S(2)}) collective-permute-start(bf16[2,112,128]{2,1,0:T(8,128)(2,1)S(1)} %pad_maximum_fusion), channel_id=1, source_target_pairs={{0,4},{2,6},{4,0},{6,2},{8,12},{10,14},{12,8},{14,10},{1,5},{3,7},... | collective-permute-start | bytes 172040 | tf_op jit(solution)/shard_map/ppermute | solution.py:298
  11.7 0.0 collective-permute-start.3
  11.7 1.7 %collective-permute-done.1 = bf16[2,112,128]{2,1,0:T(8,128)(2,1)S(1)} collective-permute-done((bf16[2,112,128]{2,1,0:T(8,128)(2,1)S(1)}, bf16[2,112,128]{2,1,0:T(8,128)(2,1)S(1)}, u32[]{:S(2)}, u32[]{:S(2)}) %collective-permute-start.1) | collective-permute-done | bytes 57376 | tf_op jit(solution)/shard_map/ppermute | solution.py:298
  13.4 0.0 copy-start.1
  13.4 1.8 %collective-permute-done.2 = bf16[2,112,128]{2,1,0:T(8,128)(2,1)S(1)} collective-permute-done((bf16[2,112,128]{2,1,0:T(8,128)(2,1)S(1)}, bf16[2,112,128]{2,1,0:T(8,128)(2,1)S(1)}, u32[]{:S(2)}, u32[]{:S(2)}) %collective-permute-start.2) | collective-permute-done | bytes 57376 | tf_op jit(solution)/shard_map/ppermute | solution.py:298
  15.2 0.0 copy-start.5
  15.2 0.6 %collective-permute-done.3 = bf16[2,112,128]{2,1,0:T(8,128)(2,1)S(1)} collective-permute-done((bf16[2,112,128]{2,1,0:T(8,128)(2,1)S(1)}, bf16[2,112,128]{2,1,0:T(8,128)(2,1)S(1)}, u32[]{:S(2)}, u32[]{:S(2)}) %collective-permute-start.3) | collective-permute-done | bytes 57376 | tf_op jit(solution)/shard_map/ppermute | solution.py:298
  15.9 0.1 collective-permute-start.4
  15.9 1.5 %collective-permute-done.4.other_ref = bf16[8,112,128]{2,1,0:T(8,128)(2,1)S(1)} collective-permute-done((bf16[8,112,128]{2,1,0:T(8,128)(2,1)S(1)}, bf16[8,112,128]{2,1,0:T(8,128)(2,1)S(1)}, u32[]{:S(2)}, u32[]{:S(2)}) %collective-permute-start.4) | collective-permute-done | bytes 229408 | tf_op jit(solution)/shard_map/ppermute | solution.py:302
  17.4 0.0 copy-done.3
  17.4 0.0 copy-done.6
  17.4 0.0 copy-done.2
  17.4 0.0 copy-done
  17.4 0.0 copy-done.1
  17.4 0.0 copy-done.5
  17.4 3.9 %shard_map.111 = bf16[2,32,128]{2,1,0:T(8,128)(2,1)} custom-call(bf16[8,112,128]{2,1,0:T(8,128)(2,1)S(1)} %constant_dynamic-update-slice_fusion.held_ref, bf16[8,112,128]{2,1,0:T(8,128)(2,1)S(1)} %collective-permute-done.4.other_ref, bf16[32,32,128]{2,1,0:T(8,128)(2,1)S(1)} %copy-done, bf16[4,128,128]{2,1,0:T(8,128)(2,1)S(1)} %copy-done.1, ...), custom_call_target="tpu_custom_call" | custom-call | tf_op jit(solution)/shard_map/pallas_call | solution.py:362
  (9 shorter events, 0.1 us)
Async XLA Ops:
  0.0 17.4 %copy-start.3 = (bf16[512,128]{1,0:T(8,128)(2,1)S(1)}, bf16[512,128]{1,0:T(8,128)(2,1)}, u32[]{:S(2)}) copy-start(bf16[512,128]{1,0:T(8,128)(2,1)} %down_ref.1) | copy-start | bytes 393220
  2.0 6.2 %collective-permute-start = (bf16[1,112,128]{2,1,0:T(8,128)(2,1)}, bf16[1,112,128]{2,1,0:T(8,128)(2,1)S(1)}, u32[]{:S(2)}, u32[]{:S(2)}) collective-permute-start(bf16[1,112,128]{2,1,0:T(8,128)(2,1)} %bitcast.3), channel_id=1, source_target_pairs={{0,8},{2,10},{4,12},{6,14},{8,0},{10,2},{12,4},{14,6},{1,9},{3,11}... | collective-permute-start | bytes 86024 | tf_op jit(solution)/shard_map/ppermute | solution.py:288
  6.1 0.8 %copy-start.4 = (bf16[112,128]{1,0:T(8,128)(2,1)S(1)}, bf16[112,128]{1,0:T(8,128)(2,1)}, u32[]{:S(2)}) copy-start(bf16[112,128]{1,0:T(8,128)(2,1)} %shard_map.109.packed_ref) | copy-start | bytes 86020
  6.8 10.6 %copy-start.6 = (bf16[128,128]{1,0:T(8,128)(2,1)S(1)}, bf16[128,128]{1,0:T(8,128)(2,1)}, u32[]{:S(2)}) copy-start(bf16[128,128]{1,0:T(8,128)(2,1)} %output_ref.1) | copy-start | bytes 98308
  6.9 10.6 %copy-start.2 = (bf16[128,512]{1,0:T(8,128)(2,1)S(1)}, bf16[128,512]{1,0:T(8,128)(2,1)}, u32[]{:S(2)}) copy-start(bf16[128,512]{1,0:T(8,128)(2,1)} %up_ref.1) | copy-start | bytes 393220
  6.9 10.6 %copy-start = (bf16[32,32,128]{2,1,0:T(8,128)(2,1)S(1)}, bf16[32,32,128]{2,1,0:T(8,128)(2,1)}, u32[]{:S(2)}) copy-start(bf16[32,32,128]{2,1,0:T(8,128)(2,1)} %outer_ref.1) | copy-start | bytes 786436
  8.1 5.2 %collective-permute-start.1 = (bf16[2,112,128]{2,1,0:T(8,128)(2,1)S(1)}, bf16[2,112,128]{2,1,0:T(8,128)(2,1)S(1)}, u32[]{:S(2)}, u32[]{:S(2)}) collective-permute-start(bf16[2,112,128]{2,1,0:T(8,128)(2,1)S(1)} %pad_maximum_fusion), channel_id=1, source_target_pairs={{0,6},{2,4},{4,2},{6,0},{8,14},{10,12},{12,10},{14,8},{1,7},{3,5},... | collective-permute-start | bytes 172040 | tf_op jit(solution)/shard_map/ppermute | solution.py:298
  11.0 4.2 %collective-permute-start.2 = (bf16[2,112,128]{2,1,0:T(8,128)(2,1)S(1)}, bf16[2,112,128]{2,1,0:T(8,128)(2,1)S(1)}, u32[]{:S(2)}, u32[]{:S(2)}) collective-permute-start(bf16[2,112,128]{2,1,0:T(8,128)(2,1)S(1)} %pad_maximum_fusion), channel_id=1, source_target_pairs={{0,4},{2,6},{4,0},{6,2},{8,12},{10,14},{12,8},{14,10},{1,5},{3,7},... | collective-permute-start | bytes 172040 | tf_op jit(solution)/shard_map/ppermute | solution.py:298
  11.7 4.2 %collective-permute-start.3 = (bf16[2,112,128]{2,1,0:T(8,128)(2,1)S(1)}, bf16[2,112,128]{2,1,0:T(8,128)(2,1)S(1)}, u32[]{:S(2)}, u32[]{:S(2)}) collective-permute-start(bf16[2,112,128]{2,1,0:T(8,128)(2,1)S(1)} %pad_maximum_fusion), channel_id=1, source_target_pairs={{0,2},{2,0},{4,6},{6,4},{8,10},{10,8},{12,14},{14,12},{1,3},{3,1},... | collective-permute-start | bytes 172040 | tf_op jit(solution)/shard_map/ppermute | solution.py:298
  13.4 4.0 %copy-start.1 = (bf16[4,128,128]{2,1,0:T(8,128)(2,1)S(1)}, bf16[4,128,128]{2,1,0:T(8,128)(2,1)}, u32[]{:S(2)}) copy-start(bf16[4,128,128]{2,1,0:T(8,128)(2,1)} %triangle_ref.1) | copy-start | bytes 393220
  15.2 2.2 %copy-start.5 = (bf16[128,128]{1,0:T(8,128)(2,1)S(1)}, bf16[128,128]{1,0:T(8,128)(2,1)}, u32[]{:S(2)}) copy-start(bf16[128,128]{1,0:T(8,128)(2,1)} %gate_ref.1) | copy-start | bytes 98308
  15.9 1.6 %collective-permute-start.4 = (bf16[8,112,128]{2,1,0:T(8,128)(2,1)S(1)}, bf16[8,112,128]{2,1,0:T(8,128)(2,1)S(1)}, u32[]{:S(2)}, u32[]{:S(2)}) collective-permute-start(bf16[8,112,128]{2,1,0:T(8,128)(2,1)S(1)} %constant_dynamic-update-slice_fusion.held_ref), channel_id=1, source_target_pairs={{0,1},{1,0},{2,3},{3,2},{4,5},{5,4},{6,7},{7,6},{8,9},{9,8},{10,11... | collective-permute-start | bytes 688136 | tf_op jit(solution)/shard_map/ppermute | solution.py:302

commit v14 on v13

--- a/solution.py
+++ b/solution.py
@@ -169,13 +169,16 @@
         blocks = [jnp.where(second_core, other, mine), jnp.where(second_core, mine, other)]
         packed = [block[base : base + sequences].astype(f32) for block in blocks]
         right = jnp.where(low, packed[0], packed[1])
-        for turn, value in enumerate((right, pltpu.roll(right, half, 1))):
-            for copy in range(group):
+        turned = pltpu.roll(right, half, 1)
+        for turn, (near, far) in enumerate(((right, turned), (turned, right))):
+            near = jnp.where(low, near, 0.0).astype(bf16)
+            far = jnp.where(low, 0.0, far).astype(bf16)
+            for copy in range(2 * group):
                 right_ref[
                     turn,
                     copy * sequences : (copy + 1) * sequences,
                     chip * wide : (chip + 1) * wide,
-                ] = value.astype(bf16)
+                ] = near if copy < group else far
         for core in range(cores):
             residue = (chip * cores + core) * rows
             for row in range(rows):
@@ -198,33 +201,27 @@
     )
     inverse = 1.0 / jnp.maximum(count, 1.0)
 
-    low = lax.broadcasted_iota(jnp.int32, (residues, wide), 1) < half
     totals = [0.0, 0.0]
     for part in range(parts):
-        outer = []
-        for turn in range(2):
-            left = jnp.concatenate(
-                [left_ref[:, d] for d in range(part * span + turn, (part + 1) * span, 2)], axis=0
-            ).astype(bf16)
-            outer.append(jnp.dot(left, right_ref[turn], preferred_element_type=f32))
-
-        def piece(turn, at, chip):
-            return outer[turn][
-                at * residues : (at + 1) * residues, chip * wide : (chip + 1) * wide
-            ]
-
-        for at in range(span // 2):
-            follow = (at + 1) % (span // 2)
-            for chip in range(chips):
-                place = (
-                    part,
-                    slice(chip * residues, (chip + 1) * residues),
-                    slice(at * wide, (at + 1) * wide),
-                )
-                first_ref[place] = jnp.where(low, piece(0, at, chip), piece(1, at, chip)).astype(bf16)
-                second_ref[place] = jnp.where(
-                    low, piece(1, at, chip), piece(0, follow, chip)
-                ).astype(bf16)
+        left = [left_ref[:, d].astype(bf16) for d in range(part * span, (part + 1) * span)]
+        for turn, outer_ref_part in enumerate((first_ref, second_ref)):
+            pairs = jnp.concatenate(
+                [
+                    jnp.concatenate([left[d], left[(d + 1) % span]], axis=1)
+                    for d in range(turn, span, 2)
+                ],
+                axis=0,
+            )
+            outer = jnp.dot(pairs, right_ref[turn], preferred_element_type=f32).astype(bf16)
+            for at in range(span // 2):
+                for chip in range(chips):
+                    outer_ref_part[
+                        part,
+                        chip * residues : (chip + 1) * residues,
+                        at * wide : (at + 1) * wide,
+                    ] = outer[
+                        at * residues : (at + 1) * residues, chip * wide : (chip + 1) * wide
+                    ]
         depth = span * 2 * channels
         totals[0] += jnp.dot(first_ref[part], block_ref[part, :depth], preferred_element_type=f32)
         totals[1] += jnp.dot(
@@ -298,8 +295,10 @@
         lax.ppermute(both, "dap", [(src, src ^ offset) for src in range(dap_count)])
         for offset in swap_order(dap_count)
     ]
-    held = jnp.concatenate(held, axis=0)
-    return held, lax.ppermute(held, "sub", [(0, 1), (1, 0)])
+    sibling = [(0, 1), (1, 0)]
+    early = lax.ppermute(jnp.concatenate(held[:-1], axis=0), "sub", sibling)
+    late = lax.ppermute(held[-1], "sub", sibling)
+    return jnp.concatenate(held, axis=0), jnp.concatenate([early, late], axis=0)
 
 
 def swap_order(dap_count):
@@ -367,7 +366,7 @@
         scratch_shapes=[
             pltpu.VMEM((parts, (channels // parts + 1) * 2 * channels, 2 * wide), jnp.bfloat16),
             pltpu.VMEM((residues, channels, wide), jnp.float32),
-            pltpu.VMEM((2, group * sequences, chips * wide), jnp.bfloat16),
+            pltpu.VMEM((2, 2 * group * sequences, chips * wide), jnp.bfloat16),
             pltpu.VMEM((residues, wide), jnp.float32),
             pltpu.VMEM((parts, chips * residues, channels // parts * wide // 2), jnp.bfloat16),
             pltpu.VMEM((parts, chips * residues, channels // parts * wide // 2), jnp.bfloat16),

time: 21.5 us -> 21.6 us (level)
  waiting for transfers between devices: 6.82 us -> 6.38 us
  Pallas kernels: 5.86 us -> 6.09 us
    ppermute x1 -> x2, waiting for transfers between devices: 1.48 us -> 1.1 us  [the longest x1 1.1 us: gather_all(): late = lax.ppermute(held[-1], 'sub', sibling)]
    pallas_call x1, Pallas kernels: 3.9 us -> 4.17 us  [shards_replicated(): pl.pallas_call(update_kernel, out_shape=jax.ShapeDtypeStruct(pairwise_sta...]
  transfers between devices with their start and end apart: 5 -> 6, of which waited for: 5 -> 5; matrix products, arithmetic and copies ran while one was open for 0% -> 0% of each run, Pallas kernels for 0% -> 0%
where the time goes in v14:
time: 21.6 us; the launch traced here: 21.3 us
  starting transfers between devices  7.78 us (36%)
  waiting for transfers between devices  6.38 us (30%)
  Pallas kernels  6.09 us (28%)
  local copies, waits for them, and re-layouts  0.87 us (4%)
    pallas_call x1, Pallas kernels, shards_replicated(): pl.pallas_call(update_kernel, out_shape=jax.ShapeDtypeStruct(pairwise_sta...  4.17 us
    ppermute x1, starting transfers between devices, gather_all(): lax.ppermute(packed[None], 'dap', [(src, src ^ half) for src in range(dap...  4.1 us
    ppermute x3, waiting for transfers between devices, gather_all(): lax.ppermute(both, 'dap', [(src, src ^ offset) for src in range(dap_count)])  4 us
    ppermute x3, starting transfers between devices, gather_all(): lax.ppermute(both, 'dap', [(src, src ^ offset) for src in range(dap_count)])  3.55 us
    pallas_call x1, Pallas kernels, shards_replicated(): pl.pallas_call(pack_kernel, out_shape=jax.ShapeDtypeStruct((rows * residu...  1.92 us
    ppermute x1, waiting for transfers between devices, gather_all(): lax.ppermute(packed[None], 'dap', [(src, src ^ half) for src in range(dap...  1.28 us
    ppermute x1, waiting for transfers between devices, gather_all(): late = lax.ppermute(held[-1], 'sub', sibling)  1.1 us
    unnamed x18, local copies, waits for them, and re-layouts  0.85 us
  transfers between devices with their start and end apart: 6, of which 5 were waited for; matrix products, arithmetic and copies ran while one was open for 0% of the time, Pallas kernels for 0%

profile of v14, /device:TPU:0, one launch (start us, length us, event | category | flops | bytes accessed | tf_op | source)
XLA Modules:
  0.0 21.3 jit_solution(6328080074888423741)
XLA Ops:
  0.0 1.9 %shard_map.109.packed_ref = bf16[112,128]{1,0:T(8,128)(2,1)} custom-call(s32[32]{0:T(128)} %mask_hbm.1, s32[2,32]{1,0:T(2,128)} %bitcast.5, bf16[32,2,256]{2,1,0:T(2,128)(2,1)} %state_hbm.1, bf16[2,32,256]{2,1,0:T(8,128)(2,1)} %bitcast.4, bf16[2,32,128]{2,1,0:T(8,128)(2,1)} %pair_hbm.1), custom_call_target="tpu_custom_call" | custom-call | tf_op jit(solution)/shard_map/pallas_call | solution.py:335
  1.9 4.1 %collective-permute-start = (bf16[1,112,128]{2,1,0:T(8,128)(2,1)}, bf16[1,112,128]{2,1,0:T(8,128)(2,1)S(1)}, u32[]{:S(2)}, u32[]{:S(2)}) collective-permute-start(bf16[1,112,128]{2,1,0:T(8,128)(2,1)} %bitcast.3), channel_id=1, source_target_pairs={{0,8},{2,10},{4,12},{6,14},{8,0},{10,2},{12,4},{14,6},{1,9},{3,11}... | collective-permute-start | bytes 86024 | tf_op jit(solution)/shard_map/ppermute | solution.py:285
  6.0 0.8 %copy-done.4 = bf16[112,128]{1,0:T(8,128)(2,1)S(1)} copy-done((bf16[112,128]{1,0:T(8,128)(2,1)S(1)}, bf16[112,128]{1,0:T(8,128)(2,1)}, u32[]{:S(2)}) %copy-start.4) | copy-done | bytes 28696
  6.8 1.3 %collective-permute-done = bf16[1,112,128]{2,1,0:T(8,128)(2,1)S(1)} collective-permute-done((bf16[1,112,128]{2,1,0:T(8,128)(2,1)}, bf16[1,112,128]{2,1,0:T(8,128)(2,1)S(1)}, u32[]{:S(2)}, u32[]{:S(2)}) %collective-permute-start) | collective-permute-done | bytes 28704 | tf_op jit(solution)/shard_map/ppermute | solution.py:285
  8.1 2.9 %collective-permute-start.1 = (bf16[2,112,128]{2,1,0:T(8,128)(2,1)S(1)}, bf16[2,112,128]{2,1,0:T(8,128)(2,1)S(1)}, u32[]{:S(2)}, u32[]{:S(2)}) collective-permute-start(bf16[2,112,128]{2,1,0:T(8,128)(2,1)S(1)} %pad_maximum_fusion.2), channel_id=1, source_target_pairs={{0,6},{2,4},{4,2},{6,0},{8,14},{10,12},{12,10},{14,8},{1,7},{3,5},... | collective-permute-start | bytes 172040 | tf_op jit(solution)/shard_map/ppermute | solution.py:295
  11.0 0.6 %collective-permute-start.2 = (bf16[2,112,128]{2,1,0:T(8,128)(2,1)S(1)}, bf16[2,112,128]{2,1,0:T(8,128)(2,1)S(1)}, u32[]{:S(2)}, u32[]{:S(2)}) collective-permute-start(bf16[2,112,128]{2,1,0:T(8,128)(2,1)S(1)} %pad_maximum_fusion.2), channel_id=1, source_target_pairs={{0,4},{2,6},{4,0},{6,2},{8,12},{10,14},{12,8},{14,10},{1,5},{3,7},... | collective-permute-start | bytes 172040 | tf_op jit(solution)/shard_map/ppermute | solution.py:295
  11.6 0.0 collective-permute-start.3
  11.7 1.7 %collective-permute-done.1 = bf16[2,112,128]{2,1,0:T(8,128)(2,1)S(1)} collective-permute-done((bf16[2,112,128]{2,1,0:T(8,128)(2,1)S(1)}, bf16[2,112,128]{2,1,0:T(8,128)(2,1)S(1)}, u32[]{:S(2)}, u32[]{:S(2)}) %collective-permute-start.1) | collective-permute-done | bytes 57376 | tf_op jit(solution)/shard_map/ppermute | solution.py:295
  13.4 1.8 %collective-permute-done.2 = bf16[2,112,128]{2,1,0:T(8,128)(2,1)S(1)} collective-permute-done((bf16[2,112,128]{2,1,0:T(8,128)(2,1)S(1)}, bf16[2,112,128]{2,1,0:T(8,128)(2,1)S(1)}, u32[]{:S(2)}, u32[]{:S(2)}) %collective-permute-start.2) | collective-permute-done | bytes 57376 | tf_op jit(solution)/shard_map/ppermute | solution.py:295
  15.2 0.1 collective-permute-start.4
  15.3 0.0 copy-start.6
  15.3 0.5 %collective-permute-done.3 = bf16[2,112,128]{2,1,0:T(8,128)(2,1)S(1)} collective-permute-done((bf16[2,112,128]{2,1,0:T(8,128)(2,1)S(1)}, bf16[2,112,128]{2,1,0:T(8,128)(2,1)S(1)}, u32[]{:S(2)}, u32[]{:S(2)}) %collective-permute-start.3) | collective-permute-done | bytes 57376 | tf_op jit(solution)/shard_map/ppermute | solution.py:295
  15.8 0.1 collective-permute-start.5
  15.9 0.0 copy-start
  15.9 0.0 copy-start.1
  15.9 0.0 copy-start.2
  15.9 0.0 copy-start.5
  15.9 1.1 %collective-permute-done.5 = bf16[2,112,128]{2,1,0:T(8,128)(2,1)S(1)} collective-permute-done((bf16[2,112,128]{2,1,0:T(8,128)(2,1)S(1)}, bf16[2,112,128]{2,1,0:T(8,128)(2,1)S(1)}, u32[]{:S(2)}, u32[]{:S(2)}) %collective-permute-start.5) | collective-permute-done | bytes 57376 | tf_op jit(solution)/shard_map/ppermute | solution.py:300
  17.0 0.0 collective-permute-done.4
  17.1 0.0 copy-done.6
  17.1 0.0 copy-done.3
  17.1 0.0 copy-done
  17.1 0.0 copy-done.1
  17.1 4.2 %shard_map.111 = bf16[2,32,128]{2,1,0:T(8,128)(2,1)} custom-call(bf16[8,112,128]{2,1,0:T(8,128)(2,1)S(1)} %constant_dynamic-update-slice_fusion.held_ref, bf16[8,112,128]{2,1,0:T(8,128)(2,1)S(1)} %pad_maximum_fusion.other_ref, bf16[32,32,128]{2,1,0:T(8,128)(2,1)S(1)} %copy-done, bf16[4,128,128]{2,1,0:T(8,128)(2,1)S(1)} %copy-done.1, ...), custom_call_target="tpu_custom_call" | custom-call | tf_op jit(solution)/shard_map/pallas_call | solution.py:361
  (13 shorter events, 0.1 us)
Async XLA Ops:
  1.9 6.2 %collective-permute-start = (bf16[1,112,128]{2,1,0:T(8,128)(2,1)}, bf16[1,112,128]{2,1,0:T(8,128)(2,1)S(1)}, u32[]{:S(2)}, u32[]{:S(2)}) collective-permute-start(bf16[1,112,128]{2,1,0:T(8,128)(2,1)} %bitcast.3), channel_id=1, source_target_pairs={{0,8},{2,10},{4,12},{6,14},{8,0},{10,2},{12,4},{14,6},{1,9},{3,11}... | collective-permute-start | bytes 86024 | tf_op jit(solution)/shard_map/ppermute | solution.py:285
  6.0 0.8 %copy-start.4 = (bf16[112,128]{1,0:T(8,128)(2,1)S(1)}, bf16[112,128]{1,0:T(8,128)(2,1)}, u32[]{:S(2)}) copy-start(bf16[112,128]{1,0:T(8,128)(2,1)} %shard_map.109.packed_ref) | copy-start | bytes 86020
  8.1 5.2 %collective-permute-start.1 = (bf16[2,112,128]{2,1,0:T(8,128)(2,1)S(1)}, bf16[2,112,128]{2,1,0:T(8,128)(2,1)S(1)}, u32[]{:S(2)}, u32[]{:S(2)}) collective-permute-start(bf16[2,112,128]{2,1,0:T(8,128)(2,1)S(1)} %pad_maximum_fusion.2), channel_id=1, source_target_pairs={{0,6},{2,4},{4,2},{6,0},{8,14},{10,12},{12,10},{14,8},{1,7},{3,5},... | collective-permute-start | bytes 172040 | tf_op jit(solution)/shard_map/ppermute | solution.py:295
  11.0 4.2 %collective-permute-start.2 = (bf16[2,112,128]{2,1,0:T(8,128)(2,1)S(1)}, bf16[2,112,128]{2,1,0:T(8,128)(2,1)S(1)}, u32[]{:S(2)}, u32[]{:S(2)}) collective-permute-start(bf16[2,112,128]{2,1,0:T(8,128)(2,1)S(1)} %pad_maximum_fusion.2), channel_id=1, source_target_pairs={{0,4},{2,6},{4,0},{6,2},{8,12},{10,14},{12,8},{14,10},{1,5},{3,7},... | collective-permute-start | bytes 172040 | tf_op jit(solution)/shard_map/ppermute | solution.py:295
  11.6 4.2 %collective-permute-start.3 = (bf16[2,112,128]{2,1,0:T(8,128)(2,1)S(1)}, bf16[2,112,128]{2,1,0:T(8,128)(2,1)S(1)}, u32[]{:S(2)}, u32[]{:S(2)}) collective-permute-start(bf16[2,112,128]{2,1,0:T(8,128)(2,1)S(1)} %pad_maximum_fusion.2), channel_id=1, source_target_pairs={{0,2},{2,0},{4,6},{6,4},{8,10},{10,8},{12,14},{14,12},{1,3},{3,1},... | collective-permute-start | bytes 172040 | tf_op jit(solution)/shard_map/ppermute | solution.py:295
  15.2 1.9 %collective-permute-start.4 = (bf16[6,112,128]{2,1,0:T(8,128)(2,1)S(1)}, bf16[6,112,128]{2,1,0:T(8,128)(2,1)S(1)}, u32[]{:S(2)}, u32[]{:S(2)}) collective-permute-start(bf16[6,112,128]{2,1,0:T(8,128)(2,1)S(1)} %pad_maximum_fusion.1), channel_id=1, source_target_pairs={{0,1},{1,0},{2,3},{3,2},{4,5},{5,4},{6,7},{7,6},{8,9},{9,8},{10,11... | collective-permute-start | bytes 516104 | tf_op jit(solution)/shard_map/ppermute | solution.py:299
  15.3 1.8 %copy-start.6 = (bf16[128,128]{1,0:T(8,128)(2,1)S(1)}, bf16[128,128]{1,0:T(8,128)(2,1)}, u32[]{:S(2)}) copy-start(bf16[128,128]{1,0:T(8,128)(2,1)} %output_ref.1) | copy-start | bytes 98308
  15.8 1.2 %collective-permute-start.5 = (bf16[2,112,128]{2,1,0:T(8,128)(2,1)S(1)}, bf16[2,112,128]{2,1,0:T(8,128)(2,1)S(1)}, u32[]{:S(2)}, u32[]{:S(2)}) collective-permute-start(bf16[2,112,128]{2,1,0:T(8,128)(2,1)S(1)} %collective-permute-done.3), channel_id=1, source_target_pairs={{0,1},{1,0},{2,3},{3,2},{4,5},{5,4},{6,7},{7,6},{8,9},{9,8},{10,11... | collective-permute-start | bytes 172040 | tf_op jit(solution)/shard_map/ppermute | solution.py:300
  15.9 1.2 %copy-start.3 = (bf16[512,128]{1,0:T(8,128)(2,1)S(1)}, bf16[512,128]{1,0:T(8,128)(2,1)}, u32[]{:S(2)}) copy-start(bf16[512,128]{1,0:T(8,128)(2,1)} %down_ref.1) | copy-start | bytes 393220
  15.9 1.2 %copy-start = (bf16[32,32,128]{2,1,0:T(8,128)(2,1)S(1)}, bf16[32,32,128]{2,1,0:T(8,128)(2,1)}, u32[]{:S(2)}) copy-start(bf16[32,32,128]{2,1,0:T(8,128)(2,1)} %outer_ref.1) | copy-start | bytes 786436
  15.9 1.2 %copy-start.1 = (bf16[4,128,128]{2,1,0:T(8,128)(2,1)S(1)}, bf16[4,128,128]{2,1,0:T(8,128)(2,1)}, u32[]{:S(2)}) copy-start(bf16[4,128,128]{2,1,0:T(8,128)(2,1)} %triangle_ref.1) | copy-start | bytes 393220
  15.9 1.2 %copy-start.2 = (bf16[128,512]{1,0:T(8,128)(2,1)S(1)}, bf16[128,512]{1,0:T(8,128)(2,1)}, u32[]{:S(2)}) copy-start(bf16[128,512]{1,0:T(8,128)(2,1)} %up_ref.1) | copy-start | bytes 393220
  15.9 1.2 %copy-start.5 = (bf16[128,128]{1,0:T(8,128)(2,1)S(1)}, bf16[128,128]{1,0:T(8,128)(2,1)}, u32[]{:S(2)}) copy-start(bf16[128,128]{1,0:T(8,128)(2,1)} %gate_ref.1) | copy-start | bytes 98308

commit v15 on v13

--- a/solution.py
+++ b/solution.py
@@ -42,13 +42,12 @@
     state_hbm,
     weight_hbm,
     pair_hbm,
-    out_hbm,
+    out_ref,
     mask_ref,
     keep_ref,
     state_ref,
     weight_ref,
     wide_ref,
-    out_ref,
     sems,
 ):
     rows, residues, wide = pair_hbm.shape
@@ -63,7 +62,7 @@
         pltpu.make_async_copy(mask_hbm, mask_ref, sems.at[3]),
     ] + [
         pltpu.make_async_copy(
-            pair_hbm.at[row], out_hbm.at[pl.ds(row * residues, residues)], sems.at[5 + row]
+            pair_hbm.at[row], out_ref.at[pl.ds(row * residues, residues)], sems.at[4 + row]
         )
         for row in range(rows)
     ]
@@ -99,15 +98,10 @@
     right = jnp.concatenate(rights, axis=1)
     first = jnp.concatenate([right, left], axis=1)
     other = jnp.concatenate([left, right], axis=1)
-    out_ref[:sequences] = jnp.where(second_core, other, first).astype(jnp.bfloat16)
-    out_ref[sequences:] = jnp.concatenate(
+    out_ref[base : base + sequences] = jnp.where(second_core, other, first).astype(jnp.bfloat16)
+    out_ref[base + sequences :] = jnp.concatenate(
         keeps + [jnp.zeros((16 - rows, wide), jnp.float32)], axis=0
     ).astype(jnp.bfloat16)
-    store = pltpu.make_async_copy(
-        out_ref, out_hbm.at[pl.ds(base, sequences + 16)], sems.at[4]
-    )
-    store.start()
-    store.wait()
     for load in loads[4:]:
         load.wait()
 
@@ -278,28 +272,19 @@
     out_ref[...] = result.astype(bf16).reshape(rows, residues, wide)
 
 
-def copy_kernel(packed_ref, out_ref):
-    out_ref[0] = packed_ref[...]
-
-
 def gather_all(packed):
     dap_count = lax.axis_size("dap")
     half = dap_count // 2
     far = lax.ppermute(packed[None], "dap", [(src, src ^ half) for src in range(dap_count)])
-    own = pl.pallas_call(
-        copy_kernel,
-        out_shape=jax.ShapeDtypeStruct((1,) + packed.shape, packed.dtype),
-        in_specs=[pl.BlockSpec(memory_space=pltpu.VMEM)],
-        out_specs=pl.BlockSpec(memory_space=pltpu.VMEM),
-        compiler_params=pltpu.CompilerParams(vmem_limit_bytes=4 << 20),
-    )(packed)
-    both = jnp.concatenate([own, far], axis=0)
+    both = jnp.concatenate([packed[None], far], axis=0)
     held = [both] + [
         lax.ppermute(both, "dap", [(src, src ^ offset) for src in range(dap_count)])
         for offset in swap_order(dap_count)
     ]
-    held = jnp.concatenate(held, axis=0)
-    return held, lax.ppermute(held, "sub", [(0, 1), (1, 0)])
+    sibling = [(0, 1), (1, 0)]
+    early = lax.ppermute(jnp.concatenate(held[:-1], axis=0), "sub", sibling)
+    late = lax.ppermute(held[-1], "sub", sibling)
+    return jnp.concatenate(held, axis=0), jnp.concatenate([early, late], axis=0)
 
 
 def swap_order(dap_count):
@@ -337,23 +322,27 @@
         pack_kernel,
         out_shape=jax.ShapeDtypeStruct((rows * residues + sequences + 16, wide), jnp.bfloat16),
         in_specs=[hbm] * 5,
-        out_specs=hbm,
+        out_specs=vector,
         scratch_shapes=[
             pltpu.SMEM((residues,), jnp.int32),
             pltpu.VMEM((rows, sequences), jnp.int32),
             pltpu.VMEM(alignment_state.shape, jnp.bfloat16),
             pltpu.VMEM((2, channels, alignment_state.shape[2]), jnp.bfloat16),
             pltpu.VMEM(alignment_state.shape, jnp.float32),
-            pltpu.VMEM((sequences + 16, wide), jnp.bfloat16),
-            pltpu.SemaphoreType.DMA((5 + rows,)),
+            pltpu.SemaphoreType.DMA((4 + rows,)),
         ],
-        compiler_params=pltpu.CompilerParams(vmem_limit_bytes=63 << 20),
+        compiler_params=pltpu.CompilerParams(vmem_limit_bytes=8 << 20),
     )(
-        residue_crop_mask,
-        alignment_mask.T,
-        alignment_state,
-        outer_input_weight.transpose(0, 2, 1),
-        pairwise_state,
+        *(
+            pltpu.with_memory_space_constraint(array, pltpu.HBM)
+            for array in (
+                residue_crop_mask,
+                alignment_mask.T,
+                alignment_state,
+                outer_input_weight.transpose(0, 2, 1),
+                pairwise_state,
+            )
+        )
     )
     held, other = gather_all(packed)
     cores, chips = lax.axis_size("sub"), lax.axis_size("dap")

time: 21.5 us -> 20.4 us (0.949)
  local copies, waits for them, and re-layouts: 0.86 us -> 0.08 us
  Pallas kernels: 5.86 us -> 5.22 us
    unnamed x18 -> x16, local copies, waits for them, and re-layouts: 0.84 us -> 0.07 us
    pallas_call x1, Pallas kernels: 1.95 us -> 1.31 us  [shards_replicated(): pl.pallas_call(pack_kernel, out_shape=jax.ShapeDtypeStruct((rows * residu...]
    ppermute x1, waiting for transfers between devices: 1.26 us -> 1.86 us  [gather_all(): lax.ppermute(packed[None], 'dap', [(src, src ^ half) for src in range(dap...]
    ppermute x1 -> x2, waiting for transfers between devices: 1.48 us -> 1.1 us  [the longest x1 1.1 us: gather_all(): late = lax.ppermute(held[-1], 'sub', sibling)]
  transfers between devices with their start and end apart: 5 -> 6, of which waited for: 5 -> 5; matrix products, arithmetic and copies ran while one was open for 0% -> 0% of each run, Pallas kernels for 0% -> 0%
where the time goes in v15:
time: 20.4 us; the launch traced here: 20.2 us
  starting transfers between devices  7.78 us (38%)
  waiting for transfers between devices  6.96 us (34%)
  Pallas kernels  5.22 us (26%)
    ppermute x1, starting transfers between devices, gather_all(): lax.ppermute(packed[None], 'dap', [(src, src ^ half) for src in range(dap...  4.1 us
    ppermute x3, waiting for transfers between devices, gather_all(): lax.ppermute(both, 'dap', [(src, src ^ offset) for src in range(dap_count)])  4 us
    pallas_call x1, Pallas kernels, shards_replicated(): pl.pallas_call(update_kernel, out_shape=jax.ShapeDtypeStruct(pairwise_sta...  3.9 us
    ppermute x3, starting transfers between devices, gather_all(): lax.ppermute(both, 'dap', [(src, src ^ offset) for src in range(dap_count)])  3.55 us
    ppermute x1, waiting for transfers between devices, gather_all(): lax.ppermute(packed[None], 'dap', [(src, src ^ half) for src in range(dap...  1.86 us
    pallas_call x1, Pallas kernels, shards_replicated(): pl.pallas_call(pack_kernel, out_shape=jax.ShapeDtypeStruct((rows * residu...  1.31 us
    ppermute x1, waiting for transfers between devices, gather_all(): late = lax.ppermute(held[-1], 'sub', sibling)  1.1 us
  transfers between devices with their start and end apart: 6, of which 5 were waited for; matrix products, arithmetic and copies ran while one was open for 0% of the time, Pallas kernels for 0%

profile of v15, /device:TPU:0, one launch (start us, length us, event | category | flops | bytes accessed | tf_op | source)
XLA Modules:
  0.0 20.2 jit_solution(13552963206092988575)
XLA Ops:
  0.0 1.3 %shard_map.109 = bf16[112,128]{1,0:T(8,128)(2,1)S(1)} custom-call(s32[32]{0:T(128)} %mask_hbm.1, s32[2,32]{1,0:T(2,128)} %bitcast.8, bf16[32,2,256]{2,1,0:T(2,128)(2,1)} %state_hbm.1, bf16[2,32,256]{2,1,0:T(8,128)(2,1)} %bitcast.7, bf16[2,32,128]{2,1,0:T(8,128)(2,1)} %pair_hbm.1), custom_call_target="tpu_custom_call" | custom-call | tf_op jit(solution)/shard_map/pallas_call | solution.py:321
  1.3 4.1 %collective-permute-start = (bf16[1,112,128]{2,1,0:T(8,128)(2,1)S(1)}, bf16[1,112,128]{2,1,0:T(8,128)(2,1)S(1)}, u32[]{:S(2)}, u32[]{:S(2)}) collective-permute-start(bf16[1,112,128]{2,1,0:T(8,128)(2,1)S(1)} %bitcast.4), channel_id=1, source_target_pairs={{0,8},{2,10},{4,12},{6,14},{8,0},{10,2},{12,4},{14,6},{1,9},{3,11}... | collective-permute-start | bytes 86024 | tf_op jit(solution)/shard_map/ppermute | solution.py:278
  5.4 1.9 %collective-permute-done = bf16[1,112,128]{2,1,0:T(8,128)(2,1)S(1)} collective-permute-done((bf16[1,112,128]{2,1,0:T(8,128)(2,1)S(1)}, bf16[1,112,128]{2,1,0:T(8,128)(2,1)S(1)}, u32[]{:S(2)}, u32[]{:S(2)}) %collective-permute-start) | collective-permute-done | bytes 28704 | tf_op jit(solution)/shard_map/ppermute | solution.py:278
  7.3 2.9 %collective-permute-start.1 = (bf16[2,112,128]{2,1,0:T(8,128)(2,1)S(1)}, bf16[2,112,128]{2,1,0:T(8,128)(2,1)S(1)}, u32[]{:S(2)}, u32[]{:S(2)}) collective-permute-start(bf16[2,112,128]{2,1,0:T(8,128)(2,1)S(1)} %pad_maximum_fusion.2), channel_id=1, source_target_pairs={{0,6},{2,4},{4,2},{6,0},{8,14},{10,12},{12,10},{14,8},{1,7},{3,5},... | collective-permute-start | bytes 172040 | tf_op jit(solution)/shard_map/ppermute | solution.py:281
  10.2 0.6 %collective-permute-start.2 = (bf16[2,112,128]{2,1,0:T(8,128)(2,1)S(1)}, bf16[2,112,128]{2,1,0:T(8,128)(2,1)S(1)}, u32[]{:S(2)}, u32[]{:S(2)}) collective-permute-start(bf16[2,112,128]{2,1,0:T(8,128)(2,1)S(1)} %pad_maximum_fusion.2), channel_id=1, source_target_pairs={{0,4},{2,6},{4,0},{6,2},{8,12},{10,14},{12,8},{14,10},{1,5},{3,7},... | collective-permute-start | bytes 172040 | tf_op jit(solution)/shard_map/ppermute | solution.py:281
  10.8 0.0 collective-permute-start.3
  10.9 1.7 %collective-permute-done.1 = bf16[2,112,128]{2,1,0:T(8,128)(2,1)S(1)} collective-permute-done((bf16[2,112,128]{2,1,0:T(8,128)(2,1)S(1)}, bf16[2,112,128]{2,1,0:T(8,128)(2,1)S(1)}, u32[]{:S(2)}, u32[]{:S(2)}) %collective-permute-start.1) | collective-permute-done | bytes 57376 | tf_op jit(solution)/shard_map/ppermute | solution.py:281
  12.5 1.8 %collective-permute-done.2 = bf16[2,112,128]{2,1,0:T(8,128)(2,1)S(1)} collective-permute-done((bf16[2,112,128]{2,1,0:T(8,128)(2,1)S(1)}, bf16[2,112,128]{2,1,0:T(8,128)(2,1)S(1)}, u32[]{:S(2)}, u32[]{:S(2)}) %collective-permute-start.2) | collective-permute-done | bytes 57376 | tf_op jit(solution)/shard_map/ppermute | solution.py:281
  14.4 0.1 collective-permute-start.4
  14.5 0.0 copy-start.5
  14.5 0.5 %collective-permute-done.3 = bf16[2,112,128]{2,1,0:T(8,128)(2,1)S(1)} collective-permute-done((bf16[2,112,128]{2,1,0:T(8,128)(2,1)S(1)}, bf16[2,112,128]{2,1,0:T(8,128)(2,1)S(1)}, u32[]{:S(2)}, u32[]{:S(2)}) %collective-permute-start.3) | collective-permute-done | bytes 57376 | tf_op jit(solution)/shard_map/ppermute | solution.py:281
  15.0 0.1 collective-permute-start.5
  15.1 0.0 copy-start
  15.1 0.0 copy-start.1
  15.1 0.0 copy-start.2
  15.1 0.0 copy-start.4
  15.1 1.1 %collective-permute-done.5 = bf16[2,112,128]{2,1,0:T(8,128)(2,1)S(1)} collective-permute-done((bf16[2,112,128]{2,1,0:T(8,128)(2,1)S(1)}, bf16[2,112,128]{2,1,0:T(8,128)(2,1)S(1)}, u32[]{:S(2)}, u32[]{:S(2)}) %collective-permute-start.5) | collective-permute-done | bytes 57376 | tf_op jit(solution)/shard_map/ppermute | solution.py:286
  16.2 0.0 collective-permute-done.4
  16.3 0.0 copy-done.5
  16.3 0.0 copy-done.3
  16.3 0.0 copy-done
  16.3 0.0 copy-done.1
  16.3 0.0 copy-done.2
  16.3 3.9 %shard_map.110 = bf16[2,32,128]{2,1,0:T(8,128)(2,1)} custom-call(bf16[8,112,128]{2,1,0:T(8,128)(2,1)S(1)} %constant_dynamic-update-slice_fusion.held_ref, bf16[8,112,128]{2,1,0:T(8,128)(2,1)S(1)} %pad_maximum_fusion.other_ref, bf16[32,32,128]{2,1,0:T(8,128)(2,1)S(1)} %copy-done, bf16[4,128,128]{2,1,0:T(8,128)(2,1)S(1)} %copy-done.1, ...), custom_call_target="tpu_custom_call" | custom-call | tf_op jit(solution)/shard_map/pallas_call | solution.py:351
  (10 shorter events, 0.1 us)
Async XLA Ops:
  1.3 6.0 %collective-permute-start = (bf16[1,112,128]{2,1,0:T(8,128)(2,1)S(1)}, bf16[1,112,128]{2,1,0:T(8,128)(2,1)S(1)}, u32[]{:S(2)}, u32[]{:S(2)}) collective-permute-start(bf16[1,112,128]{2,1,0:T(8,128)(2,1)S(1)} %bitcast.4), channel_id=1, source_target_pairs={{0,8},{2,10},{4,12},{6,14},{8,0},{10,2},{12,4},{14,6},{1,9},{3,11}... | collective-permute-start | bytes 86024 | tf_op jit(solution)/shard_map/ppermute | solution.py:278
  7.3 5.2 %collective-permute-start.1 = (bf16[2,112,128]{2,1,0:T(8,128)(2,1)S(1)}, bf16[2,112,128]{2,1,0:T(8,128)(2,1)S(1)}, u32[]{:S(2)}, u32[]{:S(2)}) collective-permute-start(bf16[2,112,128]{2,1,0:T(8,128)(2,1)S(1)} %pad_maximum_fusion.2), channel_id=1, source_target_pairs={{0,6},{2,4},{4,2},{6,0},{8,14},{10,12},{12,10},{14,8},{1,7},{3,5},... | collective-permute-start | bytes 172040 | tf_op jit(solution)/shard_map/ppermute | solution.py:281
  10.2 4.2 %collective-permute-start.2 = (bf16[2,112,128]{2,1,0:T(8,128)(2,1)S(1)}, bf16[2,112,128]{2,1,0:T(8,128)(2,1)S(1)}, u32[]{:S(2)}, u32[]{:S(2)}) collective-permute-start(bf16[2,112,128]{2,1,0:T(8,128)(2,1)S(1)} %pad_maximum_fusion.2), channel_id=1, source_target_pairs={{0,4},{2,6},{4,0},{6,2},{8,12},{10,14},{12,8},{14,10},{1,5},{3,7},... | collective-permute-start | bytes 172040 | tf_op jit(solution)/shard_map/ppermute | solution.py:281
  10.8 4.2 %collective-permute-start.3 = (bf16[2,112,128]{2,1,0:T(8,128)(2,1)S(1)}, bf16[2,112,128]{2,1,0:T(8,128)(2,1)S(1)}, u32[]{:S(2)}, u32[]{:S(2)}) collective-permute-start(bf16[2,112,128]{2,1,0:T(8,128)(2,1)S(1)} %pad_maximum_fusion.2), channel_id=1, source_target_pairs={{0,2},{2,0},{4,6},{6,4},{8,10},{10,8},{12,14},{14,12},{1,3},{3,1},... | collective-permute-start | bytes 172040 | tf_op jit(solution)/shard_map/ppermute | solution.py:281
  14.4 1.9 %collective-permute-start.4 = (bf16[6,112,128]{2,1,0:T(8,128)(2,1)S(1)}, bf16[6,112,128]{2,1,0:T(8,128)(2,1)S(1)}, u32[]{:S(2)}, u32[]{:S(2)}) collective-permute-start(bf16[6,112,128]{2,1,0:T(8,128)(2,1)S(1)} %pad_maximum_fusion.1), channel_id=1, source_target_pairs={{0,1},{1,0},{2,3},{3,2},{4,5},{5,4},{6,7},{7,6},{8,9},{9,8},{10,11... | collective-permute-start | bytes 516104 | tf_op jit(solution)/shard_map/ppermute | solution.py:285
  14.5 1.8 %copy-start.5 = (bf16[128,128]{1,0:T(8,128)(2,1)S(1)}, bf16[128,128]{1,0:T(8,128)(2,1)}, u32[]{:S(2)}) copy-start(bf16[128,128]{1,0:T(8,128)(2,1)} %output_ref.1) | copy-start | bytes 98308
  15.0 1.2 %collective-permute-start.5 = (bf16[2,112,128]{2,1,0:T(8,128)(2,1)S(1)}, bf16[2,112,128]{2,1,0:T(8,128)(2,1)S(1)}, u32[]{:S(2)}, u32[]{:S(2)}) collective-permute-start(bf16[2,112,128]{2,1,0:T(8,128)(2,1)S(1)} %collective-permute-done.3), channel_id=1, source_target_pairs={{0,1},{1,0},{2,3},{3,2},{4,5},{5,4},{6,7},{7,6},{8,9},{9,8},{10,11... | collective-permute-start | bytes 172040 | tf_op jit(solution)/shard_map/ppermute | solution.py:286
  15.0 1.2 %copy-start.3 = (bf16[512,128]{1,0:T(8,128)(2,1)S(1)}, bf16[512,128]{1,0:T(8,128)(2,1)}, u32[]{:S(2)}) copy-start(bf16[512,128]{1,0:T(8,128)(2,1)} %down_ref.1) | copy-start | bytes 393220
  15.1 1.2 %copy-start = (bf16[32,32,128]{2,1,0:T(8,128)(2,1)S(1)}, bf16[32,32,128]{2,1,0:T(8,128)(2,1)}, u32[]{:S(2)}) copy-start(bf16[32,32,128]{2,1,0:T(8,128)(2,1)} %outer_ref.1) | copy-start | bytes 786436
  15.1 1.2 %copy-start.1 = (bf16[4,128,128]{2,1,0:T(8,128)(2,1)S(1)}, bf16[4,128,128]{2,1,0:T(8,128)(2,1)}, u32[]{:S(2)}) copy-start(bf16[4,128,128]{2,1,0:T(8,128)(2,1)} %triangle_ref.1) | copy-start | bytes 393220
  15.1 1.2 %copy-start.2 = (bf16[128,512]{1,0:T(8,128)(2,1)S(1)}, bf16[128,512]{1,0:T(8,128)(2,1)}, u32[]{:S(2)}) copy-start(bf16[128,512]{1,0:T(8,128)(2,1)} %up_ref.1) | copy-start | bytes 393220
  15.1 1.2 %copy-start.4 = (bf16[128,128]{1,0:T(8,128)(2,1)S(1)}, bf16[128,128]{1,0:T(8,128)(2,1)}, u32[]{:S(2)}) copy-start(bf16[128,128]{1,0:T(8,128)(2,1)} %gate_ref.1) | copy-start | bytes 98308

commit v16 on v15

--- a/solution.py
+++ b/solution.py
@@ -110,17 +110,68 @@
     return 0.5 * jnp.tanh(0.5 * values) + 0.5
 
 
+def weight_kernel(
+    outer_hbm,
+    triangle_hbm,
+    gate_hbm,
+    output_hbm,
+    up_hbm,
+    down_hbm,
+    packed_hbm,
+    block_ref,
+    right_ref,
+    left_ref,
+    output_ref,
+    up_ref,
+    down_ref,
+    outer_ref,
+    sems,
+):
+    channels, _, wide = outer_hbm.shape
+    loads = [
+        pltpu.make_async_copy(source, target, sems.at[place])
+        for place, (source, target) in enumerate(
+            (
+                (outer_hbm, outer_ref),
+                (triangle_hbm.at[2], right_ref.at[:, pl.ds(0, wide)]),
+                (triangle_hbm.at[3], right_ref.at[:, pl.ds(wide, wide)]),
+                (triangle_hbm.at[0], left_ref.at[:, pl.ds(0, wide)]),
+                (triangle_hbm.at[1], left_ref.at[:, pl.ds(wide, wide)]),
+                (gate_hbm, left_ref.at[:, pl.ds(2 * wide, wide)]),
+                (output_hbm, output_ref),
+                (up_hbm, up_ref),
+                (down_hbm, down_ref),
+            )
+        )
+    ]
+    for load in loads:
+        load.start()
+    parts = block_ref.shape[0]
+    span = channels // parts
+    nothing = jnp.zeros((channels, wide), block_ref.dtype)
+    loads[0].wait()
+    for part in range(parts):
+        for step in range(span + 1):
+            weight = outer_ref[part * span + step % span]
+            at = step * 2 * channels
+            block_ref[part, at : at + channels, :wide] = weight
+            block_ref[part, at : at + channels, wide:] = nothing
+            block_ref[part, at + channels : at + 2 * channels, :wide] = nothing
+            block_ref[part, at + channels : at + 2 * channels, wide:] = weight
+    for load in loads[1:]:
+        load.wait()
+
+
 def update_kernel(
     held_ref,
     other_ref,
-    outer_ref,
-    triangle_ref,
-    gate_ref,
+    block_ref,
+    right_weight_ref,
+    left_weight_ref,
     output_ref,
     up_ref,
     down_ref,
     out_ref,
-    block_ref,
     left_ref,
     right_ref,
     keep_ref,
@@ -132,8 +183,10 @@
 ):
     rows, residues, wide = out_ref.shape
     cores, chips = 2, lax.axis_size("dap")
-    channels = outer_ref.shape[0]
+    channels = left_ref.shape[1]
     sequences = channels
+    parts = block_ref.shape[0]
+    span = channels // parts
     base = rows * residues
     half = wide // 2
     group = cores * rows
@@ -141,18 +194,6 @@
     second_core = lax.axis_index("sub") == 1
     bf16 = jnp.bfloat16
     f32 = jnp.float32
-
-    parts = block_ref.shape[0]
-    span = channels // parts
-    nothing = jnp.zeros((channels, wide), bf16)
-    for part in range(parts):
-        for step in range(span + 1):
-            weight = outer_ref[part * span + step % span]
-            at = step * 2 * channels
-            block_ref[part, at : at + channels, :wide] = weight
-            block_ref[part, at : at + channels, wide:] = nothing
-            block_ref[part, at + channels : at + 2 * channels, :wide] = nothing
-            block_ref[part, at + channels : at + 2 * channels, wide:] = weight
 
     lane = lax.broadcasted_iota(jnp.int32, (channels, wide), 1)
     lane_block = lane // channels
@@ -225,9 +266,9 @@
             second_ref[part], block_ref[part, 2 * channels :], preferred_element_type=f32
         )
 
-    right_weight = jnp.concatenate([triangle_ref[2], triangle_ref[3]], axis=1)
-    right_tri = []
     stride = 8
+    sums = [[jnp.zeros((residues, wide), f32) for _ in range(2)] for _ in range(rows)]
+    gates = [[] for _ in range(rows)]
     for first in range(0, residues, stride):
         normed = []
         for k in range(first, first + stride):
@@ -240,31 +281,35 @@
             ln_one = layer_norm(pair_one)
             ln_one_ref[k] = ln_one
             normed.append(ln_one.astype(bf16))
+        own_ln = jnp.concatenate(
+            [ln_one_ref[first : first + stride, start + row] for row in range(rows)], axis=0
+        ).astype(bf16)
+        both = jnp.dot(own_ln, left_weight_ref[...], preferred_element_type=f32)
+        own_mask = jnp.concatenate([mask[first : first + stride]] * rows, axis=0)
+        left_tri = sigmoid(both[:, :wide]) * both[:, wide : 2 * wide] * own_mask
+        left_tri = left_tri.astype(bf16).astype(f32)
+        gate_out = sigmoid(both[:, 2 * wide :])
         both = jnp.dot(
-            jnp.concatenate(normed, axis=0), right_weight, preferred_element_type=f32
-        )
-        right_tri.append((sigmoid(both[:, :wide]) * both[:, wide:]).astype(bf16).astype(f32))
+            jnp.concatenate(normed, axis=0), right_weight_ref[...], preferred_element_type=f32
+        )
+        right_tri = (sigmoid(both[:, :wide]) * both[:, wide:]).astype(bf16).astype(f32)
+        for row in range(rows):
+            gates[row].append(gate_out[row * stride : (row + 1) * stride])
+            for k in range(stride):
+                at = row * stride + k
+                sums[row][k % 2] += (
+                    left_tri[at : at + 1] * right_tri[k * residues : (k + 1) * residues]
+                )
 
     own_pair = jnp.concatenate([pair_one_ref[:, start + row] for row in range(rows)], axis=0)
-    own_ln = jnp.concatenate([ln_one_ref[:, start + row] for row in range(rows)], axis=0).astype(bf16)
-    left_weight = jnp.concatenate([triangle_ref[0], triangle_ref[1]], axis=1)
-    both = jnp.dot(own_ln, left_weight, preferred_element_type=f32)
-    left_tri = sigmoid(both[:, :wide]) * both[:, wide:] * jnp.concatenate([mask] * rows, axis=0)
-    left_tri = left_tri.astype(bf16).astype(f32)
+    gate_out = jnp.concatenate(sum(gates, []), axis=0)
     products = []
     for row in range(rows):
-        sums = [jnp.zeros((residues, wide), f32) for _ in range(4)]
-        for k in range(residues):
-            at = row * residues + k
-            place = (k % stride) * residues
-            sums[k % 4] += left_tri[at : at + 1] * right_tri[k // stride][place : place + residues]
-        total = (sums[0] + sums[1]) + (sums[2] + sums[3])
         own_mask = keep_ref[pl.ds(start + row, 1), :][:, sequences : sequences + 1]
-        products.append(total * (mask * own_mask))
+        products.append((sums[row][0] + sums[row][1]) * (mask * own_mask))
     product = jnp.concatenate(products, axis=0).astype(bf16).astype(f32)
     normed = layer_norm(product).astype(bf16)
     update = jnp.dot(normed, output_ref[...], preferred_element_type=f32)
-    gate_out = sigmoid(jnp.dot(own_ln, gate_ref[...], preferred_element_type=f32))
     pair_two = (own_pair + gate_out * update).astype(bf16).astype(f32)
     ln_two = layer_norm(pair_two).astype(bf16)
     hidden = jnp.maximum(jnp.dot(ln_two, up_ref[...], preferred_element_type=f32), 0.0).astype(bf16)
@@ -344,17 +389,48 @@
             )
         )
     )
-    held, other = gather_all(packed)
     cores, chips = lax.axis_size("sub"), lax.axis_size("dap")
     group = cores * rows
     parts = 2
+    hidden = transition_up_weight.shape[1]
+    weights = pl.pallas_call(
+        weight_kernel,
+        out_shape=(
+            pltpu.VMEM((parts, (channels // parts + 1) * 2 * channels, 2 * wide), jnp.bfloat16),
+            pltpu.VMEM((wide, 2 * wide), jnp.bfloat16),
+            pltpu.VMEM((wide, 3 * wide), jnp.bfloat16),
+            pltpu.VMEM((wide, wide), jnp.bfloat16),
+            pltpu.VMEM((wide, hidden), jnp.bfloat16),
+            pltpu.VMEM((hidden, wide), jnp.bfloat16),
+        ),
+        in_specs=[hbm] * 6 + [pl.BlockSpec(memory_space=pl.ANY)],
+        out_specs=(vector,) * 6,
+        scratch_shapes=[
+            pltpu.VMEM(outer_output_weight.shape, jnp.bfloat16),
+            pltpu.SemaphoreType.DMA((9,)),
+        ],
+        compiler_params=pltpu.CompilerParams(vmem_limit_bytes=8 << 20),
+    )(
+        *(
+            pltpu.with_memory_space_constraint(array, pltpu.HBM)
+            for array in (
+                outer_output_weight,
+                triangle_input_weight,
+                triangle_gate,
+                triangle_output_weight,
+                transition_up_weight,
+                transition_down_weight,
+            )
+        ),
+        packed,
+    )
+    held, other = gather_all(packed)
     return pl.pallas_call(
         update_kernel,
         out_shape=jax.ShapeDtypeStruct(pairwise_state.shape, jnp.bfloat16),
         in_specs=[vector] * 8,
         out_specs=vector,
         scratch_shapes=[
-            pltpu.VMEM((parts, (channels // parts + 1) * 2 * channels, 2 * wide), jnp.bfloat16),
             pltpu.VMEM((residues, channels, wide), jnp.float32),
             pltpu.VMEM((2, group * sequences, chips * wide), jnp.bfloat16),
             pltpu.VMEM((residues, wide), jnp.float32),
@@ -368,12 +444,7 @@
     )(
         held,
         other,
-        outer_output_weight,
-        triangle_input_weight,
-        triangle_gate,
-        triangle_output_weight,
-        transition_up_weight,
-        transition_down_weight,
+        *weights,
     )
 
 

time: 20.4 us -> 21.5 us (1.054)
  Pallas kernels: 5.22 us -> 6.37 us
  waiting for transfers between devices: 6.96 us -> 6.47 us
  starting transfers between devices: 7.78 us -> 8.26 us
    ppermute x1, waiting for transfers between devices: 1.86 us -> 0.62 us  [gather_all(): lax.ppermute(packed[None], 'dap', [(src, src ^ half) for src in range(dap...]
    pallas_call x0 -> x1, Pallas kernels: none -> 1.23 us  [shards_replicated(): pl.pallas_call(weight_kernel, out_shape=(pltpu.VMEM((parts, (channels //...]
    ppermute x3, waiting for transfers between devices: 4 us -> 4.92 us  [gather_all(): lax.ppermute(both, 'dap', [(src, src ^ offset) for src in range(dap_count)])]
    ppermute x1, starting transfers between devices: 0.06 us -> 0.49 us  [gather_all(): late = lax.ppermute(held[-1], 'sub', sibling)]
  transfers between devices with their start and end apart: 6 -> 6, of which waited for: 5 -> 4; matrix products, arithmetic and copies ran while one was open for 0% -> 0% of each run, Pallas kernels for 0% -> 6%
where the time goes in v16:
time: 21.5 us; the launch traced here: 21.3 us
  starting transfers between devices  8.26 us (38%)
  waiting for transfers between devices  6.47 us (30%)
  Pallas kernels  6.37 us (30%)
    ppermute x3, waiting for transfers between devices, gather_all(): lax.ppermute(both, 'dap', [(src, src ^ offset) for src in range(dap_count)])  4.92 us
    ppermute x1, starting transfers between devices, gather_all(): lax.ppermute(packed[None], 'dap', [(src, src ^ half) for src in range(dap...  4.1 us
    pallas_call x1, Pallas kernels, shards_replicated(): pl.pallas_call(update_kernel, out_shape=jax.ShapeDtypeStruct(pairwise_sta...  3.83 us
    ppermute x3, starting transfers between devices, gather_all(): lax.ppermute(both, 'dap', [(src, src ^ offset) for src in range(dap_count)])  3.59 us
    pallas_call x1, Pallas kernels, shards_replicated(): pl.pallas_call(pack_kernel, out_shape=jax.ShapeDtypeStruct((rows * residu...  1.31 us
    pallas_call x1, Pallas kernels, shards_replicated(): pl.pallas_call(weight_kernel, out_shape=(pltpu.VMEM((parts, (channels //...  1.23 us
    ppermute x1, waiting for transfers between devices, gather_all(): late = lax.ppermute(held[-1], 'sub', sibling)  0.93 us
    ppermute x1, waiting for transfers between devices, gather_all(): lax.ppermute(packed[None], 'dap', [(src, src ^ half) for src in range(dap...  0.62 us
  transfers between devices with their start and end apart: 6, of which 4 were waited for; matrix products, arithmetic and copies ran while one was open for 0% of the time, Pallas kernels for 6%

profile of v16, /device:TPU:0, one launch (start us, length us, event | category | flops | bytes accessed | tf_op | source)
XLA Modules:
  0.0 21.3 jit_solution(8986052427885916286)
XLA Ops:
  0.0 1.3 %shard_map.109.packed_hbm = bf16[112,128]{1,0:T(8,128)(2,1)S(1)} custom-call(s32[32]{0:T(128)} %mask_hbm.1, s32[2,32]{1,0:T(2,128)} %bitcast.8, bf16[32,2,256]{2,1,0:T(2,128)(2,1)} %state_hbm.1, bf16[2,32,256]{2,1,0:T(8,128)(2,1)} %bitcast.7, bf16[2,32,128]{2,1,0:T(8,128)(2,1)} %pair_hbm.1), custom_call_target="tpu_custom_call" | custom-call | tf_op jit(solution)/shard_map/pallas_call | solution.py:366
  1.3 4.1 %collective-permute-start = (bf16[1,112,128]{2,1,0:T(8,128)(2,1)S(1)}, bf16[1,112,128]{2,1,0:T(8,128)(2,1)S(1)}, u32[]{:S(2)}, u32[]{:S(2)}) collective-permute-start(bf16[1,112,128]{2,1,0:T(8,128)(2,1)S(1)} %bitcast.4), channel_id=1, source_target_pairs={{0,8},{2,10},{4,12},{6,14},{8,0},{10,2},{12,4},{14,6},{1,9},{3,11}... | collective-permute-start | bytes 86024 | tf_op jit(solution)/shard_map/ppermute | solution.py:323
  5.4 1.2 %shard_map.110 = (bf16[2,1088,256]{2,1,0:T(8,128)(2,1)S(1)}, bf16[128,256]{1,0:T(8,128)(2,1)S(1)}, bf16[128,384]{1,0:T(8,128)(2,1)S(1)}, bf16[128,128]{1,0:T(8,1...) custom-call(bf16[32,32,128]{2,1,0:T(8,128)(2,1)} %outer_hbm.1, ...), custom_call_target="tpu_custom_call" | custom-call | tf_op jit(solution)/shard_map/pallas_call | solution.py:396
  6.7 0.6 %collective-permute-done = bf16[1,112,128]{2,1,0:T(8,128)(2,1)S(1)} collective-permute-done((bf16[1,112,128]{2,1,0:T(8,128)(2,1)S(1)}, bf16[1,112,128]{2,1,0:T(8,128)(2,1)S(1)}, u32[]{:S(2)}, u32[]{:S(2)}) %collective-permute-start) | collective-permute-done | bytes 28704 | tf_op jit(solution)/shard_map/ppermute | solution.py:323
  7.3 2.1 %collective-permute-start.3 = (bf16[2,112,128]{2,1,0:T(8,128)(2,1)S(1)}, bf16[2,112,128]{2,1,0:T(8,128)(2,1)S(1)}, u32[]{:S(2)}, u32[]{:S(2)}) collective-permute-start(bf16[2,112,128]{2,1,0:T(8,128)(2,1)S(1)} %pad_maximum_fusion.2), channel_id=1, source_target_pairs={{0,2},{2,0},{4,6},{6,4},{8,10},{10,8},{12,14},{14,12},{1,3},{3,1},... | collective-permute-start | bytes 172040 | tf_op jit(solution)/shard_map/ppermute | solution.py:326
  9.3 1.4 %collective-permute-start.2 = (bf16[2,112,128]{2,1,0:T(8,128)(2,1)S(1)}, bf16[2,112,128]{2,1,0:T(8,128)(2,1)S(1)}, u32[]{:S(2)}, u32[]{:S(2)}) collective-permute-start(bf16[2,112,128]{2,1,0:T(8,128)(2,1)S(1)} %pad_maximum_fusion.2), channel_id=1, source_target_pairs={{0,4},{2,6},{4,0},{6,2},{8,12},{10,14},{12,8},{14,10},{1,5},{3,7},... | collective-permute-start | bytes 172040 | tf_op jit(solution)/shard_map/ppermute | solution.py:326
  10.7 0.1 collective-permute-start.1
  10.9 2.6 %collective-permute-done.2 = bf16[2,112,128]{2,1,0:T(8,128)(2,1)S(1)} collective-permute-done((bf16[2,112,128]{2,1,0:T(8,128)(2,1)S(1)}, bf16[2,112,128]{2,1,0:T(8,128)(2,1)S(1)}, u32[]{:S(2)}, u32[]{:S(2)}) %collective-permute-start.2) | collective-permute-done | bytes 57376 | tf_op jit(solution)/shard_map/ppermute | solution.py:326
  13.5 2.3 %collective-permute-done.1 = bf16[2,112,128]{2,1,0:T(8,128)(2,1)S(1)} collective-permute-done((bf16[2,112,128]{2,1,0:T(8,128)(2,1)S(1)}, bf16[2,112,128]{2,1,0:T(8,128)(2,1)S(1)}, u32[]{:S(2)}, u32[]{:S(2)}) %collective-permute-start.1) | collective-permute-done | bytes 57376 | tf_op jit(solution)/shard_map/ppermute | solution.py:326
  15.8 0.1 collective-permute-start.4
  15.9 0.0 collective-permute-done.3
  15.9 0.5 %collective-permute-start.5 = (bf16[2,112,128]{2,1,0:T(8,128)(2,1)S(1)}, bf16[2,112,128]{2,1,0:T(8,128)(2,1)S(1)}, u32[]{:S(2)}, u32[]{:S(2)}) collective-permute-start(bf16[2,112,128]{2,1,0:T(8,128)(2,1)S(1)} %collective-permute-done.3), channel_id=1, source_target_pairs={{0,1},{1,0},{2,3},{3,2},{4,5},{5,4},{6,7},{7,6},{8,9},{9,8},{10,11... | collective-permute-start | bytes 172040 | tf_op jit(solution)/shard_map/ppermute | solution.py:331
  16.5 0.9 %collective-permute-done.5 = bf16[2,112,128]{2,1,0:T(8,128)(2,1)S(1)} collective-permute-done((bf16[2,112,128]{2,1,0:T(8,128)(2,1)S(1)}, bf16[2,112,128]{2,1,0:T(8,128)(2,1)S(1)}, u32[]{:S(2)}, u32[]{:S(2)}) %collective-permute-start.5) | collective-permute-done | bytes 57376 | tf_op jit(solution)/shard_map/ppermute | solution.py:331
  17.4 0.0 collective-permute-done.4
  17.4 3.8 %shard_map.111 = bf16[2,32,128]{2,1,0:T(8,128)(2,1)} custom-call(bf16[8,112,128]{2,1,0:T(8,128)(2,1)S(1)} %constant_dynamic-update-slice_fusion.held_ref, bf16[8,112,128]{2,1,0:T(8,128)(2,1)S(1)} %pad_maximum_fusion.other_ref, bf16[2,1088,256]{2,1,0:T(8,128)(2,1)S(1)} %get-tuple-element.11.block_ref, ...), custom_call_target="tpu_custom_call" | custom-call | tf_op jit(solution)/shard_map/pallas_call | solution.py:428
  (8 shorter events, 0.1 us)
Async XLA Ops:
  1.3 6.0 %collective-permute-start = (bf16[1,112,128]{2,1,0:T(8,128)(2,1)S(1)}, bf16[1,112,128]{2,1,0:T(8,128)(2,1)S(1)}, u32[]{:S(2)}, u32[]{:S(2)}) collective-permute-start(bf16[1,112,128]{2,1,0:T(8,128)(2,1)S(1)} %bitcast.4), channel_id=1, source_target_pairs={{0,8},{2,10},{4,12},{6,14},{8,0},{10,2},{12,4},{14,6},{1,9},{3,11}... | collective-permute-start | bytes 86024 | tf_op jit(solution)/shard_map/ppermute | solution.py:323
  7.3 8.6 %collective-permute-start.3 = (bf16[2,112,128]{2,1,0:T(8,128)(2,1)S(1)}, bf16[2,112,128]{2,1,0:T(8,128)(2,1)S(1)}, u32[]{:S(2)}, u32[]{:S(2)}) collective-permute-start(bf16[2,112,128]{2,1,0:T(8,128)(2,1)S(1)} %pad_maximum_fusion.2), channel_id=1, source_target_pairs={{0,2},{2,0},{4,6},{6,4},{8,10},{10,8},{12,14},{14,12},{1,3},{3,1},... | collective-permute-start | bytes 172040 | tf_op jit(solution)/shard_map/ppermute | solution.py:326
  9.3 4.2 %collective-permute-start.2 = (bf16[2,112,128]{2,1,0:T(8,128)(2,1)S(1)}, bf16[2,112,128]{2,1,0:T(8,128)(2,1)S(1)}, u32[]{:S(2)}, u32[]{:S(2)}) collective-permute-start(bf16[2,112,128]{2,1,0:T(8,128)(2,1)S(1)} %pad_maximum_fusion.2), channel_id=1, source_target_pairs={{0,4},{2,6},{4,0},{6,2},{8,12},{10,14},{12,8},{14,10},{1,5},{3,7},... | collective-permute-start | bytes 172040 | tf_op jit(solution)/shard_map/ppermute | solution.py:326
  10.7 5.1 %collective-permute-start.1 = (bf16[2,112,128]{2,1,0:T(8,128)(2,1)S(1)}, bf16[2,112,128]{2,1,0:T(8,128)(2,1)S(1)}, u32[]{:S(2)}, u32[]{:S(2)}) collective-permute-start(bf16[2,112,128]{2,1,0:T(8,128)(2,1)S(1)} %pad_maximum_fusion.2), channel_id=1, source_target_pairs={{0,6},{2,4},{4,2},{6,0},{8,14},{10,12},{12,10},{14,8},{1,7},{3,5},... | collective-permute-start | bytes 172040 | tf_op jit(solution)/shard_map/ppermute | solution.py:326
  15.8 1.6 %collective-permute-start.4 = (bf16[6,112,128]{2,1,0:T(8,128)(2,1)S(1)}, bf16[6,112,128]{2,1,0:T(8,128)(2,1)S(1)}, u32[]{:S(2)}, u32[]{:S(2)}) collective-permute-start(bf16[6,112,128]{2,1,0:T(8,128)(2,1)S(1)} %pad_maximum_fusion.1), channel_id=1, source_target_pairs={{0,1},{1,0},{2,3},{3,2},{4,5},{5,4},{6,7},{7,6},{8,9},{9,8},{10,11... | collective-permute-start | bytes 516104 | tf_op jit(solution)/shard_map/ppermute | solution.py:330
  15.9 1.5 %collective-permute-start.5 = (bf16[2,112,128]{2,1,0:T(8,128)(2,1)S(1)}, bf16[2,112,128]{2,1,0:T(8,128)(2,1)S(1)}, u32[]{:S(2)}, u32[]{:S(2)}) collective-permute-start(bf16[2,112,128]{2,1,0:T(8,128)(2,1)S(1)} %collective-permute-done.3), channel_id=1, source_target_pairs={{0,1},{1,0},{2,3},{3,2},{4,5},{5,4},{6,7},{7,6},{8,9},{9,8},{10,11... | collective-permute-start | bytes 172040 | tf_op jit(solution)/shard_map/ppermute | solution.py:331

commit v17 on v16

--- a/solution.py
+++ b/solution.py
@@ -3,7 +3,7 @@
 from jax import lax
 from jax.experimental import pallas as pl
 from jax.experimental.pallas import tpu as pltpu
-from jax.sharding import PartitionSpec as P
+from jax.sharding import Mesh, PartitionSpec as P
 
 REPLICATED_PAIR_BYTES = 1 << 20
 
@@ -33,7 +33,8 @@
 
 
 def first_row(rows):
-    return (lax.axis_index("dap") * lax.axis_size("sub") + lax.axis_index("sub")) * rows
+    chip = lax.axis_index("far") * lax.axis_size("near") + lax.axis_index("near")
+    return (chip * lax.axis_size("sub") + lax.axis_index("sub")) * rows
 
 
 def pack_kernel(
@@ -182,7 +183,7 @@
     ln_one_ref,
 ):
     rows, residues, wide = out_ref.shape
-    cores, chips = 2, lax.axis_size("dap")
+    cores, chips = 2, held_ref.shape[0]
     channels = left_ref.shape[1]
     sequences = channels
     parts = block_ref.shape[0]
@@ -318,30 +319,19 @@
 
 
 def gather_all(packed):
-    dap_count = lax.axis_size("dap")
-    half = dap_count // 2
-    far = lax.ppermute(packed[None], "dap", [(src, src ^ half) for src in range(dap_count)])
+    near_count = lax.axis_size("near")
+    sibling = [(0, 1), (1, 0)]
+    far = lax.ppermute(packed[None], "far", sibling)
     both = jnp.concatenate([packed[None], far], axis=0)
-    held = [both] + [
-        lax.ppermute(both, "dap", [(src, src ^ offset) for src in range(dap_count)])
-        for offset in swap_order(dap_count)
-    ]
-    sibling = [(0, 1), (1, 0)]
-    early = lax.ppermute(jnp.concatenate(held[:-1], axis=0), "sub", sibling)
-    late = lax.ppermute(held[-1], "sub", sibling)
-    return jnp.concatenate(held, axis=0), jnp.concatenate([early, late], axis=0)
-
-
-def swap_order(dap_count):
-    return list(range(dap_count // 2 - 1, 0, -1))
+    copies = jnp.broadcast_to(both, (near_count,) + both.shape)
+    held = lax.all_to_all(copies, "near", split_axis=0, concat_axis=0)
+    held = held.reshape((-1,) + packed.shape)
+    return held, lax.ppermute(held, "sub", sibling)
 
 
 def block_place(chip, chips):
-    offset = lax.bitwise_xor(lax.axis_index("dap"), chip)
     half = chips // 2
-    near = jnp.where(offset >= half, offset - half, offset)
-    turn = jnp.where(near == 0, 0, half - near)
-    return 2 * turn + jnp.where(offset >= half, 1, 0)
+    return 2 * (chip % half) + lax.bitwise_xor(lax.axis_index("far"), chip // half)
 
 
 def shards_replicated(
@@ -389,7 +379,7 @@
             )
         )
     )
-    cores, chips = lax.axis_size("sub"), lax.axis_size("dap")
+    cores, chips = lax.axis_size("sub"), lax.axis_size("far") * lax.axis_size("near")
     group = cores * rows
     parts = 2
     hidden = transition_up_weight.shape[1]
@@ -552,16 +542,33 @@
 
     small = mesh.shape["sub"] == 2 and mesh.shape["dap"] == 8
 
-    def body(pairwise_state, *rest):
+    def distributed(*arrays):
+        return jax.shard_map(
+            shards,
+            mesh=mesh,
+            in_specs=placed,
+            out_specs=P(("crop", "dap", "sub"), None, None),
+            check_vma=False,
+        )(*arrays)
+
+    def replicated(*arrays):
+        rows = ("far", "near", "sub")
+        fine = Mesh(
+            mesh.devices.reshape(mesh.shape["crop"], 2, -1, mesh.shape["sub"]), ("crop",) + rows
+        )
+        return jax.shard_map(
+            shards_replicated,
+            mesh=fine,
+            in_specs=(P(("crop",) + rows, None, None), P("crop", rows, None), P("crop", rows))
+            + placed[3:],
+            out_specs=P(("crop",) + rows, None, None),
+            check_vma=False,
+        )(*arrays)
+
+    def whole(pairwise_state, *rest):
         residues, channels = pairwise_state.shape[1:]
         if small and residues * residues * channels * 2 <= REPLICATED_PAIR_BYTES:
-            return shards_replicated(pairwise_state, *rest)
-        return shards(pairwise_state, *rest)
-
-    return jax.shard_map(
-        body,
-        mesh=mesh,
-        in_specs=placed,
-        out_specs=P(("crop", "dap", "sub"), None, None),
-        check_vma=False,
-    )
+            return replicated(pairwise_state, *rest)
+        return distributed(pairwise_state, *rest)
+
+    return whole

time: 21.5 us -> 22.4 us (1.042)
  blocking collectives: 0 us -> 9.53 us
  waiting for transfers between devices: 6.47 us -> 2.11 us
  starting transfers between devices: 8.26 us -> 4.1 us
    all_to_all x0 -> x1, blocking collectives: none -> 9.53 us  [gather_all(): held = lax.all_to_all(copies, 'near', split_axis=0, concat_axis=0)]
    ppermute x6 -> x2, waiting for transfers between devices: 6.47 us -> 2.11 us  [the longest x1 1.86 us: gather_all(): far = lax.ppermute(packed[None], 'far', sibling)]
    ppermute x6 -> x2, starting transfers between devices: 8.26 us -> 4.1 us  [the longest x1 4.1 us: gather_all(): far = lax.ppermute(packed[None], 'far', sibling)]
  transfers between devices with their start and end apart: 6 -> 2, of which waited for: 4 -> 2; matrix products, arithmetic and copies ran while one was open for 0% -> 0% of each run, Pallas kernels for 6% -> 6%
where the time goes in v17:
time: 22.4 us; the launch traced here: 22.2 us
  blocking collectives  9.53 us (43%)
  Pallas kernels  6.35 us (28%)
  starting transfers between devices  4.1 us (18%)
  waiting for transfers between devices  2.11 us (9%)
    all_to_all x1, blocking collectives, gather_all(): held = lax.all_to_all(copies, 'near', split_axis=0, concat_axis=0)  9.53 us
    ppermute x1, starting transfers between devices, gather_all(): far = lax.ppermute(packed[None], 'far', sibling)  4.1 us
    pallas_call x1, Pallas kernels, shards_replicated(): pl.pallas_call(update_kernel, out_shape=jax.ShapeDtypeStruct(pairwise_sta...  3.81 us
    ppermute x1, waiting for transfers between devices, gather_all(): far = lax.ppermute(packed[None], 'far', sibling)  1.86 us
    pallas_call x1, Pallas kernels, shards_replicated(): pl.pallas_call(pack_kernel, out_shape=jax.ShapeDtypeStruct((rows * residu...  1.31 us
    pallas_call x1, Pallas kernels, shards_replicated(): pl.pallas_call(weight_kernel, out_shape=(pltpu.VMEM((parts, (channels //...  1.23 us
  transfers between devices with their start and end apart: 2, of which 2 were waited for; matrix products, arithmetic and copies ran while one was open for 0% of the time, Pallas kernels for 6%

profile of v17, /device:TPU:0, one launch (start us, length us, event | category | flops | bytes accessed | tf_op | source)
XLA Modules:
  0.0 22.2 jit_solution(11718312830426902318)
XLA Ops:
  0.0 1.3 %shard_map.109.packed_hbm = bf16[112,128]{1,0:T(8,128)(2,1)S(1)} custom-call(s32[32]{0:T(128)} %mask_hbm.1, s32[2,32]{1,0:T(2,128)} %bitcast.9, bf16[32,2,256]{2,1,0:T(2,128)(2,1)} %state_hbm.1, bf16[2,32,256]{2,1,0:T(8,128)(2,1)} %bitcast.8, bf16[2,32,128]{2,1,0:T(8,128)(2,1)} %pair_hbm.1), custom_call_target="tpu_custom_call" | custom-call | tf_op jit(solution)/shard_map/pallas_call | solution.py:356
  1.3 4.1 %collective-permute-start = (bf16[1,112,128]{2,1,0:T(8,128)(2,1)S(1)}, bf16[1,112,128]{2,1,0:T(8,128)(2,1)S(1)}, u32[]{:S(2)}, u32[]{:S(2)}) collective-permute-start(bf16[1,112,128]{2,1,0:T(8,128)(2,1)S(1)} %bitcast.6), channel_id=1, source_target_pairs={{0,8},{8,0},{1,9},{9,1},{2,10},{10,2},{3,11},{11,3},{4,12},{12,4},... | collective-permute-start | bytes 86024 | tf_op jit(solution)/shard_map/ppermute | solution.py:324
  5.4 1.9 %collective-permute-done = bf16[1,112,128]{2,1,0:T(8,128)(2,1)S(1)} collective-permute-done((bf16[1,112,128]{2,1,0:T(8,128)(2,1)S(1)}, bf16[1,112,128]{2,1,0:T(8,128)(2,1)S(1)}, u32[]{:S(2)}, u32[]{:S(2)}) %collective-permute-start) | collective-permute-done | bytes 28704 | tf_op jit(solution)/shard_map/ppermute | solution.py:324
  7.3 9.5 %all_to_all.5 = bf16[4,2,112,128]{3,2,1,0:T(8,128)(2,1)S(1)} all-to-all(bf16[4,2,112,128]{3,2,1,0:T(8,128)(2,1)S(1)} %broadcast_in_dim.8), channel_id=1, replica_groups=mesh['crop'=2,'far'=2,'near'=4,'sub'=2] {'near'}, dimensions={0} | all-to-all | bytes 458752 | tf_op jit(solution)/shard_map/all_to_all | solution.py:327
  16.9 0.0 collective-permute-start.1
  16.9 1.2 %shard_map.110 = (bf16[2,1088,256]{2,1,0:T(8,128)(2,1)S(1)}, bf16[128,256]{1,0:T(8,128)(2,1)S(1)}, bf16[128,384]{1,0:T(8,128)(2,1)S(1)}, bf16[128,128]{1,0:T(8,1...) custom-call(bf16[32,32,128]{2,1,0:T(8,128)(2,1)} %outer_hbm.1, ...), custom_call_target="tpu_custom_call" | custom-call | tf_op jit(solution)/shard_map/pallas_call | solution.py:386
  18.1 0.2 %collective-permute-done.1.other_ref = bf16[8,112,128]{2,1,0:T(8,128)(2,1)S(1)} collective-permute-done((bf16[8,112,128]{2,1,0:T(8,128)(2,1)S(1)}, bf16[8,112,128]{2,1,0:T(8,128)(2,1)S(1)}, u32[]{:S(2)}, u32[]{:S(2)}) %collective-permute-start.1) | collective-permute-done | bytes 229408 | tf_op jit(solution)/shard_map/ppermute | solution.py:329
  18.3 3.8 %shard_map.111 = bf16[2,32,128]{2,1,0:T(8,128)(2,1)} custom-call(bf16[8,112,128]{2,1,0:T(8,128)(2,1)S(1)} %bitcast.5, bf16[8,112,128]{2,1,0:T(8,128)(2,1)S(1)} %collective-permute-done.1.other_ref, bf16[2,1088,256]{2,1,0:T(8,128)(2,1)S(1)} %get-tuple-element.11.block_ref, bf16[128,256]{1,0:T(8,128)(2,1)S(1)} %get-tuple-element.12.right_weight_ref, ...), custom_call_target="tpu_custom_call" | custom-call | tf_op jit(solution)/shard_map/pallas_call | solution.py:418
  (2 shorter events, 0.0 us)
Async XLA Ops:
  1.3 6.0 %collective-permute-start = (bf16[1,112,128]{2,1,0:T(8,128)(2,1)S(1)}, bf16[1,112,128]{2,1,0:T(8,128)(2,1)S(1)}, u32[]{:S(2)}, u32[]{:S(2)}) collective-permute-start(bf16[1,112,128]{2,1,0:T(8,128)(2,1)S(1)} %bitcast.6), channel_id=1, source_target_pairs={{0,8},{8,0},{1,9},{9,1},{2,10},{10,2},{3,11},{11,3},{4,12},{12,4},... | collective-permute-start | bytes 86024 | tf_op jit(solution)/shard_map/ppermute | solution.py:324
  16.9 1.5 %collective-permute-start.1 = (bf16[8,112,128]{2,1,0:T(8,128)(2,1)S(1)}, bf16[8,112,128]{2,1,0:T(8,128)(2,1)S(1)}, u32[]{:S(2)}, u32[]{:S(2)}) collective-permute-start(bf16[8,112,128]{2,1,0:T(8,128)(2,1)S(1)} %bitcast.4), channel_id=1, source_target_pairs={{0,1},{1,0},{2,3},{3,2},{4,5},{5,4},{6,7},{7,6},{8,9},{9,8},{10,11... | collective-permute-start | bytes 688136 | tf_op jit(solution)/shard_map/ppermute | solution.py:329

commit v18 on v15

--- a/solution.py
+++ b/solution.py
@@ -288,14 +288,15 @@
 
 
 def swap_order(dap_count):
-    return list(range(dap_count // 2 - 1, 0, -1))
+    near = dap_count // 2
+    return [1, near - 1] + list(range(2, near - 1))
 
 
 def block_place(chip, chips):
     offset = lax.bitwise_xor(lax.axis_index("dap"), chip)
     half = chips // 2
     near = jnp.where(offset >= half, offset - half, offset)
-    turn = jnp.where(near == 0, 0, half - near)
+    turn = jnp.where(near > 1, jnp.where(near == half - 1, 2, near + 1), near)
     return 2 * turn + jnp.where(offset >= half, 1, 0)
 
 
@@ -347,7 +348,7 @@
     held, other = gather_all(packed)
     cores, chips = lax.axis_size("sub"), lax.axis_size("dap")
     group = cores * rows
-    parts = 2
+    parts = 1
     return pl.pallas_call(
         update_kernel,
         out_shape=jax.ShapeDtypeStruct(pairwise_state.shape, jnp.bfloat16),

time: 20.4 us -> 20.3 us (level)
  waiting for transfers between devices: 6.96 us -> 6.65 us
  starting transfers between devices: 7.78 us -> 7.99 us
where the time goes in v18:
time: 20.3 us; the launch traced here: 20.1 us
  starting transfers between devices  7.99 us (39%)
  waiting for transfers between devices  6.65 us (33%)
  Pallas kernels  5.15 us (25%)
    ppermute x1, starting transfers between devices, gather_all(): lax.ppermute(packed[None], 'dap', [(src, src ^ half) for src in range(dap...  4.1 us
    ppermute x3, waiting for transfers between devices, gather_all(): lax.ppermute(both, 'dap', [(src, src ^ offset) for src in range(dap_count)])  3.85 us
    pallas_call x1, Pallas kernels, shards_replicated(): pl.pallas_call(update_kernel, out_shape=jax.ShapeDtypeStruct(pairwise_sta...  3.84 us
    ppermute x3, starting transfers between devices, gather_all(): lax.ppermute(both, 'dap', [(src, src ^ offset) for src in range(dap_count)])  3.59 us
    ppermute x1, waiting for transfers between devices, gather_all(): lax.ppermute(packed[None], 'dap', [(src, src ^ half) for src in range(dap...  1.86 us
    pallas_call x1, Pallas kernels, shards_replicated(): pl.pallas_call(pack_kernel, out_shape=jax.ShapeDtypeStruct((rows * residu...  1.31 us
    ppermute x1, waiting for transfers between devices, gather_all(): late = lax.ppermute(held[-1], 'sub', sibling)  0.93 us
  transfers between devices with their start and end apart: 6, of which 5 were waited for; matrix products, arithmetic and copies ran while one was open for 0% of the time, Pallas kernels for 0%

profile of v18, /device:TPU:0, one launch (start us, length us, event | category | flops | bytes accessed | tf_op | source)
XLA Modules:
  0.0 20.1 jit_solution(12054800574948762925)
XLA Ops:
  0.0 1.3 %shard_map.109 = bf16[112,128]{1,0:T(8,128)(2,1)S(1)} custom-call(s32[32]{0:T(128)} %mask_hbm.1, s32[2,32]{1,0:T(2,128)} %bitcast.8, bf16[32,2,256]{2,1,0:T(2,128)(2,1)} %state_hbm.1, bf16[2,32,256]{2,1,0:T(8,128)(2,1)} %bitcast.7, bf16[2,32,128]{2,1,0:T(8,128)(2,1)} %pair_hbm.1), custom_call_target="tpu_custom_call" | custom-call | tf_op jit(solution)/shard_map/pallas_call | solution.py:322
  1.3 4.1 %collective-permute-start = (bf16[1,112,128]{2,1,0:T(8,128)(2,1)S(1)}, bf16[1,112,128]{2,1,0:T(8,128)(2,1)S(1)}, u32[]{:S(2)}, u32[]{:S(2)}) collective-permute-start(bf16[1,112,128]{2,1,0:T(8,128)(2,1)S(1)} %bitcast.4), channel_id=1, source_target_pairs={{0,8},{2,10},{4,12},{6,14},{8,0},{10,2},{12,4},{14,6},{1,9},{3,11}... | collective-permute-start | bytes 86024 | tf_op jit(solution)/shard_map/ppermute | solution.py:278
  5.4 1.9 %collective-permute-done = bf16[1,112,128]{2,1,0:T(8,128)(2,1)S(1)} collective-permute-done((bf16[1,112,128]{2,1,0:T(8,128)(2,1)S(1)}, bf16[1,112,128]{2,1,0:T(8,128)(2,1)S(1)}, u32[]{:S(2)}, u32[]{:S(2)}) %collective-permute-start) | collective-permute-done | bytes 28704 | tf_op jit(solution)/shard_map/ppermute | solution.py:278
  7.3 2.1 %collective-permute-start.1 = (bf16[2,112,128]{2,1,0:T(8,128)(2,1)S(1)}, bf16[2,112,128]{2,1,0:T(8,128)(2,1)S(1)}, u32[]{:S(2)}, u32[]{:S(2)}) collective-permute-start(bf16[2,112,128]{2,1,0:T(8,128)(2,1)S(1)} %pad_maximum_fusion.2), channel_id=1, source_target_pairs={{0,2},{2,0},{4,6},{6,4},{8,10},{10,8},{12,14},{14,12},{1,3},{3,1},... | collective-permute-start | bytes 172040 | tf_op jit(solution)/shard_map/ppermute | solution.py:281
  9.3 1.4 %collective-permute-start.2 = (bf16[2,112,128]{2,1,0:T(8,128)(2,1)S(1)}, bf16[2,112,128]{2,1,0:T(8,128)(2,1)S(1)}, u32[]{:S(2)}, u32[]{:S(2)}) collective-permute-start(bf16[2,112,128]{2,1,0:T(8,128)(2,1)S(1)} %pad_maximum_fusion.2), channel_id=1, source_target_pairs={{0,6},{2,4},{4,2},{6,0},{8,14},{10,12},{12,10},{14,8},{1,7},{3,5},... | collective-permute-start | bytes 172040 | tf_op jit(solution)/shard_map/ppermute | solution.py:281
  10.7 0.2 collective-permute-start.3
  10.9 1.2 %collective-permute-done.1 = bf16[2,112,128]{2,1,0:T(8,128)(2,1)S(1)} collective-permute-done((bf16[2,112,128]{2,1,0:T(8,128)(2,1)S(1)}, bf16[2,112,128]{2,1,0:T(8,128)(2,1)S(1)}, u32[]{:S(2)}, u32[]{:S(2)}) %collective-permute-start.1) | collective-permute-done | bytes 57376 | tf_op jit(solution)/shard_map/ppermute | solution.py:281
  12.1 2.3 %collective-permute-done.2 = bf16[2,112,128]{2,1,0:T(8,128)(2,1)S(1)} collective-permute-done((bf16[2,112,128]{2,1,0:T(8,128)(2,1)S(1)}, bf16[2,112,128]{2,1,0:T(8,128)(2,1)S(1)}, u32[]{:S(2)}, u32[]{:S(2)}) %collective-permute-start.2) | collective-permute-done | bytes 57376 | tf_op jit(solution)/shard_map/ppermute | solution.py:281
  14.5 0.1 collective-permute-start.4
  14.5 0.0 copy-start.5
  14.6 0.3 %collective-permute-done.3 = bf16[2,112,128]{2,1,0:T(8,128)(2,1)S(1)} collective-permute-done((bf16[2,112,128]{2,1,0:T(8,128)(2,1)S(1)}, bf16[2,112,128]{2,1,0:T(8,128)(2,1)S(1)}, u32[]{:S(2)}, u32[]{:S(2)}) %collective-permute-start.3) | collective-permute-done | bytes 57376 | tf_op jit(solution)/shard_map/ppermute | solution.py:281
  14.9 0.2 %collective-permute-start.5 = (bf16[2,112,128]{2,1,0:T(8,128)(2,1)S(1)}, bf16[2,112,128]{2,1,0:T(8,128)(2,1)S(1)}, u32[]{:S(2)}, u32[]{:S(2)}) collective-permute-start(bf16[2,112,128]{2,1,0:T(8,128)(2,1)S(1)} %collective-permute-done.3), channel_id=1, source_target_pairs={{0,1},{1,0},{2,3},{3,2},{4,5},{5,4},{6,7},{7,6},{8,9},{9,8},{10,11... | collective-permute-start | bytes 172040 | tf_op jit(solution)/shard_map/ppermute | solution.py:286
  15.1 0.0 copy-start
  15.2 0.0 copy-start.1
  15.2 0.0 copy-start.2
  15.2 0.0 copy-start.4
  15.2 0.9 %collective-permute-done.5 = bf16[2,112,128]{2,1,0:T(8,128)(2,1)S(1)} collective-permute-done((bf16[2,112,128]{2,1,0:T(8,128)(2,1)S(1)}, bf16[2,112,128]{2,1,0:T(8,128)(2,1)S(1)}, u32[]{:S(2)}, u32[]{:S(2)}) %collective-permute-start.5) | collective-permute-done | bytes 57376 | tf_op jit(solution)/shard_map/ppermute | solution.py:286
  16.1 0.0 collective-permute-done.4
  16.2 0.0 copy-done.5
  16.2 0.0 copy-done.3
  16.2 0.0 copy-done
  16.2 0.0 copy-done.1
  16.2 0.0 copy-done.2
  16.2 3.8 %shard_map.110 = bf16[2,32,128]{2,1,0:T(8,128)(2,1)} custom-call(bf16[8,112,128]{2,1,0:T(8,128)(2,1)S(1)} %constant_dynamic-update-slice_fusion.held_ref, bf16[8,112,128]{2,1,0:T(8,128)(2,1)S(1)} %pad_maximum_fusion.other_ref, bf16[32,32,128]{2,1,0:T(8,128)(2,1)S(1)} %copy-done, bf16[4,128,128]{2,1,0:T(8,128)(2,1)S(1)} %copy-done.1, ...), custom_call_target="tpu_custom_call" | custom-call | tf_op jit(solution)/shard_map/pallas_call | solution.py:352
  (10 shorter events, 0.1 us)
Async XLA Ops:
  1.3 6.0 %collective-permute-start = (bf16[1,112,128]{2,1,0:T(8,128)(2,1)S(1)}, bf16[1,112,128]{2,1,0:T(8,128)(2,1)S(1)}, u32[]{:S(2)}, u32[]{:S(2)}) collective-permute-start(bf16[1,112,128]{2,1,0:T(8,128)(2,1)S(1)} %bitcast.4), channel_id=1, source_target_pairs={{0,8},{2,10},{4,12},{6,14},{8,0},{10,2},{12,4},{14,6},{1,9},{3,11}... | collective-permute-start | bytes 86024 | tf_op jit(solution)/shard_map/ppermute | solution.py:278
  7.3 4.9 %collective-permute-start.1 = (bf16[2,112,128]{2,1,0:T(8,128)(2,1)S(1)}, bf16[2,112,128]{2,1,0:T(8,128)(2,1)S(1)}, u32[]{:S(2)}, u32[]{:S(2)}) collective-permute-start(bf16[2,112,128]{2,1,0:T(8,128)(2,1)S(1)} %pad_maximum_fusion.2), channel_id=1, source_target_pairs={{0,2},{2,0},{4,6},{6,4},{8,10},{10,8},{12,14},{14,12},{1,3},{3,1},... | collective-permute-start | bytes 172040 | tf_op jit(solution)/shard_map/ppermute | solution.py:281
  9.3 5.1 %collective-permute-start.2 = (bf16[2,112,128]{2,1,0:T(8,128)(2,1)S(1)}, bf16[2,112,128]{2,1,0:T(8,128)(2,1)S(1)}, u32[]{:S(2)}, u32[]{:S(2)}) collective-permute-start(bf16[2,112,128]{2,1,0:T(8,128)(2,1)S(1)} %pad_maximum_fusion.2), channel_id=1, source_target_pairs={{0,6},{2,4},{4,2},{6,0},{8,14},{10,12},{12,10},{14,8},{1,7},{3,5},... | collective-permute-start | bytes 172040 | tf_op jit(solution)/shard_map/ppermute | solution.py:281
  10.7 4.2 %collective-permute-start.3 = (bf16[2,112,128]{2,1,0:T(8,128)(2,1)S(1)}, bf16[2,112,128]{2,1,0:T(8,128)(2,1)S(1)}, u32[]{:S(2)}, u32[]{:S(2)}) collective-permute-start(bf16[2,112,128]{2,1,0:T(8,128)(2,1)S(1)} %pad_maximum_fusion.2), channel_id=1, source_target_pairs={{0,4},{2,6},{4,0},{6,2},{8,12},{10,14},{12,8},{14,10},{1,5},{3,7},... | collective-permute-start | bytes 172040 | tf_op jit(solution)/shard_map/ppermute | solution.py:281
  14.5 1.7 %collective-permute-start.4 = (bf16[6,112,128]{2,1,0:T(8,128)(2,1)S(1)}, bf16[6,112,128]{2,1,0:T(8,128)(2,1)S(1)}, u32[]{:S(2)}, u32[]{:S(2)}) collective-permute-start(bf16[6,112,128]{2,1,0:T(8,128)(2,1)S(1)} %pad_maximum_fusion.1), channel_id=1, source_target_pairs={{0,1},{1,0},{2,3},{3,2},{4,5},{5,4},{6,7},{7,6},{8,9},{9,8},{10,11... | collective-permute-start | bytes 516104 | tf_op jit(solution)/shard_map/ppermute | solution.py:285
  14.5 1.6 %copy-start.5 = (bf16[128,128]{1,0:T(8,128)(2,1)S(1)}, bf16[128,128]{1,0:T(8,128)(2,1)}, u32[]{:S(2)}) copy-start(bf16[128,128]{1,0:T(8,128)(2,1)} %output_ref.1) | copy-start | bytes 98308
  14.9 1.2 %collective-permute-start.5 = (bf16[2,112,128]{2,1,0:T(8,128)(2,1)S(1)}, bf16[2,112,128]{2,1,0:T(8,128)(2,1)S(1)}, u32[]{:S(2)}, u32[]{:S(2)}) collective-permute-start(bf16[2,112,128]{2,1,0:T(8,128)(2,1)S(1)} %collective-permute-done.3), channel_id=1, source_target_pairs={{0,1},{1,0},{2,3},{3,2},{4,5},{5,4},{6,7},{7,6},{8,9},{9,8},{10,11... | collective-permute-start | bytes 172040 | tf_op jit(solution)/shard_map/ppermute | solution.py:286
  15.1 1.1 %copy-start.3 = (bf16[512,128]{1,0:T(8,128)(2,1)S(1)}, bf16[512,128]{1,0:T(8,128)(2,1)}, u32[]{:S(2)}) copy-start(bf16[512,128]{1,0:T(8,128)(2,1)} %down_ref.1) | copy-start | bytes 393220
  15.1 1.1 %copy-start = (bf16[32,32,128]{2,1,0:T(8,128)(2,1)S(1)}, bf16[32,32,128]{2,1,0:T(8,128)(2,1)}, u32[]{:S(2)}) copy-start(bf16[32,32,128]{2,1,0:T(8,128)(2,1)} %outer_ref.1) | copy-start | bytes 786436
  15.2 1.0 %copy-start.1 = (bf16[4,128,128]{2,1,0:T(8,128)(2,1)S(1)}, bf16[4,128,128]{2,1,0:T(8,128)(2,1)}, u32[]{:S(2)}) copy-start(bf16[4,128,128]{2,1,0:T(8,128)(2,1)} %triangle_ref.1) | copy-start | bytes 393220
  15.2 1.1 %copy-start.2 = (bf16[128,512]{1,0:T(8,128)(2,1)S(1)}, bf16[128,512]{1,0:T(8,128)(2,1)}, u32[]{:S(2)}) copy-start(bf16[128,512]{1,0:T(8,128)(2,1)} %up_ref.1) | copy-start | bytes 393220
  15.2 1.1 %copy-start.4 = (bf16[128,128]{1,0:T(8,128)(2,1)S(1)}, bf16[128,128]{1,0:T(8,128)(2,1)}, u32[]{:S(2)}) copy-start(bf16[128,128]{1,0:T(8,128)(2,1)} %gate_ref.1) | copy-start | bytes 98308

commit v19 on v18

--- a/solution.py
+++ b/solution.py
@@ -127,8 +127,6 @@
     first_ref,
     second_ref,
     pair_ref,
-    pair_one_ref,
-    ln_one_ref,
 ):
     rows, residues, wide = out_ref.shape
     cores, chips = 2, lax.axis_size("dap")
@@ -200,7 +198,7 @@
             left = jnp.concatenate(
                 [left_ref[:, d] for d in range(part * span + turn, (part + 1) * span, 2)], axis=0
             ).astype(bf16)
-            outer.append(jnp.dot(left, right_ref[turn], preferred_element_type=f32))
+            outer.append(jnp.dot(left, right_ref[turn], preferred_element_type=f32).astype(bf16))
 
         def piece(turn, at, chip):
             return outer[turn][
@@ -215,38 +213,47 @@
                     slice(chip * residues, (chip + 1) * residues),
                     slice(at * wide, (at + 1) * wide),
                 )
-                first_ref[place] = jnp.where(low, piece(0, at, chip), piece(1, at, chip)).astype(bf16)
-                second_ref[place] = jnp.where(
-                    low, piece(1, at, chip), piece(0, follow, chip)
-                ).astype(bf16)
+                first_ref[place] = jnp.where(low, piece(0, at, chip), piece(1, at, chip))
+                second_ref[place] = jnp.where(low, piece(1, at, chip), piece(0, follow, chip))
         depth = span * 2 * channels
         totals[0] += jnp.dot(first_ref[part], block_ref[part, :depth], preferred_element_type=f32)
         totals[1] += jnp.dot(
             second_ref[part], block_ref[part, 2 * channels :], preferred_element_type=f32
         )
 
-    right_weight = jnp.concatenate([triangle_ref[2], triangle_ref[3]], axis=1)
-    right_tri = []
-    stride = 8
-    for first in range(0, residues, stride):
-        normed = []
-        for k in range(first, first + stride):
-            chip, pick = k // group, k % group
-            at = (pick % 2) * wide
-            numerator = totals[pick // 2][chip * residues : (chip + 1) * residues, at : at + wide]
-            opm = numerator * jnp.broadcast_to(inverse[:, k : k + 1], (residues, wide))
-            pair_one = (pair_ref[:, k] + opm).astype(bf16).astype(f32)
-            pair_one_ref[k] = pair_one
-            ln_one = layer_norm(pair_one)
-            ln_one_ref[k] = ln_one
-            normed.append(ln_one.astype(bf16))
-        both = jnp.dot(
-            jnp.concatenate(normed, axis=0), right_weight, preferred_element_type=f32
-        )
-        right_tri.append((sigmoid(both[:, :wide]) * both[:, wide:]).astype(bf16).astype(f32))
-
-    own_pair = jnp.concatenate([pair_one_ref[:, start + row] for row in range(rows)], axis=0)
-    own_ln = jnp.concatenate([ln_one_ref[:, start + row] for row in range(rows)], axis=0).astype(bf16)
+    pairs = residues * residues
+    pair_one = []
+    for k in range(residues):
+        chip, pick = k // group, k % group
+        at = (pick % 2) * wide
+        numerator = totals[pick // 2][chip * residues : (chip + 1) * residues, at : at + wide]
+        opm = numerator * jnp.broadcast_to(inverse[:, k : k + 1], (residues, wide))
+        pair_one.append((pair_ref[:, k] + opm).astype(bf16))
+    pair_one = jnp.concatenate(pair_one, axis=0)
+    average = jnp.full((2 * wide, wide), 1.0 / wide, bf16)
+    mean = jnp.dot(pair_one, average[:wide], preferred_element_type=f32)
+    centered = pair_one.astype(f32) - mean
+    square = centered * centered
+    coarse = square.astype(bf16)
+    fine = (square - coarse.astype(f32)).astype(bf16)
+    variance = jnp.dot(
+        jnp.concatenate([coarse, fine], axis=1), average, preferred_element_type=f32
+    )
+    ln_all = (centered * lax.rsqrt(variance + 1e-05)).astype(bf16)
+    both = jnp.dot(
+        ln_all,
+        jnp.concatenate([triangle_ref[2], triangle_ref[3]], axis=1),
+        preferred_element_type=f32,
+    )
+    right_tri = (sigmoid(both[:, :wide]) * both[:, wide:]).astype(bf16).astype(f32)
+
+    own = lax.broadcasted_iota(jnp.int32, (rows * residues, pairs), 0)
+    own = (own % residues) * residues + own // residues + start
+    chosen = (lax.broadcasted_iota(jnp.int32, (rows * residues, pairs), 1) == own).astype(bf16)
+    own = jnp.dot(
+        chosen, jnp.concatenate([ln_all, pair_one], axis=1), preferred_element_type=f32
+    )
+    own_ln, own_pair = own[:, :wide].astype(bf16), own[:, wide:]
     left_weight = jnp.concatenate([triangle_ref[0], triangle_ref[1]], axis=1)
     both = jnp.dot(own_ln, left_weight, preferred_element_type=f32)
     left_tri = sigmoid(both[:, :wide]) * both[:, wide:] * jnp.concatenate([mask] * rows, axis=0)
@@ -256,8 +263,7 @@
         sums = [jnp.zeros((residues, wide), f32) for _ in range(4)]
         for k in range(residues):
             at = row * residues + k
-            place = (k % stride) * residues
-            sums[k % 4] += left_tri[at : at + 1] * right_tri[k // stride][place : place + residues]
+            sums[k % 4] += left_tri[at : at + 1] * right_tri[k * residues : (k + 1) * residues]
         total = (sums[0] + sums[1]) + (sums[2] + sums[3])
         own_mask = keep_ref[pl.ds(start + row, 1), :][:, sequences : sequences + 1]
         products.append(total * (mask * own_mask))
@@ -362,8 +368,6 @@
             pltpu.VMEM((parts, chips * residues, channels // parts * wide // 2), jnp.bfloat16),
             pltpu.VMEM((parts, chips * residues, channels // parts * wide // 2), jnp.bfloat16),
             pltpu.VMEM((residues, residues, wide), jnp.float32),
-            pltpu.VMEM((residues, residues, wide), jnp.float32),
-            pltpu.VMEM((residues, residues, wide), jnp.float32),
         ],
         compiler_params=params,
     )(

time: 20.3 us -> 20.5 us (level)
  no operation moved by 1% of the time
where the time goes in v19:
time: 20.5 us; the launch traced here: 20.3 us
  starting transfers between devices  7.99 us (39%)
  waiting for transfers between devices  6.65 us (32%)
  Pallas kernels  5.33 us (26%)
    ppermute x1, starting transfers between devices, gather_all(): lax.ppermute(packed[None], 'dap', [(src, src ^ half) for src in range(dap...  4.1 us
    pallas_call x1, Pallas kernels, shards_replicated(): pl.pallas_call(update_kernel, out_shape=jax.ShapeDtypeStruct(pairwise_sta...  4.01 us
    ppermute x3, waiting for transfers between devices, gather_all(): lax.ppermute(both, 'dap', [(src, src ^ offset) for src in range(dap_count)])  3.85 us
    ppermute x3, starting transfers between devices, gather_all(): lax.ppermute(both, 'dap', [(src, src ^ offset) for src in range(dap_count)])  3.59 us
    ppermute x1, waiting for transfers between devices, gather_all(): lax.ppermute(packed[None], 'dap', [(src, src ^ half) for src in range(dap...  1.86 us
    pallas_call x1, Pallas kernels, shards_replicated(): pl.pallas_call(pack_kernel, out_shape=jax.ShapeDtypeStruct((rows * residu...  1.31 us
    ppermute x1, waiting for transfers between devices, gather_all(): late = lax.ppermute(held[-1], 'sub', sibling)  0.93 us
  transfers between devices with their start and end apart: 6, of which 5 were waited for; matrix products, arithmetic and copies ran while one was open for 0% of the time, Pallas kernels for 0%

profile of v19, /device:TPU:0, one launch (start us, length us, event | category | flops | bytes accessed | tf_op | source)
XLA Modules:
  0.0 20.3 jit_solution(8020647529250841111)
XLA Ops:
  0.0 1.3 %shard_map.109 = bf16[112,128]{1,0:T(8,128)(2,1)S(1)} custom-call(s32[32]{0:T(128)} %mask_hbm.1, s32[2,32]{1,0:T(2,128)} %bitcast.8, bf16[32,2,256]{2,1,0:T(2,128)(2,1)} %state_hbm.1, bf16[2,32,256]{2,1,0:T(8,128)(2,1)} %bitcast.7, bf16[2,32,128]{2,1,0:T(8,128)(2,1)} %pair_hbm.1), custom_call_target="tpu_custom_call" | custom-call | tf_op jit(solution)/shard_map/pallas_call | solution.py:328
  1.3 4.1 %collective-permute-start = (bf16[1,112,128]{2,1,0:T(8,128)(2,1)S(1)}, bf16[1,112,128]{2,1,0:T(8,128)(2,1)S(1)}, u32[]{:S(2)}, u32[]{:S(2)}) collective-permute-start(bf16[1,112,128]{2,1,0:T(8,128)(2,1)S(1)} %bitcast.4), channel_id=1, source_target_pairs={{0,8},{2,10},{4,12},{6,14},{8,0},{10,2},{12,4},{14,6},{1,9},{3,11}... | collective-permute-start | bytes 86024 | tf_op jit(solution)/shard_map/ppermute | solution.py:284
  5.4 1.9 %collective-permute-done = bf16[1,112,128]{2,1,0:T(8,128)(2,1)S(1)} collective-permute-done((bf16[1,112,128]{2,1,0:T(8,128)(2,1)S(1)}, bf16[1,112,128]{2,1,0:T(8,128)(2,1)S(1)}, u32[]{:S(2)}, u32[]{:S(2)}) %collective-permute-start) | collective-permute-done | bytes 28704 | tf_op jit(solution)/shard_map/ppermute | solution.py:284
  7.3 2.1 %collective-permute-start.1 = (bf16[2,112,128]{2,1,0:T(8,128)(2,1)S(1)}, bf16[2,112,128]{2,1,0:T(8,128)(2,1)S(1)}, u32[]{:S(2)}, u32[]{:S(2)}) collective-permute-start(bf16[2,112,128]{2,1,0:T(8,128)(2,1)S(1)} %pad_maximum_fusion.2), channel_id=1, source_target_pairs={{0,2},{2,0},{4,6},{6,4},{8,10},{10,8},{12,14},{14,12},{1,3},{3,1},... | collective-permute-start | bytes 172040 | tf_op jit(solution)/shard_map/ppermute | solution.py:287
  9.3 1.4 %collective-permute-start.2 = (bf16[2,112,128]{2,1,0:T(8,128)(2,1)S(1)}, bf16[2,112,128]{2,1,0:T(8,128)(2,1)S(1)}, u32[]{:S(2)}, u32[]{:S(2)}) collective-permute-start(bf16[2,112,128]{2,1,0:T(8,128)(2,1)S(1)} %pad_maximum_fusion.2), channel_id=1, source_target_pairs={{0,6},{2,4},{4,2},{6,0},{8,14},{10,12},{12,10},{14,8},{1,7},{3,5},... | collective-permute-start | bytes 172040 | tf_op jit(solution)/shard_map/ppermute | solution.py:287
  10.7 0.2 collective-permute-start.3
  10.9 1.2 %collective-permute-done.1 = bf16[2,112,128]{2,1,0:T(8,128)(2,1)S(1)} collective-permute-done((bf16[2,112,128]{2,1,0:T(8,128)(2,1)S(1)}, bf16[2,112,128]{2,1,0:T(8,128)(2,1)S(1)}, u32[]{:S(2)}, u32[]{:S(2)}) %collective-permute-start.1) | collective-permute-done | bytes 57376 | tf_op jit(solution)/shard_map/ppermute | solution.py:287
  12.1 2.3 %collective-permute-done.2 = bf16[2,112,128]{2,1,0:T(8,128)(2,1)S(1)} collective-permute-done((bf16[2,112,128]{2,1,0:T(8,128)(2,1)S(1)}, bf16[2,112,128]{2,1,0:T(8,128)(2,1)S(1)}, u32[]{:S(2)}, u32[]{:S(2)}) %collective-permute-start.2) | collective-permute-done | bytes 57376 | tf_op jit(solution)/shard_map/ppermute | solution.py:287
  14.5 0.1 collective-permute-start.4
  14.5 0.0 copy-start.5
  14.6 0.3 %collective-permute-done.3 = bf16[2,112,128]{2,1,0:T(8,128)(2,1)S(1)} collective-permute-done((bf16[2,112,128]{2,1,0:T(8,128)(2,1)S(1)}, bf16[2,112,128]{2,1,0:T(8,128)(2,1)S(1)}, u32[]{:S(2)}, u32[]{:S(2)}) %collective-permute-start.3) | collective-permute-done | bytes 57376 | tf_op jit(solution)/shard_map/ppermute | solution.py:287
  14.9 0.2 %collective-permute-start.5 = (bf16[2,112,128]{2,1,0:T(8,128)(2,1)S(1)}, bf16[2,112,128]{2,1,0:T(8,128)(2,1)S(1)}, u32[]{:S(2)}, u32[]{:S(2)}) collective-permute-start(bf16[2,112,128]{2,1,0:T(8,128)(2,1)S(1)} %collective-permute-done.3), channel_id=1, source_target_pairs={{0,1},{1,0},{2,3},{3,2},{4,5},{5,4},{6,7},{7,6},{8,9},{9,8},{10,11... | collective-permute-start | bytes 172040 | tf_op jit(solution)/shard_map/ppermute | solution.py:292
  15.1 0.0 copy-start
  15.2 0.0 copy-start.1
  15.2 0.0 copy-start.2
  15.2 0.0 copy-start.4
  15.2 0.9 %collective-permute-done.5 = bf16[2,112,128]{2,1,0:T(8,128)(2,1)S(1)} collective-permute-done((bf16[2,112,128]{2,1,0:T(8,128)(2,1)S(1)}, bf16[2,112,128]{2,1,0:T(8,128)(2,1)S(1)}, u32[]{:S(2)}, u32[]{:S(2)}) %collective-permute-start.5) | collective-permute-done | bytes 57376 | tf_op jit(solution)/shard_map/ppermute | solution.py:292
  16.1 0.0 collective-permute-done.4
  16.2 0.0 copy-done.5
  16.2 0.0 copy-done.3
  16.2 0.0 copy-done
  16.2 0.0 copy-done.1
  16.2 0.0 copy-done.2
  16.2 4.0 %shard_map.110 = bf16[2,32,128]{2,1,0:T(8,128)(2,1)} custom-call(bf16[8,112,128]{2,1,0:T(8,128)(2,1)S(1)} %constant_dynamic-update-slice_fusion.held_ref, bf16[8,112,128]{2,1,0:T(8,128)(2,1)S(1)} %pad_maximum_fusion.other_ref, bf16[32,32,128]{2,1,0:T(8,128)(2,1)S(1)} %copy-done, bf16[4,128,128]{2,1,0:T(8,128)(2,1)S(1)} %copy-done.1, ...), custom_call_target="tpu_custom_call" | custom-call | tf_op jit(solution)/shard_map/pallas_call | solution.py:358
  (10 shorter events, 0.1 us)
Async XLA Ops:
  1.3 6.0 %collective-permute-start = (bf16[1,112,128]{2,1,0:T(8,128)(2,1)S(1)}, bf16[1,112,128]{2,1,0:T(8,128)(2,1)S(1)}, u32[]{:S(2)}, u32[]{:S(2)}) collective-permute-start(bf16[1,112,128]{2,1,0:T(8,128)(2,1)S(1)} %bitcast.4), channel_id=1, source_target_pairs={{0,8},{2,10},{4,12},{6,14},{8,0},{10,2},{12,4},{14,6},{1,9},{3,11}... | collective-permute-start | bytes 86024 | tf_op jit(solution)/shard_map/ppermute | solution.py:284
  7.3 4.9 %collective-permute-start.1 = (bf16[2,112,128]{2,1,0:T(8,128)(2,1)S(1)}, bf16[2,112,128]{2,1,0:T(8,128)(2,1)S(1)}, u32[]{:S(2)}, u32[]{:S(2)}) collective-permute-start(bf16[2,112,128]{2,1,0:T(8,128)(2,1)S(1)} %pad_maximum_fusion.2), channel_id=1, source_target_pairs={{0,2},{2,0},{4,6},{6,4},{8,10},{10,8},{12,14},{14,12},{1,3},{3,1},... | collective-permute-start | bytes 172040 | tf_op jit(solution)/shard_map/ppermute | solution.py:287
  9.3 5.1 %collective-permute-start.2 = (bf16[2,112,128]{2,1,0:T(8,128)(2,1)S(1)}, bf16[2,112,128]{2,1,0:T(8,128)(2,1)S(1)}, u32[]{:S(2)}, u32[]{:S(2)}) collective-permute-start(bf16[2,112,128]{2,1,0:T(8,128)(2,1)S(1)} %pad_maximum_fusion.2), channel_id=1, source_target_pairs={{0,6},{2,4},{4,2},{6,0},{8,14},{10,12},{12,10},{14,8},{1,7},{3,5},... | collective-permute-start | bytes 172040 | tf_op jit(solution)/shard_map/ppermute | solution.py:287
  10.7 4.2 %collective-permute-start.3 = (bf16[2,112,128]{2,1,0:T(8,128)(2,1)S(1)}, bf16[2,112,128]{2,1,0:T(8,128)(2,1)S(1)}, u32[]{:S(2)}, u32[]{:S(2)}) collective-permute-start(bf16[2,112,128]{2,1,0:T(8,128)(2,1)S(1)} %pad_maximum_fusion.2), channel_id=1, source_target_pairs={{0,4},{2,6},{4,0},{6,2},{8,12},{10,14},{12,8},{14,10},{1,5},{3,7},... | collective-permute-start | bytes 172040 | tf_op jit(solution)/shard_map/ppermute | solution.py:287
  14.5 1.7 %collective-permute-start.4 = (bf16[6,112,128]{2,1,0:T(8,128)(2,1)S(1)}, bf16[6,112,128]{2,1,0:T(8,128)(2,1)S(1)}, u32[]{:S(2)}, u32[]{:S(2)}) collective-permute-start(bf16[6,112,128]{2,1,0:T(8,128)(2,1)S(1)} %pad_maximum_fusion.1), channel_id=1, source_target_pairs={{0,1},{1,0},{2,3},{3,2},{4,5},{5,4},{6,7},{7,6},{8,9},{9,8},{10,11... | collective-permute-start | bytes 516104 | tf_op jit(solution)/shard_map/ppermute | solution.py:291
  14.5 1.6 %copy-start.5 = (bf16[128,128]{1,0:T(8,128)(2,1)S(1)}, bf16[128,128]{1,0:T(8,128)(2,1)}, u32[]{:S(2)}) copy-start(bf16[128,128]{1,0:T(8,128)(2,1)} %output_ref.1) | copy-start | bytes 98308
  14.9 1.2 %collective-permute-start.5 = (bf16[2,112,128]{2,1,0:T(8,128)(2,1)S(1)}, bf16[2,112,128]{2,1,0:T(8,128)(2,1)S(1)}, u32[]{:S(2)}, u32[]{:S(2)}) collective-permute-start(bf16[2,112,128]{2,1,0:T(8,128)(2,1)S(1)} %collective-permute-done.3), channel_id=1, source_target_pairs={{0,1},{1,0},{2,3},{3,2},{4,5},{5,4},{6,7},{7,6},{8,9},{9,8},{10,11... | collective-permute-start | bytes 172040 | tf_op jit(solution)/shard_map/ppermute | solution.py:292
  15.1 1.1 %copy-start.3 = (bf16[512,128]{1,0:T(8,128)(2,1)S(1)}, bf16[512,128]{1,0:T(8,128)(2,1)}, u32[]{:S(2)}) copy-start(bf16[512,128]{1,0:T(8,128)(2,1)} %down_ref.1) | copy-start | bytes 393220
  15.1 1.1 %copy-start = (bf16[32,32,128]{2,1,0:T(8,128)(2,1)S(1)}, bf16[32,32,128]{2,1,0:T(8,128)(2,1)}, u32[]{:S(2)}) copy-start(bf16[32,32,128]{2,1,0:T(8,128)(2,1)} %outer_ref.1) | copy-start | bytes 786436
  15.2 1.0 %copy-start.1 = (bf16[4,128,128]{2,1,0:T(8,128)(2,1)S(1)}, bf16[4,128,128]{2,1,0:T(8,128)(2,1)}, u32[]{:S(2)}) copy-start(bf16[4,128,128]{2,1,0:T(8,128)(2,1)} %triangle_ref.1) | copy-start | bytes 393220
  15.2 1.1 %copy-start.2 = (bf16[128,512]{1,0:T(8,128)(2,1)S(1)}, bf16[128,512]{1,0:T(8,128)(2,1)}, u32[]{:S(2)}) copy-start(bf16[128,512]{1,0:T(8,128)(2,1)} %up_ref.1) | copy-start | bytes 393220
  15.2 1.1 %copy-start.4 = (bf16[128,128]{1,0:T(8,128)(2,1)S(1)}, bf16[128,128]{1,0:T(8,128)(2,1)}, u32[]{:S(2)}) copy-start(bf16[128,128]{1,0:T(8,128)(2,1)} %gate_ref.1) | copy-start | bytes 98308

commit v20 on v18

--- a/solution.py
+++ b/solution.py
@@ -68,37 +68,39 @@
     ]
     for load in loads:
         load.start()
-    loads[0].wait()
-    wide_ref[...] = state_ref[...].astype(jnp.float32)
-    normed_rows = [layer_norm(wide_ref[:, row]).astype(jnp.bfloat16) for row in range(rows)]
+    for load in loads[:4]:
+        load.wait()
+    f32, bf16 = jnp.float32, jnp.bfloat16
+    wide_ref[...] = state_ref[...].astype(f32)
     eye = lax.broadcasted_iota(jnp.int32, (sequences, sequences), 0) == lax.broadcasted_iota(
         jnp.int32, (sequences, sequences), 1
     )
-    lefts, rights, keeps = [], [], []
-    for load in loads[1:4]:
-        load.wait()
+    last = (((1,), (1,)), ((), ()))
+    weight = weight_ref[1]
+    nothing = jnp.zeros_like(weight)
+    here = jnp.where(second_core, nothing, weight), jnp.where(second_core, weight, nothing)
+    keeps, fronts, backs = [], [], []
+    projected = 0.0
     for row in range(rows):
-        present = mask_ref[start + row].astype(jnp.float32)
-        keep_row = keep_ref[row : row + 1].astype(jnp.float32) * present
+        present = mask_ref[start + row].astype(f32)
+        keep_row = keep_ref[row : row + 1].astype(f32) * present
         keep_column = jnp.sum(
             jnp.where(eye, jnp.broadcast_to(keep_row, eye.shape), 0.0), axis=1, keepdims=True
         )
-        normed = normed_rows[row]
-        last = (((1,), (1,)), ((), ()))
-        left = lax.dot_general(weight_ref[0], normed, last, preferred_element_type=jnp.float32)
-        right = lax.dot_general(normed, weight_ref[1], last, preferred_element_type=jnp.float32)
-        lefts.append(left * keep_row)
-        rights.append(right * keep_column)
+        normed = (layer_norm(wide_ref[:, row]) * keep_column).astype(bf16)
+        fronts.append(jnp.where(second_core, normed, jnp.zeros_like(normed)))
+        backs.append(jnp.where(second_core, jnp.zeros_like(normed), normed))
+        placed = [here[0] if at == row else here[1] if at == rows + row else nothing for at in range(2 * rows)]
+        projected += lax.dot_general(
+            normed, jnp.concatenate(placed, axis=0), last, preferred_element_type=f32
+        )
         keeps.append(
-            jnp.concatenate(
-                [keep_row, jnp.full((1, wide - sequences), present, jnp.float32)], axis=1
-            )
-        )
-    left = jnp.concatenate(lefts, axis=1)
-    right = jnp.concatenate(rights, axis=1)
-    first = jnp.concatenate([right, left], axis=1)
-    other = jnp.concatenate([left, right], axis=1)
-    out_ref[base : base + sequences] = jnp.where(second_core, other, first).astype(jnp.bfloat16)
+            jnp.concatenate([keep_row, jnp.full((1, wide - sequences), present, f32)], axis=1)
+        )
+    projected += lax.dot_general(
+        weight_ref[0], jnp.concatenate(fronts + backs, axis=0), last, preferred_element_type=f32
+    )
+    out_ref[base : base + sequences] = projected.astype(bf16)
     out_ref[base + sequences :] = jnp.concatenate(
         keeps + [jnp.zeros((16 - rows, wide), jnp.float32)], axis=0
     ).astype(jnp.bfloat16)
@@ -200,7 +202,7 @@
             left = jnp.concatenate(
                 [left_ref[:, d] for d in range(part * span + turn, (part + 1) * span, 2)], axis=0
             ).astype(bf16)
-            outer.append(jnp.dot(left, right_ref[turn], preferred_element_type=f32))
+            outer.append(jnp.dot(left, right_ref[turn], preferred_element_type=f32).astype(bf16))
 
         def piece(turn, at, chip):
             return outer[turn][
@@ -215,10 +217,8 @@
                     slice(chip * residues, (chip + 1) * residues),
                     slice(at * wide, (at + 1) * wide),
                 )
-                first_ref[place] = jnp.where(low, piece(0, at, chip), piece(1, at, chip)).astype(bf16)
-                second_ref[place] = jnp.where(
-                    low, piece(1, at, chip), piece(0, follow, chip)
-                ).astype(bf16)
+                first_ref[place] = jnp.where(low, piece(0, at, chip), piece(1, at, chip))
+                second_ref[place] = jnp.where(low, piece(1, at, chip), piece(0, follow, chip))
         depth = span * 2 * channels
         totals[0] += jnp.dot(first_ref[part], block_ref[part, :depth], preferred_element_type=f32)
         totals[1] += jnp.dot(

time: 20.3 us -> 20.1 us (level)
  no operation moved by 1% of the time
where the time goes in v20:
time: 20.1 us; the launch traced here: 19.9 us
  starting transfers between devices  8 us (40%)
  waiting for transfers between devices  6.65 us (33%)
  Pallas kernels  5 us (25%)
    ppermute x1, starting transfers between devices, gather_all(): lax.ppermute(packed[None], 'dap', [(src, src ^ half) for src in range(dap...  4.1 us
    ppermute x3, waiting for transfers between devices, gather_all(): lax.ppermute(both, 'dap', [(src, src ^ offset) for src in range(dap_count)])  3.85 us
    pallas_call x1, Pallas kernels, shards_replicated(): pl.pallas_call(update_kernel, out_shape=jax.ShapeDtypeStruct(pairwise_sta...  3.8 us
    ppermute x3, starting transfers between devices, gather_all(): lax.ppermute(both, 'dap', [(src, src ^ offset) for src in range(dap_count)])  3.6 us
    ppermute x1, waiting for transfers between devices, gather_all(): lax.ppermute(packed[None], 'dap', [(src, src ^ half) for src in range(dap...  1.86 us
    pallas_call x1, Pallas kernels, shards_replicated(): pl.pallas_call(pack_kernel, out_shape=jax.ShapeDtypeStruct((rows * residu...  1.2 us
    ppermute x1, waiting for transfers between devices, gather_all(): late = lax.ppermute(held[-1], 'sub', sibling)  0.93 us
  transfers between devices with their start and end apart: 6, of which 5 were waited for; matrix products, arithmetic and copies ran while one was open for 0% of the time, Pallas kernels for 0%

profile of v20, /device:TPU:0, one launch (start us, length us, event | category | flops | bytes accessed | tf_op | source)
XLA Modules:
  0.0 19.9 jit_solution(1396404756904840939)
XLA Ops:
  0.0 1.2 %shard_map.109 = bf16[112,128]{1,0:T(8,128)(2,1)S(1)} custom-call(s32[32]{0:T(128)} %mask_hbm.1, s32[2,32]{1,0:T(2,128)} %bitcast.8, bf16[32,2,256]{2,1,0:T(2,128)(2,1)} %state_hbm.1, bf16[2,32,256]{2,1,0:T(8,128)(2,1)} %bitcast.7, bf16[2,32,128]{2,1,0:T(8,128)(2,1)} %pair_hbm.1), custom_call_target="tpu_custom_call" | custom-call | tf_op jit(solution)/shard_map/pallas_call | solution.py:322
  1.2 4.1 %collective-permute-start = (bf16[1,112,128]{2,1,0:T(8,128)(2,1)S(1)}, bf16[1,112,128]{2,1,0:T(8,128)(2,1)S(1)}, u32[]{:S(2)}, u32[]{:S(2)}) collective-permute-start(bf16[1,112,128]{2,1,0:T(8,128)(2,1)S(1)} %bitcast.4), channel_id=1, source_target_pairs={{0,8},{2,10},{4,12},{6,14},{8,0},{10,2},{12,4},{14,6},{1,9},{3,11}... | collective-permute-start | bytes 86024 | tf_op jit(solution)/shard_map/ppermute | solution.py:278
  5.3 1.9 %collective-permute-done = bf16[1,112,128]{2,1,0:T(8,128)(2,1)S(1)} collective-permute-done((bf16[1,112,128]{2,1,0:T(8,128)(2,1)S(1)}, bf16[1,112,128]{2,1,0:T(8,128)(2,1)S(1)}, u32[]{:S(2)}, u32[]{:S(2)}) %collective-permute-start) | collective-permute-done | bytes 28704 | tf_op jit(solution)/shard_map/ppermute | solution.py:278
  7.2 2.1 %collective-permute-start.1 = (bf16[2,112,128]{2,1,0:T(8,128)(2,1)S(1)}, bf16[2,112,128]{2,1,0:T(8,128)(2,1)S(1)}, u32[]{:S(2)}, u32[]{:S(2)}) collective-permute-start(bf16[2,112,128]{2,1,0:T(8,128)(2,1)S(1)} %pad_maximum_fusion.2), channel_id=1, source_target_pairs={{0,2},{2,0},{4,6},{6,4},{8,10},{10,8},{12,14},{14,12},{1,3},{3,1},... | collective-permute-start | bytes 172040 | tf_op jit(solution)/shard_map/ppermute | solution.py:281
  9.2 1.4 %collective-permute-start.2 = (bf16[2,112,128]{2,1,0:T(8,128)(2,1)S(1)}, bf16[2,112,128]{2,1,0:T(8,128)(2,1)S(1)}, u32[]{:S(2)}, u32[]{:S(2)}) collective-permute-start(bf16[2,112,128]{2,1,0:T(8,128)(2,1)S(1)} %pad_maximum_fusion.2), channel_id=1, source_target_pairs={{0,6},{2,4},{4,2},{6,0},{8,14},{10,12},{12,10},{14,8},{1,7},{3,5},... | collective-permute-start | bytes 172040 | tf_op jit(solution)/shard_map/ppermute | solution.py:281
  10.6 0.2 collective-permute-start.3
  10.8 1.2 %collective-permute-done.1 = bf16[2,112,128]{2,1,0:T(8,128)(2,1)S(1)} collective-permute-done((bf16[2,112,128]{2,1,0:T(8,128)(2,1)S(1)}, bf16[2,112,128]{2,1,0:T(8,128)(2,1)S(1)}, u32[]{:S(2)}, u32[]{:S(2)}) %collective-permute-start.1) | collective-permute-done | bytes 57376 | tf_op jit(solution)/shard_map/ppermute | solution.py:281
  12.0 2.3 %collective-permute-done.2 = bf16[2,112,128]{2,1,0:T(8,128)(2,1)S(1)} collective-permute-done((bf16[2,112,128]{2,1,0:T(8,128)(2,1)S(1)}, bf16[2,112,128]{2,1,0:T(8,128)(2,1)S(1)}, u32[]{:S(2)}, u32[]{:S(2)}) %collective-permute-start.2) | collective-permute-done | bytes 57376 | tf_op jit(solution)/shard_map/ppermute | solution.py:281
  14.3 0.1 collective-permute-start.4
  14.4 0.0 copy-start.5
  14.4 0.3 %collective-permute-done.3 = bf16[2,112,128]{2,1,0:T(8,128)(2,1)S(1)} collective-permute-done((bf16[2,112,128]{2,1,0:T(8,128)(2,1)S(1)}, bf16[2,112,128]{2,1,0:T(8,128)(2,1)S(1)}, u32[]{:S(2)}, u32[]{:S(2)}) %collective-permute-start.3) | collective-permute-done | bytes 57376 | tf_op jit(solution)/shard_map/ppermute | solution.py:281
  14.8 0.2 %collective-permute-start.5 = (bf16[2,112,128]{2,1,0:T(8,128)(2,1)S(1)}, bf16[2,112,128]{2,1,0:T(8,128)(2,1)S(1)}, u32[]{:S(2)}, u32[]{:S(2)}) collective-permute-start(bf16[2,112,128]{2,1,0:T(8,128)(2,1)S(1)} %collective-permute-done.3), channel_id=1, source_target_pairs={{0,1},{1,0},{2,3},{3,2},{4,5},{5,4},{6,7},{7,6},{8,9},{9,8},{10,11... | collective-permute-start | bytes 172040 | tf_op jit(solution)/shard_map/ppermute | solution.py:286
  15.0 0.0 copy-start
  15.0 0.0 copy-start.1
  15.1 0.0 copy-start.2
  15.1 0.0 copy-start.4
  15.1 0.9 %collective-permute-done.5 = bf16[2,112,128]{2,1,0:T(8,128)(2,1)S(1)} collective-permute-done((bf16[2,112,128]{2,1,0:T(8,128)(2,1)S(1)}, bf16[2,112,128]{2,1,0:T(8,128)(2,1)S(1)}, u32[]{:S(2)}, u32[]{:S(2)}) %collective-permute-start.5) | collective-permute-done | bytes 57376 | tf_op jit(solution)/shard_map/ppermute | solution.py:286
  16.0 0.0 collective-permute-done.4
  16.0 0.0 copy-done.5
  16.1 0.0 copy-done.3
  16.1 0.0 copy-done
  16.1 0.0 copy-done.1
  16.1 0.0 copy-done.2
  16.1 3.8 %shard_map.110 = bf16[2,32,128]{2,1,0:T(8,128)(2,1)} custom-call(bf16[8,112,128]{2,1,0:T(8,128)(2,1)S(1)} %constant_dynamic-update-slice_fusion.held_ref, bf16[8,112,128]{2,1,0:T(8,128)(2,1)S(1)} %pad_maximum_fusion.other_ref, bf16[32,32,128]{2,1,0:T(8,128)(2,1)S(1)} %copy-done, bf16[4,128,128]{2,1,0:T(8,128)(2,1)S(1)} %copy-done.1, ...), custom_call_target="tpu_custom_call" | custom-call | tf_op jit(solution)/shard_map/pallas_call | solution.py:352
  (10 shorter events, 0.1 us)
Async XLA Ops:
  1.2 6.0 %collective-permute-start = (bf16[1,112,128]{2,1,0:T(8,128)(2,1)S(1)}, bf16[1,112,128]{2,1,0:T(8,128)(2,1)S(1)}, u32[]{:S(2)}, u32[]{:S(2)}) collective-permute-start(bf16[1,112,128]{2,1,0:T(8,128)(2,1)S(1)} %bitcast.4), channel_id=1, source_target_pairs={{0,8},{2,10},{4,12},{6,14},{8,0},{10,2},{12,4},{14,6},{1,9},{3,11}... | collective-permute-start | bytes 86024 | tf_op jit(solution)/shard_map/ppermute | solution.py:278
  7.2 4.9 %collective-permute-start.1 = (bf16[2,112,128]{2,1,0:T(8,128)(2,1)S(1)}, bf16[2,112,128]{2,1,0:T(8,128)(2,1)S(1)}, u32[]{:S(2)}, u32[]{:S(2)}) collective-permute-start(bf16[2,112,128]{2,1,0:T(8,128)(2,1)S(1)} %pad_maximum_fusion.2), channel_id=1, source_target_pairs={{0,2},{2,0},{4,6},{6,4},{8,10},{10,8},{12,14},{14,12},{1,3},{3,1},... | collective-permute-start | bytes 172040 | tf_op jit(solution)/shard_map/ppermute | solution.py:281
  9.2 5.1 %collective-permute-start.2 = (bf16[2,112,128]{2,1,0:T(8,128)(2,1)S(1)}, bf16[2,112,128]{2,1,0:T(8,128)(2,1)S(1)}, u32[]{:S(2)}, u32[]{:S(2)}) collective-permute-start(bf16[2,112,128]{2,1,0:T(8,128)(2,1)S(1)} %pad_maximum_fusion.2), channel_id=1, source_target_pairs={{0,6},{2,4},{4,2},{6,0},{8,14},{10,12},{12,10},{14,8},{1,7},{3,5},... | collective-permute-start | bytes 172040 | tf_op jit(solution)/shard_map/ppermute | solution.py:281
  10.6 4.2 %collective-permute-start.3 = (bf16[2,112,128]{2,1,0:T(8,128)(2,1)S(1)}, bf16[2,112,128]{2,1,0:T(8,128)(2,1)S(1)}, u32[]{:S(2)}, u32[]{:S(2)}) collective-permute-start(bf16[2,112,128]{2,1,0:T(8,128)(2,1)S(1)} %pad_maximum_fusion.2), channel_id=1, source_target_pairs={{0,4},{2,6},{4,0},{6,2},{8,12},{10,14},{12,8},{14,10},{1,5},{3,7},... | collective-permute-start | bytes 172040 | tf_op jit(solution)/shard_map/ppermute | solution.py:281
  14.3 1.7 %collective-permute-start.4 = (bf16[6,112,128]{2,1,0:T(8,128)(2,1)S(1)}, bf16[6,112,128]{2,1,0:T(8,128)(2,1)S(1)}, u32[]{:S(2)}, u32[]{:S(2)}) collective-permute-start(bf16[6,112,128]{2,1,0:T(8,128)(2,1)S(1)} %pad_maximum_fusion.1), channel_id=1, source_target_pairs={{0,1},{1,0},{2,3},{3,2},{4,5},{5,4},{6,7},{7,6},{8,9},{9,8},{10,11... | collective-permute-start | bytes 516104 | tf_op jit(solution)/shard_map/ppermute | solution.py:285
  14.4 1.6 %copy-start.5 = (bf16[128,128]{1,0:T(8,128)(2,1)S(1)}, bf16[128,128]{1,0:T(8,128)(2,1)}, u32[]{:S(2)}) copy-start(bf16[128,128]{1,0:T(8,128)(2,1)} %output_ref.1) | copy-start | bytes 98308
  14.8 1.2 %collective-permute-start.5 = (bf16[2,112,128]{2,1,0:T(8,128)(2,1)S(1)}, bf16[2,112,128]{2,1,0:T(8,128)(2,1)S(1)}, u32[]{:S(2)}, u32[]{:S(2)}) collective-permute-start(bf16[2,112,128]{2,1,0:T(8,128)(2,1)S(1)} %collective-permute-done.3), channel_id=1, source_target_pairs={{0,1},{1,0},{2,3},{3,2},{4,5},{5,4},{6,7},{7,6},{8,9},{9,8},{10,11... | collective-permute-start | bytes 172040 | tf_op jit(solution)/shard_map/ppermute | solution.py:286
  15.0 1.1 %copy-start.3 = (bf16[512,128]{1,0:T(8,128)(2,1)S(1)}, bf16[512,128]{1,0:T(8,128)(2,1)}, u32[]{:S(2)}) copy-start(bf16[512,128]{1,0:T(8,128)(2,1)} %down_ref.1) | copy-start | bytes 393220
  15.0 1.1 %copy-start = (bf16[32,32,128]{2,1,0:T(8,128)(2,1)S(1)}, bf16[32,32,128]{2,1,0:T(8,128)(2,1)}, u32[]{:S(2)}) copy-start(bf16[32,32,128]{2,1,0:T(8,128)(2,1)} %outer_ref.1) | copy-start | bytes 786436
  15.0 1.0 %copy-start.1 = (bf16[4,128,128]{2,1,0:T(8,128)(2,1)S(1)}, bf16[4,128,128]{2,1,0:T(8,128)(2,1)}, u32[]{:S(2)}) copy-start(bf16[4,128,128]{2,1,0:T(8,128)(2,1)} %triangle_ref.1) | copy-start | bytes 393220
  15.1 1.1 %copy-start.2 = (bf16[128,512]{1,0:T(8,128)(2,1)S(1)}, bf16[128,512]{1,0:T(8,128)(2,1)}, u32[]{:S(2)}) copy-start(bf16[128,512]{1,0:T(8,128)(2,1)} %up_ref.1) | copy-start | bytes 393220
  15.1 1.1 %copy-start.4 = (bf16[128,128]{1,0:T(8,128)(2,1)S(1)}, bf16[128,128]{1,0:T(8,128)(2,1)}, u32[]{:S(2)}) copy-start(bf16[128,128]{1,0:T(8,128)(2,1)} %gate_ref.1) | copy-start | bytes 98308

commit v21 on v20

--- a/solution.py
+++ b/solution.py
@@ -160,9 +160,11 @@
     lane_block = lane // channels
     low = lane < half
     for chip in range(chips):
-        place = block_place(chip, chips)
-        mine, other = held_ref[place], other_ref[place]
-        blocks = [jnp.where(second_core, other, mine), jnp.where(second_core, mine, other)]
+        places = [block_place(chip, chips, core) for core in range(cores)]
+        blocks = [
+            jnp.where(second_core, other_ref[places[0]], held_ref[places[0]]),
+            jnp.where(second_core, held_ref[places[1]], other_ref[places[1]]),
+        ]
         packed = [block[base : base + sequences].astype(f32) for block in blocks]
         right = jnp.where(low, packed[0], packed[1])
         for turn, value in enumerate((right, pltpu.roll(right, half, 1))):
@@ -277,26 +279,34 @@
     half = dap_count // 2
     far = lax.ppermute(packed[None], "dap", [(src, src ^ half) for src in range(dap_count)])
     both = jnp.concatenate([packed[None], far], axis=0)
-    held = [both] + [
-        lax.ppermute(both, "dap", [(src, src ^ offset) for src in range(dap_count)])
-        for offset in swap_order(dap_count)
-    ]
+    orders = [swap_order(dap_count, core) for core in range(2)]
+    held = [both]
+    for turn in range(half - 1):
+        pairs = [
+            (2 * chip + core, 2 * (chip ^ orders[core][turn]) + core)
+            for core in range(2)
+            for chip in range(dap_count)
+        ]
+        held.append(lax.ppermute(both, ("dap", "sub"), pairs))
     sibling = [(0, 1), (1, 0)]
     early = lax.ppermute(jnp.concatenate(held[:-1], axis=0), "sub", sibling)
     late = lax.ppermute(held[-1], "sub", sibling)
     return jnp.concatenate(held, axis=0), jnp.concatenate([early, late], axis=0)
 
 
-def swap_order(dap_count):
+def swap_order(dap_count, core):
     near = dap_count // 2
-    return [1, near - 1] + list(range(2, near - 1))
-
-
-def block_place(chip, chips):
+    order = [1, near - 1] + list(range(2, near - 1))
+    return order if core == 0 else order[::-1]
+
+
+def block_place(chip, chips, core):
     offset = lax.bitwise_xor(lax.axis_index("dap"), chip)
     half = chips // 2
     near = jnp.where(offset >= half, offset - half, offset)
-    turn = jnp.where(near > 1, jnp.where(near == half - 1, 2, near + 1), near)
+    turn = 0
+    for place, one in enumerate(swap_order(chips, core)):
+        turn = turn + jnp.where(near == one, place + 1, 0)
     return 2 * turn + jnp.where(offset >= half, 1, 0)
 
 

time: 20.1 us -> 20.2 us (level)
  no operation moved by 1% of the time
where the time goes in v21:
time: 20.2 us; the launch traced here: 20 us
  starting transfers between devices  8 us (40%)
  waiting for transfers between devices  6.65 us (33%)
  Pallas kernels  5.03 us (25%)
    ppermute x1, starting transfers between devices, gather_all(): lax.ppermute(packed[None], 'dap', [(src, src ^ half) for src in range(dap...  4.1 us
    ppermute x3, waiting for transfers between devices, gather_all(): held.append(lax.ppermute(both, ('dap', 'sub'), pairs))  3.85 us
    pallas_call x1, Pallas kernels, shards_replicated(): pl.pallas_call(update_kernel, out_shape=jax.ShapeDtypeStruct(pairwise_sta...  3.84 us
    ppermute x3, starting transfers between devices, gather_all(): held.append(lax.ppermute(both, ('dap', 'sub'), pairs))  3.6 us
    ppermute x1, waiting for transfers between devices, gather_all(): lax.ppermute(packed[None], 'dap', [(src, src ^ half) for src in range(dap...  1.86 us
    pallas_call x1, Pallas kernels, shards_replicated(): pl.pallas_call(pack_kernel, out_shape=jax.ShapeDtypeStruct((rows * residu...  1.2 us
    ppermute x1, waiting for transfers between devices, gather_all(): late = lax.ppermute(held[-1], 'sub', sibling)  0.93 us
  transfers between devices with their start and end apart: 6, of which 5 were waited for; matrix products, arithmetic and copies ran while one was open for 0% of the time, Pallas kernels for 0%

profile of v21, /device:TPU:0, one launch (start us, length us, event | category | flops | bytes accessed | tf_op | source)
XLA Modules:
  0.0 20.0 jit_solution(9588882443415209807)
XLA Ops:
  0.0 1.2 %shard_map.109 = bf16[112,128]{1,0:T(8,128)(2,1)S(1)} custom-call(s32[32]{0:T(128)} %mask_hbm.1, s32[2,32]{1,0:T(2,128)} %bitcast.8, bf16[32,2,256]{2,1,0:T(2,128)(2,1)} %state_hbm.1, bf16[2,32,256]{2,1,0:T(8,128)(2,1)} %bitcast.7, bf16[2,32,128]{2,1,0:T(8,128)(2,1)} %pair_hbm.1), custom_call_target="tpu_custom_call" | custom-call | tf_op jit(solution)/shard_map/pallas_call | solution.py:332
  1.2 4.1 %collective-permute-start = (bf16[1,112,128]{2,1,0:T(8,128)(2,1)S(1)}, bf16[1,112,128]{2,1,0:T(8,128)(2,1)S(1)}, u32[]{:S(2)}, u32[]{:S(2)}) collective-permute-start(bf16[1,112,128]{2,1,0:T(8,128)(2,1)S(1)} %bitcast.4), channel_id=1, source_target_pairs={{0,8},{2,10},{4,12},{6,14},{8,0},{10,2},{12,4},{14,6},{1,9},{3,11}... | collective-permute-start | bytes 86024 | tf_op jit(solution)/shard_map/ppermute | solution.py:280
  5.3 1.9 %collective-permute-done = bf16[1,112,128]{2,1,0:T(8,128)(2,1)S(1)} collective-permute-done((bf16[1,112,128]{2,1,0:T(8,128)(2,1)S(1)}, bf16[1,112,128]{2,1,0:T(8,128)(2,1)S(1)}, u32[]{:S(2)}, u32[]{:S(2)}) %collective-permute-start) | collective-permute-done | bytes 28704 | tf_op jit(solution)/shard_map/ppermute | solution.py:280
  7.2 2.1 %collective-permute-start.1 = (bf16[2,112,128]{2,1,0:T(8,128)(2,1)S(1)}, bf16[2,112,128]{2,1,0:T(8,128)(2,1)S(1)}, u32[]{:S(2)}, u32[]{:S(2)}) collective-permute-start(bf16[2,112,128]{2,1,0:T(8,128)(2,1)S(1)} %pad_maximum_fusion.2), channel_id=1, source_target_pairs={{0,2},{2,0},{4,6},{6,4},{8,10},{10,8},{12,14},{14,12},{1,5},{3,7},... | collective-permute-start | bytes 172040 | tf_op jit(solution)/shard_map/ppermute | solution.py:290
  9.2 1.4 %collective-permute-start.2 = (bf16[2,112,128]{2,1,0:T(8,128)(2,1)S(1)}, bf16[2,112,128]{2,1,0:T(8,128)(2,1)S(1)}, u32[]{:S(2)}, u32[]{:S(2)}) collective-permute-start(bf16[2,112,128]{2,1,0:T(8,128)(2,1)S(1)} %pad_maximum_fusion.2), channel_id=1, source_target_pairs={{0,6},{2,4},{4,2},{6,0},{8,14},{10,12},{12,10},{14,8},{1,7},{3,5},... | collective-permute-start | bytes 172040 | tf_op jit(solution)/shard_map/ppermute | solution.py:290
  10.6 0.2 collective-permute-start.3
  10.8 1.5 %collective-permute-done.1 = bf16[2,112,128]{2,1,0:T(8,128)(2,1)S(1)} collective-permute-done((bf16[2,112,128]{2,1,0:T(8,128)(2,1)S(1)}, bf16[2,112,128]{2,1,0:T(8,128)(2,1)S(1)}, u32[]{:S(2)}, u32[]{:S(2)}) %collective-permute-start.1) | collective-permute-done | bytes 57376 | tf_op jit(solution)/shard_map/ppermute | solution.py:290
  12.3 2.0 %collective-permute-done.2 = bf16[2,112,128]{2,1,0:T(8,128)(2,1)S(1)} collective-permute-done((bf16[2,112,128]{2,1,0:T(8,128)(2,1)S(1)}, bf16[2,112,128]{2,1,0:T(8,128)(2,1)S(1)}, u32[]{:S(2)}, u32[]{:S(2)}) %collective-permute-start.2) | collective-permute-done | bytes 57376 | tf_op jit(solution)/shard_map/ppermute | solution.py:290
  14.3 0.1 collective-permute-start.4
  14.4 0.0 copy-start.5
  14.4 0.3 %collective-permute-done.3 = bf16[2,112,128]{2,1,0:T(8,128)(2,1)S(1)} collective-permute-done((bf16[2,112,128]{2,1,0:T(8,128)(2,1)S(1)}, bf16[2,112,128]{2,1,0:T(8,128)(2,1)S(1)}, u32[]{:S(2)}, u32[]{:S(2)}) %collective-permute-start.3) | collective-permute-done | bytes 57376 | tf_op jit(solution)/shard_map/ppermute | solution.py:290
  14.8 0.2 %collective-permute-start.5 = (bf16[2,112,128]{2,1,0:T(8,128)(2,1)S(1)}, bf16[2,112,128]{2,1,0:T(8,128)(2,1)S(1)}, u32[]{:S(2)}, u32[]{:S(2)}) collective-permute-start(bf16[2,112,128]{2,1,0:T(8,128)(2,1)S(1)} %collective-permute-done.3), channel_id=1, source_target_pairs={{0,1},{1,0},{2,3},{3,2},{4,5},{5,4},{6,7},{7,6},{8,9},{9,8},{10,11... | collective-permute-start | bytes 172040 | tf_op jit(solution)/shard_map/ppermute | solution.py:293
  15.0 0.0 copy-start
  15.0 0.0 copy-start.1
  15.1 0.0 copy-start.2
  15.1 0.0 copy-start.4
  15.1 0.9 %collective-permute-done.5 = bf16[2,112,128]{2,1,0:T(8,128)(2,1)S(1)} collective-permute-done((bf16[2,112,128]{2,1,0:T(8,128)(2,1)S(1)}, bf16[2,112,128]{2,1,0:T(8,128)(2,1)S(1)}, u32[]{:S(2)}, u32[]{:S(2)}) %collective-permute-start.5) | collective-permute-done | bytes 57376 | tf_op jit(solution)/shard_map/ppermute | solution.py:293
  16.0 0.0 collective-permute-done.4
  16.0 0.0 copy-done.5
  16.1 0.0 copy-done.3
  16.1 0.0 copy-done
  16.1 0.0 copy-done.2
  16.1 0.0 copy-done.4
  16.1 3.8 %shard_map.110 = bf16[2,32,128]{2,1,0:T(8,128)(2,1)} custom-call(bf16[8,112,128]{2,1,0:T(8,128)(2,1)S(1)} %constant_dynamic-update-slice_fusion.held_ref, bf16[8,112,128]{2,1,0:T(8,128)(2,1)S(1)} %pad_maximum_fusion.other_ref, bf16[32,32,128]{2,1,0:T(8,128)(2,1)S(1)} %copy-done, bf16[4,128,128]{2,1,0:T(8,128)(2,1)S(1)} %copy-done.1, ...), custom_call_target="tpu_custom_call" | custom-call | tf_op jit(solution)/shard_map/pallas_call | solution.py:362
  (10 shorter events, 0.1 us)
Async XLA Ops:
  1.2 6.0 %collective-permute-start = (bf16[1,112,128]{2,1,0:T(8,128)(2,1)S(1)}, bf16[1,112,128]{2,1,0:T(8,128)(2,1)S(1)}, u32[]{:S(2)}, u32[]{:S(2)}) collective-permute-start(bf16[1,112,128]{2,1,0:T(8,128)(2,1)S(1)} %bitcast.4), channel_id=1, source_target_pairs={{0,8},{2,10},{4,12},{6,14},{8,0},{10,2},{12,4},{14,6},{1,9},{3,11}... | collective-permute-start | bytes 86024 | tf_op jit(solution)/shard_map/ppermute | solution.py:280
  7.2 5.1 %collective-permute-start.1 = (bf16[2,112,128]{2,1,0:T(8,128)(2,1)S(1)}, bf16[2,112,128]{2,1,0:T(8,128)(2,1)S(1)}, u32[]{:S(2)}, u32[]{:S(2)}) collective-permute-start(bf16[2,112,128]{2,1,0:T(8,128)(2,1)S(1)} %pad_maximum_fusion.2), channel_id=1, source_target_pairs={{0,2},{2,0},{4,6},{6,4},{8,10},{10,8},{12,14},{14,12},{1,5},{3,7},... | collective-permute-start | bytes 172040 | tf_op jit(solution)/shard_map/ppermute | solution.py:290
  9.2 5.1 %collective-permute-start.2 = (bf16[2,112,128]{2,1,0:T(8,128)(2,1)S(1)}, bf16[2,112,128]{2,1,0:T(8,128)(2,1)S(1)}, u32[]{:S(2)}, u32[]{:S(2)}) collective-permute-start(bf16[2,112,128]{2,1,0:T(8,128)(2,1)S(1)} %pad_maximum_fusion.2), channel_id=1, source_target_pairs={{0,6},{2,4},{4,2},{6,0},{8,14},{10,12},{12,10},{14,8},{1,7},{3,5},... | collective-permute-start | bytes 172040 | tf_op jit(solution)/shard_map/ppermute | solution.py:290
  10.6 4.2 %collective-permute-start.3 = (bf16[2,112,128]{2,1,0:T(8,128)(2,1)S(1)}, bf16[2,112,128]{2,1,0:T(8,128)(2,1)S(1)}, u32[]{:S(2)}, u32[]{:S(2)}) collective-permute-start(bf16[2,112,128]{2,1,0:T(8,128)(2,1)S(1)} %pad_maximum_fusion.2), channel_id=1, source_target_pairs={{0,4},{2,6},{4,0},{6,2},{8,12},{10,14},{12,8},{14,10},{1,3},{3,1},... | collective-permute-start | bytes 172040 | tf_op jit(solution)/shard_map/ppermute | solution.py:290
  14.3 1.7 %collective-permute-start.4 = (bf16[6,112,128]{2,1,0:T(8,128)(2,1)S(1)}, bf16[6,112,128]{2,1,0:T(8,128)(2,1)S(1)}, u32[]{:S(2)}, u32[]{:S(2)}) collective-permute-start(bf16[6,112,128]{2,1,0:T(8,128)(2,1)S(1)} %pad_maximum_fusion.1), channel_id=1, source_target_pairs={{0,1},{1,0},{2,3},{3,2},{4,5},{5,4},{6,7},{7,6},{8,9},{9,8},{10,11... | collective-permute-start | bytes 516104 | tf_op jit(solution)/shard_map/ppermute | solution.py:292
  14.4 1.6 %copy-start.5 = (bf16[128,128]{1,0:T(8,128)(2,1)S(1)}, bf16[128,128]{1,0:T(8,128)(2,1)}, u32[]{:S(2)}) copy-start(bf16[128,128]{1,0:T(8,128)(2,1)} %output_ref.1) | copy-start | bytes 98308
  14.8 1.2 %collective-permute-start.5 = (bf16[2,112,128]{2,1,0:T(8,128)(2,1)S(1)}, bf16[2,112,128]{2,1,0:T(8,128)(2,1)S(1)}, u32[]{:S(2)}, u32[]{:S(2)}) collective-permute-start(bf16[2,112,128]{2,1,0:T(8,128)(2,1)S(1)} %collective-permute-done.3), channel_id=1, source_target_pairs={{0,1},{1,0},{2,3},{3,2},{4,5},{5,4},{6,7},{7,6},{8,9},{9,8},{10,11... | collective-permute-start | bytes 172040 | tf_op jit(solution)/shard_map/ppermute | solution.py:293
  15.0 1.1 %copy-start.3 = (bf16[512,128]{1,0:T(8,128)(2,1)S(1)}, bf16[512,128]{1,0:T(8,128)(2,1)}, u32[]{:S(2)}) copy-start(bf16[512,128]{1,0:T(8,128)(2,1)} %down_ref.1) | copy-start | bytes 393220
  15.0 1.1 %copy-start = (bf16[32,32,128]{2,1,0:T(8,128)(2,1)S(1)}, bf16[32,32,128]{2,1,0:T(8,128)(2,1)}, u32[]{:S(2)}) copy-start(bf16[32,32,128]{2,1,0:T(8,128)(2,1)} %outer_ref.1) | copy-start | bytes 786436
  15.0 1.0 %copy-start.1 = (bf16[4,128,128]{2,1,0:T(8,128)(2,1)S(1)}, bf16[4,128,128]{2,1,0:T(8,128)(2,1)}, u32[]{:S(2)}) copy-start(bf16[4,128,128]{2,1,0:T(8,128)(2,1)} %triangle_ref.1) | copy-start | bytes 393220
  15.1 1.1 %copy-start.2 = (bf16[128,512]{1,0:T(8,128)(2,1)S(1)}, bf16[128,512]{1,0:T(8,128)(2,1)}, u32[]{:S(2)}) copy-start(bf16[128,512]{1,0:T(8,128)(2,1)} %up_ref.1) | copy-start | bytes 393220
  15.1 1.1 %copy-start.4 = (bf16[128,128]{1,0:T(8,128)(2,1)S(1)}, bf16[128,128]{1,0:T(8,128)(2,1)}, u32[]{:S(2)}) copy-start(bf16[128,128]{1,0:T(8,128)(2,1)} %gate_ref.1) | copy-start | bytes 98308

commit v22 on v20

--- a/solution.py
+++ b/solution.py
@@ -282,9 +282,10 @@
         for offset in swap_order(dap_count)
     ]
     sibling = [(0, 1), (1, 0)]
-    early = lax.ppermute(jnp.concatenate(held[:-1], axis=0), "sub", sibling)
+    first = lax.ppermute(both, "sub", sibling)
+    early = lax.ppermute(jnp.concatenate(held[1:-1], axis=0), "sub", sibling)
     late = lax.ppermute(held[-1], "sub", sibling)
-    return jnp.concatenate(held, axis=0), jnp.concatenate([early, late], axis=0)
+    return jnp.concatenate(held, axis=0), jnp.concatenate([first, early, late], axis=0)
 
 
 def swap_order(dap_count):

time: 20.1 us -> 20.1 us (level)
  transfers between devices with their start and end apart: 6 -> 7, of which waited for: 5 -> 5; matrix products, arithmetic and copies ran while one was open for 0% -> 0% of each run, Pallas kernels for 0% -> 0%
where the time goes in v22:
time: 20.1 us; the launch traced here: 19.9 us
  starting transfers between devices  8.03 us (40%)
  waiting for transfers between devices  6.6 us (33%)
  Pallas kernels  5 us (25%)
    ppermute x1, starting transfers between devices, gather_all(): lax.ppermute(packed[None], 'dap', [(src, src ^ half) for src in range(dap...  4.1 us
    ppermute x3, waiting for transfers between devices, gather_all(): lax.ppermute(both, 'dap', [(src, src ^ offset) for src in range(dap_count)])  3.82 us
    pallas_call x1, Pallas kernels, shards_replicated(): pl.pallas_call(update_kernel, out_shape=jax.ShapeDtypeStruct(pairwise_sta...  3.8 us
    ppermute x3, starting transfers between devices, gather_all(): lax.ppermute(both, 'dap', [(src, src ^ offset) for src in range(dap_count)])  3.6 us
    ppermute x1, waiting for transfers between devices, gather_all(): lax.ppermute(packed[None], 'dap', [(src, src ^ half) for src in range(dap...  1.86 us
    pallas_call x1, Pallas kernels, shards_replicated(): pl.pallas_call(pack_kernel, out_shape=jax.ShapeDtypeStruct((rows * residu...  1.2 us
    ppermute x1, waiting for transfers between devices, gather_all(): late = lax.ppermute(held[-1], 'sub', sibling)  0.92 us
  transfers between devices with their start and end apart: 7, of which 5 were waited for; matrix products, arithmetic and copies ran while one was open for 0% of the time, Pallas kernels for 0%

profile of v22, /device:TPU:0, one launch (start us, length us, event | category | flops | bytes accessed | tf_op | source)
XLA Modules:
  0.0 19.9 jit_solution(163591763430319457)
XLA Ops:
  0.0 1.2 %shard_map.109 = bf16[112,128]{1,0:T(8,128)(2,1)S(1)} custom-call(s32[32]{0:T(128)} %mask_hbm.1, s32[2,32]{1,0:T(2,128)} %bitcast.7, bf16[32,2,256]{2,1,0:T(2,128)(2,1)} %state_hbm.1, bf16[2,32,256]{2,1,0:T(8,128)(2,1)} %bitcast.6, bf16[2,32,128]{2,1,0:T(8,128)(2,1)} %pair_hbm.1), custom_call_target="tpu_custom_call" | custom-call | tf_op jit(solution)/shard_map/pallas_call | solution.py:323
  1.2 4.1 %collective-permute-start = (bf16[1,112,128]{2,1,0:T(8,128)(2,1)S(1)}, bf16[1,112,128]{2,1,0:T(8,128)(2,1)S(1)}, u32[]{:S(2)}, u32[]{:S(2)}) collective-permute-start(bf16[1,112,128]{2,1,0:T(8,128)(2,1)S(1)} %bitcast.4), channel_id=1, source_target_pairs={{0,8},{2,10},{4,12},{6,14},{8,0},{10,2},{12,4},{14,6},{1,9},{3,11}... | collective-permute-start | bytes 86024 | tf_op jit(solution)/shard_map/ppermute | solution.py:278
  5.3 1.9 %collective-permute-done = bf16[1,112,128]{2,1,0:T(8,128)(2,1)S(1)} collective-permute-done((bf16[1,112,128]{2,1,0:T(8,128)(2,1)S(1)}, bf16[1,112,128]{2,1,0:T(8,128)(2,1)S(1)}, u32[]{:S(2)}, u32[]{:S(2)}) %collective-permute-start) | collective-permute-done | bytes 28704 | tf_op jit(solution)/shard_map/ppermute | solution.py:278
  7.2 2.1 %collective-permute-start.1 = (bf16[2,112,128]{2,1,0:T(8,128)(2,1)S(1)}, bf16[2,112,128]{2,1,0:T(8,128)(2,1)S(1)}, u32[]{:S(2)}, u32[]{:S(2)}) collective-permute-start(bf16[2,112,128]{2,1,0:T(8,128)(2,1)S(1)} %pad_maximum_fusion.2), channel_id=1, source_target_pairs={{0,2},{2,0},{4,6},{6,4},{8,10},{10,8},{12,14},{14,12},{1,3},{3,1},... | collective-permute-start | bytes 172040 | tf_op jit(solution)/shard_map/ppermute | solution.py:281
  9.2 1.4 %collective-permute-start.2 = (bf16[2,112,128]{2,1,0:T(8,128)(2,1)S(1)}, bf16[2,112,128]{2,1,0:T(8,128)(2,1)S(1)}, u32[]{:S(2)}, u32[]{:S(2)}) collective-permute-start(bf16[2,112,128]{2,1,0:T(8,128)(2,1)S(1)} %pad_maximum_fusion.2), channel_id=1, source_target_pairs={{0,6},{2,4},{4,2},{6,0},{8,14},{10,12},{12,10},{14,8},{1,7},{3,5},... | collective-permute-start | bytes 172040 | tf_op jit(solution)/shard_map/ppermute | solution.py:281
  10.6 0.2 collective-permute-start.3
  10.8 0.0 collective-permute-start.4
  10.8 1.2 %collective-permute-done.1 = bf16[2,112,128]{2,1,0:T(8,128)(2,1)S(1)} collective-permute-done((bf16[2,112,128]{2,1,0:T(8,128)(2,1)S(1)}, bf16[2,112,128]{2,1,0:T(8,128)(2,1)S(1)}, u32[]{:S(2)}, u32[]{:S(2)}) %collective-permute-start.1) | collective-permute-done | bytes 57376 | tf_op jit(solution)/shard_map/ppermute | solution.py:281
  12.0 2.3 %collective-permute-done.2 = bf16[2,112,128]{2,1,0:T(8,128)(2,1)S(1)} collective-permute-done((bf16[2,112,128]{2,1,0:T(8,128)(2,1)S(1)}, bf16[2,112,128]{2,1,0:T(8,128)(2,1)S(1)}, u32[]{:S(2)}, u32[]{:S(2)}) %collective-permute-start.2) | collective-permute-done | bytes 57376 | tf_op jit(solution)/shard_map/ppermute | solution.py:281
  14.3 0.1 collective-permute-start.5
  14.4 0.0 copy-start.5
  14.4 0.0 copy-start.3
  14.5 0.0 copy-start
  14.5 0.3 %collective-permute-done.3 = bf16[2,112,128]{2,1,0:T(8,128)(2,1)S(1)} collective-permute-done((bf16[2,112,128]{2,1,0:T(8,128)(2,1)S(1)}, bf16[2,112,128]{2,1,0:T(8,128)(2,1)S(1)}, u32[]{:S(2)}, u32[]{:S(2)}) %collective-permute-start.3) | collective-permute-done | bytes 57376 | tf_op jit(solution)/shard_map/ppermute | solution.py:281
  14.8 0.3 %collective-permute-start.6 = (bf16[2,112,128]{2,1,0:T(8,128)(2,1)S(1)}, bf16[2,112,128]{2,1,0:T(8,128)(2,1)S(1)}, u32[]{:S(2)}, u32[]{:S(2)}) collective-permute-start(bf16[2,112,128]{2,1,0:T(8,128)(2,1)S(1)} %collective-permute-done.3), channel_id=1, source_target_pairs={{0,1},{1,0},{2,3},{3,2},{4,5},{5,4},{6,7},{7,6},{8,9},{9,8},{10,11... | collective-permute-start | bytes 172040 | tf_op jit(solution)/shard_map/ppermute | solution.py:287
  15.0 0.0 copy-start.1
  15.1 0.0 copy-start.2
  15.1 0.0 copy-start.4
  15.1 0.0 collective-permute-done.4
  15.1 0.9 %collective-permute-done.6 = bf16[2,112,128]{2,1,0:T(8,128)(2,1)S(1)} collective-permute-done((bf16[2,112,128]{2,1,0:T(8,128)(2,1)S(1)}, bf16[2,112,128]{2,1,0:T(8,128)(2,1)S(1)}, u32[]{:S(2)}, u32[]{:S(2)}) %collective-permute-start.6) | collective-permute-done | bytes 57376 | tf_op jit(solution)/shard_map/ppermute | solution.py:287
  16.0 0.0 collective-permute-done.5
  16.1 0.0 copy-done.5
  16.1 0.0 copy-done.3
  16.1 3.8 %shard_map.110 = bf16[2,32,128]{2,1,0:T(8,128)(2,1)} custom-call(bf16[8,112,128]{2,1,0:T(8,128)(2,1)S(1)} %constant_dynamic-update-slice_fusion.held_ref, bf16[8,112,128]{2,1,0:T(8,128)(2,1)S(1)} %pad_maximum_fusion.other_ref, bf16[32,32,128]{2,1,0:T(8,128)(2,1)S(1)} %copy-done, bf16[4,128,128]{2,1,0:T(8,128)(2,1)S(1)} %copy-done.1, ...), custom_call_target="tpu_custom_call" | custom-call | tf_op jit(solution)/shard_map/pallas_call | solution.py:353
  (12 shorter events, 0.1 us)
Async XLA Ops:
  1.2 6.0 %collective-permute-start = (bf16[1,112,128]{2,1,0:T(8,128)(2,1)S(1)}, bf16[1,112,128]{2,1,0:T(8,128)(2,1)S(1)}, u32[]{:S(2)}, u32[]{:S(2)}) collective-permute-start(bf16[1,112,128]{2,1,0:T(8,128)(2,1)S(1)} %bitcast.4), channel_id=1, source_target_pairs={{0,8},{2,10},{4,12},{6,14},{8,0},{10,2},{12,4},{14,6},{1,9},{3,11}... | collective-permute-start | bytes 86024 | tf_op jit(solution)/shard_map/ppermute | solution.py:278
  7.2 4.9 %collective-permute-start.1 = (bf16[2,112,128]{2,1,0:T(8,128)(2,1)S(1)}, bf16[2,112,128]{2,1,0:T(8,128)(2,1)S(1)}, u32[]{:S(2)}, u32[]{:S(2)}) collective-permute-start(bf16[2,112,128]{2,1,0:T(8,128)(2,1)S(1)} %pad_maximum_fusion.2), channel_id=1, source_target_pairs={{0,2},{2,0},{4,6},{6,4},{8,10},{10,8},{12,14},{14,12},{1,3},{3,1},... | collective-permute-start | bytes 172040 | tf_op jit(solution)/shard_map/ppermute | solution.py:281
  9.2 5.1 %collective-permute-start.2 = (bf16[2,112,128]{2,1,0:T(8,128)(2,1)S(1)}, bf16[2,112,128]{2,1,0:T(8,128)(2,1)S(1)}, u32[]{:S(2)}, u32[]{:S(2)}) collective-permute-start(bf16[2,112,128]{2,1,0:T(8,128)(2,1)S(1)} %pad_maximum_fusion.2), channel_id=1, source_target_pairs={{0,6},{2,4},{4,2},{6,0},{8,14},{10,12},{12,10},{14,8},{1,7},{3,5},... | collective-permute-start | bytes 172040 | tf_op jit(solution)/shard_map/ppermute | solution.py:281
  10.6 4.2 %collective-permute-start.3 = (bf16[2,112,128]{2,1,0:T(8,128)(2,1)S(1)}, bf16[2,112,128]{2,1,0:T(8,128)(2,1)S(1)}, u32[]{:S(2)}, u32[]{:S(2)}) collective-permute-start(bf16[2,112,128]{2,1,0:T(8,128)(2,1)S(1)} %pad_maximum_fusion.2), channel_id=1, source_target_pairs={{0,4},{2,6},{4,0},{6,2},{8,12},{10,14},{12,8},{14,10},{1,5},{3,7},... | collective-permute-start | bytes 172040 | tf_op jit(solution)/shard_map/ppermute | solution.py:281
  10.8 4.3 %collective-permute-start.4 = (bf16[2,112,128]{2,1,0:T(8,128)(2,1)S(1)}, bf16[2,112,128]{2,1,0:T(8,128)(2,1)S(1)}, u32[]{:S(2)}, u32[]{:S(2)}) collective-permute-start(bf16[2,112,128]{2,1,0:T(8,128)(2,1)S(1)} %pad_maximum_fusion.2), channel_id=1, source_target_pairs={{0,1},{1,0},{2,3},{3,2},{4,5},{5,4},{6,7},{7,6},{8,9},{9,8},{10,11... | collective-permute-start | bytes 172040 | tf_op jit(solution)/shard_map/ppermute | solution.py:285
  14.3 1.7 %collective-permute-start.5 = (bf16[4,112,128]{2,1,0:T(8,128)(2,1)S(1)}, bf16[4,112,128]{2,1,0:T(8,128)(2,1)S(1)}, u32[]{:S(2)}, u32[]{:S(2)}) collective-permute-start(bf16[4,112,128]{2,1,0:T(8,128)(2,1)S(1)} %pad_maximum_fusion.1), channel_id=1, source_target_pairs={{0,1},{1,0},{2,3},{3,2},{4,5},{5,4},{6,7},{7,6},{8,9},{9,8},{10,11... | collective-permute-start | bytes 344072 | tf_op jit(solution)/shard_map/ppermute | solution.py:286
  14.4 1.7 %copy-start.5 = (bf16[128,128]{1,0:T(8,128)(2,1)S(1)}, bf16[128,128]{1,0:T(8,128)(2,1)}, u32[]{:S(2)}) copy-start(bf16[128,128]{1,0:T(8,128)(2,1)} %output_ref.1) | copy-start | bytes 98308
  14.4 1.6 %copy-start.3 = (bf16[512,128]{1,0:T(8,128)(2,1)S(1)}, bf16[512,128]{1,0:T(8,128)(2,1)}, u32[]{:S(2)}) copy-start(bf16[512,128]{1,0:T(8,128)(2,1)} %down_ref.1) | copy-start | bytes 393220
  14.5 1.6 %copy-start = (bf16[32,32,128]{2,1,0:T(8,128)(2,1)S(1)}, bf16[32,32,128]{2,1,0:T(8,128)(2,1)}, u32[]{:S(2)}) copy-start(bf16[32,32,128]{2,1,0:T(8,128)(2,1)} %outer_ref.1) | copy-start | bytes 786436
  14.8 1.2 %collective-permute-start.6 = (bf16[2,112,128]{2,1,0:T(8,128)(2,1)S(1)}, bf16[2,112,128]{2,1,0:T(8,128)(2,1)S(1)}, u32[]{:S(2)}, u32[]{:S(2)}) collective-permute-start(bf16[2,112,128]{2,1,0:T(8,128)(2,1)S(1)} %collective-permute-done.3), channel_id=1, source_target_pairs={{0,1},{1,0},{2,3},{3,2},{4,5},{5,4},{6,7},{7,6},{8,9},{9,8},{10,11... | collective-permute-start | bytes 172040 | tf_op jit(solution)/shard_map/ppermute | solution.py:287
  15.0 1.0 %copy-start.1 = (bf16[4,128,128]{2,1,0:T(8,128)(2,1)S(1)}, bf16[4,128,128]{2,1,0:T(8,128)(2,1)}, u32[]{:S(2)}) copy-start(bf16[4,128,128]{2,1,0:T(8,128)(2,1)} %triangle_ref.1) | copy-start | bytes 393220
  15.1 1.0 %copy-start.2 = (bf16[128,512]{1,0:T(8,128)(2,1)S(1)}, bf16[128,512]{1,0:T(8,128)(2,1)}, u32[]{:S(2)}) copy-start(bf16[128,512]{1,0:T(8,128)(2,1)} %up_ref.1) | copy-start | bytes 393220
  15.1 1.0 %copy-start.4 = (bf16[128,128]{1,0:T(8,128)(2,1)S(1)}, bf16[128,128]{1,0:T(8,128)(2,1)}, u32[]{:S(2)}) copy-start(bf16[128,128]{1,0:T(8,128)(2,1)} %gate_ref.1) | copy-start | bytes 98308

commit v23 on v22

--- a/solution.py
+++ b/solution.py
@@ -146,16 +146,6 @@
 
     parts = block_ref.shape[0]
     span = channels // parts
-    nothing = jnp.zeros((channels, wide), bf16)
-    for part in range(parts):
-        for step in range(span + 1):
-            weight = outer_ref[part * span + step % span]
-            at = step * 2 * channels
-            block_ref[part, at : at + channels, :wide] = weight
-            block_ref[part, at : at + channels, wide:] = nothing
-            block_ref[part, at + channels : at + 2 * channels, :wide] = nothing
-            block_ref[part, at + channels : at + 2 * channels, wide:] = weight
-
     lane = lax.broadcasted_iota(jnp.int32, (channels, wide), 1)
     lane_block = lane // channels
     low = lane < half
@@ -203,6 +193,15 @@
                 [left_ref[:, d] for d in range(part * span + turn, (part + 1) * span, 2)], axis=0
             ).astype(bf16)
             outer.append(jnp.dot(left, right_ref[turn], preferred_element_type=f32).astype(bf16))
+
+        nothing = jnp.zeros((channels, wide), bf16)
+        for step in range(span + 1):
+            weight = outer_ref[part * span + step % span]
+            at = step * 2 * channels
+            block_ref[part, at : at + channels, :wide] = weight
+            block_ref[part, at : at + channels, wide:] = nothing
+            block_ref[part, at + channels : at + 2 * channels, :wide] = nothing
+            block_ref[part, at + channels : at + 2 * channels, wide:] = weight
 
         def piece(turn, at, chip):
             return outer[turn][

time: 20.1 us -> 20.1 us (level)
  no operation moved by 1% of the time
where the time goes in v23:
time: 20.1 us; the launch traced here: 19.9 us
  starting transfers between devices  8.03 us (40%)
  waiting for transfers between devices  6.6 us (33%)
  Pallas kernels  5 us (25%)
    ppermute x1, starting transfers between devices, gather_all(): lax.ppermute(packed[None], 'dap', [(src, src ^ half) for src in range(dap...  4.1 us
    ppermute x3, waiting for transfers between devices, gather_all(): lax.ppermute(both, 'dap', [(src, src ^ offset) for src in range(dap_count)])  3.82 us
    pallas_call x1, Pallas kernels, shards_replicated(): pl.pallas_call(update_kernel, out_shape=jax.ShapeDtypeStruct(pairwise_sta...  3.8 us
    ppermute x3, starting transfers between devices, gather_all(): lax.ppermute(both, 'dap', [(src, src ^ offset) for src in range(dap_count)])  3.6 us
    ppermute x1, waiting for transfers between devices, gather_all(): lax.ppermute(packed[None], 'dap', [(src, src ^ half) for src in range(dap...  1.86 us
    pallas_call x1, Pallas kernels, shards_replicated(): pl.pallas_call(pack_kernel, out_shape=jax.ShapeDtypeStruct((rows * residu...  1.2 us
    ppermute x1, waiting for transfers between devices, gather_all(): late = lax.ppermute(held[-1], 'sub', sibling)  0.92 us
  transfers between devices with their start and end apart: 7, of which 5 were waited for; matrix products, arithmetic and copies ran while one was open for 0% of the time, Pallas kernels for 0%

profile of v23, /device:TPU:0, one launch (start us, length us, event | category | flops | bytes accessed | tf_op | source)
XLA Modules:
  0.0 19.9 jit_solution(163591763430319457)
XLA Ops:
  0.0 1.2 %shard_map.109 = bf16[112,128]{1,0:T(8,128)(2,1)S(1)} custom-call(s32[32]{0:T(128)} %mask_hbm.1, s32[2,32]{1,0:T(2,128)} %bitcast.7, bf16[32,2,256]{2,1,0:T(2,128)(2,1)} %state_hbm.1, bf16[2,32,256]{2,1,0:T(8,128)(2,1)} %bitcast.6, bf16[2,32,128]{2,1,0:T(8,128)(2,1)} %pair_hbm.1), custom_call_target="tpu_custom_call" | custom-call | tf_op jit(solution)/shard_map/pallas_call | solution.py:322
  1.2 4.1 %collective-permute-start = (bf16[1,112,128]{2,1,0:T(8,128)(2,1)S(1)}, bf16[1,112,128]{2,1,0:T(8,128)(2,1)S(1)}, u32[]{:S(2)}, u32[]{:S(2)}) collective-permute-start(bf16[1,112,128]{2,1,0:T(8,128)(2,1)S(1)} %bitcast.4), channel_id=1, source_target_pairs={{0,8},{2,10},{4,12},{6,14},{8,0},{10,2},{12,4},{14,6},{1,9},{3,11}... | collective-permute-start | bytes 86024 | tf_op jit(solution)/shard_map/ppermute | solution.py:277
  5.3 1.9 %collective-permute-done = bf16[1,112,128]{2,1,0:T(8,128)(2,1)S(1)} collective-permute-done((bf16[1,112,128]{2,1,0:T(8,128)(2,1)S(1)}, bf16[1,112,128]{2,1,0:T(8,128)(2,1)S(1)}, u32[]{:S(2)}, u32[]{:S(2)}) %collective-permute-start) | collective-permute-done | bytes 28704 | tf_op jit(solution)/shard_map/ppermute | solution.py:277
  7.2 2.1 %collective-permute-start.1 = (bf16[2,112,128]{2,1,0:T(8,128)(2,1)S(1)}, bf16[2,112,128]{2,1,0:T(8,128)(2,1)S(1)}, u32[]{:S(2)}, u32[]{:S(2)}) collective-permute-start(bf16[2,112,128]{2,1,0:T(8,128)(2,1)S(1)} %pad_maximum_fusion.2), channel_id=1, source_target_pairs={{0,2},{2,0},{4,6},{6,4},{8,10},{10,8},{12,14},{14,12},{1,3},{3,1},... | collective-permute-start | bytes 172040 | tf_op jit(solution)/shard_map/ppermute | solution.py:280
  9.2 1.4 %collective-permute-start.2 = (bf16[2,112,128]{2,1,0:T(8,128)(2,1)S(1)}, bf16[2,112,128]{2,1,0:T(8,128)(2,1)S(1)}, u32[]{:S(2)}, u32[]{:S(2)}) collective-permute-start(bf16[2,112,128]{2,1,0:T(8,128)(2,1)S(1)} %pad_maximum_fusion.2), channel_id=1, source_target_pairs={{0,6},{2,4},{4,2},{6,0},{8,14},{10,12},{12,10},{14,8},{1,7},{3,5},... | collective-permute-start | bytes 172040 | tf_op jit(solution)/shard_map/ppermute | solution.py:280
  10.6 0.2 collective-permute-start.3
  10.8 0.0 collective-permute-start.4
  10.8 1.2 %collective-permute-done.1 = bf16[2,112,128]{2,1,0:T(8,128)(2,1)S(1)} collective-permute-done((bf16[2,112,128]{2,1,0:T(8,128)(2,1)S(1)}, bf16[2,112,128]{2,1,0:T(8,128)(2,1)S(1)}, u32[]{:S(2)}, u32[]{:S(2)}) %collective-permute-start.1) | collective-permute-done | bytes 57376 | tf_op jit(solution)/shard_map/ppermute | solution.py:280
  12.0 2.3 %collective-permute-done.2 = bf16[2,112,128]{2,1,0:T(8,128)(2,1)S(1)} collective-permute-done((bf16[2,112,128]{2,1,0:T(8,128)(2,1)S(1)}, bf16[2,112,128]{2,1,0:T(8,128)(2,1)S(1)}, u32[]{:S(2)}, u32[]{:S(2)}) %collective-permute-start.2) | collective-permute-done | bytes 57376 | tf_op jit(solution)/shard_map/ppermute | solution.py:280
  14.3 0.1 collective-permute-start.5
  14.4 0.0 copy-start.5
  14.4 0.0 copy-start.3
  14.5 0.0 copy-start
  14.5 0.3 %collective-permute-done.3 = bf16[2,112,128]{2,1,0:T(8,128)(2,1)S(1)} collective-permute-done((bf16[2,112,128]{2,1,0:T(8,128)(2,1)S(1)}, bf16[2,112,128]{2,1,0:T(8,128)(2,1)S(1)}, u32[]{:S(2)}, u32[]{:S(2)}) %collective-permute-start.3) | collective-permute-done | bytes 57376 | tf_op jit(solution)/shard_map/ppermute | solution.py:280
  14.8 0.3 %collective-permute-start.6 = (bf16[2,112,128]{2,1,0:T(8,128)(2,1)S(1)}, bf16[2,112,128]{2,1,0:T(8,128)(2,1)S(1)}, u32[]{:S(2)}, u32[]{:S(2)}) collective-permute-start(bf16[2,112,128]{2,1,0:T(8,128)(2,1)S(1)} %collective-permute-done.3), channel_id=1, source_target_pairs={{0,1},{1,0},{2,3},{3,2},{4,5},{5,4},{6,7},{7,6},{8,9},{9,8},{10,11... | collective-permute-start | bytes 172040 | tf_op jit(solution)/shard_map/ppermute | solution.py:286
  15.0 0.0 copy-start.1
  15.1 0.0 copy-start.2
  15.1 0.0 copy-start.4
  15.1 0.0 collective-permute-done.4
  15.1 0.9 %collective-permute-done.6 = bf16[2,112,128]{2,1,0:T(8,128)(2,1)S(1)} collective-permute-done((bf16[2,112,128]{2,1,0:T(8,128)(2,1)S(1)}, bf16[2,112,128]{2,1,0:T(8,128)(2,1)S(1)}, u32[]{:S(2)}, u32[]{:S(2)}) %collective-permute-start.6) | collective-permute-done | bytes 57376 | tf_op jit(solution)/shard_map/ppermute | solution.py:286
  16.0 0.0 collective-permute-done.5
  16.1 0.0 copy-done.5
  16.1 0.0 copy-done.3
  16.1 3.8 %shard_map.110 = bf16[2,32,128]{2,1,0:T(8,128)(2,1)} custom-call(bf16[8,112,128]{2,1,0:T(8,128)(2,1)S(1)} %constant_dynamic-update-slice_fusion.held_ref, bf16[8,112,128]{2,1,0:T(8,128)(2,1)S(1)} %pad_maximum_fusion.other_ref, bf16[32,32,128]{2,1,0:T(8,128)(2,1)S(1)} %copy-done, bf16[4,128,128]{2,1,0:T(8,128)(2,1)S(1)} %copy-done.1, ...), custom_call_target="tpu_custom_call" | custom-call | tf_op jit(solution)/shard_map/pallas_call | solution.py:352
  (12 shorter events, 0.1 us)
Async XLA Ops:
  1.2 6.0 %collective-permute-start = (bf16[1,112,128]{2,1,0:T(8,128)(2,1)S(1)}, bf16[1,112,128]{2,1,0:T(8,128)(2,1)S(1)}, u32[]{:S(2)}, u32[]{:S(2)}) collective-permute-start(bf16[1,112,128]{2,1,0:T(8,128)(2,1)S(1)} %bitcast.4), channel_id=1, source_target_pairs={{0,8},{2,10},{4,12},{6,14},{8,0},{10,2},{12,4},{14,6},{1,9},{3,11}... | collective-permute-start | bytes 86024 | tf_op jit(solution)/shard_map/ppermute | solution.py:277
  7.2 4.9 %collective-permute-start.1 = (bf16[2,112,128]{2,1,0:T(8,128)(2,1)S(1)}, bf16[2,112,128]{2,1,0:T(8,128)(2,1)S(1)}, u32[]{:S(2)}, u32[]{:S(2)}) collective-permute-start(bf16[2,112,128]{2,1,0:T(8,128)(2,1)S(1)} %pad_maximum_fusion.2), channel_id=1, source_target_pairs={{0,2},{2,0},{4,6},{6,4},{8,10},{10,8},{12,14},{14,12},{1,3},{3,1},... | collective-permute-start | bytes 172040 | tf_op jit(solution)/shard_map/ppermute | solution.py:280
  9.2 5.1 %collective-permute-start.2 = (bf16[2,112,128]{2,1,0:T(8,128)(2,1)S(1)}, bf16[2,112,128]{2,1,0:T(8,128)(2,1)S(1)}, u32[]{:S(2)}, u32[]{:S(2)}) collective-permute-start(bf16[2,112,128]{2,1,0:T(8,128)(2,1)S(1)} %pad_maximum_fusion.2), channel_id=1, source_target_pairs={{0,6},{2,4},{4,2},{6,0},{8,14},{10,12},{12,10},{14,8},{1,7},{3,5},... | collective-permute-start | bytes 172040 | tf_op jit(solution)/shard_map/ppermute | solution.py:280
  10.6 4.2 %collective-permute-start.3 = (bf16[2,112,128]{2,1,0:T(8,128)(2,1)S(1)}, bf16[2,112,128]{2,1,0:T(8,128)(2,1)S(1)}, u32[]{:S(2)}, u32[]{:S(2)}) collective-permute-start(bf16[2,112,128]{2,1,0:T(8,128)(2,1)S(1)} %pad_maximum_fusion.2), channel_id=1, source_target_pairs={{0,4},{2,6},{4,0},{6,2},{8,12},{10,14},{12,8},{14,10},{1,5},{3,7},... | collective-permute-start | bytes 172040 | tf_op jit(solution)/shard_map/ppermute | solution.py:280
  10.8 4.3 %collective-permute-start.4 = (bf16[2,112,128]{2,1,0:T(8,128)(2,1)S(1)}, bf16[2,112,128]{2,1,0:T(8,128)(2,1)S(1)}, u32[]{:S(2)}, u32[]{:S(2)}) collective-permute-start(bf16[2,112,128]{2,1,0:T(8,128)(2,1)S(1)} %pad_maximum_fusion.2), channel_id=1, source_target_pairs={{0,1},{1,0},{2,3},{3,2},{4,5},{5,4},{6,7},{7,6},{8,9},{9,8},{10,11... | collective-permute-start | bytes 172040 | tf_op jit(solution)/shard_map/ppermute | solution.py:284
  14.3 1.7 %collective-permute-start.5 = (bf16[4,112,128]{2,1,0:T(8,128)(2,1)S(1)}, bf16[4,112,128]{2,1,0:T(8,128)(2,1)S(1)}, u32[]{:S(2)}, u32[]{:S(2)}) collective-permute-start(bf16[4,112,128]{2,1,0:T(8,128)(2,1)S(1)} %pad_maximum_fusion.1), channel_id=1, source_target_pairs={{0,1},{1,0},{2,3},{3,2},{4,5},{5,4},{6,7},{7,6},{8,9},{9,8},{10,11... | collective-permute-start | bytes 344072 | tf_op jit(solution)/shard_map/ppermute | solution.py:285
  14.4 1.7 %copy-start.5 = (bf16[128,128]{1,0:T(8,128)(2,1)S(1)}, bf16[128,128]{1,0:T(8,128)(2,1)}, u32[]{:S(2)}) copy-start(bf16[128,128]{1,0:T(8,128)(2,1)} %output_ref.1) | copy-start | bytes 98308
  14.4 1.6 %copy-start.3 = (bf16[512,128]{1,0:T(8,128)(2,1)S(1)}, bf16[512,128]{1,0:T(8,128)(2,1)}, u32[]{:S(2)}) copy-start(bf16[512,128]{1,0:T(8,128)(2,1)} %down_ref.1) | copy-start | bytes 393220
  14.5 1.6 %copy-start = (bf16[32,32,128]{2,1,0:T(8,128)(2,1)S(1)}, bf16[32,32,128]{2,1,0:T(8,128)(2,1)}, u32[]{:S(2)}) copy-start(bf16[32,32,128]{2,1,0:T(8,128)(2,1)} %outer_ref.1) | copy-start | bytes 786436
  14.8 1.2 %collective-permute-start.6 = (bf16[2,112,128]{2,1,0:T(8,128)(2,1)S(1)}, bf16[2,112,128]{2,1,0:T(8,128)(2,1)S(1)}, u32[]{:S(2)}, u32[]{:S(2)}) collective-permute-start(bf16[2,112,128]{2,1,0:T(8,128)(2,1)S(1)} %collective-permute-done.3), channel_id=1, source_target_pairs={{0,1},{1,0},{2,3},{3,2},{4,5},{5,4},{6,7},{7,6},{8,9},{9,8},{10,11... | collective-permute-start | bytes 172040 | tf_op jit(solution)/shard_map/ppermute | solution.py:286
  15.0 1.0 %copy-start.1 = (bf16[4,128,128]{2,1,0:T(8,128)(2,1)S(1)}, bf16[4,128,128]{2,1,0:T(8,128)(2,1)}, u32[]{:S(2)}) copy-start(bf16[4,128,128]{2,1,0:T(8,128)(2,1)} %triangle_ref.1) | copy-start | bytes 393220
  15.1 1.0 %copy-start.2 = (bf16[128,512]{1,0:T(8,128)(2,1)S(1)}, bf16[128,512]{1,0:T(8,128)(2,1)}, u32[]{:S(2)}) copy-start(bf16[128,512]{1,0:T(8,128)(2,1)} %up_ref.1) | copy-start | bytes 393220
  15.1 1.0 %copy-start.4 = (bf16[128,128]{1,0:T(8,128)(2,1)S(1)}, bf16[128,128]{1,0:T(8,128)(2,1)}, u32[]{:S(2)}) copy-start(bf16[128,128]{1,0:T(8,128)(2,1)} %gate_ref.1) | copy-start | bytes 98308

commit v24 on v22

--- a/solution.py
+++ b/solution.py
@@ -225,9 +225,11 @@
             second_ref[part], block_ref[part, 2 * channels :], preferred_element_type=f32
         )
 
+    left_weight = jnp.concatenate([triangle_ref[0], triangle_ref[1], gate_ref[...]], axis=1)
     right_weight = jnp.concatenate([triangle_ref[2], triangle_ref[3]], axis=1)
-    right_tri = []
     stride = 8
+    sums = [[jnp.zeros((residues, wide), f32) for _ in range(2)] for _ in range(rows)]
+    gates = [[] for _ in range(rows)]
     for first in range(0, residues, stride):
         normed = []
         for k in range(first, first + stride):
@@ -240,31 +242,35 @@
             ln_one = layer_norm(pair_one)
             ln_one_ref[k] = ln_one
             normed.append(ln_one.astype(bf16))
+        own_ln = jnp.concatenate(
+            [ln_one_ref[first : first + stride, start + row] for row in range(rows)], axis=0
+        ).astype(bf16)
+        both = jnp.dot(own_ln, left_weight, preferred_element_type=f32)
+        own_mask = jnp.concatenate([mask[first : first + stride]] * rows, axis=0)
+        left_tri = sigmoid(both[:, :wide]) * both[:, wide : 2 * wide] * own_mask
+        left_tri = left_tri.astype(bf16).astype(f32)
+        gate_out = sigmoid(both[:, 2 * wide :])
         both = jnp.dot(
             jnp.concatenate(normed, axis=0), right_weight, preferred_element_type=f32
         )
-        right_tri.append((sigmoid(both[:, :wide]) * both[:, wide:]).astype(bf16).astype(f32))
+        right_tri = (sigmoid(both[:, :wide]) * both[:, wide:]).astype(bf16).astype(f32)
+        for row in range(rows):
+            gates[row].append(gate_out[row * stride : (row + 1) * stride])
+            for k in range(stride):
+                at = row * stride + k
+                sums[row][k % 2] += (
+                    left_tri[at : at + 1] * right_tri[k * residues : (k + 1) * residues]
+                )
 
     own_pair = jnp.concatenate([pair_one_ref[:, start + row] for row in range(rows)], axis=0)
-    own_ln = jnp.concatenate([ln_one_ref[:, start + row] for row in range(rows)], axis=0).astype(bf16)
-    left_weight = jnp.concatenate([triangle_ref[0], triangle_ref[1]], axis=1)
-    both = jnp.dot(own_ln, left_weight, preferred_element_type=f32)
-    left_tri = sigmoid(both[:, :wide]) * both[:, wide:] * jnp.concatenate([mask] * rows, axis=0)
-    left_tri = left_tri.astype(bf16).astype(f32)
+    gate_out = jnp.concatenate(sum(gates, []), axis=0)
     products = []
     for row in range(rows):
-        sums = [jnp.zeros((residues, wide), f32) for _ in range(4)]
-        for k in range(residues):
-            at = row * residues + k
-            place = (k % stride) * residues
-            sums[k % 4] += left_tri[at : at + 1] * right_tri[k // stride][place : place + residues]
-        total = (sums[0] + sums[1]) + (sums[2] + sums[3])
         own_mask = keep_ref[pl.ds(start + row, 1), :][:, sequences : sequences + 1]
-        products.append(total * (mask * own_mask))
+        products.append((sums[row][0] + sums[row][1]) * (mask * own_mask))
     product = jnp.concatenate(products, axis=0).astype(bf16).astype(f32)
     normed = layer_norm(product).astype(bf16)
     update = jnp.dot(normed, output_ref[...], preferred_element_type=f32)
-    gate_out = sigmoid(jnp.dot(own_ln, gate_ref[...], preferred_element_type=f32))
     pair_two = (own_pair + gate_out * update).astype(bf16).astype(f32)
     ln_two = layer_norm(pair_two).astype(bf16)
     hidden = jnp.maximum(jnp.dot(ln_two, up_ref[...], preferred_element_type=f32), 0.0).astype(bf16)

time: 20.1 us -> 20.1 us (level)
  no operation moved by 1% of the time
where the time goes in v24:
time: 20.1 us; the launch traced here: 19.9 us
  starting transfers between devices  8.03 us (40%)
  waiting for transfers between devices  6.6 us (33%)
  Pallas kernels  5.01 us (25%)
    ppermute x1, starting transfers between devices, gather_all(): lax.ppermute(packed[None], 'dap', [(src, src ^ half) for src in range(dap...  4.1 us
    ppermute x3, waiting for transfers between devices, gather_all(): lax.ppermute(both, 'dap', [(src, src ^ offset) for src in range(dap_count)])  3.82 us
    pallas_call x1, Pallas kernels, shards_replicated(): pl.pallas_call(update_kernel, out_shape=jax.ShapeDtypeStruct(pairwise_sta...  3.81 us
    ppermute x3, starting transfers between devices, gather_all(): lax.ppermute(both, 'dap', [(src, src ^ offset) for src in range(dap_count)])  3.6 us
    ppermute x1, waiting for transfers between devices, gather_all(): lax.ppermute(packed[None], 'dap', [(src, src ^ half) for src in range(dap...  1.86 us
    pallas_call x1, Pallas kernels, shards_replicated(): pl.pallas_call(pack_kernel, out_shape=jax.ShapeDtypeStruct((rows * residu...  1.2 us
    ppermute x1, waiting for transfers between devices, gather_all(): late = lax.ppermute(held[-1], 'sub', sibling)  0.92 us
  transfers between devices with their start and end apart: 7, of which 5 were waited for; matrix products, arithmetic and copies ran while one was open for 0% of the time, Pallas kernels for 0%

profile of v24, /device:TPU:0, one launch (start us, length us, event | category | flops | bytes accessed | tf_op | source)
XLA Modules:
  0.0 19.9 jit_solution(11595307943558295977)
XLA Ops:
  0.0 1.2 %shard_map.109 = bf16[112,128]{1,0:T(8,128)(2,1)S(1)} custom-call(s32[32]{0:T(128)} %mask_hbm.1, s32[2,32]{1,0:T(2,128)} %bitcast.7, bf16[32,2,256]{2,1,0:T(2,128)(2,1)} %state_hbm.1, bf16[2,32,256]{2,1,0:T(8,128)(2,1)} %bitcast.6, bf16[2,32,128]{2,1,0:T(8,128)(2,1)} %pair_hbm.1), custom_call_target="tpu_custom_call" | custom-call | tf_op jit(solution)/shard_map/pallas_call | solution.py:329
  1.2 4.1 %collective-permute-start = (bf16[1,112,128]{2,1,0:T(8,128)(2,1)S(1)}, bf16[1,112,128]{2,1,0:T(8,128)(2,1)S(1)}, u32[]{:S(2)}, u32[]{:S(2)}) collective-permute-start(bf16[1,112,128]{2,1,0:T(8,128)(2,1)S(1)} %bitcast.4), channel_id=1, source_target_pairs={{0,8},{2,10},{4,12},{6,14},{8,0},{10,2},{12,4},{14,6},{1,9},{3,11}... | collective-permute-start | bytes 86024 | tf_op jit(solution)/shard_map/ppermute | solution.py:284
  5.3 1.9 %collective-permute-done = bf16[1,112,128]{2,1,0:T(8,128)(2,1)S(1)} collective-permute-done((bf16[1,112,128]{2,1,0:T(8,128)(2,1)S(1)}, bf16[1,112,128]{2,1,0:T(8,128)(2,1)S(1)}, u32[]{:S(2)}, u32[]{:S(2)}) %collective-permute-start) | collective-permute-done | bytes 28704 | tf_op jit(solution)/shard_map/ppermute | solution.py:284
  7.2 2.1 %collective-permute-start.1 = (bf16[2,112,128]{2,1,0:T(8,128)(2,1)S(1)}, bf16[2,112,128]{2,1,0:T(8,128)(2,1)S(1)}, u32[]{:S(2)}, u32[]{:S(2)}) collective-permute-start(bf16[2,112,128]{2,1,0:T(8,128)(2,1)S(1)} %pad_maximum_fusion.2), channel_id=1, source_target_pairs={{0,2},{2,0},{4,6},{6,4},{8,10},{10,8},{12,14},{14,12},{1,3},{3,1},... | collective-permute-start | bytes 172040 | tf_op jit(solution)/shard_map/ppermute | solution.py:287
  9.2 1.4 %collective-permute-start.2 = (bf16[2,112,128]{2,1,0:T(8,128)(2,1)S(1)}, bf16[2,112,128]{2,1,0:T(8,128)(2,1)S(1)}, u32[]{:S(2)}, u32[]{:S(2)}) collective-permute-start(bf16[2,112,128]{2,1,0:T(8,128)(2,1)S(1)} %pad_maximum_fusion.2), channel_id=1, source_target_pairs={{0,6},{2,4},{4,2},{6,0},{8,14},{10,12},{12,10},{14,8},{1,7},{3,5},... | collective-permute-start | bytes 172040 | tf_op jit(solution)/shard_map/ppermute | solution.py:287
  10.6 0.2 collective-permute-start.3
  10.8 0.0 collective-permute-start.4
  10.8 1.2 %collective-permute-done.1 = bf16[2,112,128]{2,1,0:T(8,128)(2,1)S(1)} collective-permute-done((bf16[2,112,128]{2,1,0:T(8,128)(2,1)S(1)}, bf16[2,112,128]{2,1,0:T(8,128)(2,1)S(1)}, u32[]{:S(2)}, u32[]{:S(2)}) %collective-permute-start.1) | collective-permute-done | bytes 57376 | tf_op jit(solution)/shard_map/ppermute | solution.py:287
  12.0 2.3 %collective-permute-done.2 = bf16[2,112,128]{2,1,0:T(8,128)(2,1)S(1)} collective-permute-done((bf16[2,112,128]{2,1,0:T(8,128)(2,1)S(1)}, bf16[2,112,128]{2,1,0:T(8,128)(2,1)S(1)}, u32[]{:S(2)}, u32[]{:S(2)}) %collective-permute-start.2) | collective-permute-done | bytes 57376 | tf_op jit(solution)/shard_map/ppermute | solution.py:287
  14.3 0.1 collective-permute-start.5
  14.4 0.0 copy-start.5
  14.4 0.0 copy-start.3
  14.5 0.0 copy-start
  14.5 0.3 %collective-permute-done.3 = bf16[2,112,128]{2,1,0:T(8,128)(2,1)S(1)} collective-permute-done((bf16[2,112,128]{2,1,0:T(8,128)(2,1)S(1)}, bf16[2,112,128]{2,1,0:T(8,128)(2,1)S(1)}, u32[]{:S(2)}, u32[]{:S(2)}) %collective-permute-start.3) | collective-permute-done | bytes 57376 | tf_op jit(solution)/shard_map/ppermute | solution.py:287
  14.8 0.3 %collective-permute-start.6 = (bf16[2,112,128]{2,1,0:T(8,128)(2,1)S(1)}, bf16[2,112,128]{2,1,0:T(8,128)(2,1)S(1)}, u32[]{:S(2)}, u32[]{:S(2)}) collective-permute-start(bf16[2,112,128]{2,1,0:T(8,128)(2,1)S(1)} %collective-permute-done.3), channel_id=1, source_target_pairs={{0,1},{1,0},{2,3},{3,2},{4,5},{5,4},{6,7},{7,6},{8,9},{9,8},{10,11... | collective-permute-start | bytes 172040 | tf_op jit(solution)/shard_map/ppermute | solution.py:293
  15.0 0.0 copy-start.1
  15.1 0.0 copy-start.2
  15.1 0.0 copy-start.4
  15.1 0.0 collective-permute-done.4
  15.1 0.9 %collective-permute-done.6 = bf16[2,112,128]{2,1,0:T(8,128)(2,1)S(1)} collective-permute-done((bf16[2,112,128]{2,1,0:T(8,128)(2,1)S(1)}, bf16[2,112,128]{2,1,0:T(8,128)(2,1)S(1)}, u32[]{:S(2)}, u32[]{:S(2)}) %collective-permute-start.6) | collective-permute-done | bytes 57376 | tf_op jit(solution)/shard_map/ppermute | solution.py:293
  16.0 0.0 collective-permute-done.5
  16.1 0.0 copy-done.5
  16.1 0.0 copy-done.3
  16.1 3.8 %shard_map.110 = bf16[2,32,128]{2,1,0:T(8,128)(2,1)} custom-call(bf16[8,112,128]{2,1,0:T(8,128)(2,1)S(1)} %constant_dynamic-update-slice_fusion.held_ref, bf16[8,112,128]{2,1,0:T(8,128)(2,1)S(1)} %pad_maximum_fusion.other_ref, bf16[32,32,128]{2,1,0:T(8,128)(2,1)S(1)} %copy-done, bf16[4,128,128]{2,1,0:T(8,128)(2,1)S(1)} %copy-done.1, ...), custom_call_target="tpu_custom_call" | custom-call | tf_op jit(solution)/shard_map/pallas_call | solution.py:359
  (12 shorter events, 0.1 us)
Async XLA Ops:
  1.2 6.0 %collective-permute-start = (bf16[1,112,128]{2,1,0:T(8,128)(2,1)S(1)}, bf16[1,112,128]{2,1,0:T(8,128)(2,1)S(1)}, u32[]{:S(2)}, u32[]{:S(2)}) collective-permute-start(bf16[1,112,128]{2,1,0:T(8,128)(2,1)S(1)} %bitcast.4), channel_id=1, source_target_pairs={{0,8},{2,10},{4,12},{6,14},{8,0},{10,2},{12,4},{14,6},{1,9},{3,11}... | collective-permute-start | bytes 86024 | tf_op jit(solution)/shard_map/ppermute | solution.py:284
  7.2 4.9 %collective-permute-start.1 = (bf16[2,112,128]{2,1,0:T(8,128)(2,1)S(1)}, bf16[2,112,128]{2,1,0:T(8,128)(2,1)S(1)}, u32[]{:S(2)}, u32[]{:S(2)}) collective-permute-start(bf16[2,112,128]{2,1,0:T(8,128)(2,1)S(1)} %pad_maximum_fusion.2), channel_id=1, source_target_pairs={{0,2},{2,0},{4,6},{6,4},{8,10},{10,8},{12,14},{14,12},{1,3},{3,1},... | collective-permute-start | bytes 172040 | tf_op jit(solution)/shard_map/ppermute | solution.py:287
  9.2 5.1 %collective-permute-start.2 = (bf16[2,112,128]{2,1,0:T(8,128)(2,1)S(1)}, bf16[2,112,128]{2,1,0:T(8,128)(2,1)S(1)}, u32[]{:S(2)}, u32[]{:S(2)}) collective-permute-start(bf16[2,112,128]{2,1,0:T(8,128)(2,1)S(1)} %pad_maximum_fusion.2), channel_id=1, source_target_pairs={{0,6},{2,4},{4,2},{6,0},{8,14},{10,12},{12,10},{14,8},{1,7},{3,5},... | collective-permute-start | bytes 172040 | tf_op jit(solution)/shard_map/ppermute | solution.py:287
  10.6 4.2 %collective-permute-start.3 = (bf16[2,112,128]{2,1,0:T(8,128)(2,1)S(1)}, bf16[2,112,128]{2,1,0:T(8,128)(2,1)S(1)}, u32[]{:S(2)}, u32[]{:S(2)}) collective-permute-start(bf16[2,112,128]{2,1,0:T(8,128)(2,1)S(1)} %pad_maximum_fusion.2), channel_id=1, source_target_pairs={{0,4},{2,6},{4,0},{6,2},{8,12},{10,14},{12,8},{14,10},{1,5},{3,7},... | collective-permute-start | bytes 172040 | tf_op jit(solution)/shard_map/ppermute | solution.py:287
  10.8 4.3 %collective-permute-start.4 = (bf16[2,112,128]{2,1,0:T(8,128)(2,1)S(1)}, bf16[2,112,128]{2,1,0:T(8,128)(2,1)S(1)}, u32[]{:S(2)}, u32[]{:S(2)}) collective-permute-start(bf16[2,112,128]{2,1,0:T(8,128)(2,1)S(1)} %pad_maximum_fusion.2), channel_id=1, source_target_pairs={{0,1},{1,0},{2,3},{3,2},{4,5},{5,4},{6,7},{7,6},{8,9},{9,8},{10,11... | collective-permute-start | bytes 172040 | tf_op jit(solution)/shard_map/ppermute | solution.py:291
  14.3 1.7 %collective-permute-start.5 = (bf16[4,112,128]{2,1,0:T(8,128)(2,1)S(1)}, bf16[4,112,128]{2,1,0:T(8,128)(2,1)S(1)}, u32[]{:S(2)}, u32[]{:S(2)}) collective-permute-start(bf16[4,112,128]{2,1,0:T(8,128)(2,1)S(1)} %pad_maximum_fusion.1), channel_id=1, source_target_pairs={{0,1},{1,0},{2,3},{3,2},{4,5},{5,4},{6,7},{7,6},{8,9},{9,8},{10,11... | collective-permute-start | bytes 344072 | tf_op jit(solution)/shard_map/ppermute | solution.py:292
  14.4 1.7 %copy-start.5 = (bf16[128,128]{1,0:T(8,128)(2,1)S(1)}, bf16[128,128]{1,0:T(8,128)(2,1)}, u32[]{:S(2)}) copy-start(bf16[128,128]{1,0:T(8,128)(2,1)} %output_ref.1) | copy-start | bytes 98308
  14.4 1.6 %copy-start.3 = (bf16[512,128]{1,0:T(8,128)(2,1)S(1)}, bf16[512,128]{1,0:T(8,128)(2,1)}, u32[]{:S(2)}) copy-start(bf16[512,128]{1,0:T(8,128)(2,1)} %down_ref.1) | copy-start | bytes 393220
  14.5 1.6 %copy-start = (bf16[32,32,128]{2,1,0:T(8,128)(2,1)S(1)}, bf16[32,32,128]{2,1,0:T(8,128)(2,1)}, u32[]{:S(2)}) copy-start(bf16[32,32,128]{2,1,0:T(8,128)(2,1)} %outer_ref.1) | copy-start | bytes 786436
  14.8 1.2 %collective-permute-start.6 = (bf16[2,112,128]{2,1,0:T(8,128)(2,1)S(1)}, bf16[2,112,128]{2,1,0:T(8,128)(2,1)S(1)}, u32[]{:S(2)}, u32[]{:S(2)}) collective-permute-start(bf16[2,112,128]{2,1,0:T(8,128)(2,1)S(1)} %collective-permute-done.3), channel_id=1, source_target_pairs={{0,1},{1,0},{2,3},{3,2},{4,5},{5,4},{6,7},{7,6},{8,9},{9,8},{10,11... | collective-permute-start | bytes 172040 | tf_op jit(solution)/shard_map/ppermute | solution.py:293
  15.0 1.0 %copy-start.1 = (bf16[4,128,128]{2,1,0:T(8,128)(2,1)S(1)}, bf16[4,128,128]{2,1,0:T(8,128)(2,1)}, u32[]{:S(2)}) copy-start(bf16[4,128,128]{2,1,0:T(8,128)(2,1)} %triangle_ref.1) | copy-start | bytes 393220
  15.1 1.0 %copy-start.2 = (bf16[128,512]{1,0:T(8,128)(2,1)S(1)}, bf16[128,512]{1,0:T(8,128)(2,1)}, u32[]{:S(2)}) copy-start(bf16[128,512]{1,0:T(8,128)(2,1)} %up_ref.1) | copy-start | bytes 393220
  15.1 1.0 %copy-start.4 = (bf16[128,128]{1,0:T(8,128)(2,1)S(1)}, bf16[128,128]{1,0:T(8,128)(2,1)}, u32[]{:S(2)}) copy-start(bf16[128,128]{1,0:T(8,128)(2,1)} %gate_ref.1) | copy-start | bytes 98308

commit v25 on v22

--- a/solution.py
+++ b/solution.py
@@ -290,14 +290,16 @@
 
 def swap_order(dap_count):
     near = dap_count // 2
-    return [1, near - 1] + list(range(2, near - 1))
+    return list(range(2, near - 1)) + [near - 1, 1]
 
 
 def block_place(chip, chips):
     offset = lax.bitwise_xor(lax.axis_index("dap"), chip)
     half = chips // 2
     near = jnp.where(offset >= half, offset - half, offset)
-    turn = jnp.where(near > 1, jnp.where(near == half - 1, 2, near + 1), near)
+    turn = 0
+    for place, one in enumerate(swap_order(chips)):
+        turn = turn + jnp.where(near == one, place + 1, 0)
     return 2 * turn + jnp.where(offset >= half, 1, 0)
 
 

time: 20.1 us -> 20.2 us (level)
  waiting for transfers between devices: 6.6 us -> 6.95 us
  starting transfers between devices: 8.03 us -> 7.79 us
where the time goes in v25:
time: 20.2 us; the launch traced here: 20 us
  starting transfers between devices  7.79 us (39%)
  waiting for transfers between devices  6.95 us (34%)
  Pallas kernels  5.01 us (25%)
    ppermute x1, starting transfers between devices, gather_all(): lax.ppermute(packed[None], 'dap', [(src, src ^ half) for src in range(dap...  4.1 us
    ppermute x3, waiting for transfers between devices, gather_all(): lax.ppermute(both, 'dap', [(src, src ^ offset) for src in range(dap_count)])  3.96 us
    pallas_call x1, Pallas kernels, shards_replicated(): pl.pallas_call(update_kernel, out_shape=jax.ShapeDtypeStruct(pairwise_sta...  3.81 us
    ppermute x3, starting transfers between devices, gather_all(): lax.ppermute(both, 'dap', [(src, src ^ offset) for src in range(dap_count)])  3.55 us
    ppermute x1, waiting for transfers between devices, gather_all(): lax.ppermute(packed[None], 'dap', [(src, src ^ half) for src in range(dap...  1.86 us
    pallas_call x1, Pallas kernels, shards_replicated(): pl.pallas_call(pack_kernel, out_shape=jax.ShapeDtypeStruct((rows * residu...  1.2 us
    ppermute x1, waiting for transfers between devices, gather_all(): late = lax.ppermute(held[-1], 'sub', sibling)  1.12 us
  transfers between devices with their start and end apart: 7, of which 5 were waited for; matrix products, arithmetic and copies ran while one was open for 0% of the time, Pallas kernels for 0%

profile of v25, /device:TPU:0, one launch (start us, length us, event | category | flops | bytes accessed | tf_op | source)
XLA Modules:
  0.0 20.0 jit_solution(18088992303200526874)
XLA Ops:
  0.0 1.2 %shard_map.109 = bf16[112,128]{1,0:T(8,128)(2,1)S(1)} custom-call(s32[32]{0:T(128)} %mask_hbm.1, s32[2,32]{1,0:T(2,128)} %bitcast.7, bf16[32,2,256]{2,1,0:T(2,128)(2,1)} %state_hbm.1, bf16[2,32,256]{2,1,0:T(8,128)(2,1)} %bitcast.6, bf16[2,32,128]{2,1,0:T(8,128)(2,1)} %pair_hbm.1), custom_call_target="tpu_custom_call" | custom-call | tf_op jit(solution)/shard_map/pallas_call | solution.py:325
  1.2 4.1 %collective-permute-start = (bf16[1,112,128]{2,1,0:T(8,128)(2,1)S(1)}, bf16[1,112,128]{2,1,0:T(8,128)(2,1)S(1)}, u32[]{:S(2)}, u32[]{:S(2)}) collective-permute-start(bf16[1,112,128]{2,1,0:T(8,128)(2,1)S(1)} %bitcast.4), channel_id=1, source_target_pairs={{0,8},{2,10},{4,12},{6,14},{8,0},{10,2},{12,4},{14,6},{1,9},{3,11}... | collective-permute-start | bytes 86024 | tf_op jit(solution)/shard_map/ppermute | solution.py:278
  5.3 1.9 %collective-permute-done = bf16[1,112,128]{2,1,0:T(8,128)(2,1)S(1)} collective-permute-done((bf16[1,112,128]{2,1,0:T(8,128)(2,1)S(1)}, bf16[1,112,128]{2,1,0:T(8,128)(2,1)S(1)}, u32[]{:S(2)}, u32[]{:S(2)}) %collective-permute-start) | collective-permute-done | bytes 28704 | tf_op jit(solution)/shard_map/ppermute | solution.py:278
  7.2 2.0 %collective-permute-start.1 = (bf16[2,112,128]{2,1,0:T(8,128)(2,1)S(1)}, bf16[2,112,128]{2,1,0:T(8,128)(2,1)S(1)}, u32[]{:S(2)}, u32[]{:S(2)}) collective-permute-start(bf16[2,112,128]{2,1,0:T(8,128)(2,1)S(1)} %pad_maximum_fusion.2), channel_id=1, source_target_pairs={{0,4},{2,6},{4,0},{6,2},{8,12},{10,14},{12,8},{14,10},{1,5},{3,7},... | collective-permute-start | bytes 172040 | tf_op jit(solution)/shard_map/ppermute | solution.py:281
  9.1 1.6 %collective-permute-start.2 = (bf16[2,112,128]{2,1,0:T(8,128)(2,1)S(1)}, bf16[2,112,128]{2,1,0:T(8,128)(2,1)S(1)}, u32[]{:S(2)}, u32[]{:S(2)}) collective-permute-start(bf16[2,112,128]{2,1,0:T(8,128)(2,1)S(1)} %pad_maximum_fusion.2), channel_id=1, source_target_pairs={{0,6},{2,4},{4,2},{6,0},{8,14},{10,12},{12,10},{14,8},{1,7},{3,5},... | collective-permute-start | bytes 172040 | tf_op jit(solution)/shard_map/ppermute | solution.py:281
  10.7 0.0 collective-permute-start.3
  10.7 0.0 collective-permute-start.4
  10.7 1.0 %collective-permute-done.1 = bf16[2,112,128]{2,1,0:T(8,128)(2,1)S(1)} collective-permute-done((bf16[2,112,128]{2,1,0:T(8,128)(2,1)S(1)}, bf16[2,112,128]{2,1,0:T(8,128)(2,1)S(1)}, u32[]{:S(2)}, u32[]{:S(2)}) %collective-permute-start.1) | collective-permute-done | bytes 57376 | tf_op jit(solution)/shard_map/ppermute | solution.py:281
  11.8 2.5 %collective-permute-done.2 = bf16[2,112,128]{2,1,0:T(8,128)(2,1)S(1)} collective-permute-done((bf16[2,112,128]{2,1,0:T(8,128)(2,1)S(1)}, bf16[2,112,128]{2,1,0:T(8,128)(2,1)S(1)}, u32[]{:S(2)}, u32[]{:S(2)}) %collective-permute-start.2) | collective-permute-done | bytes 57376 | tf_op jit(solution)/shard_map/ppermute | solution.py:281
  14.2 0.1 collective-permute-start.5
  14.3 0.0 copy-start.5
  14.3 0.0 copy-start.3
  14.4 0.0 copy-start
  14.4 0.5 %collective-permute-done.3 = bf16[2,112,128]{2,1,0:T(8,128)(2,1)S(1)} collective-permute-done((bf16[2,112,128]{2,1,0:T(8,128)(2,1)S(1)}, bf16[2,112,128]{2,1,0:T(8,128)(2,1)S(1)}, u32[]{:S(2)}, u32[]{:S(2)}) %collective-permute-start.3) | collective-permute-done | bytes 57376 | tf_op jit(solution)/shard_map/ppermute | solution.py:281
  14.9 0.1 collective-permute-start.6
  14.9 0.0 copy-start.1
  15.0 0.0 copy-start.2
  15.0 0.0 copy-start.4
  15.0 0.0 collective-permute-done.4
  15.0 1.1 %collective-permute-done.6 = bf16[2,112,128]{2,1,0:T(8,128)(2,1)S(1)} collective-permute-done((bf16[2,112,128]{2,1,0:T(8,128)(2,1)S(1)}, bf16[2,112,128]{2,1,0:T(8,128)(2,1)S(1)}, u32[]{:S(2)}, u32[]{:S(2)}) %collective-permute-start.6) | collective-permute-done | bytes 57376 | tf_op jit(solution)/shard_map/ppermute | solution.py:287
  16.1 0.0 collective-permute-done.5
  16.2 0.0 copy-done.5
  16.2 0.0 copy-done.3
  16.2 3.8 %shard_map.110 = bf16[2,32,128]{2,1,0:T(8,128)(2,1)} custom-call(bf16[8,112,128]{2,1,0:T(8,128)(2,1)S(1)} %constant_dynamic-update-slice_fusion.held_ref, bf16[8,112,128]{2,1,0:T(8,128)(2,1)S(1)} %pad_maximum_fusion.other_ref, bf16[32,32,128]{2,1,0:T(8,128)(2,1)S(1)} %copy-done, bf16[4,128,128]{2,1,0:T(8,128)(2,1)S(1)} %copy-done.1, ...), custom_call_target="tpu_custom_call" | custom-call | tf_op jit(solution)/shard_map/pallas_call | solution.py:355
  (12 shorter events, 0.1 us)
Async XLA Ops:
  1.2 6.0 %collective-permute-start = (bf16[1,112,128]{2,1,0:T(8,128)(2,1)S(1)}, bf16[1,112,128]{2,1,0:T(8,128)(2,1)S(1)}, u32[]{:S(2)}, u32[]{:S(2)}) collective-permute-start(bf16[1,112,128]{2,1,0:T(8,128)(2,1)S(1)} %bitcast.4), channel_id=1, source_target_pairs={{0,8},{2,10},{4,12},{6,14},{8,0},{10,2},{12,4},{14,6},{1,9},{3,11}... | collective-permute-start | bytes 86024 | tf_op jit(solution)/shard_map/ppermute | solution.py:278
  7.2 4.6 %collective-permute-start.1 = (bf16[2,112,128]{2,1,0:T(8,128)(2,1)S(1)}, bf16[2,112,128]{2,1,0:T(8,128)(2,1)S(1)}, u32[]{:S(2)}, u32[]{:S(2)}) collective-permute-start(bf16[2,112,128]{2,1,0:T(8,128)(2,1)S(1)} %pad_maximum_fusion.2), channel_id=1, source_target_pairs={{0,4},{2,6},{4,0},{6,2},{8,12},{10,14},{12,8},{14,10},{1,5},{3,7},... | collective-permute-start | bytes 172040 | tf_op jit(solution)/shard_map/ppermute | solution.py:281
  9.1 5.1 %collective-permute-start.2 = (bf16[2,112,128]{2,1,0:T(8,128)(2,1)S(1)}, bf16[2,112,128]{2,1,0:T(8,128)(2,1)S(1)}, u32[]{:S(2)}, u32[]{:S(2)}) collective-permute-start(bf16[2,112,128]{2,1,0:T(8,128)(2,1)S(1)} %pad_maximum_fusion.2), channel_id=1, source_target_pairs={{0,6},{2,4},{4,2},{6,0},{8,14},{10,12},{12,10},{14,8},{1,7},{3,5},... | collective-permute-start | bytes 172040 | tf_op jit(solution)/shard_map/ppermute | solution.py:281
  10.7 4.2 %collective-permute-start.3 = (bf16[2,112,128]{2,1,0:T(8,128)(2,1)S(1)}, bf16[2,112,128]{2,1,0:T(8,128)(2,1)S(1)}, u32[]{:S(2)}, u32[]{:S(2)}) collective-permute-start(bf16[2,112,128]{2,1,0:T(8,128)(2,1)S(1)} %pad_maximum_fusion.2), channel_id=1, source_target_pairs={{0,2},{2,0},{4,6},{6,4},{8,10},{10,8},{12,14},{14,12},{1,3},{3,1},... | collective-permute-start | bytes 172040 | tf_op jit(solution)/shard_map/ppermute | solution.py:281
  10.7 4.3 %collective-permute-start.4 = (bf16[2,112,128]{2,1,0:T(8,128)(2,1)S(1)}, bf16[2,112,128]{2,1,0:T(8,128)(2,1)S(1)}, u32[]{:S(2)}, u32[]{:S(2)}) collective-permute-start(bf16[2,112,128]{2,1,0:T(8,128)(2,1)S(1)} %pad_maximum_fusion.2), channel_id=1, source_target_pairs={{0,1},{1,0},{2,3},{3,2},{4,5},{5,4},{6,7},{7,6},{8,9},{9,8},{10,11... | collective-permute-start | bytes 172040 | tf_op jit(solution)/shard_map/ppermute | solution.py:285
  14.2 1.9 %collective-permute-start.5 = (bf16[4,112,128]{2,1,0:T(8,128)(2,1)S(1)}, bf16[4,112,128]{2,1,0:T(8,128)(2,1)S(1)}, u32[]{:S(2)}, u32[]{:S(2)}) collective-permute-start(bf16[4,112,128]{2,1,0:T(8,128)(2,1)S(1)} %pad_maximum_fusion.1), channel_id=1, source_target_pairs={{0,1},{1,0},{2,3},{3,2},{4,5},{5,4},{6,7},{7,6},{8,9},{9,8},{10,11... | collective-permute-start | bytes 344072 | tf_op jit(solution)/shard_map/ppermute | solution.py:286
  14.3 1.8 %copy-start.5 = (bf16[128,128]{1,0:T(8,128)(2,1)S(1)}, bf16[128,128]{1,0:T(8,128)(2,1)}, u32[]{:S(2)}) copy-start(bf16[128,128]{1,0:T(8,128)(2,1)} %output_ref.1) | copy-start | bytes 98308
  14.3 1.8 %copy-start.3 = (bf16[512,128]{1,0:T(8,128)(2,1)S(1)}, bf16[512,128]{1,0:T(8,128)(2,1)}, u32[]{:S(2)}) copy-start(bf16[512,128]{1,0:T(8,128)(2,1)} %down_ref.1) | copy-start | bytes 393220
  14.4 1.8 %copy-start = (bf16[32,32,128]{2,1,0:T(8,128)(2,1)S(1)}, bf16[32,32,128]{2,1,0:T(8,128)(2,1)}, u32[]{:S(2)}) copy-start(bf16[32,32,128]{2,1,0:T(8,128)(2,1)} %outer_ref.1) | copy-start | bytes 786436
  14.9 1.2 %collective-permute-start.6 = (bf16[2,112,128]{2,1,0:T(8,128)(2,1)S(1)}, bf16[2,112,128]{2,1,0:T(8,128)(2,1)S(1)}, u32[]{:S(2)}, u32[]{:S(2)}) collective-permute-start(bf16[2,112,128]{2,1,0:T(8,128)(2,1)S(1)} %collective-permute-done.3), channel_id=1, source_target_pairs={{0,1},{1,0},{2,3},{3,2},{4,5},{5,4},{6,7},{7,6},{8,9},{9,8},{10,11... | collective-permute-start | bytes 172040 | tf_op jit(solution)/shard_map/ppermute | solution.py:287
  14.9 1.2 %copy-start.1 = (bf16[4,128,128]{2,1,0:T(8,128)(2,1)S(1)}, bf16[4,128,128]{2,1,0:T(8,128)(2,1)}, u32[]{:S(2)}) copy-start(bf16[4,128,128]{2,1,0:T(8,128)(2,1)} %triangle_ref.1) | copy-start | bytes 393220
  15.0 1.2 %copy-start.2 = (bf16[128,512]{1,0:T(8,128)(2,1)S(1)}, bf16[128,512]{1,0:T(8,128)(2,1)}, u32[]{:S(2)}) copy-start(bf16[128,512]{1,0:T(8,128)(2,1)} %up_ref.1) | copy-start | bytes 393220
  15.0 1.2 %copy-start.4 = (bf16[128,128]{1,0:T(8,128)(2,1)S(1)}, bf16[128,128]{1,0:T(8,128)(2,1)}, u32[]{:S(2)}) copy-start(bf16[128,128]{1,0:T(8,128)(2,1)} %gate_ref.1) | copy-start | bytes 98308

commit v26 on v22

--- a/solution.py
+++ b/solution.py
@@ -349,7 +349,7 @@
     held, other = gather_all(packed)
     cores, chips = lax.axis_size("sub"), lax.axis_size("dap")
     group = cores * rows
-    parts = 1
+    parts = 2
     return pl.pallas_call(
         update_kernel,
         out_shape=jax.ShapeDtypeStruct(pairwise_state.shape, jnp.bfloat16),

time: 20.1 us -> 20.2 us (level)
  no operation moved by 1% of the time
where the time goes in v26:
time: 20.2 us; the launch traced here: 20 us
  starting transfers between devices  8.03 us (40%)
  waiting for transfers between devices  6.6 us (33%)
  Pallas kernels  5.1 us (25%)
    ppermute x1, starting transfers between devices, gather_all(): lax.ppermute(packed[None], 'dap', [(src, src ^ half) for src in range(dap...  4.1 us
    pallas_call x1, Pallas kernels, shards_replicated(): pl.pallas_call(update_kernel, out_shape=jax.ShapeDtypeStruct(pairwise_sta...  3.91 us
    ppermute x3, waiting for transfers between devices, gather_all(): lax.ppermute(both, 'dap', [(src, src ^ offset) for src in range(dap_count)])  3.82 us
    ppermute x3, starting transfers between devices, gather_all(): lax.ppermute(both, 'dap', [(src, src ^ offset) for src in range(dap_count)])  3.6 us
    ppermute x1, waiting for transfers between devices, gather_all(): lax.ppermute(packed[None], 'dap', [(src, src ^ half) for src in range(dap...  1.86 us
    pallas_call x1, Pallas kernels, shards_replicated(): pl.pallas_call(pack_kernel, out_shape=jax.ShapeDtypeStruct((rows * residu...  1.2 us
    ppermute x1, waiting for transfers between devices, gather_all(): late = lax.ppermute(held[-1], 'sub', sibling)  0.92 us
  transfers between devices with their start and end apart: 7, of which 5 were waited for; matrix products, arithmetic and copies ran while one was open for 0% of the time, Pallas kernels for 0%

profile of v26, /device:TPU:0, one launch (start us, length us, event | category | flops | bytes accessed | tf_op | source)
XLA Modules:
  0.0 20.0 jit_solution(9392104058336281580)
XLA Ops:
  0.0 1.2 %shard_map.109 = bf16[112,128]{1,0:T(8,128)(2,1)S(1)} custom-call(s32[32]{0:T(128)} %mask_hbm.1, s32[2,32]{1,0:T(2,128)} %bitcast.7, bf16[32,2,256]{2,1,0:T(2,128)(2,1)} %state_hbm.1, bf16[2,32,256]{2,1,0:T(8,128)(2,1)} %bitcast.6, bf16[2,32,128]{2,1,0:T(8,128)(2,1)} %pair_hbm.1), custom_call_target="tpu_custom_call" | custom-call | tf_op jit(solution)/shard_map/pallas_call | solution.py:323
  1.2 4.1 %collective-permute-start = (bf16[1,112,128]{2,1,0:T(8,128)(2,1)S(1)}, bf16[1,112,128]{2,1,0:T(8,128)(2,1)S(1)}, u32[]{:S(2)}, u32[]{:S(2)}) collective-permute-start(bf16[1,112,128]{2,1,0:T(8,128)(2,1)S(1)} %bitcast.4), channel_id=1, source_target_pairs={{0,8},{2,10},{4,12},{6,14},{8,0},{10,2},{12,4},{14,6},{1,9},{3,11}... | collective-permute-start | bytes 86024 | tf_op jit(solution)/shard_map/ppermute | solution.py:278
  5.3 1.9 %collective-permute-done = bf16[1,112,128]{2,1,0:T(8,128)(2,1)S(1)} collective-permute-done((bf16[1,112,128]{2,1,0:T(8,128)(2,1)S(1)}, bf16[1,112,128]{2,1,0:T(8,128)(2,1)S(1)}, u32[]{:S(2)}, u32[]{:S(2)}) %collective-permute-start) | collective-permute-done | bytes 28704 | tf_op jit(solution)/shard_map/ppermute | solution.py:278
  7.2 2.1 %collective-permute-start.1 = (bf16[2,112,128]{2,1,0:T(8,128)(2,1)S(1)}, bf16[2,112,128]{2,1,0:T(8,128)(2,1)S(1)}, u32[]{:S(2)}, u32[]{:S(2)}) collective-permute-start(bf16[2,112,128]{2,1,0:T(8,128)(2,1)S(1)} %pad_maximum_fusion.2), channel_id=1, source_target_pairs={{0,2},{2,0},{4,6},{6,4},{8,10},{10,8},{12,14},{14,12},{1,3},{3,1},... | collective-permute-start | bytes 172040 | tf_op jit(solution)/shard_map/ppermute | solution.py:281
  9.2 1.4 %collective-permute-start.2 = (bf16[2,112,128]{2,1,0:T(8,128)(2,1)S(1)}, bf16[2,112,128]{2,1,0:T(8,128)(2,1)S(1)}, u32[]{:S(2)}, u32[]{:S(2)}) collective-permute-start(bf16[2,112,128]{2,1,0:T(8,128)(2,1)S(1)} %pad_maximum_fusion.2), channel_id=1, source_target_pairs={{0,6},{2,4},{4,2},{6,0},{8,14},{10,12},{12,10},{14,8},{1,7},{3,5},... | collective-permute-start | bytes 172040 | tf_op jit(solution)/shard_map/ppermute | solution.py:281
  10.6 0.2 collective-permute-start.3
  10.8 0.0 collective-permute-start.4
  10.8 1.2 %collective-permute-done.1 = bf16[2,112,128]{2,1,0:T(8,128)(2,1)S(1)} collective-permute-done((bf16[2,112,128]{2,1,0:T(8,128)(2,1)S(1)}, bf16[2,112,128]{2,1,0:T(8,128)(2,1)S(1)}, u32[]{:S(2)}, u32[]{:S(2)}) %collective-permute-start.1) | collective-permute-done | bytes 57376 | tf_op jit(solution)/shard_map/ppermute | solution.py:281
  12.0 2.3 %collective-permute-done.2 = bf16[2,112,128]{2,1,0:T(8,128)(2,1)S(1)} collective-permute-done((bf16[2,112,128]{2,1,0:T(8,128)(2,1)S(1)}, bf16[2,112,128]{2,1,0:T(8,128)(2,1)S(1)}, u32[]{:S(2)}, u32[]{:S(2)}) %collective-permute-start.2) | collective-permute-done | bytes 57376 | tf_op jit(solution)/shard_map/ppermute | solution.py:281
  14.3 0.1 collective-permute-start.5
  14.4 0.0 copy-start.5
  14.4 0.0 copy-start.3
  14.5 0.0 copy-start
  14.5 0.3 %collective-permute-done.3 = bf16[2,112,128]{2,1,0:T(8,128)(2,1)S(1)} collective-permute-done((bf16[2,112,128]{2,1,0:T(8,128)(2,1)S(1)}, bf16[2,112,128]{2,1,0:T(8,128)(2,1)S(1)}, u32[]{:S(2)}, u32[]{:S(2)}) %collective-permute-start.3) | collective-permute-done | bytes 57376 | tf_op jit(solution)/shard_map/ppermute | solution.py:281
  14.8 0.3 %collective-permute-start.6 = (bf16[2,112,128]{2,1,0:T(8,128)(2,1)S(1)}, bf16[2,112,128]{2,1,0:T(8,128)(2,1)S(1)}, u32[]{:S(2)}, u32[]{:S(2)}) collective-permute-start(bf16[2,112,128]{2,1,0:T(8,128)(2,1)S(1)} %collective-permute-done.3), channel_id=1, source_target_pairs={{0,1},{1,0},{2,3},{3,2},{4,5},{5,4},{6,7},{7,6},{8,9},{9,8},{10,11... | collective-permute-start | bytes 172040 | tf_op jit(solution)/shard_map/ppermute | solution.py:287
  15.0 0.0 copy-start.1
  15.1 0.0 copy-start.2
  15.1 0.0 copy-start.4
  15.1 0.0 collective-permute-done.4
  15.1 0.9 %collective-permute-done.6 = bf16[2,112,128]{2,1,0:T(8,128)(2,1)S(1)} collective-permute-done((bf16[2,112,128]{2,1,0:T(8,128)(2,1)S(1)}, bf16[2,112,128]{2,1,0:T(8,128)(2,1)S(1)}, u32[]{:S(2)}, u32[]{:S(2)}) %collective-permute-start.6) | collective-permute-done | bytes 57376 | tf_op jit(solution)/shard_map/ppermute | solution.py:287
  16.0 0.0 collective-permute-done.5
  16.1 0.0 copy-done.5
  16.1 0.0 copy-done.3
  16.1 3.9 %shard_map.110 = bf16[2,32,128]{2,1,0:T(8,128)(2,1)} custom-call(bf16[8,112,128]{2,1,0:T(8,128)(2,1)S(1)} %constant_dynamic-update-slice_fusion.held_ref, bf16[8,112,128]{2,1,0:T(8,128)(2,1)S(1)} %pad_maximum_fusion.other_ref, bf16[32,32,128]{2,1,0:T(8,128)(2,1)S(1)} %copy-done, bf16[4,128,128]{2,1,0:T(8,128)(2,1)S(1)} %copy-done.1, ...), custom_call_target="tpu_custom_call" | custom-call | tf_op jit(solution)/shard_map/pallas_call | solution.py:353
  (12 shorter events, 0.1 us)
Async XLA Ops:
  1.2 6.0 %collective-permute-start = (bf16[1,112,128]{2,1,0:T(8,128)(2,1)S(1)}, bf16[1,112,128]{2,1,0:T(8,128)(2,1)S(1)}, u32[]{:S(2)}, u32[]{:S(2)}) collective-permute-start(bf16[1,112,128]{2,1,0:T(8,128)(2,1)S(1)} %bitcast.4), channel_id=1, source_target_pairs={{0,8},{2,10},{4,12},{6,14},{8,0},{10,2},{12,4},{14,6},{1,9},{3,11}... | collective-permute-start | bytes 86024 | tf_op jit(solution)/shard_map/ppermute | solution.py:278
  7.2 4.9 %collective-permute-start.1 = (bf16[2,112,128]{2,1,0:T(8,128)(2,1)S(1)}, bf16[2,112,128]{2,1,0:T(8,128)(2,1)S(1)}, u32[]{:S(2)}, u32[]{:S(2)}) collective-permute-start(bf16[2,112,128]{2,1,0:T(8,128)(2,1)S(1)} %pad_maximum_fusion.2), channel_id=1, source_target_pairs={{0,2},{2,0},{4,6},{6,4},{8,10},{10,8},{12,14},{14,12},{1,3},{3,1},... | collective-permute-start | bytes 172040 | tf_op jit(solution)/shard_map/ppermute | solution.py:281
  9.2 5.1 %collective-permute-start.2 = (bf16[2,112,128]{2,1,0:T(8,128)(2,1)S(1)}, bf16[2,112,128]{2,1,0:T(8,128)(2,1)S(1)}, u32[]{:S(2)}, u32[]{:S(2)}) collective-permute-start(bf16[2,112,128]{2,1,0:T(8,128)(2,1)S(1)} %pad_maximum_fusion.2), channel_id=1, source_target_pairs={{0,6},{2,4},{4,2},{6,0},{8,14},{10,12},{12,10},{14,8},{1,7},{3,5},... | collective-permute-start | bytes 172040 | tf_op jit(solution)/shard_map/ppermute | solution.py:281
  10.6 4.2 %collective-permute-start.3 = (bf16[2,112,128]{2,1,0:T(8,128)(2,1)S(1)}, bf16[2,112,128]{2,1,0:T(8,128)(2,1)S(1)}, u32[]{:S(2)}, u32[]{:S(2)}) collective-permute-start(bf16[2,112,128]{2,1,0:T(8,128)(2,1)S(1)} %pad_maximum_fusion.2), channel_id=1, source_target_pairs={{0,4},{2,6},{4,0},{6,2},{8,12},{10,14},{12,8},{14,10},{1,5},{3,7},... | collective-permute-start | bytes 172040 | tf_op jit(solution)/shard_map/ppermute | solution.py:281
  10.8 4.3 %collective-permute-start.4 = (bf16[2,112,128]{2,1,0:T(8,128)(2,1)S(1)}, bf16[2,112,128]{2,1,0:T(8,128)(2,1)S(1)}, u32[]{:S(2)}, u32[]{:S(2)}) collective-permute-start(bf16[2,112,128]{2,1,0:T(8,128)(2,1)S(1)} %pad_maximum_fusion.2), channel_id=1, source_target_pairs={{0,1},{1,0},{2,3},{3,2},{4,5},{5,4},{6,7},{7,6},{8,9},{9,8},{10,11... | collective-permute-start | bytes 172040 | tf_op jit(solution)/shard_map/ppermute | solution.py:285
  14.3 1.7 %collective-permute-start.5 = (bf16[4,112,128]{2,1,0:T(8,128)(2,1)S(1)}, bf16[4,112,128]{2,1,0:T(8,128)(2,1)S(1)}, u32[]{:S(2)}, u32[]{:S(2)}) collective-permute-start(bf16[4,112,128]{2,1,0:T(8,128)(2,1)S(1)} %pad_maximum_fusion.1), channel_id=1, source_target_pairs={{0,1},{1,0},{2,3},{3,2},{4,5},{5,4},{6,7},{7,6},{8,9},{9,8},{10,11... | collective-permute-start | bytes 344072 | tf_op jit(solution)/shard_map/ppermute | solution.py:286
  14.4 1.7 %copy-start.5 = (bf16[128,128]{1,0:T(8,128)(2,1)S(1)}, bf16[128,128]{1,0:T(8,128)(2,1)}, u32[]{:S(2)}) copy-start(bf16[128,128]{1,0:T(8,128)(2,1)} %output_ref.1) | copy-start | bytes 98308
  14.4 1.6 %copy-start.3 = (bf16[512,128]{1,0:T(8,128)(2,1)S(1)}, bf16[512,128]{1,0:T(8,128)(2,1)}, u32[]{:S(2)}) copy-start(bf16[512,128]{1,0:T(8,128)(2,1)} %down_ref.1) | copy-start | bytes 393220
  14.5 1.6 %copy-start = (bf16[32,32,128]{2,1,0:T(8,128)(2,1)S(1)}, bf16[32,32,128]{2,1,0:T(8,128)(2,1)}, u32[]{:S(2)}) copy-start(bf16[32,32,128]{2,1,0:T(8,128)(2,1)} %outer_ref.1) | copy-start | bytes 786436
  14.8 1.2 %collective-permute-start.6 = (bf16[2,112,128]{2,1,0:T(8,128)(2,1)S(1)}, bf16[2,112,128]{2,1,0:T(8,128)(2,1)S(1)}, u32[]{:S(2)}, u32[]{:S(2)}) collective-permute-start(bf16[2,112,128]{2,1,0:T(8,128)(2,1)S(1)} %collective-permute-done.3), channel_id=1, source_target_pairs={{0,1},{1,0},{2,3},{3,2},{4,5},{5,4},{6,7},{7,6},{8,9},{9,8},{10,11... | collective-permute-start | bytes 172040 | tf_op jit(solution)/shard_map/ppermute | solution.py:287
  15.0 1.0 %copy-start.1 = (bf16[4,128,128]{2,1,0:T(8,128)(2,1)S(1)}, bf16[4,128,128]{2,1,0:T(8,128)(2,1)}, u32[]{:S(2)}) copy-start(bf16[4,128,128]{2,1,0:T(8,128)(2,1)} %triangle_ref.1) | copy-start | bytes 393220
  15.1 1.0 %copy-start.2 = (bf16[128,512]{1,0:T(8,128)(2,1)S(1)}, bf16[128,512]{1,0:T(8,128)(2,1)}, u32[]{:S(2)}) copy-start(bf16[128,512]{1,0:T(8,128)(2,1)} %up_ref.1) | copy-start | bytes 393220
  15.1 1.0 %copy-start.4 = (bf16[128,128]{1,0:T(8,128)(2,1)S(1)}, bf16[128,128]{1,0:T(8,128)(2,1)}, u32[]{:S(2)}) copy-start(bf16[128,128]{1,0:T(8,128)(2,1)} %gate_ref.1) | copy-start | bytes 98308
